TPU v7x, 32 devices: a whole 2x2x4 slice. The times are simulated.
32 devices in a mesh: dp: 8 (over y, x, core), head: 4 (over z).
Axes of the slice: x: 2, y: 2, z: 4, core: 2. Of those that a mesh axis runs over, the one named last changes fastest.
Arguments:
- tokens: bfloat16 [32768, 256], P(('dp', 'head')), may hold values from -6 to 6
- lengths: int32 [128], P('dp'), may hold values from 32 to 256, as said below
- cotangent: bfloat16 [32768, 256], P(('dp', 'head')), may hold values from -6 to 6
- gain_attn: float32 [2, 256], replicated, may hold values from 0.1 to 1.9
- gain_mlp: float32 [2, 256], replicated, may hold values from 0.1 to 1.9
- w_qkv: bfloat16 [2, 256, 3, 256], P(None, None, None, 'head'), may hold values from -4 to 4, as said below
- w_out: bfloat16 [2, 256, 256], P(None, 'head'), may hold values from -4 to 4, as said below
- w_up: bfloat16 [2, 256, 1024], P(None, None, 'head'), may hold values from -4 to 4, as said below
- w_down: bfloat16 [2, 1024, 256], P(None, 'head'), may hold values from -0.1875 to 0.1875
- w_cross: bfloat16 [2, 256, 256], P(None, None, 'head'), may hold values from -4 to 4, as said below
- b_cross: bfloat16 [2, 256], P(None, 'head'), may hold values from -1 to 1, as said below
Outputs:
- output: float32 [32768, 256], P(('dp', 'head'))
- grad_tokens: float32 [32768, 256], P(('dp', 'head'))
- grad_gain_attn: float32 [2, 256], replicated
- grad_gain_mlp: float32 [2, 256], replicated
- grad_w_qkv: float32 [2, 256, 3, 256], P(None, None, None, 'head')
- grad_w_out: float32 [2, 256, 256], P(None, 'head')
- grad_w_up: float32 [2, 256, 1024], P(None, None, 'head')
- grad_w_down: float32 [2, 1024, 256], P(None, 'head')
- grad_w_cross: float32 [2, 256, 256], P(None, None, 'head')
- grad_b_cross: float32 [2, 256], P(None, 'head')
Inputs may be any that keep to these rules, and one draw needn't show every extreme that they name: lengths[b] slots of sample b are present and the rest are absent; some sample has exactly 256 and some exactly 32. `w_qkv`: independent entries with deviation about 1 / sqrt(128). `w_out`: independent entries with deviation about 1 / sqrt(16). `w_up`: independent entries with deviation about 1 / sqrt(256). `w_cross`: independent entries with deviation about 1 / sqrt(1024). `b_cross`: independent entries with deviation about 0.25.
All inputs are finite; a program needn't handle non-finite values.
Results may differ from a plain program's by a relative error of at most 0.019.
The roundings to bfloat16 on the way count: a program that leaves them out, or rounds other values in their place, can miss the bound.
Values may be sent and summed in bfloat16 or wider, within the bound.
No kernel may reach another device: no remote copies, remote signals or barrier semaphores. Data moves between devices by JAX's collectives and lax.ppermute only.
A program may use at most 128 MiB of HBM per device.

v0:
```python
import functools

import jax
import jax.numpy as jnp
from jax import lax
from jax.experimental import pallas as pl
from jax.experimental.pallas import tpu as pltpu
from jax.sharding import PartitionSpec as P

HD = 64
LAYERS = 2
EPSILON = 1e-06
MASKED_SCORE = -1000000000.0
BF = jnp.bfloat16
F32 = jnp.float32

VMEM_LIMIT = 32 * 2**20
SMALL_LIMIT = 12 * 2**20
CUT = 96
UNROLL = {"attn_fwd": 4, "mlp_fwd": 4, "mlp_both": 4, "mlp_bwd": 4, "attn_bwd": 2, "attn_pre": 2, "attn_post": 2}
KERNEL_FLOPS = 1000
LONG = 50 * 10**9


def nn(a, b):
    return lax.dot_general(a, b, (((1,), (0,)), ((), ())), preferred_element_type=F32)


def nt(a, b):
    return lax.dot_general(a, b, (((1,), (1,)), ((), ())), preferred_element_type=F32)


def tn(a, b):
    return lax.dot_general(a, b, (((0,), (0,)), ((), ())), preferred_element_type=F32)


def rescale_of(values):
    return lax.rsqrt(jnp.mean(values * values, axis=-1, keepdims=True) + EPSILON)


def norm_back(values, rescale, gain, gradient):
    scaled = gradient * gain
    product_mean = jnp.mean(values * scaled, axis=-1, keepdims=True)
    normal = values * rescale
    grad_values = rescale * (scaled - normal * (rescale * product_mean))
    return grad_values, jnp.sum(gradient * normal, axis=0, keepdims=True)


def gelu_and_slope(u):
    d = 1.0 + (0.3275911 * 0.7071067811865476) * jnp.abs(u)
    t = pl.reciprocal(d, approx=True)
    t = t * (2.0 - d * t)
    e = jnp.exp2((-0.5 * 1.4426950408889634) * (u * u))
    poly = ((((0.5 * 1.061405429) * t - 0.5 * 1.453152027) * t + 0.5 * 1.421413741) * t - 0.5 * 0.284496736) * t + 0.5 * 0.254829592
    tail = poly * t * e
    cdf = jnp.where(u >= 0.0, 1.0 - tail, tail)
    return u * cdf, cdf + u * (e * 0.3989422804014327)


def head_index():
    return lax.axis_index("head")


def half_index():
    return lax.axis_index("dp") & 1


def quarter_index():
    return (lax.axis_index("dp") >> 1) & 1


def place_pieces(own, mine, theirs, dst, first=0):
    half = dst.shape[1] // 2
    keep = pl.multiple_of(half_index() * half, 16)
    other = pl.multiple_of((1 - half_index()) * half, 16)
    at = 0
    for part in own:
        dst[0, at:at + part.shape[0], :] = part
        at += part.shape[0]
    for m in range(3):
        dst[m + 1, pl.ds(keep, half), :] = mine[m][first:first + half, :]
        dst[m + 1, pl.ds(other, half), :] = theirs[m][first:first + half, :]


def place_attn(first, pieces, wa, w_cross, w_out):
    place_pieces((pieces[0][...],), pieces[1:4], pieces[4:7], wa, first)
    total = jnp.zeros((1, 256), F32)
    for m in range(4):
        place = pl.multiple_of((head_index() ^ m) * HD, HD)
        w_cross[pl.ds(place, HD), :] = wa[m, 192:256, :]
        w_out[m * HD:(m + 1) * HD, :] = wa[m, 256:320, :]
        total = total + wa[m, 320:336, :].astype(F32)[0:1, :]
    return total


def place_mlp(layer, first, pieces, wm):
    place_pieces((pieces[0][layer], pieces[1][layer]), pieces[2:5], pieces[5:8], wm, first)


def each_sample(rows, unroll, step, *init):
    def body(i, carried):
        return step(pl.ds(pl.multiple_of(i * 256, 256), 256), *carried)

    return lax.fori_loop(0, rows // 256, body, init, unroll=unroll)


def attn_fwd_kernel(layer, first, cur_ref, mask_ref, gain_ref, p0, p1, p2, p3, p4, p5, p6,
                    middle_ref, base_ref, nrm_ref, qkv_ref, mix_ref, lse_ref, wa, w_cross, w_out):
    bias = place_attn(first, (p0, p1, p2, p3, p4, p5, p6), wa, w_cross, w_out)
    gain = gain_ref[layer:layer + 1, :]
    def step(rows):
        cur = cur_ref[rows, :].astype(F32)
        nrm = (cur * rescale_of(cur) * gain).astype(BF)
        nrm_ref[rows, :] = nrm
        mask = jnp.concatenate([mask_ref[rows, :]] * 2, axis=1)
        qkv = [nt(wa[m, 0:192, :], nrm).astype(BF) for m in range(4)]
        scores = [tn(qkv[m][64:128], qkv[m][0:64] * BF(0.125)) + mask for m in range(4)]
        cross = nt(nrm, w_cross[...]) + bias
        probs = []
        for m in range(4):
            qkv_ref[m * 192:(m + 1) * 192, rows] = qkv[m]
            top = jnp.max(scores[m], axis=0, keepdims=True)
            e = jnp.exp(scores[m] - top)
            total = jnp.sum(e, axis=0, keepdims=True)
            probs.append((e * (1.0 / total)).astype(BF))
            lse_ref[m:m + 1, rows] = top + jnp.log(total)
        mix = jnp.concatenate([nn(qkv[m][128:192], probs[m]).astype(BF) for m in range(4)], axis=0)
        mix_ref[:, rows] = mix
        middle = cur + tn(mix, w_out[...])
        middle_ref[rows, :] = middle
        base_ref[rows, :] = middle + cur * cross
        return ()

    each_sample(cur_ref.shape[0], UNROLL["attn_fwd"], step)


def mlp_fwd_block(middle, gain, wm):
    r = rescale_of(middle)
    n2 = (middle * r * gain).astype(BF)
    us = [nn(n2, wm[m, 0:256, :]) for m in range(4)]
    kept = []
    for u in us:
        hid, slope = gelu_and_slope(u)
        kept.append((hid.astype(BF), slope.astype(BF)))
    feed = [nn(kept[m][0], wm[m, 256:512, :]) for m in range(4)]
    return r, n2, kept, (feed[0] + feed[1]) + (feed[2] + feed[3])


def mlp_fwd_kernel(layer, first, middle_ref, base_ref, gain_ref, p0, p1, p2, p3, p4, p5, p6, p7,
                   out_ref, hid_ref, slope_ref, wm):
    place_mlp(layer, first, (p0, p1, p2, p3, p4, p5, p6, p7), wm)
    gain = gain_ref[layer:layer + 1, :]
    def step(rows):
        _, _, kept, feed = mlp_fwd_block(middle_ref[rows, :], gain, wm)
        for m, (hid, slope) in enumerate(kept):
            hid_ref[rows, m * 256:(m + 1) * 256] = hid
            slope_ref[rows, m * 256:(m + 1) * 256] = slope
        out_ref[rows, :] = base_ref[rows, :] + feed
        return ()

    each_sample(middle_ref.shape[0], UNROLL["mlp_fwd"], step)


def mlp_bwd_block(gf, kept, wm):
    ghs = [nt(gf, wm[m, 256:512, :]) for m in range(4)]
    gps = [(gh * slope.astype(F32)).astype(BF) for gh, (_, slope) in zip(ghs, kept)]
    gn = [nt(gps[m], wm[m, 0:256, :]) for m in range(4)]
    return gps, (gn[0] + gn[1]) + (gn[2] + gn[3])


def put_mlp_grads(hid, gp, n2, gf, keep_ref, send_ref):
    for m in range(4):
        columns = slice(m * 256, (m + 1) * 256)
        up = tn(n2[...], gp[:, columns]).astype(BF)
        down = tn(hid[:, columns], gf[...]).astype(BF)
        own_up = half_index() == 0
        keep_ref[m] = jnp.where(own_up, up, down)
        send_ref[m] = jnp.where(own_up, down, up)


def mlp_both_kernel(layer, first, middle_ref, base_ref, cot_ref, gain_ref, p0, p1, p2, p3, p4, p5, p6, p7,
                    out_ref, gm_ref, keep_ref, send_ref, small_ref, wm, hid_all, gp_all, n2_all):
    place_mlp(layer, first, (p0, p1, p2, p3, p4, p5, p6, p7), wm)
    gain = gain_ref[layer:layer + 1, :]
    def step(rows, gain_grad):
        middle = middle_ref[rows, :]
        r, n2, kept, feed = mlp_fwd_block(middle, gain, wm)
        out_ref[rows, :] = base_ref[rows, :] + feed
        gf = cot_ref[rows, :]
        gps, gn = mlp_bwd_block(gf, kept, wm)
        n2_all[rows, :] = n2
        for m in range(4):
            hid_all[rows, m * 256:(m + 1) * 256] = kept[m][0]
            gp_all[rows, m * 256:(m + 1) * 256] = gps[m]
        back, part = norm_back(middle, r, gain, gn)
        gain_grad = gain_grad + part
        gm_ref[rows, :] = gf.astype(F32) + back
        return (gain_grad, )

    gain_grad, = each_sample(middle_ref.shape[0], UNROLL["mlp_both"], step, jnp.zeros((1, 256), F32))
    small_ref[...] = jnp.broadcast_to(gain_grad, small_ref.shape)
    put_mlp_grads(hid_all, gp_all, n2_all, cot_ref, keep_ref, send_ref)


def mlp_bwd_kernel(layer, first, grad_ref, middle_ref, hid_ref, slope_ref, gain_ref, p0, p1, p2, p3, p4, p5, p6, p7,
                   gm_ref, keep_ref, send_ref, small_ref, wm, gp_all, n2_all, gf_all):
    place_mlp(layer, first, (p0, p1, p2, p3, p4, p5, p6, p7), wm)
    gain = gain_ref[layer:layer + 1, :]
    def step(rows, gain_grad):
        middle = middle_ref[rows, :]
        r = rescale_of(middle)
        n2_all[rows, :] = (middle * r * gain).astype(BF)
        grad = grad_ref[rows, :]
        gf = grad.astype(BF)
        gf_all[rows, :] = gf
        kept = [(None, slope_ref[rows, m * 256:(m + 1) * 256]) for m in range(4)]
        gps, gn = mlp_bwd_block(gf, kept, wm)
        for m in range(4):
            gp_all[rows, m * 256:(m + 1) * 256] = gps[m]
        back, part = norm_back(middle, r, gain, gn)
        gain_grad = gain_grad + part
        gm_ref[rows, :] = grad + back
        return (gain_grad, )

    gain_grad, = each_sample(middle_ref.shape[0], UNROLL["mlp_bwd"], step, jnp.zeros((1, 256), F32))
    small_ref[...] = jnp.broadcast_to(gain_grad, small_ref.shape)
    put_mlp_grads(hid_ref, gp_all, n2_all, gf_all, keep_ref, send_ref)


def attn_pre_kernel(layer, first, grad_ref, gm_ref, cur_ref, nrm_ref, mix_ref, p0, p1, p2, p3, p4, p5, p6,
                    gmix_ref, d_cross_ref, d_out_ref, base_ref, gn_ref, small_ref,
                    wa, w_cross, w_out, ga_all, gc_all):
    bias = place_attn(first, (p0, p1, p2, p3, p4, p5, p6), wa, w_cross, w_out)

    def step(rows, bias_grad):
        grad = grad_ref[rows, :].astype(F32)
        gm = gm_ref[rows, :]
        ga = gm.astype(BF)
        ga_all[rows, :] = ga
        gc = (grad * cur_ref[rows, :].astype(F32)).astype(BF)
        gc_all[rows, :] = gc
        gmix_ref[:, rows] = nt(w_out[...], ga).astype(BF)
        gn_ref[rows, :] = nn(gc, w_cross[...])
        base_ref[rows, :] = gm + grad * (nt(nrm_ref[rows, :], w_cross[...]) + bias)
        return (bias_grad + jnp.sum(gc.astype(F32), axis=0, keepdims=True), )

    bias_grad, = each_sample(cur_ref.shape[0], UNROLL["attn_pre"], step, jnp.zeros((1, 256), F32))
    d_cross = tn(gc_all[...], nrm_ref[...])
    d_cross_ref[...] = d_cross.astype(BF)
    d_out_ref[...] = nn(mix_ref[...], ga_all[...]).astype(BF)
    small_ref[0:1, :] = bias_grad
    small_ref[1:2, :] = jnp.sum(d_cross * w_cross[...].astype(F32), axis=0, keepdims=True)


def qkv_back(rows, mask_ref, qkv_ref, lse_ref, gmix_ref):
    mask = jnp.concatenate([mask_ref[rows, :]] * 2, axis=1)
    parts = []
    for m in range(4):
        q, k, v = (qkv_ref[m * 192 + i * HD:m * 192 + (i + 1) * HD, rows] for i in range(3))
        parts.append((q, k, v, gmix_ref[m * HD:(m + 1) * HD, rows]))
    scores = [tn(k, q * BF(0.125)) + mask for q, k, v, go in parts]
    gps = [tn(v, go) for q, k, v, go in parts]
    ps, gss = [], []
    for m in range(4):
        p = jnp.exp(scores[m] - lse_ref[m:m + 1, rows])
        weighted = gps[m] * p
        dot = jnp.sum(weighted, axis=0, keepdims=True)
        ps.append(p.astype(BF))
        gss.append((weighted - p * dot).astype(BF))
    return [
        jnp.concatenate([nn(k, gs) * 0.125, nt(q, gs) * 0.125, nt(go, p)], axis=0).astype(BF)
        for (q, k, v, go), p, gs in zip(parts, ps, gss)
    ]


def norm_grad(cur, gain, gn):
    r = rescale_of(cur)
    scaled = gn * gain
    return r * (scaled - cur * (r * r * jnp.mean(cur * scaled, axis=-1, keepdims=True)))


def place_qkv(first, pieces, wa):
    place_pieces((pieces[0][...],), pieces[1:4], pieces[4:7], wa, first)


def put_attn_grads(layer, nrm, gqkv_all, wa, gain_ref, d_cross_ref, d_out_ref, small, mlp_small, payload, keep_ref, sends):
    gain_grad = small[1:2, :]
    for m in range(4):
        place = pl.multiple_of((head_index() ^ m) * HD, HD)
        d_qkv = nn(gqkv_all[m * 192:(m + 1) * 192, :], nrm)
        gain_grad = gain_grad + jnp.sum(d_qkv * wa[m, 0:192, :].astype(F32), axis=0, keepdims=True)
        payload[m, 0:192, :] = d_qkv.astype(BF)
        payload[m, 192:256, :] = d_cross_ref[pl.ds(place, HD), :]
        payload[m, 256:320, :] = d_out_ref[m * HD:(m + 1) * HD, :]
    gain_grad = gain_grad / gain_ref[layer:layer + 1, :]
    high, low = split_rows(jnp.concatenate([gain_grad, small[0:1, :], mlp_small[0:1, :], jnp.zeros((5, 256), F32)], axis=0))
    keep = pl.multiple_of(half_index() * 160, 16)
    other = pl.multiple_of((1 - half_index()) * 160, 16)
    for m in range(4):
        each = 4 // len(sends)
        for ref, i, at in ((keep_ref, m, keep), (sends[m // each], m % each, other)):
            ref[i, 0:160, :] = payload[m, pl.ds(at, 160), :]
            ref[i, 160:168, :] = high
            ref[i, 168:176, :] = low


def attn_bwd_kernel(layer, first, mask_ref, nrm_ref, qkv_ref, lse_ref, gain_ref, gmix_ref, d_cross_ref, d_out_ref, small, mlp_small,
                    cur_ref, base_ref, gn_ref, p0, p1, p2, p3, p4, p5, p6,
                    out_ref, keep_ref, send_ref, wa, gqkv_all, payload):
    place_qkv(first, (p0, p1, p2, p3, p4, p5, p6), wa)

    def step(rows):
        gn = gn_ref[rows, :]
        for m, gqkv in enumerate(qkv_back(rows, mask_ref, qkv_ref, lse_ref, gmix_ref)):
            gqkv_all[m * 192:(m + 1) * 192, rows] = gqkv
            gn = gn + tn(gqkv, wa[m, 0:192, :])
        out_ref[rows, :] = base_ref[rows, :] + norm_grad(cur_ref[rows, :].astype(F32), gain_ref[layer:layer + 1, :], gn)
        return ()

    each_sample(nrm_ref.shape[0], UNROLL["attn_bwd"], step)
    put_attn_grads(layer, nrm_ref[...], gqkv_all, wa, gain_ref, d_cross_ref, d_out_ref, small, mlp_small,
                   payload, keep_ref, (send_ref,))


def attn_grads_kernel(layer, first, mask_ref, nrm_ref, qkv_ref, lse_ref, gain_ref, gmix_ref, d_cross_ref, d_out_ref, small, mlp_small,
                      p0, p1, p2, p3, p4, p5, p6, gqkv_all, keep_ref, send_low, send_high, wa, payload):
    place_qkv(first, (p0, p1, p2, p3, p4, p5, p6), wa)

    def step(rows):
        for m, gqkv in enumerate(qkv_back(rows, mask_ref, qkv_ref, lse_ref, gmix_ref)):
            gqkv_all[m * 192:(m + 1) * 192, rows] = gqkv
        return ()

    each_sample(nrm_ref.shape[0], UNROLL["attn_bwd"], step)
    put_attn_grads(layer, nrm_ref[...], gqkv_all, wa, gain_ref, d_cross_ref, d_out_ref, small, mlp_small,
                   payload, keep_ref, (send_low, send_high))


def attn_post_kernel(layer, first, gqkv_all, gain_ref, cur_ref, base_ref, gn_ref, p0, p1, p2, p3, p4, p5, p6, out_ref, wa):
    place_qkv(first, (p0, p1, p2, p3, p4, p5, p6), wa)

    def step(rows):
        gn = gn_ref[rows, :]
        for m in range(4):
            gn = gn + tn(gqkv_all[m * 192:(m + 1) * 192, rows], wa[m, 0:192, :])
        out_ref[rows, :] = base_ref[rows, :] + norm_grad(cur_ref[rows, :].astype(F32), gain_ref[layer:layer + 1, :], gn)
        return ()

    each_sample(cur_ref.shape[0], UNROLL["attn_post"], step)


def split_rows(x):
    high = x.astype(BF)
    return high, (x - high.astype(F32)).astype(BF)


def pack_kernel(lens, qkv, cross, out, up, down, b, own0, own1, half_a0, half_r, half_m1, mask, sems):
    copies = []
    for l, own in ((0, own0), (1, own1)):
        for t in range(3):
            copies.append(pltpu.make_async_copy(qkv.at[l, t], own.at[pl.ds(t * HD, HD)], sems.at[0]))
        copies.append(pltpu.make_async_copy(cross.at[l], own.at[pl.ds(192, HD)], sems.at[0]))
        copies.append(pltpu.make_async_copy(out.at[l], own.at[pl.ds(256, HD)], sems.at[0]))
    for copy in copies:
        copy.start()

    def mlp_half(weight):
        return (pltpu.make_async_copy(weight.at[0], half_r.at[pl.ds(0, 256)], sems.at[1]),
                pltpu.make_async_copy(weight.at[1], half_m1, sems.at[1]))

    @pl.when(half_index() == 0)
    def _():
        for copy in mlp_half(up):
            copy.start()

    @pl.when(half_index() != 0)
    def _():
        for copy in mlp_half(down):
            copy.start()

    slots = lax.broadcasted_iota(jnp.int32, (256, 128), 0)
    samples = mask.shape[0] // 256
    for i in range(samples):
        length = lens[head_index() * samples + i]
        mask[i * 256:(i + 1) * 256, :] = jnp.where(slots < length, 0.0, MASKED_SCORE)
    lane = lax.broadcasted_iota(jnp.int32, (LAYERS, 256), 1) // HD
    wide = jnp.concatenate([b[...].astype(F32)] * 4, axis=1)
    wide = jnp.where(lane == head_index(), wide, 0.0)
    for l, own in ((0, own0), (1, own1)):
        own[320:352, :] = jnp.broadcast_to(wide[l:l + 1], (32, 256)).astype(BF)
    for copy in copies:
        copy.wait()
    at = pl.multiple_of(half_index() * 176, 16)
    half_a0[...] = own0[pl.ds(at, 176), :]
    half_r[256:432, :] = own1[pl.ds(at, 176), :]
    for copy in mlp_half(up):
        copy.wait()


def put_sum(out, at, small_at, rows, total):
    for low, high in ((0, small_at), (small_at + 16, rows)):
        if low < high:
            out[at + low:at + high, :] = total(low, high).astype(BF)
    if small_at < rows:
        both = total(small_at, small_at + 16)
        high, low = split_rows(both[0:8] + both[8:16])
        out[at + small_at:at + small_at + 8, :] = high
        out[at + small_at + 8:at + small_at + 16, :] = low


def core_sum_kernel(small_at, *refs):
    ins, outs = refs[:-4], refs[-4:]
    for m, out in enumerate(outs):
        at = 0
        rest = list(ins)
        for where in small_at:
            keep = rest.pop(0)
            if where is None:
                out[at:at + keep.shape[1], :] = keep[m]
                at += keep.shape[1]
                continue
            got, index = rest.pop(0), m
            if got.shape[0] < keep.shape[0]:
                got, index = (got, rest.pop(0))[m // 2], m % 2
            rows = keep.shape[1]
            put_sum(out, at, where, rows, lambda i, j: keep[m, i:j].astype(F32) + got[index, i:j].astype(F32))
            at += rows


def core_split_kernel(keep, got, keep_out, send_out):
    at = pl.multiple_of(quarter_index() * 128, 16)
    other = pl.multiple_of((1 - quarter_index()) * 128, 16)
    for out, rows in ((keep_out, pl.ds(at, 128)), (send_out, pl.ds(other, 128))):
        for m in range(4):
            out[m] = (keep[m, rows, :].astype(F32) + got[m, rows, :].astype(F32)).astype(BF)


def add_kernel(a, b, out):
    out[...] = (a[...].astype(F32) + b[...].astype(F32)).astype(BF)


def four_sum_kernel(small_at, *refs):
    s, a, b, c, out = refs
    put_sum(out, 0, small_at, s.shape[0],
            lambda i, j: (s[i:j].astype(F32) + a[i:j].astype(F32)) + (b[i:j].astype(F32) + c[i:j].astype(F32)))


def early_sum_kernel(one, s, a, b, c, low, high):
    total = (s[...].astype(F32) + a[...].astype(F32)) + (b[...].astype(F32) + c[...].astype(F32))
    low[0:176, :] = one[128:304, :]
    low[176:176 + CUT, :] = total[0:CUT].astype(BF)
    high[0:256 - CUT, :] = total[CUT:256].astype(BF)
    high[256 - CUT:384 - CUT, :] = one[0:128, :]


def pair_sum_kernel(low, low_got, high, high_got, low_out, high_out):
    put_sum(low_out, 0, 160, low.shape[0], lambda i, j: low[i:j].astype(F32) + low_got[i:j].astype(F32))
    high_out[...] = (high[...].astype(F32) + high_got[...].astype(F32)).astype(BF)


def last_pair_kernel(low, low_got, high, high_got, low_out, high_out):
    put_sum(low_out, 0, 160, low.shape[0], lambda i, j: low[i:j].astype(F32) + low_got[i:j].astype(F32))
    rows = 256 - CUT
    high_out[0:rows, :] = (high[0:rows].astype(F32) + high_got[0:rows].astype(F32)).astype(BF)
    high_out[rows:rows + 128, :] = high[rows:rows + 128]
    high_out[rows + 128:rows + 256, :] = high_got[rows:rows + 128]


def finish_kernel(low, low_other, high, high_other, late, late_other,
                  d_qkv, d_out, d_up, d_down, d_cross, gain_attn, gain_mlp, bias):
    rows = 256 - CUT
    mine = pl.multiple_of(quarter_index() * 128, 16)
    other = pl.multiple_of((1 - quarter_index()) * 128, 16)

    def place(first, second):
        for l, a, b in ((1, first[0], second[0]), (0, first[2], second[2])):
            d_qkv[l, 0] = a[0:64].astype(F32)
            d_qkv[l, 1] = a[64:128].astype(F32)
            d_qkv[l, 2, 0:32] = a[128:160].astype(F32)
            d_qkv[l, 2, 32:64] = b[0:32].astype(F32)
            d_cross[l] = b[32:96].astype(F32)
            d_out[l] = b[96:160].astype(F32)
        for dst, (lo, hi, _) in ((d_up, first), (d_down, second)):
            dst[0, 0:CUT] = lo[176:176 + CUT].astype(F32)
            dst[0, CUT:256] = hi[0:rows].astype(F32)
            dst[1, pl.ds(mine, 128)] = hi[rows:rows + 128].astype(F32)
            dst[1, pl.ds(other, 128)] = hi[rows + 128:rows + 256].astype(F32)

    @pl.when(half_index() == 0)
    def _():
        place((low, high, late), (low_other, high_other, late_other))

    @pl.when(half_index() != 0)
    def _():
        place((low_other, high_other, late_other), (low, high, late))

    for l, ref in ((0, late), (1, low)):
        small = ref[160:168].astype(F32) + ref[168:176].astype(F32)
        gain_attn[l:l + 1, :] = small[0:1]
        gain_mlp[l:l + 1, :] = small[2:3]
        total = jnp.zeros((1, HD), F32)
        for h in range(4):
            total = total + jnp.where(head_index() == h, small[1:2, h * HD:(h + 1) * HD], 0.0)
        bias[l:l + 1, :] = total


SMEM = pl.BlockSpec(memory_space=pltpu.SMEM)
ANY = pl.BlockSpec(memory_space=pl.ANY)


def call(kernel, outs, scratch, name, *args):
    return pl.pallas_call(
        kernel,
        in_specs=[VMEM] * len(args),
        out_specs=[VMEM] * len(outs),
        out_shape=[jax.ShapeDtypeStruct(shape, dtype) for shape, dtype in outs],
        scratch_shapes=[pltpu.VMEM(shape, dtype) for shape, dtype in scratch],
        compiler_params=pltpu.CompilerParams(vmem_limit_bytes=VMEM_LIMIT),
        cost_estimate=pl.CostEstimate(flops=KERNEL_FLOPS, bytes_accessed=1024, transcendentals=0),
        name=name,
    )(*args)


ATTN_SCRATCH = [((4, 352, 256), BF), ((256, 256), BF), ((256, 256), BF)]
MLP_GRADS = [((4, 256, 256), BF), ((4, 256, 256), BF), ((8, 256), F32)]


def attn_fwd(layer, first, cur, mask, gain, pieces):
    rows = cur.shape[0]
    outs = [((rows, 256), F32), ((rows, 256), F32), ((rows, 256), BF), ((768, rows), BF), ((256, rows), BF), ((8, rows), F32)]
    return call(functools.partial(attn_fwd_kernel, layer, first), outs, ATTN_SCRATCH, "attn_fwd", cur, mask, gain, *pieces)


def mlp_fwd(layer, first, middle, base, gain, pieces):
    rows = middle.shape[0]
    outs = [((rows, 256), F32), ((rows, 1024), BF), ((rows, 1024), BF)]
    return call(functools.partial(mlp_fwd_kernel, layer, first), outs, [((4, 512, 256), BF)], "mlp_fwd",
                middle, base, gain, *pieces)


def mlp_both(layer, first, middle, base, cot, gain, pieces):
    rows = middle.shape[0]
    outs = [((rows, 256), F32), ((rows, 256), F32)] + MLP_GRADS
    scratch = [((4, 512, 256), BF), ((rows, 1024), BF), ((rows, 1024), BF), ((rows, 256), BF)]
    return call(functools.partial(mlp_both_kernel, layer, first), outs, scratch, "mlp_both", middle, base, cot, gain, *pieces)


def mlp_bwd(layer, first, grad, middle, hid, slope, gain, pieces):
    rows = middle.shape[0]
    outs = [((rows, 256), F32)] + MLP_GRADS
    scratch = [((4, 512, 256), BF), ((rows, 1024), BF), ((rows, 256), BF), ((rows, 256), BF)]
    return call(functools.partial(mlp_bwd_kernel, layer, first), outs, scratch, "mlp_bwd",
                grad, middle, hid, slope, gain, *pieces)


def attn_pre(layer, first, grad, gm, cur, saved, pieces):
    rows = cur.shape[0]
    nrm, _, mix, _ = saved
    outs = [((256, rows), BF), ((256, 256), BF), ((256, 256), BF), ((rows, 256), F32), ((rows, 256), F32), ((8, 256), F32)]
    scratch = ATTN_SCRATCH + [((rows, 256), BF), ((rows, 256), BF)]
    return call(functools.partial(attn_pre_kernel, layer, first), outs, scratch, "attn_pre", grad, gm, cur, nrm, mix, *pieces)


PAYLOAD = [((4, 176, 256), BF), ((4, 176, 256), BF)]


def attn_bwd(layer, first, cur, mask, saved, gain, pre, mlp_small, pieces):
    rows = cur.shape[0]
    nrm, qkv, _, lse = saved
    gmix, d_cross, d_out, base, gn, small = pre
    scratch = [((4, 352, 256), BF), ((768, rows), BF), ((4, 320, 256), BF)]
    return call(functools.partial(attn_bwd_kernel, layer, first), [((rows, 256), F32)] + PAYLOAD, scratch, "attn_bwd",
                mask, nrm, qkv, lse, gain, gmix, d_cross, d_out, small, mlp_small, cur, base, gn, *pieces)


def attn_grads(layer, first, mask, saved, gain, pre, mlp_small, pieces):
    nrm, qkv, _, lse = saved
    gmix, d_cross, d_out, _, _, small = pre
    scratch = [((4, 352, 256), BF), ((4, 320, 256), BF)]
    return call(functools.partial(attn_grads_kernel, layer, first), [((768, nrm.shape[0]), BF), ((4, 176, 256), BF), ((2, 176, 256), BF), ((2, 176, 256), BF)], scratch, "attn_grads",
                mask, nrm, qkv, lse, gain, gmix, d_cross, d_out, small, mlp_small, *pieces)


def attn_post(layer, first, gqkv, gain, cur, pre, pieces):
    return call(functools.partial(attn_post_kernel, layer, first), [((cur.shape[0], 256), F32)], [((4, 352, 256), BF)], "attn_post",
                gqkv, gain, cur, pre[3], pre[4], *pieces)[0]


VMEM = pl.BlockSpec(memory_space=pltpu.VMEM)


def small_call(kernel, shapes, name, flops=1000):
    def run(*args):
        return pl.pallas_call(
            kernel,
            in_specs=[VMEM] * len(args),
            out_specs=[VMEM] * len(shapes),
            out_shape=[jax.ShapeDtypeStruct(shape, dtype) for shape, dtype in shapes],
            compiler_params=pltpu.CompilerParams(vmem_limit_bytes=SMALL_LIMIT),
            cost_estimate=pl.CostEstimate(flops=flops, bytes_accessed=1024, transcendentals=0),
            name=name,
        )(*args)
    return run


def core_sum(small_at, *groups):
    rows = sum(group[0].shape[1] for group in groups)
    return small_call(functools.partial(core_sum_kernel, small_at), [((rows, 256), BF)] * 4, "core_sum")(
        *[x for group in groups for x in group])


def four_sum(small_at, terms, flops=1000):
    return small_call(functools.partial(four_sum_kernel, small_at), [(terms[0].shape, BF)], "four_sum", flops)(*terms)[0]


def swap(x, axis, size, mask):
    return lax.ppermute(x, axis, [(i, i ^ mask) for i in range(size)])


def tie(x, *before):
    return lax.optimization_barrier((x,) + before)[0]


def solution(mesh):
    dp_size, head_size = mesh.shape["dp"], mesh.shape["head"]

    def core_swap(x):
        return swap(x, "dp", dp_size, 1)

    def fetch(x):
        return [swap(x, "head", head_size, m) for m in range(1, head_size)]

    def scatter(sums):
        return [sums[0]] + [swap(sums[m], "head", head_size, m) for m in range(1, head_size)]

    bits = [1 << i for i in range(1, dp_size.bit_length() - 1)]

    def late_steps():
        return [(bits[i], bits[i + 1], bits[i] + bits[i + 1]) if i + 1 < len(bits) else (bits[i],) for i in range(0, len(bits), 2)]

    def sum_early_late(low, high, late):
        pairs = list(zip(bits, bits[1:] + bits[:1]))

        def pair(low, high, masks, before, last):
            got = [tie(swap(x, "dp", dp_size, mask), *before) for x, mask in zip((low, high), masks)]
            kernel, more = (last_pair_kernel, 128) if last else (pair_sum_kernel, 0)
            return small_call(kernel, [(low.shape, BF), ((high.shape[0] + more, 256), BF)], "pair_sum")(low, got[0], high, got[1])

        low, high = pair(low, high, pairs[0], late[1:], len(pairs) == 1)
        late = four_sum(160, late)
        for masks in late_steps():
            terms = [late] + [swap(late, "dp", dp_size, mask) for mask in masks]
            before = terms[1:]
            late = four_sum(160, terms + [jnp.zeros_like(late)] * (4 - len(terms)))
        for i, masks in enumerate(pairs[1:]):
            low, high = pair(low, high, masks, before, i == len(pairs) - 2)
        return low, high, late

    def body(tokens, lengths, cotangent, gain_attn, gain_mlp, w_qkv, w_out, w_up, w_down, w_cross, b_cross):
        rows = tokens.shape[0]
        own0, own1, half_a0, half_r, half_m1, mask = pl.pallas_call(
            pack_kernel,
            in_specs=[SMEM] + [ANY] * 5 + [VMEM],
            out_specs=[VMEM] * 6,
            out_shape=[jax.ShapeDtypeStruct((n, 256), BF) for n in (352, 352, 176, 432, 256)]
            + [jax.ShapeDtypeStruct((rows, 128), F32)],
            scratch_shapes=[pltpu.SemaphoreType.DMA((2,))],
            name="pack",
        )(lengths, w_qkv.transpose(0, 2, 3, 1), w_cross.transpose(0, 2, 1), w_out, w_up, w_down, b_cross)

        a0 = fetch(half_a0)
        r = fetch(half_r)
        m1 = fetch(half_m1)
        pieces_a0 = [own0] + a0 + [core_swap(x) for x in a0]
        mid0, base0, *saved0 = attn_fwd(0, 0, tokens, mask, gain_attn, pieces_a0)
        r = [tie(x, mid0) for x in r]
        r = r + [core_swap(x) for x in r]
        cur1, hid0, slope0 = mlp_fwd(0, 0, mid0, base0, gain_mlp, [w_up, w_down] + r)
        mid1, base1, *saved1 = attn_fwd(1, 256, cur1, mask, gain_attn, [own1] + r)
        m1 = [tie(x, mid1) for x in m1]
        m1 = m1 + [core_swap(x) for x in m1]
        output, gm1, keep_m1, send_m1, small_m1 = mlp_both(1, 0, mid1, base1, cotangent, gain_mlp, [w_up, w_down] + m1)
        pre = attn_pre(1, 256, cotangent, gm1, cur1, saved1, [own1] + r)
        pre_done = pre[0]
        keep_m1, send_m1 = small_call(core_split_kernel, [((4, 128, 256), BF)] * 2, "core_split")(
            keep_m1, tie(core_swap(send_m1), pre_done))
        got_m1 = swap(send_m1, "dp", dp_size, 2)
        grad1, keep_a1, send_a1 = attn_bwd(1, 256, cur1, tie(mask, send_m1), saved1, gain_attn, pre, small_m1, [own1] + r)
        m1_sum = small_call(add_kernel, [((4, 128, 256), BF)], "add", LONG)(keep_m1, tie(got_m1, grad1))[0]
        sums = core_sum((None, 160), (m1_sum,), (keep_a1, tie(core_swap(send_a1), m1_sum)))
        got = scatter(sums)
        gm0, keep_m0, send_m0, small_m0 = mlp_bwd(0, 0, tie(grad1, *sums), mid0, hid0, slope0, gain_mlp, [w_up, w_down] + r)
        pre = attn_pre(0, 0, grad1, gm0, tokens, saved0, pieces_a0)
        gqkv, keep_a0, *send_a0 = attn_grads(0, 0, mask, saved0, gain_attn, pre, small_m0, pieces_a0)
        one = four_sum(288, [tie(x, gqkv) for x in got], LONG)
        sums = core_sum((256,), (keep_m0, tie(core_swap(send_m0), one)))
        got = scatter(sums)
        grad0 = attn_post(0, 0, tie(gqkv, *sums), gain_attn, tokens, pre, pieces_a0)
        low, high = small_call(early_sum_kernel, [((176 + CUT, 256), BF), ((384 - CUT, 256), BF)], "early_sum")(
            one, *[tie(x, grad0) for x in got])
        sums_a0 = core_sum((160,), (keep_a0, *[tie(core_swap(x), low) for x in send_a0]))
        late = scatter(sums_a0)
        low, high, late = sum_early_late(low, high, late)
        d_qkv, d_out, d_up, d_down, d_cross, d_ga, d_gm, d_bias = small_call(
            finish_kernel,
            [((LAYERS, 3, HD, 256), F32), ((LAYERS, HD, 256), F32), ((LAYERS, 256, 256), F32), ((LAYERS, 256, 256), F32),
             ((LAYERS, HD, 256), F32), ((LAYERS, 256), F32), ((LAYERS, 256), F32), ((LAYERS, HD), F32)],
            "finish",
        )(low, core_swap(low), high, core_swap(high), late, core_swap(late))
        return (output, grad0, d_ga, d_gm, d_qkv.transpose(0, 3, 1, 2), d_out, d_up, d_down,
                d_cross.transpose(0, 2, 1), d_bias)

    rows, weights = P(("dp", "head"), None), P(None, "head", None)
    return jax.shard_map(
        body,
        mesh=mesh,
        in_specs=(rows, P("dp"), rows, P(), P(), P(None, None, None, "head"), weights, P(None, None, "head"),
                  weights, P(None, None, "head"), P(None, "head")),
        out_specs=(rows, rows, P(), P(), P(None, None, None, "head"), weights, P(None, None, "head"),
                   weights, P(None, None, "head"), P(None, "head")),
        check_vma=False,
    )
```

profile of v0, /device:TPU:9, one launch (start us, length us, event | category | flops | bytes accessed | tf_op | source)
XLA Modules:
  0.0 125.1 jit_solution(14119023787554588499)
XLA Ops:
  0.7 3.0 %pack.1 = (bf16[352,256]{1,0:T(8,128)(2,1)}, bf16[352,256]{1,0:T(8,128)(2,1)}, bf16[176,256]{1,0:T(8,128)(2,1)}, bf16[432,256]{1,0:T(8,128)(2,1)}, bf16[256,256]{1,0:T(8,128)(2,1)}, /*index=5*/f32[1024,128]{1,0:T(8,128)}) custom-call(s32[16]{0:T(128)} %lens.1, bf16[2,3,64,256]{3,2,1,0:T(8,128)(2,1)} %bitcast.4, bf16[2,64,256]{2,1,0:T(8,128)(2,1)} %bitcast.5, ...), custom_call_target="tpu_custom_call" | custom-call | tf_op jit(solution)/shard_map/pack/pallas_call | solution.py:661
  3.7 1.4 %collective-permute-start.2 = (bf16[176,256]{1,0:T(8,128)(2,1)}, bf16[176,256]{1,0:T(8,128)(2,1)S(1)}, u32[]{:S(2)}, u32[]{:S(2)}) collective-permute-start(bf16[176,256]{1,0:T(8,128)(2,1)} %get-tuple-element.116), channel_id=1, source_target_pairs={{0,3},{1,2},{2,1},{3,0},{4,7},{5,6},{6,5},{7,4},{8,11},{9,10},{10,... | collective-permute-start | bytes 270344 | tf_op jit(solution)/shard_map/ppermute | solution.py:617
  5.1 2.2 %collective-permute-start.6 = (bf16[432,256]{1,0:T(8,128)(2,1)}, bf16[432,256]{1,0:T(8,128)(2,1)S(1)}, u32[]{:S(2)}, u32[]{:S(2)}) collective-permute-start(bf16[432,256]{1,0:T(8,128)(2,1)} %get-tuple-element.119), channel_id=1, source_target_pairs={{0,1},{1,0},{2,3},{3,2},{4,5},{5,4},{6,7},{7,6},{8,9},{9,8},{10,11... | collective-permute-start | bytes 663560 | tf_op jit(solution)/shard_map/ppermute | solution.py:617
  7.3 0.4 collective-permute-start
  7.6 0.9 collective-permute-done.2.p3
  8.5 2.8 %collective-permute-start.5 = (bf16[176,256]{1,0:T(8,128)(2,1)S(1)}, bf16[176,256]{1,0:T(8,128)(2,1)S(1)}, u32[]{:S(2)}, u32[]{:S(2)}) collective-permute-start(bf16[176,256]{1,0:T(8,128)(2,1)S(1)} %collective-permute-done.2.p3), channel_id=1, source_target_pairs={{0,4},{4,0},{8,12},{12,8},{16,20},{20,16},{24,28},{28,24},{1,5},{5... | collective-permute-start | bytes 270344 | tf_op jit(solution)/shard_map/ppermute | solution.py:617
  11.3 0.4 collective-permute-start.8
  11.7 3.6 %collective-permute-done.1.p2 = bf16[176,256]{1,0:T(8,128)(2,1)S(1)} collective-permute-done((bf16[176,256]{1,0:T(8,128)(2,1)}, bf16[176,256]{1,0:T(8,128)(2,1)S(1)}, u32[]{:S(2)}, u32[]{:S(2)}) %collective-permute-start.1) | collective-permute-done | bytes 90144 | tf_op jit(solution)/shard_map/ppermute | solution.py:617
  15.4 2.7 %collective-permute-done.p1 = bf16[176,256]{1,0:T(8,128)(2,1)S(1)} collective-permute-done((bf16[176,256]{1,0:T(8,128)(2,1)}, bf16[176,256]{1,0:T(8,128)(2,1)S(1)}, u32[]{:S(2)}, u32[]{:S(2)}) %collective-permute-start) | collective-permute-done | bytes 90144 | tf_op jit(solution)/shard_map/ppermute | solution.py:617
  18.1 2.7 %collective-permute-start.4 = (bf16[176,256]{1,0:T(8,128)(2,1)S(1)}, bf16[176,256]{1,0:T(8,128)(2,1)S(1)}, u32[]{:S(2)}, u32[]{:S(2)}) collective-permute-start(bf16[176,256]{1,0:T(8,128)(2,1)S(1)} %collective-permute-done.1.p2), channel_id=1, source_target_pairs={{0,4},{4,0},{8,12},{12,8},{16,20},{20,16},{24,28},{28,24},{1,5},{5... | collective-permute-start | bytes 270344 | tf_op jit(solution)/shard_map/ppermute | solution.py:617
  20.8 0.9 collective-permute-done.4.p5
  21.7 0.4 collective-permute-done.3.p4
  22.1 1.0 copy-done
  23.1 1.0 copy-done.2
  24.2 0.9 copy-done.6
  25.1 0.7 copy-done.10
  25.8 4.1 %attn_fwd.2 = (f32[1024,256]{1,0:T(8,128)S(1)}, f32[1024,256]{1,0:T(8,128)S(1)}, bf16[1024,256]{1,0:T(8,128)(2,1)S(1)}, bf16[768,1024]{1,0:T(8,128)(2,1)S(1)}, b...) custom-call(bf16[1024,256]{1,0:T(8,128)(2,1)S(1)} %copy-done.2, f32[1024,128]{1,0:T(8,128)S(1)} %copy-done, ...), custom_call_target="tpu_custom_call" | custom-call | flops 1000 | bytes 1024 | tf_op jit(solution)/shard_map/attn_fwd/pallas_call | solution.py:512
  30.1 2.9 %collective-permute-done.7.p3.p2 = bf16[432,256]{1,0:T(8,128)(2,1)S(1)} collective-permute-done((bf16[432,256]{1,0:T(8,128)(2,1)}, bf16[432,256]{1,0:T(8,128)(2,1)S(1)}, u32[]{:S(2)}, u32[]{:S(2)}) %collective-permute-start.7) | collective-permute-done | bytes 221216 | tf_op jit(solution)/shard_map/ppermute | solution.py:617
  33.0 0.8 collective-permute-start.10
  33.8 0.7 collective-permute-start.14
  34.5 3.9 %collective-permute-start.13 = (bf16[256,256]{1,0:T(8,128)(2,1)S(1)}, bf16[256,256]{1,0:T(8,128)(2,1)S(1)}, u32[]{:S(2)}, u32[]{:S(2)}) collective-permute-start(bf16[256,256]{1,0:T(8,128)(2,1)S(1)} %copy-done.13), channel_id=1, source_target_pairs={{0,2},{1,3},{2,0},{3,1},{4,6},{5,7},{6,4},{7,5},{8,10},{9,11},{10,... | collective-permute-start | bytes 393224 | tf_op jit(solution)/shard_map/ppermute | solution.py:617
  38.5 4.7 %mlp_fwd.1 = (f32[1024,256]{1,0:T(8,128)S(1)}, bf16[1024,1024]{1,0:T(8,128)(2,1)S(1)}, bf16[1024,1024]{1,0:T(8,128)(2,1)S(1)}) custom-call(f32[1024,256]{1,0:T(8,128)S(1)} %get-tuple-element.117.middle_ref, f32[1024,256]{1,0:T(8,128)S(1)} %get-tuple-element.118.base_ref, f32[2,256]{1,0:T(2,128)S(1)} %copy-done.12, bf16[2,256,256]{2,1,0:T(8,128)(2,1)S(1)} %copy-done.4, ...), custom_call_target="tpu_custom_call" | custom-call | flops 1000 | bytes 1024 | tf_op jit(solution)/shard_map/mlp_fwd/pallas_call | solution.py:512
  43.2 4.4 %attn_fwd.3 = (f32[1024,256]{1,0:T(8,128)S(1)}, f32[1024,256]{1,0:T(8,128)S(1)}, bf16[1024,256]{1,0:T(8,128)(2,1)S(1)}, bf16[768,1024]{1,0:T(8,128)(2,1)S(1)}, b...) custom-call(f32[1024,256]{1,0:T(8,128)S(1)} %get-tuple-element.123.cur_ref, f32[1024,128]{1,0:T(8,128)S(1)} %copy-done.1, ...), custom_call_target="tpu_custom_call" | custom-call | flops 1000 | bytes 1024 | tf_op jit(solution)/shard_map/attn_fwd/pallas_call | solution.py:512
  47.6 1.1 collective-permute-start.15
  48.8 0.4 collective-permute-start.17
  49.2 0.5 collective-permute-done.15.p5
  49.7 0.4 collective-permute-done.16.p6
  50.2 7.6 %mlp_both.1 = (f32[1024,256]{1,0:T(8,128)}, f32[1024,256]{1,0:T(8,128)S(1)}, bf16[4,256,256]{2,1,0:T(8,128)(2,1)S(1)}, bf16[4,256,256]{2,1,0:T(8,128)(2,1)S(1)}, f32[8,256]{1,0:T(8,128)S(1)}) custom-call(f32[1024,256]{1,0:T(8,128)S(1)} %get-tuple-element.125.middle_ref, f32[1024,256]{1,0:T(8,128)S(1)} %get-tuple-element.126.base_ref, ...), custom_call_target="tpu_custom_call" | custom-call | flops 1000 | bytes 1024 | tf_op jit(solution)/shard_map/mlp_both/pallas_call | solution.py:512
  57.8 0.3 collective-permute-start.18
  58.1 1.6 %attn_pre.2 = (bf16[256,1024]{1,0:T(8,128)(2,1)S(1)}, bf16[256,256]{1,0:T(8,128)(2,1)S(1)}, bf16[256,256]{1,0:T(8,128)(2,1)S(1)}, f32[1024,256]{1,0:T(8,128)S(1)...) custom-call(bf16[1024,256]{1,0:T(8,128)(2,1)S(1)} %copy-done.8, f32[1024,256]{1,0:T(8,128)S(1)} %get-tuple-element.137.gm_ref, ...), custom_call_target="tpu_custom_call" | custom-call | flops 1000 | bytes 1024 | tf_op jit(solution)/shard_map/attn_pre/pallas_call | solution.py:512
  59.8 1.1 collective-permute-start.19
  60.9 5.6 %attn_bwd.1 = (f32[1024,256]{1,0:T(8,128)S(1)}, bf16[4,176,256]{2,1,0:T(8,128)(2,1)S(1)}, bf16[4,176,256]{2,1,0:T(8,128)(2,1)S(1)}) custom-call(f32[1024,128]{1,0:T(8,128)S(1)} %copy-done.1, bf16[1024,256]{1,0:T(8,128)(2,1)S(1)} %get-tuple-element.138.nrm_ref, bf16[768,1024]{1,0:T(8,128)(2,1)S(1)} %get-tuple-element.144.qkv_ref, ...), custom_call_target="tpu_custom_call" | custom-call | flops 1000 | bytes 1024 | tf_op jit(solution)/shard_map/attn_bwd/pallas_call | solution.py:512
  66.6 0.7 collective-permute-start.20
  67.6 1.0 collective-permute-done.20.refs_2_
  68.6 1.1 collective-permute-start.24
  69.7 2.8 %collective-permute-start.23 = (bf16[304,256]{1,0:T(8,128)(2,1)S(1)}, bf16[304,256]{1,0:T(8,128)(2,1)S(1)}, u32[]{:S(2)}, u32[]{:S(2)}) collective-permute-start(bf16[304,256]{1,0:T(8,128)(2,1)S(1)} %get-tuple-element.160), channel_id=1, source_target_pairs={{0,2},{1,3},{2,0},{3,1},{4,6},{5,7},{6,4},{7,5},{8,10},{9,11},{10,... | collective-permute-start | bytes 466952 | tf_op jit(solution)/shard_map/ppermute | solution.py:617
  72.5 3.1 %mlp_bwd.1 = (f32[1024,256]{1,0:T(8,128)S(1)}, bf16[4,256,256]{2,1,0:T(8,128)(2,1)S(1)}, bf16[4,256,256]{2,1,0:T(8,128)(2,1)S(1)}, f32[8,256]{1,0:T(8,128)S(1)}) custom-call(f32[1024,256]{1,0:T(8,128)S(1)} %get-tuple-element.162.grad_ref, f32[1024,256]{1,0:T(8,128)S(1)} %get-tuple-element.117.middle_ref, bf16[1024,1024]{1,0:T(8,128)(2,1)S(1)} %get-tuple-element.163.hid_ref, ...), custom_call_target="tpu_custom_call" | custom-call | flops 1000 | bytes 1024 | tf_op jit(solution)/shard_map/mlp_bwd/pallas_call | solution.py:512
  75.6 1.4 %attn_pre.3 = (bf16[256,1024]{1,0:T(8,128)(2,1)S(1)}, bf16[256,256]{1,0:T(8,128)(2,1)S(1)}, bf16[256,256]{1,0:T(8,128)(2,1)S(1)}, f32[1024,256]{1,0:T(8,128)S(1)...) custom-call(f32[1024,256]{1,0:T(8,128)S(1)} %get-tuple-element.162.grad_ref, f32[1024,256]{1,0:T(8,128)S(1)} %get-tuple-element.165.gm_ref, ...), custom_call_target="tpu_custom_call" | custom-call | flops 1000 | bytes 1024 | tf_op jit(solution)/shard_map/attn_pre/pallas_call | solution.py:512
  77.0 4.5 %attn_grads.1 = (bf16[768,1024]{1,0:T(8,128)(2,1)S(1)}, bf16[4,176,256]{2,1,0:T(8,128)(2,1)S(1)}, bf16[2,176,256]{2,1,0:T(8,128)(2,1)S(1)}, bf16[2,176,256]{2,1,0:T(8,128)(2,1)S(1)}) custom-call(f32[1024,128]{1,0:T(8,128)S(1)} %copy-done.1, bf16[1024,256]{1,0:T(8,128)(2,1)S(1)} %get-tuple-element.132.nrm_ref, ...), custom_call_target="tpu_custom_call" | custom-call | flops 1000 | bytes 1024 | tf_op jit(solution)/shard_map/attn_grads/pallas_call | solution.py:512
  81.5 1.0 collective-permute-start.21
  82.5 0.3 collective-permute-done.23.refs_2_
  82.9 1.1 collective-permute-done.21.refs_1_
  84.1 1.8 %collective-permute-start.25 = (bf16[256,256]{1,0:T(8,128)(2,1)S(1)}, bf16[256,256]{1,0:T(8,128)(2,1)S(1)}, u32[]{:S(2)}, u32[]{:S(2)}) collective-permute-start(bf16[256,256]{1,0:T(8,128)(2,1)S(1)} %get-tuple-element.181), channel_id=1, source_target_pairs={{0,1},{1,0},{2,3},{3,2},{4,5},{5,4},{6,7},{7,6},{8,9},{9,8},{10,11... | collective-permute-start | bytes 393224 | tf_op jit(solution)/shard_map/ppermute | solution.py:617
  85.9 0.8 collective-permute-start.26
  86.7 0.5 collective-permute-start.27
  87.2 1.3 %collective-permute-start.30 = (bf16[2,176,256]{2,1,0:T(8,128)(2,1)S(1)}, bf16[2,176,256]{2,1,0:T(8,128)(2,1)S(1)}, u32[]{:S(2)}, u32[]{:S(2)}) collective-permute-start(bf16[2,176,256]{2,1,0:T(8,128)(2,1)S(1)} %get-tuple-element.195), channel_id=1, source_target_pairs={{0,4},{4,0},{8,12},{12,8},{16,20},{20,16},{24,28},{28,24},{1,5},{5... | collective-permute-start | bytes 540680 | tf_op jit(solution)/shard_map/ppermute | solution.py:617
  88.5 2.3 %attn_post.1 = f32[1024,256]{1,0:T(8,128)} custom-call(bf16[768,1024]{1,0:T(8,128)(2,1)S(1)} %get-tuple-element.184.gqkv_all, f32[2,256]{1,0:T(2,128)S(1)} %copy-done.11, bf16[1024,256]{1,0:T(8,128)(2,1)S(1)} %copy-done.3, f32[1024,256]{1,0:T(8,128)S(1)} %get-tuple-element.185.base_ref, f32[1024,256]{1,0:T(8,128)S(1)} %get-tuple-element.186.gn_ref, ...), custom_call_target="tpu_custom_call" | custom-call | flops 1000 | bytes 1024 | tf_op jit(solution)/shard_map/attn_post/pallas_call | solution.py:512
  90.8 1.9 %collective-permute-done.26.b = bf16[256,256]{1,0:T(8,128)(2,1)S(1)} collective-permute-done((bf16[256,256]{1,0:T(8,128)(2,1)S(1)}, bf16[256,256]{1,0:T(8,128)(2,1)S(1)}, u32[]{:S(2)}, u32[]{:S(2)}) %collective-permute-start.26) | collective-permute-done | bytes 131104 | tf_op jit(solution)/shard_map/ppermute | solution.py:617
  92.7 5.9 %collective-permute-done.27.c = bf16[256,256]{1,0:T(8,128)(2,1)S(1)} collective-permute-done((bf16[256,256]{1,0:T(8,128)(2,1)S(1)}, bf16[256,256]{1,0:T(8,128)(2,1)S(1)}, u32[]{:S(2)}, u32[]{:S(2)}) %collective-permute-start.27) | collective-permute-done | bytes 131104 | tf_op jit(solution)/shard_map/ppermute | solution.py:617
  98.7 1.3 %collective-permute-start.34 = (bf16[288,256]{1,0:T(8,128)(2,1)S(1)}, bf16[288,256]{1,0:T(8,128)(2,1)S(1)}, u32[]{:S(2)}, u32[]{:S(2)}) collective-permute-start(bf16[288,256]{1,0:T(8,128)(2,1)S(1)} %get-tuple-element.201.high), channel_id=1, source_target_pairs={{0,16},{4,20},{8,24},{12,28},{16,0},{20,4},{24,8},{28,12},{1,17},{... | collective-permute-start | bytes 442376 | tf_op jit(solution)/shard_map/ppermute | solution.py:617
  100.0 1.1 collective-permute-start.28
  101.3 2.2 %collective-permute-start.32 = (bf16[176,256]{1,0:T(8,128)(2,1)S(1)}, bf16[176,256]{1,0:T(8,128)(2,1)S(1)}, u32[]{:S(2)}, u32[]{:S(2)}) collective-permute-start(bf16[176,256]{1,0:T(8,128)(2,1)S(1)} %get-tuple-element.198), channel_id=1, source_target_pairs={{0,2},{1,3},{2,0},{3,1},{4,6},{5,7},{6,4},{7,5},{8,10},{9,11},{10,... | collective-permute-start | bytes 270344 | tf_op jit(solution)/shard_map/ppermute | solution.py:617
  103.5 0.5 collective-permute-start.33
  104.0 1.0 collective-permute-done.31.refs_1_
  105.0 1.6 %collective-permute-done.32.refs_2_ = bf16[176,256]{1,0:T(8,128)(2,1)S(1)} collective-permute-done((bf16[176,256]{1,0:T(8,128)(2,1)S(1)}, bf16[176,256]{1,0:T(8,128)(2,1)S(1)}, u32[]{:S(2)}, u32[]{:S(2)}) %collective-permute-start.32) | collective-permute-done | bytes 90144 | tf_op jit(solution)/shard_map/ppermute | solution.py:617
  106.6 4.9 %collective-permute-done.33.refs_3_ = bf16[176,256]{1,0:T(8,128)(2,1)S(1)} collective-permute-done((bf16[176,256]{1,0:T(8,128)(2,1)S(1)}, bf16[176,256]{1,0:T(8,128)(2,1)S(1)}, u32[]{:S(2)}, u32[]{:S(2)}) %collective-permute-start.33) | collective-permute-done | bytes 90144 | tf_op jit(solution)/shard_map/ppermute | solution.py:617
  111.5 0.4 collective-permute-start.39
  112.1 2.3 %collective-permute-start.38 = (bf16[176,256]{1,0:T(8,128)(2,1)S(1)}, bf16[176,256]{1,0:T(8,128)(2,1)S(1)}, u32[]{:S(2)}, u32[]{:S(2)}) collective-permute-start(bf16[176,256]{1,0:T(8,128)(2,1)S(1)} %four_sum.4.refs_0_), channel_id=1, source_target_pairs={{0,24},{4,28},{8,16},{12,20},{16,8},{20,12},{24,0},{28,4},{1,25},{... | collective-permute-start | bytes 270344 | tf_op jit(solution)/shard_map/ppermute | solution.py:617
  114.8 2.0 %collective-permute-done.38.refs_3_ = bf16[176,256]{1,0:T(8,128)(2,1)S(1)} collective-permute-done((bf16[176,256]{1,0:T(8,128)(2,1)S(1)}, bf16[176,256]{1,0:T(8,128)(2,1)S(1)}, u32[]{:S(2)}, u32[]{:S(2)}) %collective-permute-start.38) | collective-permute-done | bytes 90144 | tf_op jit(solution)/shard_map/ppermute | solution.py:617
  116.8 2.2 %collective-permute-done.37.refs_2_ = bf16[176,256]{1,0:T(8,128)(2,1)S(1)} collective-permute-done((bf16[176,256]{1,0:T(8,128)(2,1)S(1)}, bf16[176,256]{1,0:T(8,128)(2,1)S(1)}, u32[]{:S(2)}, u32[]{:S(2)}) %collective-permute-start.37) | collective-permute-done | bytes 90144 | tf_op jit(solution)/shard_map/ppermute | solution.py:617
  119.2 3.0 %collective-permute-start.41 = (bf16[416,256]{1,0:T(8,128)(2,1)S(1)}, bf16[416,256]{1,0:T(8,128)(2,1)S(1)}, u32[]{:S(2)}, u32[]{:S(2)}) collective-permute-start(bf16[416,256]{1,0:T(8,128)(2,1)S(1)} %get-tuple-element.209.high), channel_id=1, source_target_pairs={{0,4},{4,0},{8,12},{12,8},{16,20},{20,16},{24,28},{28,24},{1,5},{5... | collective-permute-start | bytes 638984 | tf_op jit(solution)/shard_map/ppermute | solution.py:617
  122.4 0.5 collective-permute-start.42
  122.9 0.9 collective-permute-done.42.late_other
  123.8 1.3 %finish.1 = (f32[2,3,64,256]{3,2,1,0:T(8,128)}, f32[2,64,256]{2,1,0:T(8,128)}, f32[2,256,256]{2,1,0:T(8,128)}, f32[2,256,256]{2,1,0:T(8,128)}, f32[2,64,256]{2,1...) custom-call(bf16[272,256]{1,0:T(8,128)(2,1)S(1)} %get-tuple-element.208.low, ...), custom_call_target="tpu_custom_call" | custom-call | flops 1000 | bytes 1024 | tf_op jit(solution)/shard_map/finish/pallas_call | solution.py:594
  (73 shorter events, 2.8 us)
Async XLA Ops:
  0.6 37.8 %copy-start.5 = (bf16[2,256,256]{2,1,0:T(8,128)(2,1)S(1)}, bf16[2,256,256]{2,1,0:T(8,128)(2,1)}, u32[]{:S(2)}) copy-start(bf16[2,256,256]{2,1,0:T(8,128)(2,1)} %p1.5) | copy-start | bytes 786436
  0.7 37.8 %copy-start.4 = (bf16[2,256,256]{2,1,0:T(8,128)(2,1)S(1)}, bf16[2,256,256]{2,1,0:T(8,128)(2,1)}, u32[]{:S(2)}) copy-start(bf16[2,256,256]{2,1,0:T(8,128)(2,1)} %p0.5) | copy-start | bytes 786436
  0.7 37.8 %copy-start.12 = (f32[2,256]{1,0:T(2,128)S(1)}, f32[2,256]{1,0:T(2,128)}, u32[]{:S(2)}) copy-start(f32[2,256]{1,0:T(2,128)} %gain_ref.13) | copy-start | bytes 6148
  3.7 4.8 %collective-permute-start.2 = (bf16[176,256]{1,0:T(8,128)(2,1)}, bf16[176,256]{1,0:T(8,128)(2,1)S(1)}, u32[]{:S(2)}, u32[]{:S(2)}) collective-permute-start(bf16[176,256]{1,0:T(8,128)(2,1)} %get-tuple-element.116), channel_id=1, source_target_pairs={{0,3},{1,2},{2,1},{3,0},{4,7},{5,6},{6,5},{7,4},{8,11},{9,10},{10,... | collective-permute-start | bytes 270344 | tf_op jit(solution)/shard_map/ppermute | solution.py:617
  5.1 24.8 %collective-permute-start.6 = (bf16[432,256]{1,0:T(8,128)(2,1)}, bf16[432,256]{1,0:T(8,128)(2,1)S(1)}, u32[]{:S(2)}, u32[]{:S(2)}) collective-permute-start(bf16[432,256]{1,0:T(8,128)(2,1)} %get-tuple-element.119), channel_id=1, source_target_pairs={{0,1},{1,0},{2,3},{3,2},{4,5},{5,4},{6,7},{7,6},{8,9},{9,8},{10,11... | collective-permute-start | bytes 663560 | tf_op jit(solution)/shard_map/ppermute | solution.py:617
  7.3 8.1 %collective-permute-start.1 = (bf16[176,256]{1,0:T(8,128)(2,1)}, bf16[176,256]{1,0:T(8,128)(2,1)S(1)}, u32[]{:S(2)}, u32[]{:S(2)}) collective-permute-start(bf16[176,256]{1,0:T(8,128)(2,1)} %get-tuple-element.116), channel_id=1, source_target_pairs={{0,2},{1,3},{2,0},{3,1},{4,6},{5,7},{6,4},{7,5},{8,10},{9,11},{10,... | collective-permute-start | bytes 270344 | tf_op jit(solution)/shard_map/ppermute | solution.py:617
  7.3 10.8 %collective-permute-start = (bf16[176,256]{1,0:T(8,128)(2,1)}, bf16[176,256]{1,0:T(8,128)(2,1)S(1)}, u32[]{:S(2)}, u32[]{:S(2)}) collective-permute-start(bf16[176,256]{1,0:T(8,128)(2,1)} %get-tuple-element.116), channel_id=1, source_target_pairs={{0,1},{1,0},{2,3},{3,2},{4,5},{5,4},{6,7},{7,6},{8,9},{9,8},{10,11... | collective-permute-start | bytes 270344 | tf_op jit(solution)/shard_map/ppermute | solution.py:617
  8.5 12.3 %collective-permute-start.5 = (bf16[176,256]{1,0:T(8,128)(2,1)S(1)}, bf16[176,256]{1,0:T(8,128)(2,1)S(1)}, u32[]{:S(2)}, u32[]{:S(2)}) collective-permute-start(bf16[176,256]{1,0:T(8,128)(2,1)S(1)} %collective-permute-done.2.p3), channel_id=1, source_target_pairs={{0,4},{4,0},{8,12},{12,8},{16,20},{20,16},{24,28},{28,24},{1,5},{5... | collective-permute-start | bytes 270344 | tf_op jit(solution)/shard_map/ppermute | solution.py:617
  11.3 18.8 %collective-permute-start.8 = (bf16[432,256]{1,0:T(8,128)(2,1)}, bf16[432,256]{1,0:T(8,128)(2,1)S(1)}, u32[]{:S(2)}, u32[]{:S(2)}) collective-permute-start(bf16[432,256]{1,0:T(8,128)(2,1)} %get-tuple-element.119), channel_id=1, source_target_pairs={{0,3},{1,2},{2,1},{3,0},{4,7},{5,6},{6,5},{7,4},{8,11},{9,10},{10,... | collective-permute-start | bytes 663560 | tf_op jit(solution)/shard_map/ppermute | solution.py:617
  15.4 17.7 %collective-permute-start.7 = (bf16[432,256]{1,0:T(8,128)(2,1)}, bf16[432,256]{1,0:T(8,128)(2,1)S(1)}, u32[]{:S(2)}, u32[]{:S(2)}) collective-permute-start(bf16[432,256]{1,0:T(8,128)(2,1)} %get-tuple-element.119), channel_id=1, source_target_pairs={{0,2},{1,3},{2,0},{3,1},{4,6},{5,7},{6,4},{7,5},{8,10},{9,11},{10,... | collective-permute-start | bytes 663560 | tf_op jit(solution)/shard_map/ppermute | solution.py:617
  18.1 3.6 %collective-permute-start.4 = (bf16[176,256]{1,0:T(8,128)(2,1)S(1)}, bf16[176,256]{1,0:T(8,128)(2,1)S(1)}, u32[]{:S(2)}, u32[]{:S(2)}) collective-permute-start(bf16[176,256]{1,0:T(8,128)(2,1)S(1)} %collective-permute-done.1.p2), channel_id=1, source_target_pairs={{0,4},{4,0},{8,12},{12,8},{16,20},{20,16},{24,28},{28,24},{1,5},{5... | collective-permute-start | bytes 270344 | tf_op jit(solution)/shard_map/ppermute | solution.py:617
  20.8 1.3 %collective-permute-start.3 = (bf16[176,256]{1,0:T(8,128)(2,1)S(1)}, bf16[176,256]{1,0:T(8,128)(2,1)S(1)}, u32[]{:S(2)}, u32[]{:S(2)}) collective-permute-start(bf16[176,256]{1,0:T(8,128)(2,1)S(1)} %collective-permute-done.p1), channel_id=1, source_target_pairs={{0,4},{4,0},{8,12},{12,8},{16,20},{20,16},{24,28},{28,24},{1,5},{5... | collective-permute-start | bytes 270344 | tf_op jit(solution)/shard_map/ppermute | solution.py:617
  22.1 1.0 copy-start
  23.1 1.0 copy-start.2
  24.2 0.9 copy-start.6
  25.1 0.7 copy-start.10
  25.8 8.1 %copy-start.13 = (bf16[256,256]{1,0:T(8,128)(2,1)S(1)}, bf16[256,256]{1,0:T(8,128)(2,1)}, u32[]{:S(2)}) copy-start(bf16[256,256]{1,0:T(8,128)(2,1)} %get-tuple-element.127) | copy-start | bytes 393220
  29.9 8.5 %collective-permute-start.9 = (bf16[432,256]{1,0:T(8,128)(2,1)S(1)}, bf16[432,256]{1,0:T(8,128)(2,1)S(1)}, u32[]{:S(2)}, u32[]{:S(2)}) collective-permute-start(bf16[432,256]{1,0:T(8,128)(2,1)S(1)} %collective-permute-done.6.p2.p1), channel_id=1, source_target_pairs={{0,4},{4,0},{8,12},{12,8},{16,20},{20,16},{24,28},{28,24},{1,5},{5... | collective-permute-start | bytes 663560 | tf_op jit(solution)/shard_map/ppermute | solution.py:617
  33.0 5.4 %collective-permute-start.10 = (bf16[432,256]{1,0:T(8,128)(2,1)S(1)}, bf16[432,256]{1,0:T(8,128)(2,1)S(1)}, u32[]{:S(2)}, u32[]{:S(2)}) collective-permute-start(bf16[432,256]{1,0:T(8,128)(2,1)S(1)} %collective-permute-done.7.p3.p2), channel_id=1, source_target_pairs={{0,4},{4,0},{8,12},{12,8},{16,20},{20,16},{24,28},{28,24},{1,5},{5... | collective-permute-start | bytes 663560 | tf_op jit(solution)/shard_map/ppermute | solution.py:617
  33.8 4.6 %collective-permute-start.11 = (bf16[432,256]{1,0:T(8,128)(2,1)S(1)}, bf16[432,256]{1,0:T(8,128)(2,1)S(1)}, u32[]{:S(2)}, u32[]{:S(2)}) collective-permute-start(bf16[432,256]{1,0:T(8,128)(2,1)S(1)} %collective-permute-done.8.p4.p3), channel_id=1, source_target_pairs={{0,4},{4,0},{8,12},{12,8},{16,20},{20,16},{24,28},{28,24},{1,5},{5... | collective-permute-start | bytes 663560 | tf_op jit(solution)/shard_map/ppermute | solution.py:617
  33.8 13.7 %collective-permute-start.14 = (bf16[256,256]{1,0:T(8,128)(2,1)S(1)}, bf16[256,256]{1,0:T(8,128)(2,1)S(1)}, u32[]{:S(2)}, u32[]{:S(2)}) collective-permute-start(bf16[256,256]{1,0:T(8,128)(2,1)S(1)} %copy-done.13), channel_id=1, source_target_pairs={{0,3},{1,2},{2,1},{3,0},{4,7},{5,6},{6,5},{7,4},{8,11},{9,10},{10,... | collective-permute-start | bytes 393224 | tf_op jit(solution)/shard_map/ppermute | solution.py:617
  34.5 13.1 %collective-permute-start.13 = (bf16[256,256]{1,0:T(8,128)(2,1)S(1)}, bf16[256,256]{1,0:T(8,128)(2,1)S(1)}, u32[]{:S(2)}, u32[]{:S(2)}) collective-permute-start(bf16[256,256]{1,0:T(8,128)(2,1)S(1)} %copy-done.13), channel_id=1, source_target_pairs={{0,2},{1,3},{2,0},{3,1},{4,6},{5,7},{6,4},{7,5},{8,10},{9,11},{10,... | collective-permute-start | bytes 393224 | tf_op jit(solution)/shard_map/ppermute | solution.py:617
  38.4 9.2 %collective-permute-start.12 = (bf16[256,256]{1,0:T(8,128)(2,1)S(1)}, bf16[256,256]{1,0:T(8,128)(2,1)S(1)}, u32[]{:S(2)}, u32[]{:S(2)}) collective-permute-start(bf16[256,256]{1,0:T(8,128)(2,1)S(1)} %copy-done.13), channel_id=1, source_target_pairs={{0,1},{1,0},{2,3},{3,2},{4,5},{5,4},{6,7},{7,6},{8,9},{9,8},{10,11... | collective-permute-start | bytes 393224 | tf_op jit(solution)/shard_map/ppermute | solution.py:617
  38.4 4.7 %copy-start.1 = (f32[1024,128]{1,0:T(8,128)S(1)}, f32[1024,128]{1,0:T(8,128)}, u32[]{:S(2)}) copy-start(f32[1024,128]{1,0:T(8,128)} %get-tuple-element.143.mask_ref) | copy-start | bytes 1572868
  38.5 4.7 %copy-start.9 = (bf16[352,256]{1,0:T(8,128)(2,1)S(1)}, bf16[352,256]{1,0:T(8,128)(2,1)}, u32[]{:S(2)}) copy-start(bf16[352,256]{1,0:T(8,128)(2,1)} %get-tuple-element.124.p0) | copy-start | bytes 540676
  38.5 4.7 %copy-start.11 = (f32[2,256]{1,0:T(2,128)S(1)}, f32[2,256]{1,0:T(2,128)}, u32[]{:S(2)}) copy-start(f32[2,256]{1,0:T(2,128)} %gain_ref.15) | copy-start | bytes 6148
  43.2 7.1 %copy-start.8 = (bf16[1024,256]{1,0:T(8,128)(2,1)S(1)}, bf16[1024,256]{1,0:T(8,128)(2,1)}, u32[]{:S(2)}) copy-start(bf16[1024,256]{1,0:T(8,128)(2,1)} %grad_ref.1) | copy-start | bytes 1572868
  47.6 2.1 %collective-permute-start.15 = (bf16[256,256]{1,0:T(8,128)(2,1)S(1)}, bf16[256,256]{1,0:T(8,128)(2,1)S(1)}, u32[]{:S(2)}, u32[]{:S(2)}) collective-permute-start(bf16[256,256]{1,0:T(8,128)(2,1)S(1)} %collective-permute-done.12.p2), channel_id=1, source_target_pairs={{0,4},{4,0},{8,12},{12,8},{16,20},{20,16},{24,28},{28,24},{1,5},{5... | collective-permute-start | bytes 393224 | tf_op jit(solution)/shard_map/ppermute | solution.py:617
  48.7 1.3 %collective-permute-start.16 = (bf16[256,256]{1,0:T(8,128)(2,1)S(1)}, bf16[256,256]{1,0:T(8,128)(2,1)S(1)}, u32[]{:S(2)}, u32[]{:S(2)}) collective-permute-start(bf16[256,256]{1,0:T(8,128)(2,1)S(1)} %collective-permute-done.13.p3), channel_id=1, source_target_pairs={{0,4},{4,0},{8,12},{12,8},{16,20},{20,16},{24,28},{28,24},{1,5},{5... | collective-permute-start | bytes 393224 | tf_op jit(solution)/shard_map/ppermute | solution.py:617
  48.8 1.5 %collective-permute-start.17 = (bf16[256,256]{1,0:T(8,128)(2,1)S(1)}, bf16[256,256]{1,0:T(8,128)(2,1)S(1)}, u32[]{:S(2)}, u32[]{:S(2)}) collective-permute-start(bf16[256,256]{1,0:T(8,128)(2,1)S(1)} %collective-permute-done.14.p4), channel_id=1, source_target_pairs={{0,4},{4,0},{8,12},{12,8},{16,20},{20,16},{24,28},{28,24},{1,5},{5... | collective-permute-start | bytes 393224 | tf_op jit(solution)/shard_map/ppermute | solution.py:617
  57.8 1.9 %collective-permute-start.18 = (bf16[4,256,256]{2,1,0:T(8,128)(2,1)S(1)}, bf16[4,256,256]{2,1,0:T(8,128)(2,1)S(1)}, u32[]{:S(2)}, u32[]{:S(2)}) collective-permute-start(bf16[4,256,256]{2,1,0:T(8,128)(2,1)S(1)} %get-tuple-element.136), channel_id=1, source_target_pairs={{0,4},{4,0},{8,12},{12,8},{16,20},{20,16},{24,28},{28,24},{1,5},{5... | collective-permute-start | bytes 1572872 | tf_op jit(solution)/shard_map/ppermute | solution.py:617
  59.8 7.7 %collective-permute-start.19 = (bf16[4,128,256]{2,1,0:T(8,128)(2,1)S(1)}, bf16[4,128,256]{2,1,0:T(8,128)(2,1)S(1)}, u32[]{:S(2)}, u32[]{:S(2)}) collective-permute-start(bf16[4,128,256]{2,1,0:T(8,128)(2,1)S(1)} %get-tuple-element.142), channel_id=1, source_target_pairs={{0,8},{4,12},{8,0},{12,4},{16,24},{20,28},{24,16},{28,20},{1,9},{5... | collective-permute-start | bytes 786440 | tf_op jit(solution)/shard_map/ppermute | solution.py:617
  66.6 2.0 %collective-permute-start.20 = (bf16[4,176,256]{2,1,0:T(8,128)(2,1)S(1)}, bf16[4,176,256]{2,1,0:T(8,128)(2,1)S(1)}, u32[]{:S(2)}, u32[]{:S(2)}) collective-permute-start(bf16[4,176,256]{2,1,0:T(8,128)(2,1)S(1)} %get-tuple-element.156), channel_id=1, source_target_pairs={{0,4},{4,0},{8,12},{12,8},{16,20},{20,16},{24,28},{28,24},{1,5},{5... | collective-permute-start | bytes 1081352 | tf_op jit(solution)/shard_map/ppermute | solution.py:617
  68.6 13.8 %collective-permute-start.24 = (bf16[304,256]{1,0:T(8,128)(2,1)S(1)}, bf16[304,256]{1,0:T(8,128)(2,1)S(1)}, u32[]{:S(2)}, u32[]{:S(2)}) collective-permute-start(bf16[304,256]{1,0:T(8,128)(2,1)S(1)} %get-tuple-element.161), channel_id=1, source_target_pairs={{0,3},{1,2},{2,1},{3,0},{4,7},{5,6},{6,5},{7,4},{8,11},{9,10},{10,... | collective-permute-start | bytes 466952 | tf_op jit(solution)/shard_map/ppermute | solution.py:617
  69.7 13.0 %collective-permute-start.23 = (bf16[304,256]{1,0:T(8,128)(2,1)S(1)}, bf16[304,256]{1,0:T(8,128)(2,1)S(1)}, u32[]{:S(2)}, u32[]{:S(2)}) collective-permute-start(bf16[304,256]{1,0:T(8,128)(2,1)S(1)} %get-tuple-element.160), channel_id=1, source_target_pairs={{0,2},{1,3},{2,0},{3,1},{4,6},{5,7},{6,4},{7,5},{8,10},{9,11},{10,... | collective-permute-start | bytes 466952 | tf_op jit(solution)/shard_map/ppermute | solution.py:617
  72.5 10.4 %collective-permute-start.22 = (bf16[304,256]{1,0:T(8,128)(2,1)S(1)}, bf16[304,256]{1,0:T(8,128)(2,1)S(1)}, u32[]{:S(2)}, u32[]{:S(2)}) collective-permute-start(bf16[304,256]{1,0:T(8,128)(2,1)S(1)} %get-tuple-element.159), channel_id=1, source_target_pairs={{0,1},{1,0},{2,3},{3,2},{4,5},{5,4},{6,7},{7,6},{8,9},{9,8},{10,11... | collective-permute-start | bytes 466952 | tf_op jit(solution)/shard_map/ppermute | solution.py:617
  72.5 3.1 %copy-start.3 = (bf16[1024,256]{1,0:T(8,128)(2,1)S(1)}, bf16[1024,256]{1,0:T(8,128)(2,1)}, u32[]{:S(2)}) copy-start(bf16[1024,256]{1,0:T(8,128)(2,1)} %cur_ref.5) | copy-start | bytes 1572868
  72.5 3.1 %copy-start.7 = (bf16[352,256]{1,0:T(8,128)(2,1)S(1)}, bf16[352,256]{1,0:T(8,128)(2,1)}, u32[]{:S(2)}) copy-start(bf16[352,256]{1,0:T(8,128)(2,1)} %get-tuple-element.115.p0) | copy-start | bytes 540676
  81.5 2.5 %collective-permute-start.21 = (bf16[4,256,256]{2,1,0:T(8,128)(2,1)S(1)}, bf16[4,256,256]{2,1,0:T(8,128)(2,1)S(1)}, u32[]{:S(2)}, u32[]{:S(2)}) collective-permute-start(bf16[4,256,256]{2,1,0:T(8,128)(2,1)S(1)} %get-tuple-element.174), channel_id=1, source_target_pairs={{0,4},{4,0},{8,12},{12,8},{16,20},{20,16},{24,28},{28,24},{1,5},{5... | collective-permute-start | bytes 1572872 | tf_op jit(solution)/shard_map/ppermute | solution.py:617
  84.1 6.7 %collective-permute-start.25 = (bf16[256,256]{1,0:T(8,128)(2,1)S(1)}, bf16[256,256]{1,0:T(8,128)(2,1)S(1)}, u32[]{:S(2)}, u32[]{:S(2)}) collective-permute-start(bf16[256,256]{1,0:T(8,128)(2,1)S(1)} %get-tuple-element.181), channel_id=1, source_target_pairs={{0,1},{1,0},{2,3},{3,2},{4,5},{5,4},{6,7},{7,6},{8,9},{9,8},{10,11... | collective-permute-start | bytes 393224 | tf_op jit(solution)/shard_map/ppermute | solution.py:617
  85.9 6.8 %collective-permute-start.26 = (bf16[256,256]{1,0:T(8,128)(2,1)S(1)}, bf16[256,256]{1,0:T(8,128)(2,1)S(1)}, u32[]{:S(2)}, u32[]{:S(2)}) collective-permute-start(bf16[256,256]{1,0:T(8,128)(2,1)S(1)} %get-tuple-element.182), channel_id=1, source_target_pairs={{0,2},{1,3},{2,0},{3,1},{4,6},{5,7},{6,4},{7,5},{8,10},{9,11},{10,... | collective-permute-start | bytes 393224 | tf_op jit(solution)/shard_map/ppermute | solution.py:617
  86.7 11.8 %collective-permute-start.27 = (bf16[256,256]{1,0:T(8,128)(2,1)S(1)}, bf16[256,256]{1,0:T(8,128)(2,1)S(1)}, u32[]{:S(2)}, u32[]{:S(2)}) collective-permute-start(bf16[256,256]{1,0:T(8,128)(2,1)S(1)} %get-tuple-element.183), channel_id=1, source_target_pairs={{0,3},{1,2},{2,1},{3,0},{4,7},{5,6},{6,5},{7,4},{8,11},{9,10},{10,... | collective-permute-start | bytes 393224 | tf_op jit(solution)/shard_map/ppermute | solution.py:617
  87.2 13.9 %collective-permute-start.30 = (bf16[2,176,256]{2,1,0:T(8,128)(2,1)S(1)}, bf16[2,176,256]{2,1,0:T(8,128)(2,1)S(1)}, u32[]{:S(2)}, u32[]{:S(2)}) collective-permute-start(bf16[2,176,256]{2,1,0:T(8,128)(2,1)S(1)} %get-tuple-element.195), channel_id=1, source_target_pairs={{0,4},{4,0},{8,12},{12,8},{16,20},{20,16},{24,28},{28,24},{1,5},{5... | collective-permute-start | bytes 540680 | tf_op jit(solution)/shard_map/ppermute | solution.py:617
  88.5 12.7 %collective-permute-start.29 = (bf16[2,176,256]{2,1,0:T(8,128)(2,1)S(1)}, bf16[2,176,256]{2,1,0:T(8,128)(2,1)S(1)}, u32[]{:S(2)}, u32[]{:S(2)}) collective-permute-start(bf16[2,176,256]{2,1,0:T(8,128)(2,1)S(1)} %get-tuple-element.193), channel_id=1, source_target_pairs={{0,4},{4,0},{8,12},{12,8},{16,20},{20,16},{24,28},{28,24},{1,5},{5... | collective-permute-start | bytes 540680 | tf_op jit(solution)/shard_map/ppermute | solution.py:617
  98.7 12.8 %collective-permute-start.34 = (bf16[288,256]{1,0:T(8,128)(2,1)S(1)}, bf16[288,256]{1,0:T(8,128)(2,1)S(1)}, u32[]{:S(2)}, u32[]{:S(2)}) collective-permute-start(bf16[288,256]{1,0:T(8,128)(2,1)S(1)} %get-tuple-element.201.high), channel_id=1, source_target_pairs={{0,16},{4,20},{8,24},{12,28},{16,0},{20,4},{24,8},{28,12},{1,17},{... | collective-permute-start | bytes 442376 | tf_op jit(solution)/shard_map/ppermute | solution.py:617
  100.0 11.5 %collective-permute-start.28 = (bf16[272,256]{1,0:T(8,128)(2,1)S(1)}, bf16[272,256]{1,0:T(8,128)(2,1)S(1)}, u32[]{:S(2)}, u32[]{:S(2)}) collective-permute-start(bf16[272,256]{1,0:T(8,128)(2,1)S(1)} %get-tuple-element.191.low), channel_id=1, source_target_pairs={{0,8},{4,12},{8,0},{12,4},{16,24},{20,28},{24,16},{28,20},{1,9},{5... | collective-permute-start | bytes 417800 | tf_op jit(solution)/shard_map/ppermute | solution.py:617
  101.2 3.7 %collective-permute-start.31 = (bf16[176,256]{1,0:T(8,128)(2,1)S(1)}, bf16[176,256]{1,0:T(8,128)(2,1)S(1)}, u32[]{:S(2)}, u32[]{:S(2)}) collective-permute-start(bf16[176,256]{1,0:T(8,128)(2,1)S(1)} %get-tuple-element.197), channel_id=1, source_target_pairs={{0,1},{1,0},{2,3},{3,2},{4,5},{5,4},{6,7},{7,6},{8,9},{9,8},{10,11... | collective-permute-start | bytes 270344 | tf_op jit(solution)/shard_map/ppermute | solution.py:617
  101.3 5.2 %collective-permute-start.32 = (bf16[176,256]{1,0:T(8,128)(2,1)S(1)}, bf16[176,256]{1,0:T(8,128)(2,1)S(1)}, u32[]{:S(2)}, u32[]{:S(2)}) collective-permute-start(bf16[176,256]{1,0:T(8,128)(2,1)S(1)} %get-tuple-element.198), channel_id=1, source_target_pairs={{0,2},{1,3},{2,0},{3,1},{4,6},{5,7},{6,4},{7,5},{8,10},{9,11},{10,... | collective-permute-start | bytes 270344 | tf_op jit(solution)/shard_map/ppermute | solution.py:617
  103.5 8.0 %collective-permute-start.33 = (bf16[176,256]{1,0:T(8,128)(2,1)S(1)}, bf16[176,256]{1,0:T(8,128)(2,1)S(1)}, u32[]{:S(2)}, u32[]{:S(2)}) collective-permute-start(bf16[176,256]{1,0:T(8,128)(2,1)S(1)} %get-tuple-element.199), channel_id=1, source_target_pairs={{0,3},{1,2},{2,1},{3,0},{4,7},{5,6},{6,5},{7,4},{8,11},{9,10},{10,... | collective-permute-start | bytes 270344 | tf_op jit(solution)/shard_map/ppermute | solution.py:617
  111.5 7.6 %collective-permute-start.39 = (bf16[288,256]{1,0:T(8,128)(2,1)S(1)}, bf16[288,256]{1,0:T(8,128)(2,1)S(1)}, u32[]{:S(2)}, u32[]{:S(2)}) collective-permute-start(bf16[288,256]{1,0:T(8,128)(2,1)S(1)} %get-tuple-element.206.high), channel_id=1, source_target_pairs={{0,8},{4,12},{8,0},{12,4},{16,24},{20,28},{24,16},{28,20},{1,9},{5... | collective-permute-start | bytes 442376 | tf_op jit(solution)/shard_map/ppermute | solution.py:617
  111.9 7.3 %collective-permute-start.35 = (bf16[272,256]{1,0:T(8,128)(2,1)S(1)}, bf16[272,256]{1,0:T(8,128)(2,1)S(1)}, u32[]{:S(2)}, u32[]{:S(2)}) collective-permute-start(bf16[272,256]{1,0:T(8,128)(2,1)S(1)} %get-tuple-element.203.low), channel_id=1, source_target_pairs={{0,16},{4,20},{8,24},{12,28},{16,0},{20,4},{24,8},{28,12},{1,17},{... | collective-permute-start | bytes 417800 | tf_op jit(solution)/shard_map/ppermute | solution.py:617
  112.1 4.7 %collective-permute-start.38 = (bf16[176,256]{1,0:T(8,128)(2,1)S(1)}, bf16[176,256]{1,0:T(8,128)(2,1)S(1)}, u32[]{:S(2)}, u32[]{:S(2)}) collective-permute-start(bf16[176,256]{1,0:T(8,128)(2,1)S(1)} %four_sum.4.refs_0_), channel_id=1, source_target_pairs={{0,24},{4,28},{8,16},{12,20},{16,8},{20,12},{24,0},{28,4},{1,25},{... | collective-permute-start | bytes 270344 | tf_op jit(solution)/shard_map/ppermute | solution.py:617
  114.4 4.7 %collective-permute-start.37 = (bf16[176,256]{1,0:T(8,128)(2,1)S(1)}, bf16[176,256]{1,0:T(8,128)(2,1)S(1)}, u32[]{:S(2)}, u32[]{:S(2)}) collective-permute-start(bf16[176,256]{1,0:T(8,128)(2,1)S(1)} %four_sum.4.refs_0_), channel_id=1, source_target_pairs={{0,16},{4,20},{8,24},{12,28},{16,0},{20,4},{24,8},{28,12},{1,17},{... | collective-permute-start | bytes 270344 | tf_op jit(solution)/shard_map/ppermute | solution.py:617
  114.6 4.6 %collective-permute-start.36 = (bf16[176,256]{1,0:T(8,128)(2,1)S(1)}, bf16[176,256]{1,0:T(8,128)(2,1)S(1)}, u32[]{:S(2)}, u32[]{:S(2)}) collective-permute-start(bf16[176,256]{1,0:T(8,128)(2,1)S(1)} %four_sum.4.refs_0_), channel_id=1, source_target_pairs={{0,8},{4,12},{8,0},{12,4},{16,24},{20,28},{24,16},{28,20},{1,9},{5... | collective-permute-start | bytes 270344 | tf_op jit(solution)/shard_map/ppermute | solution.py:617
  119.2 4.6 %collective-permute-start.41 = (bf16[416,256]{1,0:T(8,128)(2,1)S(1)}, bf16[416,256]{1,0:T(8,128)(2,1)S(1)}, u32[]{:S(2)}, u32[]{:S(2)}) collective-permute-start(bf16[416,256]{1,0:T(8,128)(2,1)S(1)} %get-tuple-element.209.high), channel_id=1, source_target_pairs={{0,4},{4,0},{8,12},{12,8},{16,20},{20,16},{24,28},{28,24},{1,5},{5... | collective-permute-start | bytes 638984 | tf_op jit(solution)/shard_map/ppermute | solution.py:617
  122.2 1.6 %collective-permute-start.40 = (bf16[272,256]{1,0:T(8,128)(2,1)S(1)}, bf16[272,256]{1,0:T(8,128)(2,1)S(1)}, u32[]{:S(2)}, u32[]{:S(2)}) collective-permute-start(bf16[272,256]{1,0:T(8,128)(2,1)S(1)} %get-tuple-element.208.low), channel_id=1, source_target_pairs={{0,4},{4,0},{8,12},{12,8},{16,20},{20,16},{24,28},{28,24},{1,5},{5... | collective-permute-start | bytes 417800 | tf_op jit(solution)/shard_map/ppermute | solution.py:617
  122.4 1.4 %collective-permute-start.42 = (bf16[176,256]{1,0:T(8,128)(2,1)S(1)}, bf16[176,256]{1,0:T(8,128)(2,1)S(1)}, u32[]{:S(2)}, u32[]{:S(2)}) collective-permute-start(bf16[176,256]{1,0:T(8,128)(2,1)S(1)} %four_sum.5.late), channel_id=1, source_target_pairs={{0,4},{4,0},{8,12},{12,8},{16,20},{20,16},{24,28},{28,24},{1,5},{5... | collective-permute-start | bytes 270344 | tf_op jit(solution)/shard_map/ppermute | solution.py:617
where the time goes:
time: 127 us; the launch traced here: 125 us
  Pallas kernels  44.4 us (35%)
  starting transfers between devices  40.2 us (32%)
  waiting for transfers between devices  35.8 us (28%)
  local copies, waits for them, and re-layouts  3.73 us (3%)
    ppermute x43, starting transfers between devices, swap(): return lax.ppermute(x, axis, [(i, i ^ mask) for i in range(size)])  40.2 us
    pallas_call x10, Pallas kernels, call(): pl.pallas_call(kernel, in_specs=[VMEM] * len(args), out_specs=[VMEM] * le...  39.2 us
    ppermute x43, waiting for transfers between devices, swap(): return lax.ppermute(x, axis, [(i, i ^ mask) for i in range(size)])  35.8 us
    unnamed x28, local copies, waits for them, and re-layouts  3.73 us
    pallas_call x1, Pallas kernels, body(): pl.pallas_call(pack_kernel, in_specs=[SMEM] + [ANY] * 5 + [VMEM], out_spe...  3.03 us
  transfers between devices with their start and end apart: 43, of which 23 were waited for; matrix products, arithmetic and copies ran while one was open for 0% of the time, Pallas kernels for 26%

commit v1 on v0

--- a/solution.py
+++ b/solution.py
@@ -47,14 +47,18 @@
 
 
 def gelu_and_slope(u):
-    d = 1.0 + (0.3275911 * 0.7071067811865476) * jnp.abs(u)
-    t = pl.reciprocal(d, approx=True)
-    t = t * (2.0 - d * t)
-    e = jnp.exp2((-0.5 * 1.4426950408889634) * (u * u))
-    poly = ((((0.5 * 1.061405429) * t - 0.5 * 1.453152027) * t + 0.5 * 1.421413741) * t - 0.5 * 0.284496736) * t + 0.5 * 0.254829592
-    tail = poly * t * e
-    cdf = jnp.where(u >= 0.0, 1.0 - tail, tail)
-    return u * cdf, cdf + u * (e * 0.3989422804014327)
+    cdf = 0.5 + 0.5 * lax.erf(u * 0.7071067811865476)
+    density = jnp.exp2((-0.5 * 1.4426950408889634) * (u * u))
+    return u * cdf, cdf + u * (density * 0.3989422804014327)
+
+
+def slot_scores(q, k, mask):
+    ones = jnp.where(lax.broadcasted_iota(jnp.int32, mask.shape, 0) == 0, 1.0, 0.0).astype(BF)
+    return tn(jnp.concatenate([k, mask], axis=0), jnp.concatenate([q * BF(0.125), ones], axis=0))
+
+
+def mask_rows(mask_ref, rows):
+    return mask_ref[pl.ds(pl.multiple_of(rows.start // 16, 16), 16), :]
 
 
 def head_index():
@@ -97,11 +101,11 @@
     place_pieces((pieces[0][layer], pieces[1][layer]), pieces[2:5], pieces[5:8], wm, first)
 
 
-def each_sample(rows, unroll, step, *init):
+def each_sample(rows, unroll, step, *init, size=256):
     def body(i, carried):
-        return step(pl.ds(pl.multiple_of(i * 256, 256), 256), *carried)
-
-    return lax.fori_loop(0, rows // 256, body, init, unroll=unroll)
+        return step(pl.ds(pl.multiple_of(i * size, size), size), *carried)
+
+    return lax.fori_loop(0, rows // size, body, init, unroll=unroll)
 
 
 def attn_fwd_kernel(layer, first, cur_ref, mask_ref, gain_ref, p0, p1, p2, p3, p4, p5, p6,
@@ -112,9 +116,9 @@
         cur = cur_ref[rows, :].astype(F32)
         nrm = (cur * rescale_of(cur) * gain).astype(BF)
         nrm_ref[rows, :] = nrm
-        mask = jnp.concatenate([mask_ref[rows, :]] * 2, axis=1)
+        mask = mask_rows(mask_ref, rows)
         qkv = [nt(wa[m, 0:192, :], nrm).astype(BF) for m in range(4)]
-        scores = [tn(qkv[m][64:128], qkv[m][0:64] * BF(0.125)) + mask for m in range(4)]
+        scores = [slot_scores(qkv[m][0:64], qkv[m][64:128], mask) for m in range(4)]
         cross = nt(nrm, w_cross[...]) + bias
         probs = []
         for m in range(4):
@@ -228,7 +232,7 @@
 
 
 def attn_pre_kernel(layer, first, grad_ref, gm_ref, cur_ref, nrm_ref, mix_ref, p0, p1, p2, p3, p4, p5, p6,
-                    gmix_ref, d_cross_ref, d_out_ref, base_ref, gn_ref, small_ref,
+                    gmix_ref, d_cross_ref, d_out_ref, base_ref, gn_ref, small_ref, dot_ref,
                     wa, w_cross, w_out, ga_all, gc_all):
     bias = place_attn(first, (p0, p1, p2, p3, p4, p5, p6), wa, w_cross, w_out)
 
@@ -239,7 +243,12 @@
         ga_all[rows, :] = ga
         gc = (grad * cur_ref[rows, :].astype(F32)).astype(BF)
         gc_all[rows, :] = gc
-        gmix_ref[:, rows] = nt(w_out[...], ga).astype(BF)
+        gmix = nt(w_out[...], ga).astype(BF)
+        gmix_ref[:, rows] = gmix
+        for m in range(4):
+            head = slice(m * HD, (m + 1) * HD)
+            product = gmix[head].astype(F32) * mix_ref[head, rows].astype(F32)
+            dot_ref[m:m + 1, rows] = jnp.sum(product, axis=0, keepdims=True)
         gn_ref[rows, :] = nn(gc, w_cross[...])
         base_ref[rows, :] = gm + grad * (nt(nrm_ref[rows, :], w_cross[...]) + bias)
         return (bias_grad + jnp.sum(gc.astype(F32), axis=0, keepdims=True), )
@@ -252,21 +261,19 @@
     small_ref[1:2, :] = jnp.sum(d_cross * w_cross[...].astype(F32), axis=0, keepdims=True)
 
 
-def qkv_back(rows, mask_ref, qkv_ref, lse_ref, gmix_ref):
-    mask = jnp.concatenate([mask_ref[rows, :]] * 2, axis=1)
+def qkv_back(rows, mask_ref, qkv_ref, lse_ref, gmix_ref, dot_ref):
+    mask = mask_rows(mask_ref, rows)
     parts = []
     for m in range(4):
         q, k, v = (qkv_ref[m * 192 + i * HD:m * 192 + (i + 1) * HD, rows] for i in range(3))
         parts.append((q, k, v, gmix_ref[m * HD:(m + 1) * HD, rows]))
-    scores = [tn(k, q * BF(0.125)) + mask for q, k, v, go in parts]
+    scores = [slot_scores(q, k, mask) for q, k, v, go in parts]
     gps = [tn(v, go) for q, k, v, go in parts]
     ps, gss = [], []
     for m in range(4):
         p = jnp.exp(scores[m] - lse_ref[m:m + 1, rows])
-        weighted = gps[m] * p
-        dot = jnp.sum(weighted, axis=0, keepdims=True)
         ps.append(p.astype(BF))
-        gss.append((weighted - p * dot).astype(BF))
+        gss.append((p * (gps[m] - dot_ref[m:m + 1, rows])).astype(BF))
     return [
         jnp.concatenate([nn(k, gs) * 0.125, nt(q, gs) * 0.125, nt(go, p)], axis=0).astype(BF)
         for (q, k, v, go), p, gs in zip(parts, ps, gss)
@@ -304,14 +311,14 @@
             ref[i, 168:176, :] = low
 
 
-def attn_bwd_kernel(layer, first, mask_ref, nrm_ref, qkv_ref, lse_ref, gain_ref, gmix_ref, d_cross_ref, d_out_ref, small, mlp_small,
+def attn_bwd_kernel(layer, first, mask_ref, nrm_ref, qkv_ref, lse_ref, gain_ref, gmix_ref, d_cross_ref, d_out_ref, small, dot_ref, mlp_small,
                     cur_ref, base_ref, gn_ref, p0, p1, p2, p3, p4, p5, p6,
                     out_ref, keep_ref, send_ref, wa, gqkv_all, payload):
     place_qkv(first, (p0, p1, p2, p3, p4, p5, p6), wa)
 
     def step(rows):
         gn = gn_ref[rows, :]
-        for m, gqkv in enumerate(qkv_back(rows, mask_ref, qkv_ref, lse_ref, gmix_ref)):
+        for m, gqkv in enumerate(qkv_back(rows, mask_ref, qkv_ref, lse_ref, gmix_ref, dot_ref)):
             gqkv_all[m * 192:(m + 1) * 192, rows] = gqkv
             gn = gn + tn(gqkv, wa[m, 0:192, :])
         out_ref[rows, :] = base_ref[rows, :] + norm_grad(cur_ref[rows, :].astype(F32), gain_ref[layer:layer + 1, :], gn)
@@ -322,12 +329,12 @@
                    payload, keep_ref, (send_ref,))
 
 
-def attn_grads_kernel(layer, first, mask_ref, nrm_ref, qkv_ref, lse_ref, gain_ref, gmix_ref, d_cross_ref, d_out_ref, small, mlp_small,
+def attn_grads_kernel(layer, first, mask_ref, nrm_ref, qkv_ref, lse_ref, gain_ref, gmix_ref, d_cross_ref, d_out_ref, small, dot_ref, mlp_small,
                       p0, p1, p2, p3, p4, p5, p6, gqkv_all, keep_ref, send_low, send_high, wa, payload):
     place_qkv(first, (p0, p1, p2, p3, p4, p5, p6), wa)
 
     def step(rows):
-        for m, gqkv in enumerate(qkv_back(rows, mask_ref, qkv_ref, lse_ref, gmix_ref)):
+        for m, gqkv in enumerate(qkv_back(rows, mask_ref, qkv_ref, lse_ref, gmix_ref, dot_ref)):
             gqkv_all[m * 192:(m + 1) * 192, rows] = gqkv
         return ()
 
@@ -378,11 +385,12 @@
         for copy in mlp_half(down):
             copy.start()
 
-    slots = lax.broadcasted_iota(jnp.int32, (256, 128), 0)
-    samples = mask.shape[0] // 256
+    slots = lax.broadcasted_iota(jnp.int32, (16, 256), 1)
+    first = lax.broadcasted_iota(jnp.int32, (16, 256), 0) == 0
+    samples = mask.shape[0] // 16
     for i in range(samples):
         length = lens[head_index() * samples + i]
-        mask[i * 256:(i + 1) * 256, :] = jnp.where(slots < length, 0.0, MASKED_SCORE)
+        mask[i * 16:(i + 1) * 16, :] = jnp.where(jnp.logical_and(first, slots >= length), MASKED_SCORE, 0.0).astype(BF)
     lane = lax.broadcasted_iota(jnp.int32, (LAYERS, 256), 1) // HD
     wide = jnp.concatenate([b[...].astype(F32)] * 4, axis=1)
     wide = jnp.where(lane == head_index(), wide, 0.0)
@@ -556,7 +564,7 @@
 def attn_pre(layer, first, grad, gm, cur, saved, pieces):
     rows = cur.shape[0]
     nrm, _, mix, _ = saved
-    outs = [((256, rows), BF), ((256, 256), BF), ((256, 256), BF), ((rows, 256), F32), ((rows, 256), F32), ((8, 256), F32)]
+    outs = [((256, rows), BF), ((256, 256), BF), ((256, 256), BF), ((rows, 256), F32), ((rows, 256), F32), ((8, 256), F32), ((8, rows), F32)]
     scratch = ATTN_SCRATCH + [((rows, 256), BF), ((rows, 256), BF)]
     return call(functools.partial(attn_pre_kernel, layer, first), outs, scratch, "attn_pre", grad, gm, cur, nrm, mix, *pieces)
 
@@ -567,18 +575,18 @@
 def attn_bwd(layer, first, cur, mask, saved, gain, pre, mlp_small, pieces):
     rows = cur.shape[0]
     nrm, qkv, _, lse = saved
-    gmix, d_cross, d_out, base, gn, small = pre
+    gmix, d_cross, d_out, base, gn, small, dot = pre
     scratch = [((4, 352, 256), BF), ((768, rows), BF), ((4, 320, 256), BF)]
     return call(functools.partial(attn_bwd_kernel, layer, first), [((rows, 256), F32)] + PAYLOAD, scratch, "attn_bwd",
-                mask, nrm, qkv, lse, gain, gmix, d_cross, d_out, small, mlp_small, cur, base, gn, *pieces)
+                mask, nrm, qkv, lse, gain, gmix, d_cross, d_out, small, dot, mlp_small, cur, base, gn, *pieces)
 
 
 def attn_grads(layer, first, mask, saved, gain, pre, mlp_small, pieces):
     nrm, qkv, _, lse = saved
-    gmix, d_cross, d_out, _, _, small = pre
+    gmix, d_cross, d_out, _, _, small, dot = pre
     scratch = [((4, 352, 256), BF), ((4, 320, 256), BF)]
     return call(functools.partial(attn_grads_kernel, layer, first), [((768, nrm.shape[0]), BF), ((4, 176, 256), BF), ((2, 176, 256), BF), ((2, 176, 256), BF)], scratch, "attn_grads",
-                mask, nrm, qkv, lse, gain, gmix, d_cross, d_out, small, mlp_small, *pieces)
+                mask, nrm, qkv, lse, gain, gmix, d_cross, d_out, small, dot, mlp_small, *pieces)
 
 
 def attn_post(layer, first, gqkv, gain, cur, pre, pieces):
@@ -646,8 +654,8 @@
             kernel, more = (last_pair_kernel, 128) if last else (pair_sum_kernel, 0)
             return small_call(kernel, [(low.shape, BF), ((high.shape[0] + more, 256), BF)], "pair_sum")(low, got[0], high, got[1])
 
-        low, high = pair(low, high, pairs[0], late[1:], len(pairs) == 1)
-        late = four_sum(160, late)
+        late = four_sum(160, late, LONG)
+        low, high = pair(low, high, pairs[0], [late], len(pairs) == 1)
         for masks in late_steps():
             terms = [late] + [swap(late, "dp", dp_size, mask) for mask in masks]
             before = terms[1:]
@@ -663,7 +671,7 @@
             in_specs=[SMEM] + [ANY] * 5 + [VMEM],
             out_specs=[VMEM] * 6,
             out_shape=[jax.ShapeDtypeStruct((n, 256), BF) for n in (352, 352, 176, 432, 256)]
-            + [jax.ShapeDtypeStruct((rows, 128), F32)],
+            + [jax.ShapeDtypeStruct((rows // 16, 256), BF)],
             scratch_shapes=[pltpu.SemaphoreType.DMA((2,))],
             name="pack",
         )(lengths, w_qkv.transpose(0, 2, 3, 1), w_cross.transpose(0, 2, 1), w_out, w_up, w_down, b_cross)
@@ -698,7 +706,7 @@
         grad0 = attn_post(0, 0, tie(gqkv, *sums), gain_attn, tokens, pre, pieces_a0)
         low, high = small_call(early_sum_kernel, [((176 + CUT, 256), BF), ((384 - CUT, 256), BF)], "early_sum")(
             one, *[tie(x, grad0) for x in got])
-        sums_a0 = core_sum((160,), (keep_a0, *[tie(core_swap(x), low) for x in send_a0]))
+        sums_a0 = core_sum((160,), (keep_a0, *[core_swap(x) for x in send_a0]))
         late = scatter(sums_a0)
         low, high, late = sum_early_late(low, high, late)
         d_qkv, d_out, d_up, d_down, d_cross, d_ga, d_gm, d_bias = small_call(

time: 127 us -> 122 us (0.961)
  Pallas kernels: 44.4 us -> 38.6 us
  starting transfers between devices: 40.2 us -> 43.7 us
    pallas_call x10, Pallas kernels: 39.2 us -> 33.5 us  [call(): pl.pallas_call(kernel, in_specs=[VMEM] * len(args), out_specs=[VMEM] * le...]
    ppermute x43, starting transfers between devices: 40.2 us -> 43.7 us  [swap(): return lax.ppermute(x, axis, [(i, i ^ mask) for i in range(size)])]
    unnamed x28 -> x24, local copies, waits for them, and re-layouts: 3.73 us -> 3.44 us
  transfers between devices with their start and end apart: 43 -> 43, of which waited for: 23 -> 23; matrix products, arithmetic and copies ran while one was open for 0% -> 0% of each run, Pallas kernels for 26% -> 23%
where the time goes in v1:
time: 122 us; the launch traced here: 121 us
  starting transfers between devices  43.7 us (36%)
  Pallas kernels  38.6 us (32%)
  waiting for transfers between devices  34.8 us (29%)
  local copies, waits for them, and re-layouts  3.44 us (3%)
    ppermute x43, starting transfers between devices, swap(): return lax.ppermute(x, axis, [(i, i ^ mask) for i in range(size)])  43.7 us
    ppermute x43, waiting for transfers between devices, swap(): return lax.ppermute(x, axis, [(i, i ^ mask) for i in range(size)])  34.8 us
    pallas_call x10, Pallas kernels, call(): pl.pallas_call(kernel, in_specs=[VMEM] * len(args), out_specs=[VMEM] * le...  33.5 us
    unnamed x24, local copies, waits for them, and re-layouts  3.44 us
    pallas_call x1, Pallas kernels, body(): pl.pallas_call(pack_kernel, in_specs=[SMEM] + [ANY] * 5 + [VMEM], out_spe...  2.85 us
  transfers between devices with their start and end apart: 43, of which 23 were waited for; matrix products, arithmetic and copies ran while one was open for 0% of the time, Pallas kernels for 23%

profile of v1, /device:TPU:9, one launch (start us, length us, event | category | flops | bytes accessed | tf_op | source)
XLA Modules:
  0.0 121.3 jit_solution(7034966476793800536)
XLA Ops:
  0.7 2.8 %pack.1 = (bf16[352,256]{1,0:T(8,128)(2,1)}, bf16[352,256]{1,0:T(8,128)(2,1)}, bf16[176,256]{1,0:T(8,128)(2,1)}, bf16[432,256]{1,0:T(8,128)(2,1)}, bf16[256,256]{1,0:T(8,128)(2,1)}, /*index=5*/bf16[64,256]{1,0:T(8,128)(2,1)}) custom-call(s32[16]{0:T(128)} %lens.1, bf16[2,3,64,256]{3,2,1,0:T(8,128)(2,1)} %bitcast.4, bf16[2,64,256]{2,1,0:T(8,128)(2,1)} %bitcast.5, ...), custom_call_target="tpu_custom_call" | custom-call | tf_op jit(solution)/shard_map/pack/pallas_call | solution.py:669
  3.5 1.4 %collective-permute-start.2 = (bf16[176,256]{1,0:T(8,128)(2,1)}, bf16[176,256]{1,0:T(8,128)(2,1)S(1)}, u32[]{:S(2)}, u32[]{:S(2)}) collective-permute-start(bf16[176,256]{1,0:T(8,128)(2,1)} %get-tuple-element.116), channel_id=1, source_target_pairs={{0,3},{1,2},{2,1},{3,0},{4,7},{5,6},{6,5},{7,4},{8,11},{9,10},{10,... | collective-permute-start | bytes 270344 | tf_op jit(solution)/shard_map/ppermute | solution.py:625
  4.9 2.2 %collective-permute-start.6 = (bf16[432,256]{1,0:T(8,128)(2,1)}, bf16[432,256]{1,0:T(8,128)(2,1)S(1)}, u32[]{:S(2)}, u32[]{:S(2)}) collective-permute-start(bf16[432,256]{1,0:T(8,128)(2,1)} %get-tuple-element.119), channel_id=1, source_target_pairs={{0,1},{1,0},{2,3},{3,2},{4,5},{5,4},{6,7},{7,6},{8,9},{9,8},{10,11... | collective-permute-start | bytes 663560 | tf_op jit(solution)/shard_map/ppermute | solution.py:625
  7.5 0.9 collective-permute-done.2.p3
  8.4 2.8 %collective-permute-start.5 = (bf16[176,256]{1,0:T(8,128)(2,1)S(1)}, bf16[176,256]{1,0:T(8,128)(2,1)S(1)}, u32[]{:S(2)}, u32[]{:S(2)}) collective-permute-start(bf16[176,256]{1,0:T(8,128)(2,1)S(1)} %collective-permute-done.2.p3), channel_id=1, source_target_pairs={{0,4},{4,0},{8,12},{12,8},{16,20},{20,16},{24,28},{28,24},{1,5},{5... | collective-permute-start | bytes 270344 | tf_op jit(solution)/shard_map/ppermute | solution.py:625
  11.1 0.4 collective-permute-start.8
  11.5 3.6 %collective-permute-done.1.p2 = bf16[176,256]{1,0:T(8,128)(2,1)S(1)} collective-permute-done((bf16[176,256]{1,0:T(8,128)(2,1)}, bf16[176,256]{1,0:T(8,128)(2,1)S(1)}, u32[]{:S(2)}, u32[]{:S(2)}) %collective-permute-start.1) | collective-permute-done | bytes 90144 | tf_op jit(solution)/shard_map/ppermute | solution.py:625
  15.2 2.7 %collective-permute-done.p1 = bf16[176,256]{1,0:T(8,128)(2,1)S(1)} collective-permute-done((bf16[176,256]{1,0:T(8,128)(2,1)}, bf16[176,256]{1,0:T(8,128)(2,1)S(1)}, u32[]{:S(2)}, u32[]{:S(2)}) %collective-permute-start) | collective-permute-done | bytes 90144 | tf_op jit(solution)/shard_map/ppermute | solution.py:625
  17.9 2.7 %collective-permute-start.4 = (bf16[176,256]{1,0:T(8,128)(2,1)S(1)}, bf16[176,256]{1,0:T(8,128)(2,1)S(1)}, u32[]{:S(2)}, u32[]{:S(2)}) collective-permute-start(bf16[176,256]{1,0:T(8,128)(2,1)S(1)} %collective-permute-done.1.p2), channel_id=1, source_target_pairs={{0,4},{4,0},{8,12},{12,8},{16,20},{20,16},{24,28},{28,24},{1,5},{5... | collective-permute-start | bytes 270344 | tf_op jit(solution)/shard_map/ppermute | solution.py:625
  20.6 0.9 collective-permute-done.4.p5
  21.9 1.0 copy-done
  23.0 0.9 copy-done.4
  23.9 0.8 copy-done.8
  24.6 0.7 copy-done.9
  25.3 4.0 %attn_fwd.2 = (f32[1024,256]{1,0:T(8,128)S(1)}, f32[1024,256]{1,0:T(8,128)S(1)}, bf16[1024,256]{1,0:T(8,128)(2,1)S(1)}, bf16[768,1024]{1,0:T(8,128)(2,1)S(1)}, b...) custom-call(bf16[1024,256]{1,0:T(8,128)(2,1)S(1)} %copy-done, bf16[64,256]{1,0:T(8,128)(2,1)S(1)} %copy-done.8, ...), custom_call_target="tpu_custom_call" | custom-call | flops 1000 | bytes 1024 | tf_op jit(solution)/shard_map/attn_fwd/pallas_call | solution.py:520
  29.6 3.3 %collective-permute-done.7.p3.p2 = bf16[432,256]{1,0:T(8,128)(2,1)S(1)} collective-permute-done((bf16[432,256]{1,0:T(8,128)(2,1)}, bf16[432,256]{1,0:T(8,128)(2,1)S(1)}, u32[]{:S(2)}, u32[]{:S(2)}) %collective-permute-start.7) | collective-permute-done | bytes 221216 | tf_op jit(solution)/shard_map/ppermute | solution.py:625
  32.9 0.8 collective-permute-start.10
  33.7 0.7 collective-permute-start.14
  34.3 3.9 %collective-permute-start.13 = (bf16[256,256]{1,0:T(8,128)(2,1)}, bf16[256,256]{1,0:T(8,128)(2,1)S(1)}, u32[]{:S(2)}, u32[]{:S(2)}) collective-permute-start(bf16[256,256]{1,0:T(8,128)(2,1)} %get-tuple-element.127), channel_id=1, source_target_pairs={{0,2},{1,3},{2,0},{3,1},{4,6},{5,7},{6,4},{7,5},{8,10},{9,11},{10,... | collective-permute-start | bytes 393224 | tf_op jit(solution)/shard_map/ppermute | solution.py:625
  38.3 2.5 %mlp_fwd.1 = (f32[1024,256]{1,0:T(8,128)S(1)}, bf16[1024,1024]{1,0:T(8,128)(2,1)S(1)}, bf16[1024,1024]{1,0:T(8,128)(2,1)S(1)}) custom-call(f32[1024,256]{1,0:T(8,128)S(1)} %get-tuple-element.117.middle_ref, f32[1024,256]{1,0:T(8,128)S(1)} %get-tuple-element.118.base_ref, f32[2,256]{1,0:T(2,128)S(1)} %copy-done.11, bf16[2,256,256]{2,1,0:T(8,128)(2,1)S(1)} %copy-done.2, ...), custom_call_target="tpu_custom_call" | custom-call | flops 1000 | bytes 1024 | tf_op jit(solution)/shard_map/mlp_fwd/pallas_call | solution.py:520
  40.8 4.0 %attn_fwd.3 = (f32[1024,256]{1,0:T(8,128)S(1)}, f32[1024,256]{1,0:T(8,128)S(1)}, bf16[1024,256]{1,0:T(8,128)(2,1)S(1)}, bf16[768,1024]{1,0:T(8,128)(2,1)S(1)}, b...) custom-call(f32[1024,256]{1,0:T(8,128)S(1)} %get-tuple-element.123.cur_ref, bf16[64,256]{1,0:T(8,128)(2,1)S(1)} %copy-done.8, ...), custom_call_target="tpu_custom_call" | custom-call | flops 1000 | bytes 1024 | tf_op jit(solution)/shard_map/attn_fwd/pallas_call | solution.py:520
  44.9 1.8 %collective-permute-done.13.p3 = bf16[256,256]{1,0:T(8,128)(2,1)S(1)} collective-permute-done((bf16[256,256]{1,0:T(8,128)(2,1)}, bf16[256,256]{1,0:T(8,128)(2,1)S(1)}, u32[]{:S(2)}, u32[]{:S(2)}) %collective-permute-start.13) | collective-permute-done | bytes 131104 | tf_op jit(solution)/shard_map/ppermute | solution.py:625
  46.8 1.4 %collective-permute-start.15 = (bf16[256,256]{1,0:T(8,128)(2,1)S(1)}, bf16[256,256]{1,0:T(8,128)(2,1)S(1)}, u32[]{:S(2)}, u32[]{:S(2)}) collective-permute-start(bf16[256,256]{1,0:T(8,128)(2,1)S(1)} %collective-permute-done.12.p2), channel_id=1, source_target_pairs={{0,4},{4,0},{8,12},{12,8},{16,20},{20,16},{24,28},{28,24},{1,5},{5... | collective-permute-start | bytes 393224 | tf_op jit(solution)/shard_map/ppermute | solution.py:625
  48.2 0.5 collective-permute-start.17
  48.7 0.5 collective-permute-done.15.p5
  49.7 5.6 %mlp_both.1 = (f32[1024,256]{1,0:T(8,128)}, f32[1024,256]{1,0:T(8,128)S(1)}, bf16[4,256,256]{2,1,0:T(8,128)(2,1)S(1)}, bf16[4,256,256]{2,1,0:T(8,128)(2,1)S(1)}, f32[8,256]{1,0:T(8,128)S(1)}) custom-call(f32[1024,256]{1,0:T(8,128)S(1)} %get-tuple-element.125.middle_ref, f32[1024,256]{1,0:T(8,128)S(1)} %get-tuple-element.126.base_ref, ...), custom_call_target="tpu_custom_call" | custom-call | flops 1000 | bytes 1024 | tf_op jit(solution)/shard_map/mlp_both/pallas_call | solution.py:520
  55.6 1.4 %attn_pre.2 = (bf16[256,1024]{1,0:T(8,128)(2,1)S(1)}, bf16[256,256]{1,0:T(8,128)(2,1)S(1)}, bf16[256,256]{1,0:T(8,128)(2,1)S(1)}, f32[1024,256]{1,0:T(8,128)S(1)...) custom-call(bf16[1024,256]{1,0:T(8,128)(2,1)S(1)} %copy-done.6, ...), custom_call_target="tpu_custom_call" | custom-call | flops 1000 | bytes 1024 | tf_op jit(solution)/shard_map/attn_pre/pallas_call | solution.py:520
  57.3 1.3 %collective-permute-start.19 = (bf16[4,128,256]{2,1,0:T(8,128)(2,1)S(1)}, bf16[4,128,256]{2,1,0:T(8,128)(2,1)S(1)}, u32[]{:S(2)}, u32[]{:S(2)}) collective-permute-start(bf16[4,128,256]{2,1,0:T(8,128)(2,1)S(1)} %get-tuple-element.142), channel_id=1, source_target_pairs={{0,8},{4,12},{8,0},{12,4},{16,24},{20,28},{24,16},{28,20},{1,9},{5... | collective-permute-start | bytes 786440 | tf_op jit(solution)/shard_map/ppermute | solution.py:625
  58.6 5.2 %attn_bwd.1 = (f32[1024,256]{1,0:T(8,128)S(1)}, bf16[4,176,256]{2,1,0:T(8,128)(2,1)S(1)}, bf16[4,176,256]{2,1,0:T(8,128)(2,1)S(1)}) custom-call(bf16[64,256]{1,0:T(8,128)(2,1)S(1)} %copy-done.8, bf16[1024,256]{1,0:T(8,128)(2,1)S(1)} %get-tuple-element.138.nrm_ref, bf16[768,1024]{1,0:T(8,128)(2,1)S(1)} %get-tuple-element.144.qkv_ref, ...), custom_call_target="tpu_custom_call" | custom-call | flops 1000 | bytes 1024 | tf_op jit(solution)/shard_map/attn_bwd/pallas_call | solution.py:520
  63.8 0.7 collective-permute-start.20
  64.5 0.5 collective-permute-done.19.b
  65.0 0.8 collective-permute-done.20.refs_2_
  65.9 0.5 collective-permute-start.24
  66.4 2.9 %collective-permute-start.23 = (bf16[304,256]{1,0:T(8,128)(2,1)S(1)}, bf16[304,256]{1,0:T(8,128)(2,1)S(1)}, u32[]{:S(2)}, u32[]{:S(2)}) collective-permute-start(bf16[304,256]{1,0:T(8,128)(2,1)S(1)} %get-tuple-element.161), channel_id=1, source_target_pairs={{0,2},{1,3},{2,0},{3,1},{4,6},{5,7},{6,4},{7,5},{8,10},{9,11},{10,... | collective-permute-start | bytes 466952 | tf_op jit(solution)/shard_map/ppermute | solution.py:625
  69.3 3.1 %mlp_bwd.1 = (f32[1024,256]{1,0:T(8,128)S(1)}, bf16[4,256,256]{2,1,0:T(8,128)(2,1)S(1)}, bf16[4,256,256]{2,1,0:T(8,128)(2,1)S(1)}, f32[8,256]{1,0:T(8,128)S(1)}) custom-call(f32[1024,256]{1,0:T(8,128)S(1)} %get-tuple-element.163.grad_ref, f32[1024,256]{1,0:T(8,128)S(1)} %get-tuple-element.117.middle_ref, bf16[1024,1024]{1,0:T(8,128)(2,1)S(1)} %get-tuple-element.164.hid_ref, ...), custom_call_target="tpu_custom_call" | custom-call | flops 1000 | bytes 1024 | tf_op jit(solution)/shard_map/mlp_bwd/pallas_call | solution.py:520
  72.5 1.4 %attn_pre.3 = (bf16[256,1024]{1,0:T(8,128)(2,1)S(1)}, bf16[256,256]{1,0:T(8,128)(2,1)S(1)}, bf16[256,256]{1,0:T(8,128)(2,1)S(1)}, f32[1024,256]{1,0:T(8,128)S(1)...) custom-call(f32[1024,256]{1,0:T(8,128)S(1)} %get-tuple-element.163.grad_ref, ...), custom_call_target="tpu_custom_call" | custom-call | flops 1000 | bytes 1024 | tf_op jit(solution)/shard_map/attn_pre/pallas_call | solution.py:520
  73.9 3.9 %attn_grads.1 = (bf16[768,1024]{1,0:T(8,128)(2,1)S(1)}, bf16[4,176,256]{2,1,0:T(8,128)(2,1)S(1)}, bf16[2,176,256]{2,1,0:T(8,128)(2,1)S(1)}, bf16[2,176,256]{2,1,0:T(8,128)(2,1)S(1)}) custom-call(bf16[64,256]{1,0:T(8,128)(2,1)S(1)} %copy-done.8, bf16[1024,256]{1,0:T(8,128)(2,1)S(1)} %get-tuple-element.132.nrm_ref, ...), custom_call_target="tpu_custom_call" | custom-call | flops 1000 | bytes 1024 | tf_op jit(solution)/shard_map/attn_grads/pallas_call | solution.py:520
  77.8 1.2 %collective-permute-start.29 = (bf16[2,176,256]{2,1,0:T(8,128)(2,1)S(1)}, bf16[2,176,256]{2,1,0:T(8,128)(2,1)S(1)}, u32[]{:S(2)}, u32[]{:S(2)}) collective-permute-start(bf16[2,176,256]{2,1,0:T(8,128)(2,1)S(1)} %get-tuple-element.195), channel_id=1, source_target_pairs={{0,4},{4,0},{8,12},{12,8},{16,20},{20,16},{24,28},{28,24},{1,5},{5... | collective-permute-start | bytes 540680 | tf_op jit(solution)/shard_map/ppermute | solution.py:625
  79.1 0.8 collective-permute-start.21
  80.0 1.4 %collective-permute-done.21.refs_1_ = bf16[4,256,256]{2,1,0:T(8,128)(2,1)S(1)} collective-permute-done((bf16[4,256,256]{2,1,0:T(8,128)(2,1)S(1)}, bf16[4,256,256]{2,1,0:T(8,128)(2,1)S(1)}, u32[]{:S(2)}, u32[]{:S(2)}) %collective-permute-start.21) | collective-permute-done | bytes 524320 | tf_op jit(solution)/shard_map/ppermute | solution.py:625
  81.6 1.6 %collective-permute-start.25 = (bf16[256,256]{1,0:T(8,128)(2,1)S(1)}, bf16[256,256]{1,0:T(8,128)(2,1)S(1)}, u32[]{:S(2)}, u32[]{:S(2)}) collective-permute-start(bf16[256,256]{1,0:T(8,128)(2,1)S(1)} %get-tuple-element.183), channel_id=1, source_target_pairs={{0,1},{1,0},{2,3},{3,2},{4,5},{5,4},{6,7},{7,6},{8,9},{9,8},{10,11... | collective-permute-start | bytes 393224 | tf_op jit(solution)/shard_map/ppermute | solution.py:625
  83.1 0.6 collective-permute-start.26
  83.7 0.7 collective-permute-start.27
  84.5 2.4 %collective-permute-start.31 = (bf16[176,256]{1,0:T(8,128)(2,1)S(1)}, bf16[176,256]{1,0:T(8,128)(2,1)S(1)}, u32[]{:S(2)}, u32[]{:S(2)}) collective-permute-start(bf16[176,256]{1,0:T(8,128)(2,1)S(1)} %get-tuple-element.198), channel_id=1, source_target_pairs={{0,1},{1,0},{2,3},{3,2},{4,5},{5,4},{6,7},{7,6},{8,9},{9,8},{10,11... | collective-permute-start | bytes 270344 | tf_op jit(solution)/shard_map/ppermute | solution.py:625
  86.8 0.6 collective-permute-start.32
  87.4 0.7 collective-permute-start.33
  88.1 2.4 %attn_post.1 = f32[1024,256]{1,0:T(8,128)} custom-call(bf16[768,1024]{1,0:T(8,128)(2,1)S(1)} %get-tuple-element.186.gqkv_all, f32[2,256]{1,0:T(2,128)S(1)} %copy-done.10, bf16[1024,256]{1,0:T(8,128)(2,1)S(1)} %copy-done.1, f32[1024,256]{1,0:T(8,128)S(1)} %get-tuple-element.187.base_ref, f32[1024,256]{1,0:T(8,128)S(1)} %get-tuple-element.188.gn_ref, ...), custom_call_target="tpu_custom_call" | custom-call | flops 1000 | bytes 1024 | tf_op jit(solution)/shard_map/attn_post/pallas_call | solution.py:520
  90.5 9.2 %collective-permute-done.27.c = bf16[256,256]{1,0:T(8,128)(2,1)S(1)} collective-permute-done((bf16[256,256]{1,0:T(8,128)(2,1)S(1)}, bf16[256,256]{1,0:T(8,128)(2,1)S(1)}, u32[]{:S(2)}, u32[]{:S(2)}) %collective-permute-start.27) | collective-permute-done | bytes 131104 | tf_op jit(solution)/shard_map/ppermute | solution.py:625
  99.7 1.4 %collective-permute-start.28 = (bf16[272,256]{1,0:T(8,128)(2,1)S(1)}, bf16[272,256]{1,0:T(8,128)(2,1)S(1)}, u32[]{:S(2)}, u32[]{:S(2)}) collective-permute-start(bf16[272,256]{1,0:T(8,128)(2,1)S(1)} %get-tuple-element.193.low), channel_id=1, source_target_pairs={{0,8},{4,12},{8,0},{12,4},{16,24},{20,28},{24,16},{28,20},{1,9},{5... | collective-permute-start | bytes 417800 | tf_op jit(solution)/shard_map/ppermute | solution.py:625
  101.2 1.2 %collective-permute-start.34 = (bf16[288,256]{1,0:T(8,128)(2,1)S(1)}, bf16[288,256]{1,0:T(8,128)(2,1)S(1)}, u32[]{:S(2)}, u32[]{:S(2)}) collective-permute-start(bf16[288,256]{1,0:T(8,128)(2,1)S(1)} %get-tuple-element.202.high), channel_id=1, source_target_pairs={{0,16},{4,20},{8,24},{12,28},{16,0},{20,4},{24,8},{28,12},{1,17},{... | collective-permute-start | bytes 442376 | tf_op jit(solution)/shard_map/ppermute | solution.py:625
  102.4 0.8 collective-permute-done.33.refs_3_
  103.3 0.7 collective-permute-done.28.low_got
  104.0 1.2 collective-permute-done.34.high_got
  105.2 0.5 collective-permute-start.39
  105.7 1.2 collective-permute-start.35
  106.9 1.1 collective-permute-start.38
  107.9 1.2 %collective-permute-start.37 = (bf16[176,256]{1,0:T(8,128)(2,1)S(1)}, bf16[176,256]{1,0:T(8,128)(2,1)S(1)}, u32[]{:S(2)}, u32[]{:S(2)}) collective-permute-start(bf16[176,256]{1,0:T(8,128)(2,1)S(1)} %four_sum.4.refs_0_), channel_id=1, source_target_pairs={{0,16},{4,20},{8,24},{12,28},{16,0},{20,4},{24,8},{28,12},{1,17},{... | collective-permute-start | bytes 270344 | tf_op jit(solution)/shard_map/ppermute | solution.py:625
  109.5 1.7 %collective-permute-done.38.refs_3_ = bf16[176,256]{1,0:T(8,128)(2,1)S(1)} collective-permute-done((bf16[176,256]{1,0:T(8,128)(2,1)S(1)}, bf16[176,256]{1,0:T(8,128)(2,1)S(1)}, u32[]{:S(2)}, u32[]{:S(2)}) %collective-permute-start.38) | collective-permute-done | bytes 90144 | tf_op jit(solution)/shard_map/ppermute | solution.py:625
  111.3 1.2 collective-permute-done.37.refs_2_
  112.5 1.3 %collective-permute-done.36.refs_1_ = bf16[176,256]{1,0:T(8,128)(2,1)S(1)} collective-permute-done((bf16[176,256]{1,0:T(8,128)(2,1)S(1)}, bf16[176,256]{1,0:T(8,128)(2,1)S(1)}, u32[]{:S(2)}, u32[]{:S(2)}) %collective-permute-start.36) | collective-permute-done | bytes 90144 | tf_op jit(solution)/shard_map/ppermute | solution.py:625
  113.8 4.6 %collective-permute-start.41 = (bf16[416,256]{1,0:T(8,128)(2,1)S(1)}, bf16[416,256]{1,0:T(8,128)(2,1)S(1)}, u32[]{:S(2)}, u32[]{:S(2)}) collective-permute-start(bf16[416,256]{1,0:T(8,128)(2,1)S(1)} %get-tuple-element.209.high), channel_id=1, source_target_pairs={{0,4},{4,0},{8,12},{12,8},{16,20},{20,16},{24,28},{28,24},{1,5},{5... | collective-permute-start | bytes 638984 | tf_op jit(solution)/shard_map/ppermute | solution.py:625
  118.6 0.5 collective-permute-start.42
  119.1 0.9 collective-permute-done.42.late_other
  120.0 1.3 %finish.1 = (f32[2,3,64,256]{3,2,1,0:T(8,128)}, f32[2,64,256]{2,1,0:T(8,128)}, f32[2,256,256]{2,1,0:T(8,128)}, f32[2,256,256]{2,1,0:T(8,128)}, f32[2,64,256]{2,1...) custom-call(bf16[272,256]{1,0:T(8,128)(2,1)S(1)} %get-tuple-element.208.low, ...), custom_call_target="tpu_custom_call" | custom-call | flops 1000 | bytes 1024 | tf_op jit(solution)/shard_map/finish/pallas_call | solution.py:602
  (69 shorter events, 3.7 us)
Async XLA Ops:
  0.6 37.6 %copy-start.3 = (bf16[2,256,256]{2,1,0:T(8,128)(2,1)S(1)}, bf16[2,256,256]{2,1,0:T(8,128)(2,1)}, u32[]{:S(2)}) copy-start(bf16[2,256,256]{2,1,0:T(8,128)(2,1)} %p1.5) | copy-start | bytes 786436
  0.7 37.6 %copy-start.2 = (bf16[2,256,256]{2,1,0:T(8,128)(2,1)S(1)}, bf16[2,256,256]{2,1,0:T(8,128)(2,1)}, u32[]{:S(2)}) copy-start(bf16[2,256,256]{2,1,0:T(8,128)(2,1)} %p0.5) | copy-start | bytes 786436
  0.7 37.6 %copy-start.11 = (f32[2,256]{1,0:T(2,128)S(1)}, f32[2,256]{1,0:T(2,128)}, u32[]{:S(2)}) copy-start(f32[2,256]{1,0:T(2,128)} %gain_ref.13) | copy-start | bytes 6148
  3.5 4.8 %collective-permute-start.2 = (bf16[176,256]{1,0:T(8,128)(2,1)}, bf16[176,256]{1,0:T(8,128)(2,1)S(1)}, u32[]{:S(2)}, u32[]{:S(2)}) collective-permute-start(bf16[176,256]{1,0:T(8,128)(2,1)} %get-tuple-element.116), channel_id=1, source_target_pairs={{0,3},{1,2},{2,1},{3,0},{4,7},{5,6},{6,5},{7,4},{8,11},{9,10},{10,... | collective-permute-start | bytes 270344 | tf_op jit(solution)/shard_map/ppermute | solution.py:625
  4.9 24.5 %collective-permute-start.6 = (bf16[432,256]{1,0:T(8,128)(2,1)}, bf16[432,256]{1,0:T(8,128)(2,1)S(1)}, u32[]{:S(2)}, u32[]{:S(2)}) collective-permute-start(bf16[432,256]{1,0:T(8,128)(2,1)} %get-tuple-element.119), channel_id=1, source_target_pairs={{0,1},{1,0},{2,3},{3,2},{4,5},{5,4},{6,7},{7,6},{8,9},{9,8},{10,11... | collective-permute-start | bytes 663560 | tf_op jit(solution)/shard_map/ppermute | solution.py:625
  7.1 8.1 %collective-permute-start.1 = (bf16[176,256]{1,0:T(8,128)(2,1)}, bf16[176,256]{1,0:T(8,128)(2,1)S(1)}, u32[]{:S(2)}, u32[]{:S(2)}) collective-permute-start(bf16[176,256]{1,0:T(8,128)(2,1)} %get-tuple-element.116), channel_id=1, source_target_pairs={{0,2},{1,3},{2,0},{3,1},{4,6},{5,7},{6,4},{7,5},{8,10},{9,11},{10,... | collective-permute-start | bytes 270344 | tf_op jit(solution)/shard_map/ppermute | solution.py:625
  7.1 10.8 %collective-permute-start = (bf16[176,256]{1,0:T(8,128)(2,1)}, bf16[176,256]{1,0:T(8,128)(2,1)S(1)}, u32[]{:S(2)}, u32[]{:S(2)}) collective-permute-start(bf16[176,256]{1,0:T(8,128)(2,1)} %get-tuple-element.116), channel_id=1, source_target_pairs={{0,1},{1,0},{2,3},{3,2},{4,5},{5,4},{6,7},{7,6},{8,9},{9,8},{10,11... | collective-permute-start | bytes 270344 | tf_op jit(solution)/shard_map/ppermute | solution.py:625
  8.4 12.3 %collective-permute-start.5 = (bf16[176,256]{1,0:T(8,128)(2,1)S(1)}, bf16[176,256]{1,0:T(8,128)(2,1)S(1)}, u32[]{:S(2)}, u32[]{:S(2)}) collective-permute-start(bf16[176,256]{1,0:T(8,128)(2,1)S(1)} %collective-permute-done.2.p3), channel_id=1, source_target_pairs={{0,4},{4,0},{8,12},{12,8},{16,20},{20,16},{24,28},{28,24},{1,5},{5... | collective-permute-start | bytes 270344 | tf_op jit(solution)/shard_map/ppermute | solution.py:625
  11.1 18.4 %collective-permute-start.8 = (bf16[432,256]{1,0:T(8,128)(2,1)}, bf16[432,256]{1,0:T(8,128)(2,1)S(1)}, u32[]{:S(2)}, u32[]{:S(2)}) collective-permute-start(bf16[432,256]{1,0:T(8,128)(2,1)} %get-tuple-element.119), channel_id=1, source_target_pairs={{0,3},{1,2},{2,1},{3,0},{4,7},{5,6},{6,5},{7,4},{8,11},{9,10},{10,... | collective-permute-start | bytes 663560 | tf_op jit(solution)/shard_map/ppermute | solution.py:625
  15.2 17.7 %collective-permute-start.7 = (bf16[432,256]{1,0:T(8,128)(2,1)}, bf16[432,256]{1,0:T(8,128)(2,1)S(1)}, u32[]{:S(2)}, u32[]{:S(2)}) collective-permute-start(bf16[432,256]{1,0:T(8,128)(2,1)} %get-tuple-element.119), channel_id=1, source_target_pairs={{0,2},{1,3},{2,0},{3,1},{4,6},{5,7},{6,4},{7,5},{8,10},{9,11},{10,... | collective-permute-start | bytes 663560 | tf_op jit(solution)/shard_map/ppermute | solution.py:625
  17.9 3.6 %collective-permute-start.4 = (bf16[176,256]{1,0:T(8,128)(2,1)S(1)}, bf16[176,256]{1,0:T(8,128)(2,1)S(1)}, u32[]{:S(2)}, u32[]{:S(2)}) collective-permute-start(bf16[176,256]{1,0:T(8,128)(2,1)S(1)} %collective-permute-done.1.p2), channel_id=1, source_target_pairs={{0,4},{4,0},{8,12},{12,8},{16,20},{20,16},{24,28},{28,24},{1,5},{5... | collective-permute-start | bytes 270344 | tf_op jit(solution)/shard_map/ppermute | solution.py:625
  20.6 1.3 %collective-permute-start.3 = (bf16[176,256]{1,0:T(8,128)(2,1)S(1)}, bf16[176,256]{1,0:T(8,128)(2,1)S(1)}, u32[]{:S(2)}, u32[]{:S(2)}) collective-permute-start(bf16[176,256]{1,0:T(8,128)(2,1)S(1)} %collective-permute-done.p1), channel_id=1, source_target_pairs={{0,4},{4,0},{8,12},{12,8},{16,20},{20,16},{24,28},{28,24},{1,5},{5... | collective-permute-start | bytes 270344 | tf_op jit(solution)/shard_map/ppermute | solution.py:625
  21.9 1.0 copy-start
  23.0 0.9 copy-start.4
  23.9 0.8 copy-start.8
  24.6 0.7 copy-start.9
  29.4 8.9 %collective-permute-start.9 = (bf16[432,256]{1,0:T(8,128)(2,1)S(1)}, bf16[432,256]{1,0:T(8,128)(2,1)S(1)}, u32[]{:S(2)}, u32[]{:S(2)}) collective-permute-start(bf16[432,256]{1,0:T(8,128)(2,1)S(1)} %collective-permute-done.6.p2.p1), channel_id=1, source_target_pairs={{0,4},{4,0},{8,12},{12,8},{16,20},{20,16},{24,28},{28,24},{1,5},{5... | collective-permute-start | bytes 663560 | tf_op jit(solution)/shard_map/ppermute | solution.py:625
  32.9 5.4 %collective-permute-start.10 = (bf16[432,256]{1,0:T(8,128)(2,1)S(1)}, bf16[432,256]{1,0:T(8,128)(2,1)S(1)}, u32[]{:S(2)}, u32[]{:S(2)}) collective-permute-start(bf16[432,256]{1,0:T(8,128)(2,1)S(1)} %collective-permute-done.7.p3.p2), channel_id=1, source_target_pairs={{0,4},{4,0},{8,12},{12,8},{16,20},{20,16},{24,28},{28,24},{1,5},{5... | collective-permute-start | bytes 663560 | tf_op jit(solution)/shard_map/ppermute | solution.py:625
  33.6 4.6 %collective-permute-start.11 = (bf16[432,256]{1,0:T(8,128)(2,1)S(1)}, bf16[432,256]{1,0:T(8,128)(2,1)S(1)}, u32[]{:S(2)}, u32[]{:S(2)}) collective-permute-start(bf16[432,256]{1,0:T(8,128)(2,1)S(1)} %collective-permute-done.8.p4.p3), channel_id=1, source_target_pairs={{0,4},{4,0},{8,12},{12,8},{16,20},{20,16},{24,28},{28,24},{1,5},{5... | collective-permute-start | bytes 663560 | tf_op jit(solution)/shard_map/ppermute | solution.py:625
  33.7 11.3 %collective-permute-start.14 = (bf16[256,256]{1,0:T(8,128)(2,1)}, bf16[256,256]{1,0:T(8,128)(2,1)S(1)}, u32[]{:S(2)}, u32[]{:S(2)}) collective-permute-start(bf16[256,256]{1,0:T(8,128)(2,1)} %get-tuple-element.127), channel_id=1, source_target_pairs={{0,3},{1,2},{2,1},{3,0},{4,7},{5,6},{6,5},{7,4},{8,11},{9,10},{10,... | collective-permute-start | bytes 393224 | tf_op jit(solution)/shard_map/ppermute | solution.py:625
  34.3 12.4 %collective-permute-start.13 = (bf16[256,256]{1,0:T(8,128)(2,1)}, bf16[256,256]{1,0:T(8,128)(2,1)S(1)}, u32[]{:S(2)}, u32[]{:S(2)}) collective-permute-start(bf16[256,256]{1,0:T(8,128)(2,1)} %get-tuple-element.127), channel_id=1, source_target_pairs={{0,2},{1,3},{2,0},{3,1},{4,6},{5,7},{6,4},{7,5},{8,10},{9,11},{10,... | collective-permute-start | bytes 393224 | tf_op jit(solution)/shard_map/ppermute | solution.py:625
  38.2 8.6 %collective-permute-start.12 = (bf16[256,256]{1,0:T(8,128)(2,1)}, bf16[256,256]{1,0:T(8,128)(2,1)S(1)}, u32[]{:S(2)}, u32[]{:S(2)}) collective-permute-start(bf16[256,256]{1,0:T(8,128)(2,1)} %get-tuple-element.127), channel_id=1, source_target_pairs={{0,1},{1,0},{2,3},{3,2},{4,5},{5,4},{6,7},{7,6},{8,9},{9,8},{10,11... | collective-permute-start | bytes 393224 | tf_op jit(solution)/shard_map/ppermute | solution.py:625
  38.3 2.6 %copy-start.7 = (bf16[352,256]{1,0:T(8,128)(2,1)S(1)}, bf16[352,256]{1,0:T(8,128)(2,1)}, u32[]{:S(2)}) copy-start(bf16[352,256]{1,0:T(8,128)(2,1)} %get-tuple-element.124.p0) | copy-start | bytes 540676
  40.8 8.9 %copy-start.6 = (bf16[1024,256]{1,0:T(8,128)(2,1)S(1)}, bf16[1024,256]{1,0:T(8,128)(2,1)}, u32[]{:S(2)}) copy-start(bf16[1024,256]{1,0:T(8,128)(2,1)} %grad_ref.1) | copy-start | bytes 1572868
  46.8 2.3 %collective-permute-start.15 = (bf16[256,256]{1,0:T(8,128)(2,1)S(1)}, bf16[256,256]{1,0:T(8,128)(2,1)S(1)}, u32[]{:S(2)}, u32[]{:S(2)}) collective-permute-start(bf16[256,256]{1,0:T(8,128)(2,1)S(1)} %collective-permute-done.12.p2), channel_id=1, source_target_pairs={{0,4},{4,0},{8,12},{12,8},{16,20},{20,16},{24,28},{28,24},{1,5},{5... | collective-permute-start | bytes 393224 | tf_op jit(solution)/shard_map/ppermute | solution.py:625
  48.2 1.3 %collective-permute-start.16 = (bf16[256,256]{1,0:T(8,128)(2,1)S(1)}, bf16[256,256]{1,0:T(8,128)(2,1)S(1)}, u32[]{:S(2)}, u32[]{:S(2)}) collective-permute-start(bf16[256,256]{1,0:T(8,128)(2,1)S(1)} %collective-permute-done.13.p3), channel_id=1, source_target_pairs={{0,4},{4,0},{8,12},{12,8},{16,20},{20,16},{24,28},{28,24},{1,5},{5... | collective-permute-start | bytes 393224 | tf_op jit(solution)/shard_map/ppermute | solution.py:625
  48.2 1.5 %collective-permute-start.17 = (bf16[256,256]{1,0:T(8,128)(2,1)S(1)}, bf16[256,256]{1,0:T(8,128)(2,1)S(1)}, u32[]{:S(2)}, u32[]{:S(2)}) collective-permute-start(bf16[256,256]{1,0:T(8,128)(2,1)S(1)} %collective-permute-done.14.p4), channel_id=1, source_target_pairs={{0,4},{4,0},{8,12},{12,8},{16,20},{20,16},{24,28},{28,24},{1,5},{5... | collective-permute-start | bytes 393224 | tf_op jit(solution)/shard_map/ppermute | solution.py:625
  55.3 1.9 %collective-permute-start.18 = (bf16[4,256,256]{2,1,0:T(8,128)(2,1)S(1)}, bf16[4,256,256]{2,1,0:T(8,128)(2,1)S(1)}, u32[]{:S(2)}, u32[]{:S(2)}) collective-permute-start(bf16[4,256,256]{2,1,0:T(8,128)(2,1)S(1)} %get-tuple-element.136), channel_id=1, source_target_pairs={{0,4},{4,0},{8,12},{12,8},{16,20},{20,16},{24,28},{28,24},{1,5},{5... | collective-permute-start | bytes 1572872 | tf_op jit(solution)/shard_map/ppermute | solution.py:625
  55.6 3.0 %copy-start.10 = (f32[2,256]{1,0:T(2,128)S(1)}, f32[2,256]{1,0:T(2,128)}, u32[]{:S(2)}) copy-start(f32[2,256]{1,0:T(2,128)} %gain_ref.15) | copy-start | bytes 6148
  57.3 7.6 %collective-permute-start.19 = (bf16[4,128,256]{2,1,0:T(8,128)(2,1)S(1)}, bf16[4,128,256]{2,1,0:T(8,128)(2,1)S(1)}, u32[]{:S(2)}, u32[]{:S(2)}) collective-permute-start(bf16[4,128,256]{2,1,0:T(8,128)(2,1)S(1)} %get-tuple-element.142), channel_id=1, source_target_pairs={{0,8},{4,12},{8,0},{12,4},{16,24},{20,28},{24,16},{28,20},{1,9},{5... | collective-permute-start | bytes 786440 | tf_op jit(solution)/shard_map/ppermute | solution.py:625
  63.8 2.0 %collective-permute-start.20 = (bf16[4,176,256]{2,1,0:T(8,128)(2,1)S(1)}, bf16[4,176,256]{2,1,0:T(8,128)(2,1)S(1)}, u32[]{:S(2)}, u32[]{:S(2)}) collective-permute-start(bf16[4,176,256]{2,1,0:T(8,128)(2,1)S(1)} %get-tuple-element.157), channel_id=1, source_target_pairs={{0,4},{4,0},{8,12},{12,8},{16,20},{20,16},{24,28},{28,24},{1,5},{5... | collective-permute-start | bytes 1081352 | tf_op jit(solution)/shard_map/ppermute | solution.py:625
  65.9 13.2 %collective-permute-start.24 = (bf16[304,256]{1,0:T(8,128)(2,1)S(1)}, bf16[304,256]{1,0:T(8,128)(2,1)S(1)}, u32[]{:S(2)}, u32[]{:S(2)}) collective-permute-start(bf16[304,256]{1,0:T(8,128)(2,1)S(1)} %get-tuple-element.162), channel_id=1, source_target_pairs={{0,3},{1,2},{2,1},{3,0},{4,7},{5,6},{6,5},{7,4},{8,11},{9,10},{10,... | collective-permute-start | bytes 466952 | tf_op jit(solution)/shard_map/ppermute | solution.py:625
  66.4 13.5 %collective-permute-start.23 = (bf16[304,256]{1,0:T(8,128)(2,1)S(1)}, bf16[304,256]{1,0:T(8,128)(2,1)S(1)}, u32[]{:S(2)}, u32[]{:S(2)}) collective-permute-start(bf16[304,256]{1,0:T(8,128)(2,1)S(1)} %get-tuple-element.161), channel_id=1, source_target_pairs={{0,2},{1,3},{2,0},{3,1},{4,6},{5,7},{6,4},{7,5},{8,10},{9,11},{10,... | collective-permute-start | bytes 466952 | tf_op jit(solution)/shard_map/ppermute | solution.py:625
  69.3 10.6 %collective-permute-start.22 = (bf16[304,256]{1,0:T(8,128)(2,1)S(1)}, bf16[304,256]{1,0:T(8,128)(2,1)S(1)}, u32[]{:S(2)}, u32[]{:S(2)}) collective-permute-start(bf16[304,256]{1,0:T(8,128)(2,1)S(1)} %get-tuple-element.160), channel_id=1, source_target_pairs={{0,1},{1,0},{2,3},{3,2},{4,5},{5,4},{6,7},{7,6},{8,9},{9,8},{10,11... | collective-permute-start | bytes 466952 | tf_op jit(solution)/shard_map/ppermute | solution.py:625
  69.3 3.1 %copy-start.1 = (bf16[1024,256]{1,0:T(8,128)(2,1)S(1)}, bf16[1024,256]{1,0:T(8,128)(2,1)}, u32[]{:S(2)}) copy-start(bf16[1024,256]{1,0:T(8,128)(2,1)} %cur_ref.5) | copy-start | bytes 1572868
  69.3 3.1 %copy-start.5 = (bf16[352,256]{1,0:T(8,128)(2,1)S(1)}, bf16[352,256]{1,0:T(8,128)(2,1)}, u32[]{:S(2)}) copy-start(bf16[352,256]{1,0:T(8,128)(2,1)} %get-tuple-element.115.p0) | copy-start | bytes 540676
  77.8 6.6 %collective-permute-start.29 = (bf16[2,176,256]{2,1,0:T(8,128)(2,1)S(1)}, bf16[2,176,256]{2,1,0:T(8,128)(2,1)S(1)}, u32[]{:S(2)}, u32[]{:S(2)}) collective-permute-start(bf16[2,176,256]{2,1,0:T(8,128)(2,1)S(1)} %get-tuple-element.195), channel_id=1, source_target_pairs={{0,4},{4,0},{8,12},{12,8},{16,20},{20,16},{24,28},{28,24},{1,5},{5... | collective-permute-start | bytes 540680 | tf_op jit(solution)/shard_map/ppermute | solution.py:625
  79.0 5.4 %collective-permute-start.30 = (bf16[2,176,256]{2,1,0:T(8,128)(2,1)S(1)}, bf16[2,176,256]{2,1,0:T(8,128)(2,1)S(1)}, u32[]{:S(2)}, u32[]{:S(2)}) collective-permute-start(bf16[2,176,256]{2,1,0:T(8,128)(2,1)S(1)} %get-tuple-element.196), channel_id=1, source_target_pairs={{0,4},{4,0},{8,12},{12,8},{16,20},{20,16},{24,28},{28,24},{1,5},{5... | collective-permute-start | bytes 540680 | tf_op jit(solution)/shard_map/ppermute | solution.py:625
  79.1 2.3 %collective-permute-start.21 = (bf16[4,256,256]{2,1,0:T(8,128)(2,1)S(1)}, bf16[4,256,256]{2,1,0:T(8,128)(2,1)S(1)}, u32[]{:S(2)}, u32[]{:S(2)}) collective-permute-start(bf16[4,256,256]{2,1,0:T(8,128)(2,1)S(1)} %get-tuple-element.176), channel_id=1, source_target_pairs={{0,4},{4,0},{8,12},{12,8},{16,20},{20,16},{24,28},{28,24},{1,5},{5... | collective-permute-start | bytes 1572872 | tf_op jit(solution)/shard_map/ppermute | solution.py:625
  81.6 5.9 %collective-permute-start.25 = (bf16[256,256]{1,0:T(8,128)(2,1)S(1)}, bf16[256,256]{1,0:T(8,128)(2,1)S(1)}, u32[]{:S(2)}, u32[]{:S(2)}) collective-permute-start(bf16[256,256]{1,0:T(8,128)(2,1)S(1)} %get-tuple-element.183), channel_id=1, source_target_pairs={{0,1},{1,0},{2,3},{3,2},{4,5},{5,4},{6,7},{7,6},{8,9},{9,8},{10,11... | collective-permute-start | bytes 393224 | tf_op jit(solution)/shard_map/ppermute | solution.py:625
  83.1 7.3 %collective-permute-start.26 = (bf16[256,256]{1,0:T(8,128)(2,1)S(1)}, bf16[256,256]{1,0:T(8,128)(2,1)S(1)}, u32[]{:S(2)}, u32[]{:S(2)}) collective-permute-start(bf16[256,256]{1,0:T(8,128)(2,1)S(1)} %get-tuple-element.184), channel_id=1, source_target_pairs={{0,2},{1,3},{2,0},{3,1},{4,6},{5,7},{6,4},{7,5},{8,10},{9,11},{10,... | collective-permute-start | bytes 393224 | tf_op jit(solution)/shard_map/ppermute | solution.py:625
  83.7 15.9 %collective-permute-start.27 = (bf16[256,256]{1,0:T(8,128)(2,1)S(1)}, bf16[256,256]{1,0:T(8,128)(2,1)S(1)}, u32[]{:S(2)}, u32[]{:S(2)}) collective-permute-start(bf16[256,256]{1,0:T(8,128)(2,1)S(1)} %get-tuple-element.185), channel_id=1, source_target_pairs={{0,3},{1,2},{2,1},{3,0},{4,7},{5,6},{6,5},{7,4},{8,11},{9,10},{10,... | collective-permute-start | bytes 393224 | tf_op jit(solution)/shard_map/ppermute | solution.py:625
  84.5 17.9 %collective-permute-start.31 = (bf16[176,256]{1,0:T(8,128)(2,1)S(1)}, bf16[176,256]{1,0:T(8,128)(2,1)S(1)}, u32[]{:S(2)}, u32[]{:S(2)}) collective-permute-start(bf16[176,256]{1,0:T(8,128)(2,1)S(1)} %get-tuple-element.198), channel_id=1, source_target_pairs={{0,1},{1,0},{2,3},{3,2},{4,5},{5,4},{6,7},{7,6},{8,9},{9,8},{10,11... | collective-permute-start | bytes 270344 | tf_op jit(solution)/shard_map/ppermute | solution.py:625
  86.8 15.5 %collective-permute-start.32 = (bf16[176,256]{1,0:T(8,128)(2,1)S(1)}, bf16[176,256]{1,0:T(8,128)(2,1)S(1)}, u32[]{:S(2)}, u32[]{:S(2)}) collective-permute-start(bf16[176,256]{1,0:T(8,128)(2,1)S(1)} %get-tuple-element.199), channel_id=1, source_target_pairs={{0,2},{1,3},{2,0},{3,1},{4,6},{5,7},{6,4},{7,5},{8,10},{9,11},{10,... | collective-permute-start | bytes 270344 | tf_op jit(solution)/shard_map/ppermute | solution.py:625
  87.4 15.8 %collective-permute-start.33 = (bf16[176,256]{1,0:T(8,128)(2,1)S(1)}, bf16[176,256]{1,0:T(8,128)(2,1)S(1)}, u32[]{:S(2)}, u32[]{:S(2)}) collective-permute-start(bf16[176,256]{1,0:T(8,128)(2,1)S(1)} %get-tuple-element.200), channel_id=1, source_target_pairs={{0,3},{1,2},{2,1},{3,0},{4,7},{5,6},{6,5},{7,4},{8,11},{9,10},{10,... | collective-permute-start | bytes 270344 | tf_op jit(solution)/shard_map/ppermute | solution.py:625
  99.7 4.3 %collective-permute-start.28 = (bf16[272,256]{1,0:T(8,128)(2,1)S(1)}, bf16[272,256]{1,0:T(8,128)(2,1)S(1)}, u32[]{:S(2)}, u32[]{:S(2)}) collective-permute-start(bf16[272,256]{1,0:T(8,128)(2,1)S(1)} %get-tuple-element.193.low), channel_id=1, source_target_pairs={{0,8},{4,12},{8,0},{12,4},{16,24},{20,28},{24,16},{28,20},{1,9},{5... | collective-permute-start | bytes 417800 | tf_op jit(solution)/shard_map/ppermute | solution.py:625
  101.2 4.0 %collective-permute-start.34 = (bf16[288,256]{1,0:T(8,128)(2,1)S(1)}, bf16[288,256]{1,0:T(8,128)(2,1)S(1)}, u32[]{:S(2)}, u32[]{:S(2)}) collective-permute-start(bf16[288,256]{1,0:T(8,128)(2,1)S(1)} %get-tuple-element.202.high), channel_id=1, source_target_pairs={{0,16},{4,20},{8,24},{12,28},{16,0},{20,4},{24,8},{28,12},{1,17},{... | collective-permute-start | bytes 442376 | tf_op jit(solution)/shard_map/ppermute | solution.py:625
  105.2 8.5 %collective-permute-start.39 = (bf16[288,256]{1,0:T(8,128)(2,1)S(1)}, bf16[288,256]{1,0:T(8,128)(2,1)S(1)}, u32[]{:S(2)}, u32[]{:S(2)}) collective-permute-start(bf16[288,256]{1,0:T(8,128)(2,1)S(1)} %get-tuple-element.206.high), channel_id=1, source_target_pairs={{0,8},{4,12},{8,0},{12,4},{16,24},{20,28},{24,16},{28,20},{1,9},{5... | collective-permute-start | bytes 442376 | tf_op jit(solution)/shard_map/ppermute | solution.py:625
  105.7 8.1 %collective-permute-start.35 = (bf16[272,256]{1,0:T(8,128)(2,1)S(1)}, bf16[272,256]{1,0:T(8,128)(2,1)S(1)}, u32[]{:S(2)}, u32[]{:S(2)}) collective-permute-start(bf16[272,256]{1,0:T(8,128)(2,1)S(1)} %get-tuple-element.204.low), channel_id=1, source_target_pairs={{0,16},{4,20},{8,24},{12,28},{16,0},{20,4},{24,8},{28,12},{1,17},{... | collective-permute-start | bytes 417800 | tf_op jit(solution)/shard_map/ppermute | solution.py:625
  106.9 4.4 %collective-permute-start.38 = (bf16[176,256]{1,0:T(8,128)(2,1)S(1)}, bf16[176,256]{1,0:T(8,128)(2,1)S(1)}, u32[]{:S(2)}, u32[]{:S(2)}) collective-permute-start(bf16[176,256]{1,0:T(8,128)(2,1)S(1)} %four_sum.4.refs_0_), channel_id=1, source_target_pairs={{0,24},{4,28},{8,16},{12,20},{16,8},{20,12},{24,0},{28,4},{1,25},{... | collective-permute-start | bytes 270344 | tf_op jit(solution)/shard_map/ppermute | solution.py:625
  107.9 4.5 %collective-permute-start.37 = (bf16[176,256]{1,0:T(8,128)(2,1)S(1)}, bf16[176,256]{1,0:T(8,128)(2,1)S(1)}, u32[]{:S(2)}, u32[]{:S(2)}) collective-permute-start(bf16[176,256]{1,0:T(8,128)(2,1)S(1)} %four_sum.4.refs_0_), channel_id=1, source_target_pairs={{0,16},{4,20},{8,24},{12,28},{16,0},{20,4},{24,8},{28,12},{1,17},{... | collective-permute-start | bytes 270344 | tf_op jit(solution)/shard_map/ppermute | solution.py:625
  109.2 4.6 %collective-permute-start.36 = (bf16[176,256]{1,0:T(8,128)(2,1)S(1)}, bf16[176,256]{1,0:T(8,128)(2,1)S(1)}, u32[]{:S(2)}, u32[]{:S(2)}) collective-permute-start(bf16[176,256]{1,0:T(8,128)(2,1)S(1)} %four_sum.4.refs_0_), channel_id=1, source_target_pairs={{0,8},{4,12},{8,0},{12,4},{16,24},{20,28},{24,16},{28,20},{1,9},{5... | collective-permute-start | bytes 270344 | tf_op jit(solution)/shard_map/ppermute | solution.py:625
  113.8 6.2 %collective-permute-start.41 = (bf16[416,256]{1,0:T(8,128)(2,1)S(1)}, bf16[416,256]{1,0:T(8,128)(2,1)S(1)}, u32[]{:S(2)}, u32[]{:S(2)}) collective-permute-start(bf16[416,256]{1,0:T(8,128)(2,1)S(1)} %get-tuple-element.209.high), channel_id=1, source_target_pairs={{0,4},{4,0},{8,12},{12,8},{16,20},{20,16},{24,28},{28,24},{1,5},{5... | collective-permute-start | bytes 638984 | tf_op jit(solution)/shard_map/ppermute | solution.py:625
  118.4 1.6 %collective-permute-start.40 = (bf16[272,256]{1,0:T(8,128)(2,1)S(1)}, bf16[272,256]{1,0:T(8,128)(2,1)S(1)}, u32[]{:S(2)}, u32[]{:S(2)}) collective-permute-start(bf16[272,256]{1,0:T(8,128)(2,1)S(1)} %get-tuple-element.208.low), channel_id=1, source_target_pairs={{0,4},{4,0},{8,12},{12,8},{16,20},{20,16},{24,28},{28,24},{1,5},{5... | collective-permute-start | bytes 417800 | tf_op jit(solution)/shard_map/ppermute | solution.py:625
  118.6 1.4 %collective-permute-start.42 = (bf16[176,256]{1,0:T(8,128)(2,1)S(1)}, bf16[176,256]{1,0:T(8,128)(2,1)S(1)}, u32[]{:S(2)}, u32[]{:S(2)}) collective-permute-start(bf16[176,256]{1,0:T(8,128)(2,1)S(1)} %four_sum.5.late), channel_id=1, source_target_pairs={{0,4},{4,0},{8,12},{12,8},{16,20},{20,16},{24,28},{28,24},{1,5},{5... | collective-permute-start | bytes 270344 | tf_op jit(solution)/shard_map/ppermute | solution.py:625

commit v2 on v1

--- a/solution.py
+++ b/solution.py
@@ -73,21 +73,30 @@
     return (lax.axis_index("dp") >> 1) & 1
 
 
-def place_pieces(own, mine, theirs, dst, first=0):
-    half = dst.shape[1] // 2
-    keep = pl.multiple_of(half_index() * half, 16)
-    other = pl.multiple_of((1 - half_index()) * half, 16)
+def place_pieces(own, parts, dst, first, rows):
     at = 0
-    for part in own:
-        dst[0, at:at + part.shape[0], :] = part
-        at += part.shape[0]
-    for m in range(3):
-        dst[m + 1, pl.ds(keep, half), :] = mine[m][first:first + half, :]
-        dst[m + 1, pl.ds(other, half), :] = theirs[m][first:first + half, :]
-
-
-def place_attn(first, pieces, wa, w_cross, w_out):
-    place_pieces((pieces[0][...],), pieces[1:4], pieces[4:7], wa, first)
+    for ref in own:
+        dst[0, at:at + ref.shape[0], :] = ref
+        at += ref.shape[0]
+    for start, refs in parts:
+        for m, ref in enumerate(refs):
+            dst[m + 1, pl.ds(pl.multiple_of(start, 16), rows), :] = ref[first:first + rows, :]
+
+
+def parts_of(pieces, rows):
+    c, x = half_index(), quarter_index()
+    if len(pieces) == 6:
+        return [(c * rows, pieces[0:3]), ((1 - c) * rows, pieces[3:6])]
+    places = [c, 1 - c] if len(pieces) == 2 else [2 * i + j for i, j in ((c, x), (c, 1 - x), (1 - c, x), (1 - c, 1 - x))]
+    return [(place * rows, [ref.at[pl.ds(m * rows, rows)] for m in range(3)]) for place, ref in zip(places, pieces)]
+
+
+def place_qkv(layer, pieces, wa):
+    place_pieces((pieces[0][...],), parts_of(pieces[1:], 176), wa, 256 * layer, 176)
+
+
+def place_attn(layer, pieces, wa, w_cross, w_out):
+    place_qkv(layer, pieces, wa)
     total = jnp.zeros((1, 256), F32)
     for m in range(4):
         place = pl.multiple_of((head_index() ^ m) * HD, HD)
@@ -97,8 +106,9 @@
     return total
 
 
-def place_mlp(layer, first, pieces, wm):
-    place_pieces((pieces[0][layer], pieces[1][layer]), pieces[2:5], pieces[5:8], wm, first)
+def place_mlp(layer, pieces, wm):
+    rows = 256 if len(pieces) == 8 else 128
+    place_pieces((pieces[0][layer], pieces[1][layer]), parts_of(pieces[2:], rows), wm, 0, rows)
 
 
 def each_sample(rows, unroll, step, *init, size=256):
@@ -108,9 +118,10 @@
     return lax.fori_loop(0, rows // size, body, init, unroll=unroll)
 
 
-def attn_fwd_kernel(layer, first, cur_ref, mask_ref, gain_ref, p0, p1, p2, p3, p4, p5, p6,
-                    middle_ref, base_ref, nrm_ref, qkv_ref, mix_ref, lse_ref, wa, w_cross, w_out):
-    bias = place_attn(first, (p0, p1, p2, p3, p4, p5, p6), wa, w_cross, w_out)
+def attn_fwd_kernel(layer, count, *refs):
+    pieces = refs[:count]
+    (cur_ref, mask_ref, gain_ref, middle_ref, base_ref, nrm_ref, qkv_ref, mix_ref, lse_ref, wa, w_cross, w_out) = refs[count:]
+    bias = place_attn(layer, pieces, wa, w_cross, w_out)
     gain = gain_ref[layer:layer + 1, :]
     def step(rows):
         cur = cur_ref[rows, :].astype(F32)
@@ -150,9 +161,10 @@
     return r, n2, kept, (feed[0] + feed[1]) + (feed[2] + feed[3])
 
 
-def mlp_fwd_kernel(layer, first, middle_ref, base_ref, gain_ref, p0, p1, p2, p3, p4, p5, p6, p7,
-                   out_ref, hid_ref, slope_ref, wm):
-    place_mlp(layer, first, (p0, p1, p2, p3, p4, p5, p6, p7), wm)
+def mlp_fwd_kernel(layer, count, *refs):
+    pieces = refs[:count]
+    (middle_ref, base_ref, gain_ref, out_ref, hid_ref, slope_ref, wm) = refs[count:]
+    place_mlp(layer, pieces, wm)
     gain = gain_ref[layer:layer + 1, :]
     def step(rows):
         _, _, kept, feed = mlp_fwd_block(middle_ref[rows, :], gain, wm)
@@ -182,9 +194,11 @@
         send_ref[m] = jnp.where(own_up, down, up)
 
 
-def mlp_both_kernel(layer, first, middle_ref, base_ref, cot_ref, gain_ref, p0, p1, p2, p3, p4, p5, p6, p7,
-                    out_ref, gm_ref, keep_ref, send_ref, small_ref, wm, hid_all, gp_all, n2_all):
-    place_mlp(layer, first, (p0, p1, p2, p3, p4, p5, p6, p7), wm)
+def mlp_both_kernel(layer, count, *refs):
+    pieces = refs[:count]
+    (middle_ref, base_ref, cot_ref, gain_ref, out_ref, gm_ref, keep_ref, send_ref, small_ref, wm, hid_all, gp_all,
+     n2_all) = refs[count:]
+    place_mlp(layer, pieces, wm)
     gain = gain_ref[layer:layer + 1, :]
     def step(rows, gain_grad):
         middle = middle_ref[rows, :]
@@ -206,9 +220,11 @@
     put_mlp_grads(hid_all, gp_all, n2_all, cot_ref, keep_ref, send_ref)
 
 
-def mlp_bwd_kernel(layer, first, grad_ref, middle_ref, hid_ref, slope_ref, gain_ref, p0, p1, p2, p3, p4, p5, p6, p7,
-                   gm_ref, keep_ref, send_ref, small_ref, wm, gp_all, n2_all, gf_all):
-    place_mlp(layer, first, (p0, p1, p2, p3, p4, p5, p6, p7), wm)
+def mlp_bwd_kernel(layer, count, *refs):
+    pieces = refs[:count]
+    (grad_ref, middle_ref, hid_ref, slope_ref, gain_ref, gm_ref, keep_ref, send_ref, small_ref, wm, gp_all, n2_all,
+     gf_all) = refs[count:]
+    place_mlp(layer, pieces, wm)
     gain = gain_ref[layer:layer + 1, :]
     def step(rows, gain_grad):
         middle = middle_ref[rows, :]
@@ -231,10 +247,11 @@
     put_mlp_grads(hid_ref, gp_all, n2_all, gf_all, keep_ref, send_ref)
 
 
-def attn_pre_kernel(layer, first, grad_ref, gm_ref, cur_ref, nrm_ref, mix_ref, p0, p1, p2, p3, p4, p5, p6,
-                    gmix_ref, d_cross_ref, d_out_ref, base_ref, gn_ref, small_ref, dot_ref,
-                    wa, w_cross, w_out, ga_all, gc_all):
-    bias = place_attn(first, (p0, p1, p2, p3, p4, p5, p6), wa, w_cross, w_out)
+def attn_pre_kernel(layer, count, *refs):
+    pieces = refs[:count]
+    (grad_ref, gm_ref, cur_ref, nrm_ref, mix_ref, gmix_ref, d_cross_ref, d_out_ref, base_ref, gn_ref, small_ref,
+     dot_ref, wa, w_cross, w_out, ga_all, gc_all) = refs[count:]
+    bias = place_attn(layer, pieces, wa, w_cross, w_out)
 
     def step(rows, bias_grad):
         grad = grad_ref[rows, :].astype(F32)
@@ -284,10 +301,6 @@
     r = rescale_of(cur)
     scaled = gn * gain
     return r * (scaled - cur * (r * r * jnp.mean(cur * scaled, axis=-1, keepdims=True)))
-
-
-def place_qkv(first, pieces, wa):
-    place_pieces((pieces[0][...],), pieces[1:4], pieces[4:7], wa, first)
 
 
 def put_attn_grads(layer, nrm, gqkv_all, wa, gain_ref, d_cross_ref, d_out_ref, small, mlp_small, payload, keep_ref, sends):
@@ -311,10 +324,11 @@
             ref[i, 168:176, :] = low
 
 
-def attn_bwd_kernel(layer, first, mask_ref, nrm_ref, qkv_ref, lse_ref, gain_ref, gmix_ref, d_cross_ref, d_out_ref, small, dot_ref, mlp_small,
-                    cur_ref, base_ref, gn_ref, p0, p1, p2, p3, p4, p5, p6,
-                    out_ref, keep_ref, send_ref, wa, gqkv_all, payload):
-    place_qkv(first, (p0, p1, p2, p3, p4, p5, p6), wa)
+def attn_bwd_kernel(layer, count, *refs):
+    pieces = refs[:count]
+    (mask_ref, nrm_ref, qkv_ref, lse_ref, gain_ref, gmix_ref, d_cross_ref, d_out_ref, small, dot_ref, mlp_small,
+     cur_ref, base_ref, gn_ref, out_ref, keep_ref, send_ref, wa, gqkv_all, payload) = refs[count:]
+    place_qkv(layer, pieces, wa)
 
     def step(rows):
         gn = gn_ref[rows, :]
@@ -329,9 +343,11 @@
                    payload, keep_ref, (send_ref,))
 
 
-def attn_grads_kernel(layer, first, mask_ref, nrm_ref, qkv_ref, lse_ref, gain_ref, gmix_ref, d_cross_ref, d_out_ref, small, dot_ref, mlp_small,
-                      p0, p1, p2, p3, p4, p5, p6, gqkv_all, keep_ref, send_low, send_high, wa, payload):
-    place_qkv(first, (p0, p1, p2, p3, p4, p5, p6), wa)
+def attn_grads_kernel(layer, count, *refs):
+    pieces = refs[:count]
+    (mask_ref, nrm_ref, qkv_ref, lse_ref, gain_ref, gmix_ref, d_cross_ref, d_out_ref, small, dot_ref, mlp_small,
+     gqkv_all, keep_ref, send_low, send_high, wa, payload) = refs[count:]
+    place_qkv(layer, pieces, wa)
 
     def step(rows):
         for m, gqkv in enumerate(qkv_back(rows, mask_ref, qkv_ref, lse_ref, gmix_ref, dot_ref)):
@@ -343,8 +359,10 @@
                    payload, keep_ref, (send_low, send_high))
 
 
-def attn_post_kernel(layer, first, gqkv_all, gain_ref, cur_ref, base_ref, gn_ref, p0, p1, p2, p3, p4, p5, p6, out_ref, wa):
-    place_qkv(first, (p0, p1, p2, p3, p4, p5, p6), wa)
+def attn_post_kernel(layer, count, *refs):
+    pieces = refs[:count]
+    (gqkv_all, gain_ref, cur_ref, base_ref, gn_ref, out_ref, wa) = refs[count:]
+    place_qkv(layer, pieces, wa)
 
     def step(rows):
         gn = gn_ref[rows, :]
@@ -361,7 +379,7 @@
     return high, (x - high.astype(F32)).astype(BF)
 
 
-def pack_kernel(lens, qkv, cross, out, up, down, b, own0, own1, half_a0, half_r, half_m1, mask, sems):
+def pack_kernel(lens, qkv, cross, out, up, down, b, own0, own1, first_l0, half_l1, mask, sems):
     copies = []
     for l, own in ((0, own0), (1, own1)):
         for t in range(3):
@@ -371,18 +389,20 @@
     for copy in copies:
         copy.start()
 
-    def mlp_half(weight):
-        return (pltpu.make_async_copy(weight.at[0], half_r.at[pl.ds(0, 256)], sems.at[1]),
-                pltpu.make_async_copy(weight.at[1], half_m1, sems.at[1]))
+    x = pl.multiple_of(quarter_index() * 128, 16)
+
+    def mlp_parts(weight):
+        return (pltpu.make_async_copy(weight.at[0, pl.ds(x, 128)], first_l0.at[pl.ds(176, 128)], sems.at[1]),
+                pltpu.make_async_copy(weight.at[1], half_l1.at[pl.ds(0, 256)], sems.at[1]))
 
     @pl.when(half_index() == 0)
     def _():
-        for copy in mlp_half(up):
+        for copy in mlp_parts(up):
             copy.start()
 
     @pl.when(half_index() != 0)
     def _():
-        for copy in mlp_half(down):
+        for copy in mlp_parts(down):
             copy.start()
 
     slots = lax.broadcasted_iota(jnp.int32, (16, 256), 1)
@@ -399,10 +419,16 @@
     for copy in copies:
         copy.wait()
     at = pl.multiple_of(half_index() * 176, 16)
-    half_a0[...] = own0[pl.ds(at, 176), :]
-    half_r[256:432, :] = own1[pl.ds(at, 176), :]
-    for copy in mlp_half(up):
+    first_l0[0:176, :] = own0[pl.ds(at, 176), :]
+    half_l1[256:432, :] = own1[pl.ds(at, 176), :]
+    for copy in mlp_parts(up):
         copy.wait()
+
+
+def stack_kernel(a, b, c, attn, mlp):
+    for m, ref in enumerate((a, b, c)):
+        attn[m * 176:(m + 1) * 176, :] = ref[0:176, :]
+        mlp[m * 128:(m + 1) * 128, :] = ref[176:304, :]
 
 
 def put_sum(out, at, small_at, rows, total):
@@ -516,7 +542,7 @@
 ANY = pl.BlockSpec(memory_space=pl.ANY)
 
 
-def call(kernel, outs, scratch, name, *args):
+def call(kernel, outs, scratch, name, *args, flops=KERNEL_FLOPS):
     return pl.pallas_call(
         kernel,
         in_specs=[VMEM] * len(args),
@@ -524,7 +550,7 @@
         out_shape=[jax.ShapeDtypeStruct(shape, dtype) for shape, dtype in outs],
         scratch_shapes=[pltpu.VMEM(shape, dtype) for shape, dtype in scratch],
         compiler_params=pltpu.CompilerParams(vmem_limit_bytes=VMEM_LIMIT),
-        cost_estimate=pl.CostEstimate(flops=KERNEL_FLOPS, bytes_accessed=1024, transcendentals=0),
+        cost_estimate=pl.CostEstimate(flops=flops, bytes_accessed=1024, transcendentals=0),
         name=name,
     )(*args)
 
@@ -533,65 +559,66 @@
 MLP_GRADS = [((4, 256, 256), BF), ((4, 256, 256), BF), ((8, 256), F32)]
 
 
-def attn_fwd(layer, first, cur, mask, gain, pieces):
+def attn_fwd(layer, cur, mask, gain, pieces):
     rows = cur.shape[0]
     outs = [((rows, 256), F32), ((rows, 256), F32), ((rows, 256), BF), ((768, rows), BF), ((256, rows), BF), ((8, rows), F32)]
-    return call(functools.partial(attn_fwd_kernel, layer, first), outs, ATTN_SCRATCH, "attn_fwd", cur, mask, gain, *pieces)
-
-
-def mlp_fwd(layer, first, middle, base, gain, pieces):
+    return call(functools.partial(attn_fwd_kernel, layer, len(pieces)), outs, ATTN_SCRATCH, "attn_fwd", *pieces, cur, mask, gain,
+                flops=(LONG, KERNEL_FLOPS)[layer])
+
+
+def mlp_fwd(layer, middle, base, gain, pieces):
     rows = middle.shape[0]
     outs = [((rows, 256), F32), ((rows, 1024), BF), ((rows, 1024), BF)]
-    return call(functools.partial(mlp_fwd_kernel, layer, first), outs, [((4, 512, 256), BF)], "mlp_fwd",
-                middle, base, gain, *pieces)
-
-
-def mlp_both(layer, first, middle, base, cot, gain, pieces):
+    return call(functools.partial(mlp_fwd_kernel, layer, len(pieces)), outs, [((4, 512, 256), BF)], "mlp_fwd", *pieces,
+                middle, base, gain)
+
+
+def mlp_both(layer, middle, base, cot, gain, pieces):
     rows = middle.shape[0]
     outs = [((rows, 256), F32), ((rows, 256), F32)] + MLP_GRADS
     scratch = [((4, 512, 256), BF), ((rows, 1024), BF), ((rows, 1024), BF), ((rows, 256), BF)]
-    return call(functools.partial(mlp_both_kernel, layer, first), outs, scratch, "mlp_both", middle, base, cot, gain, *pieces)
-
-
-def mlp_bwd(layer, first, grad, middle, hid, slope, gain, pieces):
+    return call(functools.partial(mlp_both_kernel, layer, len(pieces)), outs, scratch, "mlp_both", *pieces, middle, base, cot, gain)
+
+
+def mlp_bwd(layer, grad, middle, hid, slope, gain, pieces):
     rows = middle.shape[0]
     outs = [((rows, 256), F32)] + MLP_GRADS
     scratch = [((4, 512, 256), BF), ((rows, 1024), BF), ((rows, 256), BF), ((rows, 256), BF)]
-    return call(functools.partial(mlp_bwd_kernel, layer, first), outs, scratch, "mlp_bwd",
-                grad, middle, hid, slope, gain, *pieces)
-
-
-def attn_pre(layer, first, grad, gm, cur, saved, pieces):
+    return call(functools.partial(mlp_bwd_kernel, layer, len(pieces)), outs, scratch, "mlp_bwd", *pieces,
+                grad, middle, hid, slope, gain)
+
+
+def attn_pre(layer, grad, gm, cur, saved, pieces):
     rows = cur.shape[0]
     nrm, _, mix, _ = saved
     outs = [((256, rows), BF), ((256, 256), BF), ((256, 256), BF), ((rows, 256), F32), ((rows, 256), F32), ((8, 256), F32), ((8, rows), F32)]
     scratch = ATTN_SCRATCH + [((rows, 256), BF), ((rows, 256), BF)]
-    return call(functools.partial(attn_pre_kernel, layer, first), outs, scratch, "attn_pre", grad, gm, cur, nrm, mix, *pieces)
+    return call(functools.partial(attn_pre_kernel, layer, len(pieces)), outs, scratch, "attn_pre", *pieces, grad, gm, cur, nrm, mix)
 
 
 PAYLOAD = [((4, 176, 256), BF), ((4, 176, 256), BF)]
 
 
-def attn_bwd(layer, first, cur, mask, saved, gain, pre, mlp_small, pieces):
+def attn_bwd(layer, cur, mask, saved, gain, pre, mlp_small, pieces):
     rows = cur.shape[0]
     nrm, qkv, _, lse = saved
     gmix, d_cross, d_out, base, gn, small, dot = pre
     scratch = [((4, 352, 256), BF), ((768, rows), BF), ((4, 320, 256), BF)]
-    return call(functools.partial(attn_bwd_kernel, layer, first), [((rows, 256), F32)] + PAYLOAD, scratch, "attn_bwd",
-                mask, nrm, qkv, lse, gain, gmix, d_cross, d_out, small, dot, mlp_small, cur, base, gn, *pieces)
-
-
-def attn_grads(layer, first, mask, saved, gain, pre, mlp_small, pieces):
+    return call(functools.partial(attn_bwd_kernel, layer, len(pieces)), [((rows, 256), F32)] + PAYLOAD, scratch, "attn_bwd", *pieces,
+                mask, nrm, qkv, lse, gain, gmix, d_cross, d_out, small, dot, mlp_small, cur, base, gn)
+
+
+def attn_grads(layer, mask, saved, gain, pre, mlp_small, pieces):
     nrm, qkv, _, lse = saved
     gmix, d_cross, d_out, _, _, small, dot = pre
     scratch = [((4, 352, 256), BF), ((4, 320, 256), BF)]
-    return call(functools.partial(attn_grads_kernel, layer, first), [((768, nrm.shape[0]), BF), ((4, 176, 256), BF), ((2, 176, 256), BF), ((2, 176, 256), BF)], scratch, "attn_grads",
-                mask, nrm, qkv, lse, gain, gmix, d_cross, d_out, small, dot, mlp_small, *pieces)
-
-
-def attn_post(layer, first, gqkv, gain, cur, pre, pieces):
-    return call(functools.partial(attn_post_kernel, layer, first), [((cur.shape[0], 256), F32)], [((4, 352, 256), BF)], "attn_post",
-                gqkv, gain, cur, pre[3], pre[4], *pieces)[0]
+    return call(functools.partial(attn_grads_kernel, layer, len(pieces)), [((768, nrm.shape[0]), BF), ((4, 176, 256), BF), ((2, 176, 256), BF), ((2, 176, 256), BF)], scratch, "attn_grads", *pieces,
+                mask, nrm, qkv, lse, gain, gmix, d_cross, d_out, small, dot, mlp_small)
+
+
+def attn_post(layer, gqkv, gain, cur, pre, pieces):
+    return call(functools.partial(attn_post_kernel, layer, len(pieces)), [((cur.shape[0], 256), F32)], [((4, 352, 256), BF)], "attn_post", *pieces,
+                gqkv, gain, cur, pre[3], pre[4])[0]
 
 
 VMEM = pl.BlockSpec(memory_space=pltpu.VMEM)
@@ -666,44 +693,44 @@
 
     def body(tokens, lengths, cotangent, gain_attn, gain_mlp, w_qkv, w_out, w_up, w_down, w_cross, b_cross):
         rows = tokens.shape[0]
-        own0, own1, half_a0, half_r, half_m1, mask = pl.pallas_call(
+        own0, own1, first_l0, half_l1, mask = pl.pallas_call(
             pack_kernel,
             in_specs=[SMEM] + [ANY] * 5 + [VMEM],
-            out_specs=[VMEM] * 6,
-            out_shape=[jax.ShapeDtypeStruct((n, 256), BF) for n in (352, 352, 176, 432, 256)]
+            out_specs=[VMEM] * 5,
+            out_shape=[jax.ShapeDtypeStruct((n, 256), BF) for n in (352, 352, 304, 432)]
             + [jax.ShapeDtypeStruct((rows // 16, 256), BF)],
             scratch_shapes=[pltpu.SemaphoreType.DMA((2,))],
             name="pack",
         )(lengths, w_qkv.transpose(0, 2, 3, 1), w_cross.transpose(0, 2, 1), w_out, w_up, w_down, b_cross)
 
-        a0 = fetch(half_a0)
-        r = fetch(half_r)
-        m1 = fetch(half_m1)
-        pieces_a0 = [own0] + a0 + [core_swap(x) for x in a0]
-        mid0, base0, *saved0 = attn_fwd(0, 0, tokens, mask, gain_attn, pieces_a0)
-        r = [tie(x, mid0) for x in r]
-        r = r + [core_swap(x) for x in r]
-        cur1, hid0, slope0 = mlp_fwd(0, 0, mid0, base0, gain_mlp, [w_up, w_down] + r)
-        mid1, base1, *saved1 = attn_fwd(1, 256, cur1, mask, gain_attn, [own1] + r)
-        m1 = [tie(x, mid1) for x in m1]
-        m1 = m1 + [core_swap(x) for x in m1]
-        output, gm1, keep_m1, send_m1, small_m1 = mlp_both(1, 0, mid1, base1, cotangent, gain_mlp, [w_up, w_down] + m1)
-        pre = attn_pre(1, 256, cotangent, gm1, cur1, saved1, [own1] + r)
+        l1 = fetch(half_l1)
+        a0, m0 = small_call(stack_kernel, [((528, 256), BF), ((384, 256), BF)], "stack")(*fetch(first_l0))
+        a0 = [own0, a0, core_swap(a0)]
+        mid0, base0, *saved0 = attn_fwd(0, tokens, mask, gain_attn, a0)
+        m0 = [m0, tie(swap(m0, "dp", dp_size, 2), mid0)]
+        m0 = [w_up, w_down] + m0 + [core_swap(x) for x in m0]
+        cur1, hid0, slope0 = mlp_fwd(0, mid0, base0, gain_mlp, m0)
+        l1 = [tie(x, cur1) for x in l1]
+        l1 = l1 + [core_swap(x) for x in l1]
+        a1, m1 = [own1] + l1, [w_up, w_down] + l1
+        mid1, base1, *saved1 = attn_fwd(1, cur1, mask, gain_attn, a1)
+        output, gm1, keep_m1, send_m1, small_m1 = mlp_both(1, mid1, base1, cotangent, gain_mlp, m1)
+        pre = attn_pre(1, cotangent, gm1, cur1, saved1, a1)
         pre_done = pre[0]
         keep_m1, send_m1 = small_call(core_split_kernel, [((4, 128, 256), BF)] * 2, "core_split")(
             keep_m1, tie(core_swap(send_m1), pre_done))
         got_m1 = swap(send_m1, "dp", dp_size, 2)
-        grad1, keep_a1, send_a1 = attn_bwd(1, 256, cur1, tie(mask, send_m1), saved1, gain_attn, pre, small_m1, [own1] + r)
+        grad1, keep_a1, send_a1 = attn_bwd(1, cur1, tie(mask, send_m1), saved1, gain_attn, pre, small_m1, a1)
         m1_sum = small_call(add_kernel, [((4, 128, 256), BF)], "add", LONG)(keep_m1, tie(got_m1, grad1))[0]
         sums = core_sum((None, 160), (m1_sum,), (keep_a1, tie(core_swap(send_a1), m1_sum)))
         got = scatter(sums)
-        gm0, keep_m0, send_m0, small_m0 = mlp_bwd(0, 0, tie(grad1, *sums), mid0, hid0, slope0, gain_mlp, [w_up, w_down] + r)
-        pre = attn_pre(0, 0, grad1, gm0, tokens, saved0, pieces_a0)
-        gqkv, keep_a0, *send_a0 = attn_grads(0, 0, mask, saved0, gain_attn, pre, small_m0, pieces_a0)
+        gm0, keep_m0, send_m0, small_m0 = mlp_bwd(0, tie(grad1, *sums), mid0, hid0, slope0, gain_mlp, m0)
+        pre = attn_pre(0, grad1, gm0, tokens, saved0, a0)
+        gqkv, keep_a0, *send_a0 = attn_grads(0, mask, saved0, gain_attn, pre, small_m0, a0)
         one = four_sum(288, [tie(x, gqkv) for x in got], LONG)
         sums = core_sum((256,), (keep_m0, tie(core_swap(send_m0), one)))
         got = scatter(sums)
-        grad0 = attn_post(0, 0, tie(gqkv, *sums), gain_attn, tokens, pre, pieces_a0)
+        grad0 = attn_post(0, tie(gqkv, *sums), gain_attn, tokens, pre, a0)
         low, high = small_call(early_sum_kernel, [((176 + CUT, 256), BF), ((384 - CUT, 256), BF)], "early_sum")(
             one, *[tie(x, grad0) for x in got])
         sums_a0 = core_sum((160,), (keep_a0, *[core_swap(x) for x in send_a0]))

time: 122 us -> 119 us (0.975)
  starting transfers between devices: 43.7 us -> 39.5 us
  waiting for transfers between devices: 34.8 us -> 36.7 us
    ppermute x43 -> x38, starting transfers between devices: 43.7 us -> 39.5 us  [swap(): return lax.ppermute(x, axis, [(i, i ^ mask) for i in range(size)])]
    ppermute x43 -> x38, waiting for transfers between devices: 34.8 us -> 36.7 us  [swap(): return lax.ppermute(x, axis, [(i, i ^ mask) for i in range(size)])]
    unnamed x24 -> x26, local copies, waits for them, and re-layouts: 3.44 us -> 3.44 us
  transfers between devices with their start and end apart: 43 -> 38, of which waited for: 23 -> 20; matrix products, arithmetic and copies ran while one was open for 0% -> 0% of each run, Pallas kernels for 23% -> 21%
where the time goes in v2:
time: 119 us
  starting transfers between devices  39.5 us (33%)
  Pallas kernels  38.5 us (32%)
  waiting for transfers between devices  36.7 us (31%)
  local copies, waits for them, and re-layouts  3.44 us (3%)
    ppermute x38, starting transfers between devices, swap(): return lax.ppermute(x, axis, [(i, i ^ mask) for i in range(size)])  39.5 us
    ppermute x38, waiting for transfers between devices, swap(): return lax.ppermute(x, axis, [(i, i ^ mask) for i in range(size)])  36.7 us
    pallas_call x10, Pallas kernels, call(): pl.pallas_call(kernel, in_specs=[VMEM] * len(args), out_specs=[VMEM] * le...  33.6 us
    unnamed x26, local copies, waits for them, and re-layouts  3.44 us
    pallas_call x1, Pallas kernels, body(): pl.pallas_call(pack_kernel, in_specs=[SMEM] + [ANY] * 5 + [VMEM], out_spe...  2.66 us
  transfers between devices with their start and end apart: 38, of which 20 were waited for; matrix products, arithmetic and copies ran while one was open for 0% of the time, Pallas kernels for 21%

profile of v2, /device:TPU:9, one launch (start us, length us, event | category | flops | bytes accessed | tf_op | source)
XLA Modules:
  0.0 118.9 jit_solution(6688078090939605479)
XLA Ops:
  0.6 2.7 %pack.1 = (bf16[352,256]{1,0:T(8,128)(2,1)}, bf16[352,256]{1,0:T(8,128)(2,1)}, bf16[304,256]{1,0:T(8,128)(2,1)}, bf16[432,256]{1,0:T(8,128)(2,1)}, bf16[64,256]{1,0:T(8,128)(2,1)}) custom-call(s32[16]{0:T(128)} %lens.1, bf16[2,3,64,256]{3,2,1,0:T(8,128)(2,1)} %bitcast.4, bf16[2,64,256]{2,1,0:T(8,128)(2,1)} %bitcast.5, bf16[2,64,256]{2,1,0:T(8,128)(2,1)} %out.1, ...), custom_call_target="tpu_custom_call" | custom-call | tf_op jit(solution)/shard_map/pack/pallas_call | solution.py:696
  3.3 1.4 %collective-permute-start.3 = (bf16[304,256]{1,0:T(8,128)(2,1)}, bf16[304,256]{1,0:T(8,128)(2,1)S(1)}, u32[]{:S(2)}, u32[]{:S(2)}) collective-permute-start(bf16[304,256]{1,0:T(8,128)(2,1)} %get-tuple-element.114), channel_id=1, source_target_pairs={{0,3},{1,2},{2,1},{3,0},{4,7},{5,6},{6,5},{7,4},{8,11},{9,10},{10,... | collective-permute-start | bytes 466952 | tf_op jit(solution)/shard_map/ppermute | solution.py:652
  4.7 1.1 collective-permute-start.2
  5.8 1.1 collective-permute-start.1
  6.9 8.5 %collective-permute-done.3.c = bf16[304,256]{1,0:T(8,128)(2,1)S(1)} collective-permute-done((bf16[304,256]{1,0:T(8,128)(2,1)}, bf16[304,256]{1,0:T(8,128)(2,1)S(1)}, u32[]{:S(2)}, u32[]{:S(2)}) %collective-permute-start.3) | collective-permute-done | bytes 155680 | tf_op jit(solution)/shard_map/ppermute | solution.py:652
  15.3 2.4 %collective-permute-done.2.b = bf16[304,256]{1,0:T(8,128)(2,1)S(1)} collective-permute-done((bf16[304,256]{1,0:T(8,128)(2,1)}, bf16[304,256]{1,0:T(8,128)(2,1)S(1)}, u32[]{:S(2)}, u32[]{:S(2)}) %collective-permute-start.2) | collective-permute-done | bytes 155680 | tf_op jit(solution)/shard_map/ppermute | solution.py:652
  17.7 1.6 %collective-permute-start.5 = (bf16[528,256]{1,0:T(8,128)(2,1)S(1)}, bf16[528,256]{1,0:T(8,128)(2,1)S(1)}, u32[]{:S(2)}, u32[]{:S(2)}) collective-permute-start(bf16[528,256]{1,0:T(8,128)(2,1)S(1)} %get-tuple-element.117.refs_1_), channel_id=1, source_target_pairs={{0,4},{4,0},{8,12},{12,8},{16,20},{20,16},{24,28},{28,24},{1,5},{5... | collective-permute-start | bytes 811016 | tf_op jit(solution)/shard_map/ppermute | solution.py:652
  19.5 3.9 %collective-permute-start.8 = (bf16[432,256]{1,0:T(8,128)(2,1)}, bf16[432,256]{1,0:T(8,128)(2,1)S(1)}, u32[]{:S(2)}, u32[]{:S(2)}) collective-permute-start(bf16[432,256]{1,0:T(8,128)(2,1)} %get-tuple-element.113), channel_id=1, source_target_pairs={{0,2},{1,3},{2,0},{3,1},{4,6},{5,7},{6,4},{7,5},{8,10},{9,11},{10,... | collective-permute-start | bytes 663560 | tf_op jit(solution)/shard_map/ppermute | solution.py:652
  23.5 0.6 collective-permute-start.6
  24.2 1.2 %collective-permute-start.4 = (bf16[384,256]{1,0:T(8,128)(2,1)S(1)}, bf16[384,256]{1,0:T(8,128)(2,1)S(1)}, u32[]{:S(2)}, u32[]{:S(2)}) collective-permute-start(bf16[384,256]{1,0:T(8,128)(2,1)S(1)} %get-tuple-element.115.refs_2_), channel_id=1, source_target_pairs={{0,8},{4,12},{8,0},{12,4},{16,24},{20,28},{24,16},{28,20},{1,9},{5... | collective-permute-start | bytes 589832 | tf_op jit(solution)/shard_map/ppermute | solution.py:652
  25.4 1.0 copy-done.3
  26.4 0.9 copy-done.5
  27.3 0.8 copy-done.8
  28.1 0.7 copy-done.10
  28.8 4.0 %attn_fwd.2 = (f32[1024,256]{1,0:T(8,128)S(1)}, f32[1024,256]{1,0:T(8,128)S(1)}, bf16[1024,256]{1,0:T(8,128)(2,1)S(1)}, bf16[768,1024]{1,0:T(8,128)(2,1)S(1)}, b...) custom-call(bf16[352,256]{1,0:T(8,128)(2,1)S(1)} %copy-done.5, bf16[528,256]{1,0:T(8,128)(2,1)S(1)} %get-tuple-element.117.refs_1_, ...), custom_call_target="tpu_custom_call" | custom-call | flops 49999998976 | bytes 1024 | tf_op jit(solution)/shard_map/attn_fwd/pallas_call | solution.py:546
  32.8 0.3 collective-permute-start.7
  33.2 1.2 collective-permute-done.7.refs_5_
  34.4 2.5 %mlp_fwd.1 = (f32[1024,256]{1,0:T(8,128)S(1)}, bf16[1024,1024]{1,0:T(8,128)(2,1)S(1)}, bf16[1024,1024]{1,0:T(8,128)(2,1)S(1)}) custom-call(bf16[2,256,256]{2,1,0:T(8,128)(2,1)S(1)} %copy-done, bf16[2,256,256]{2,1,0:T(8,128)(2,1)S(1)} %copy-done.1, bf16[384,256]{1,0:T(8,128)(2,1)S(1)} %get-tuple-element.115.refs_2_, ...), custom_call_target="tpu_custom_call" | custom-call | flops 1000 | bytes 1024 | tf_op jit(solution)/shard_map/mlp_fwd/pallas_call | solution.py:546
  36.9 1.9 %collective-permute-done.8.refs_2_.refs_3_ = bf16[432,256]{1,0:T(8,128)(2,1)S(1)} collective-permute-done((bf16[432,256]{1,0:T(8,128)(2,1)}, bf16[432,256]{1,0:T(8,128)(2,1)S(1)}, u32[]{:S(2)}, u32[]{:S(2)}) %collective-permute-start.8) | collective-permute-done | bytes 221216 | tf_op jit(solution)/shard_map/ppermute | solution.py:652
  38.9 0.8 collective-permute-start.10
  39.7 0.5 collective-permute-start.12
  40.2 0.6 collective-permute-done.10.refs_4_.refs_5_
  40.8 0.4 collective-permute-done.11.refs_5_.refs_6_
  41.2 0.3 collective-permute-done.12.refs_6_.refs_7_
  41.5 4.0 %attn_fwd.3 = (f32[1024,256]{1,0:T(8,128)S(1)}, f32[1024,256]{1,0:T(8,128)S(1)}, bf16[1024,256]{1,0:T(8,128)(2,1)S(1)}, bf16[768,1024]{1,0:T(8,128)(2,1)S(1)}, b...) custom-call(bf16[352,256]{1,0:T(8,128)(2,1)S(1)} %copy-done.7, ...), custom_call_target="tpu_custom_call" | custom-call | flops 1000 | bytes 1024 | tf_op jit(solution)/shard_map/attn_fwd/pallas_call | solution.py:546
  45.6 5.6 %mlp_both.1 = (f32[1024,256]{1,0:T(8,128)}, f32[1024,256]{1,0:T(8,128)S(1)}, bf16[4,256,256]{2,1,0:T(8,128)(2,1)S(1)}, bf16[4,256,256]{2,1,0:T(8,128)(2,1)S(1)}, f32[8,256]{1,0:T(8,128)S(1)}) custom-call(bf16[2,256,256]{2,1,0:T(8,128)(2,1)S(1)} %copy-done, bf16[2,256,256]{2,1,0:T(8,128)(2,1)S(1)} %copy-done.1, ...), custom_call_target="tpu_custom_call" | custom-call | flops 1000 | bytes 1024 | tf_op jit(solution)/shard_map/mlp_both/pallas_call | solution.py:546
  51.1 0.3 collective-permute-start.13
  51.5 1.4 %attn_pre.2 = (bf16[256,1024]{1,0:T(8,128)(2,1)S(1)}, bf16[256,256]{1,0:T(8,128)(2,1)S(1)}, bf16[256,256]{1,0:T(8,128)(2,1)S(1)}, f32[1024,256]{1,0:T(8,128)S(1)...) custom-call(bf16[352,256]{1,0:T(8,128)(2,1)S(1)} %copy-done.7, ...), custom_call_target="tpu_custom_call" | custom-call | flops 1000 | bytes 1024 | tf_op jit(solution)/shard_map/attn_pre/pallas_call | solution.py:546
  52.8 0.2 collective-permute-done.13.got
  53.2 1.3 %collective-permute-start.14 = (bf16[4,128,256]{2,1,0:T(8,128)(2,1)S(1)}, bf16[4,128,256]{2,1,0:T(8,128)(2,1)S(1)}, u32[]{:S(2)}, u32[]{:S(2)}) collective-permute-start(bf16[4,128,256]{2,1,0:T(8,128)(2,1)S(1)} %get-tuple-element.140), channel_id=1, source_target_pairs={{0,8},{4,12},{8,0},{12,4},{16,24},{20,28},{24,16},{28,20},{1,9},{5... | collective-permute-start | bytes 786440 | tf_op jit(solution)/shard_map/ppermute | solution.py:652
  54.5 5.2 %attn_bwd.1 = (f32[1024,256]{1,0:T(8,128)S(1)}, bf16[4,176,256]{2,1,0:T(8,128)(2,1)S(1)}, bf16[4,176,256]{2,1,0:T(8,128)(2,1)S(1)}) custom-call(bf16[352,256]{1,0:T(8,128)(2,1)S(1)} %copy-done.7, bf16[432,256]{1,0:T(8,128)(2,1)S(1)} %collective-permute-done.refs_1_.refs_2_, bf16[432,256]{1,0:T(8,128)(2,1)S(1)} %collective-permute-done.8.refs_2_.refs_3_, ...), custom_call_target="tpu_custom_call" | custom-call | flops 1000 | bytes 1024 | tf_op jit(solution)/shard_map/attn_bwd/pallas_call | solution.py:546
  59.7 0.6 collective-permute-start.15
  60.3 0.5 collective-permute-done.14.b
  60.9 0.7 collective-permute-done.15.refs_2_
  61.7 1.4 %collective-permute-start.19 = (bf16[304,256]{1,0:T(8,128)(2,1)S(1)}, bf16[304,256]{1,0:T(8,128)(2,1)S(1)}, u32[]{:S(2)}, u32[]{:S(2)}) collective-permute-start(bf16[304,256]{1,0:T(8,128)(2,1)S(1)} %get-tuple-element.160), channel_id=1, source_target_pairs={{0,3},{1,2},{2,1},{3,0},{4,7},{5,6},{6,5},{7,4},{8,11},{9,10},{10,... | collective-permute-start | bytes 466952 | tf_op jit(solution)/shard_map/ppermute | solution.py:652
  63.1 3.9 %collective-permute-start.18 = (bf16[304,256]{1,0:T(8,128)(2,1)S(1)}, bf16[304,256]{1,0:T(8,128)(2,1)S(1)}, u32[]{:S(2)}, u32[]{:S(2)}) collective-permute-start(bf16[304,256]{1,0:T(8,128)(2,1)S(1)} %get-tuple-element.159), channel_id=1, source_target_pairs={{0,2},{1,3},{2,0},{3,1},{4,6},{5,7},{6,4},{7,5},{8,10},{9,11},{10,... | collective-permute-start | bytes 466952 | tf_op jit(solution)/shard_map/ppermute | solution.py:652
  67.0 3.2 %mlp_bwd.1 = (f32[1024,256]{1,0:T(8,128)S(1)}, bf16[4,256,256]{2,1,0:T(8,128)(2,1)S(1)}, bf16[4,256,256]{2,1,0:T(8,128)(2,1)S(1)}, f32[8,256]{1,0:T(8,128)S(1)}) custom-call(bf16[2,256,256]{2,1,0:T(8,128)(2,1)S(1)} %copy-done, bf16[2,256,256]{2,1,0:T(8,128)(2,1)S(1)} %copy-done.1, bf16[384,256]{1,0:T(8,128)(2,1)S(1)} %get-tuple-element.115.refs_2_, ...), custom_call_target="tpu_custom_call" | custom-call | flops 1000 | bytes 1024 | tf_op jit(solution)/shard_map/mlp_bwd/pallas_call | solution.py:546
  70.1 1.4 %attn_pre.3 = (bf16[256,1024]{1,0:T(8,128)(2,1)S(1)}, bf16[256,256]{1,0:T(8,128)(2,1)S(1)}, bf16[256,256]{1,0:T(8,128)(2,1)S(1)}, f32[1024,256]{1,0:T(8,128)S(1)...) custom-call(bf16[352,256]{1,0:T(8,128)(2,1)S(1)} %copy-done.6, ...), custom_call_target="tpu_custom_call" | custom-call | flops 1000 | bytes 1024 | tf_op jit(solution)/shard_map/attn_pre/pallas_call | solution.py:546
  71.5 4.0 %attn_grads.1 = (bf16[768,1024]{1,0:T(8,128)(2,1)S(1)}, bf16[4,176,256]{2,1,0:T(8,128)(2,1)S(1)}, bf16[2,176,256]{2,1,0:T(8,128)(2,1)S(1)}, bf16[2,176,256]{2,1,0:T(8,128)(2,1)S(1)}) custom-call(bf16[352,256]{1,0:T(8,128)(2,1)S(1)} %copy-done.6, bf16[528,256]{1,0:T(8,128)(2,1)S(1)} %get-tuple-element.117.refs_1_, ...), custom_call_target="tpu_custom_call" | custom-call | flops 1000 | bytes 1024 | tf_op jit(solution)/shard_map/attn_grads/pallas_call | solution.py:546
  75.5 1.1 collective-permute-start.24
  76.7 0.4 collective-permute-start.16
  77.2 1.6 %collective-permute-done.16.refs_1_ = bf16[4,256,256]{2,1,0:T(8,128)(2,1)S(1)} collective-permute-done((bf16[4,256,256]{2,1,0:T(8,128)(2,1)S(1)}, bf16[4,256,256]{2,1,0:T(8,128)(2,1)S(1)}, u32[]{:S(2)}, u32[]{:S(2)}) %collective-permute-start.16) | collective-permute-done | bytes 524320 | tf_op jit(solution)/shard_map/ppermute | solution.py:652
  78.9 1.8 %collective-permute-start.20 = (bf16[256,256]{1,0:T(8,128)(2,1)S(1)}, bf16[256,256]{1,0:T(8,128)(2,1)S(1)}, u32[]{:S(2)}, u32[]{:S(2)}) collective-permute-start(bf16[256,256]{1,0:T(8,128)(2,1)S(1)} %get-tuple-element.181), channel_id=1, source_target_pairs={{0,1},{1,0},{2,3},{3,2},{4,5},{5,4},{6,7},{7,6},{8,9},{9,8},{10,11... | collective-permute-start | bytes 393224 | tf_op jit(solution)/shard_map/ppermute | solution.py:652
  80.7 1.3 %collective-permute-start.22 = (bf16[256,256]{1,0:T(8,128)(2,1)S(1)}, bf16[256,256]{1,0:T(8,128)(2,1)S(1)}, u32[]{:S(2)}, u32[]{:S(2)}) collective-permute-start(bf16[256,256]{1,0:T(8,128)(2,1)S(1)} %get-tuple-element.183), channel_id=1, source_target_pairs={{0,3},{1,2},{2,1},{3,0},{4,7},{5,6},{6,5},{7,4},{8,11},{9,10},{10,... | collective-permute-start | bytes 393224 | tf_op jit(solution)/shard_map/ppermute | solution.py:652
  82.0 2.4 %collective-permute-start.26 = (bf16[176,256]{1,0:T(8,128)(2,1)S(1)}, bf16[176,256]{1,0:T(8,128)(2,1)S(1)}, u32[]{:S(2)}, u32[]{:S(2)}) collective-permute-start(bf16[176,256]{1,0:T(8,128)(2,1)S(1)} %get-tuple-element.196), channel_id=1, source_target_pairs={{0,1},{1,0},{2,3},{3,2},{4,5},{5,4},{6,7},{7,6},{8,9},{9,8},{10,11... | collective-permute-start | bytes 270344 | tf_op jit(solution)/shard_map/ppermute | solution.py:652
  84.4 0.4 collective-permute-done.20.a
  84.8 0.9 collective-permute-start.28
  85.7 2.4 %attn_post.1 = f32[1024,256]{1,0:T(8,128)} custom-call(bf16[352,256]{1,0:T(8,128)(2,1)S(1)} %copy-done.6, bf16[528,256]{1,0:T(8,128)(2,1)S(1)} %get-tuple-element.117.refs_1_, bf16[528,256]{1,0:T(8,128)(2,1)S(1)} %collective-permute-done.5.refs_2_, bf16[768,1024]{1,0:T(8,128)(2,1)S(1)} %get-tuple-element.184.refs_3_, f32[2,256]{1,0:T(2,128)S(1)} %copy-done.11, ...), custom_call_target="tpu_custom_call" | custom-call | flops 1000 | bytes 1024 | tf_op jit(solution)/shard_map/attn_post/pallas_call | solution.py:546
  88.1 9.6 %collective-permute-done.22.c = bf16[256,256]{1,0:T(8,128)(2,1)S(1)} collective-permute-done((bf16[256,256]{1,0:T(8,128)(2,1)S(1)}, bf16[256,256]{1,0:T(8,128)(2,1)S(1)}, u32[]{:S(2)}, u32[]{:S(2)}) %collective-permute-start.22) | collective-permute-done | bytes 131104 | tf_op jit(solution)/shard_map/ppermute | solution.py:652
  97.8 1.3 %collective-permute-start.23 = (bf16[272,256]{1,0:T(8,128)(2,1)S(1)}, bf16[272,256]{1,0:T(8,128)(2,1)S(1)}, u32[]{:S(2)}, u32[]{:S(2)}) collective-permute-start(bf16[272,256]{1,0:T(8,128)(2,1)S(1)} %get-tuple-element.191.low), channel_id=1, source_target_pairs={{0,8},{4,12},{8,0},{12,4},{16,24},{20,28},{24,16},{28,20},{1,9},{5... | collective-permute-start | bytes 417800 | tf_op jit(solution)/shard_map/ppermute | solution.py:652
  99.1 1.2 %collective-permute-start.29 = (bf16[288,256]{1,0:T(8,128)(2,1)S(1)}, bf16[288,256]{1,0:T(8,128)(2,1)S(1)}, u32[]{:S(2)}, u32[]{:S(2)}) collective-permute-start(bf16[288,256]{1,0:T(8,128)(2,1)S(1)} %get-tuple-element.200.high), channel_id=1, source_target_pairs={{0,16},{4,20},{8,24},{12,28},{16,0},{20,4},{24,8},{28,12},{1,17},{... | collective-permute-start | bytes 442376 | tf_op jit(solution)/shard_map/ppermute | solution.py:652
  100.3 1.3 %collective-permute-done.28.refs_3_ = bf16[176,256]{1,0:T(8,128)(2,1)S(1)} collective-permute-done((bf16[176,256]{1,0:T(8,128)(2,1)S(1)}, bf16[176,256]{1,0:T(8,128)(2,1)S(1)}, u32[]{:S(2)}, u32[]{:S(2)}) %collective-permute-start.28) | collective-permute-done | bytes 90144 | tf_op jit(solution)/shard_map/ppermute | solution.py:652
  101.6 0.4 collective-permute-done.23.low_got
  102.0 1.3 %collective-permute-done.29.high_got = bf16[288,256]{1,0:T(8,128)(2,1)S(1)} collective-permute-done((bf16[288,256]{1,0:T(8,128)(2,1)S(1)}, bf16[288,256]{1,0:T(8,128)(2,1)S(1)}, u32[]{:S(2)}, u32[]{:S(2)}) %collective-permute-start.29) | collective-permute-done | bytes 147488 | tf_op jit(solution)/shard_map/ppermute | solution.py:652
  103.6 1.2 %collective-permute-start.30 = (bf16[272,256]{1,0:T(8,128)(2,1)S(1)}, bf16[272,256]{1,0:T(8,128)(2,1)S(1)}, u32[]{:S(2)}, u32[]{:S(2)}) collective-permute-start(bf16[272,256]{1,0:T(8,128)(2,1)S(1)} %get-tuple-element.202.low), channel_id=1, source_target_pairs={{0,16},{4,20},{8,24},{12,28},{16,0},{20,4},{24,8},{28,12},{1,17},{... | collective-permute-start | bytes 417800 | tf_op jit(solution)/shard_map/ppermute | solution.py:652
  104.8 1.3 %collective-permute-start.33 = (bf16[176,256]{1,0:T(8,128)(2,1)S(1)}, bf16[176,256]{1,0:T(8,128)(2,1)S(1)}, u32[]{:S(2)}, u32[]{:S(2)}) collective-permute-start(bf16[176,256]{1,0:T(8,128)(2,1)S(1)} %four_sum.4.refs_0_), channel_id=1, source_target_pairs={{0,24},{4,28},{8,16},{12,20},{16,8},{20,12},{24,0},{28,4},{1,25},{... | collective-permute-start | bytes 270344 | tf_op jit(solution)/shard_map/ppermute | solution.py:652
  106.1 1.2 %collective-permute-start.32 = (bf16[176,256]{1,0:T(8,128)(2,1)S(1)}, bf16[176,256]{1,0:T(8,128)(2,1)S(1)}, u32[]{:S(2)}, u32[]{:S(2)}) collective-permute-start(bf16[176,256]{1,0:T(8,128)(2,1)S(1)} %four_sum.4.refs_0_), channel_id=1, source_target_pairs={{0,16},{4,20},{8,24},{12,28},{16,0},{20,4},{24,8},{28,12},{1,17},{... | collective-permute-start | bytes 270344 | tf_op jit(solution)/shard_map/ppermute | solution.py:652
  107.5 2.0 %collective-permute-done.33.refs_3_ = bf16[176,256]{1,0:T(8,128)(2,1)S(1)} collective-permute-done((bf16[176,256]{1,0:T(8,128)(2,1)S(1)}, bf16[176,256]{1,0:T(8,128)(2,1)S(1)}, u32[]{:S(2)}, u32[]{:S(2)}) %collective-permute-start.33) | collective-permute-done | bytes 90144 | tf_op jit(solution)/shard_map/ppermute | solution.py:652
  109.5 1.7 %collective-permute-done.32.refs_2_ = bf16[176,256]{1,0:T(8,128)(2,1)S(1)} collective-permute-done((bf16[176,256]{1,0:T(8,128)(2,1)S(1)}, bf16[176,256]{1,0:T(8,128)(2,1)S(1)}, u32[]{:S(2)}, u32[]{:S(2)}) %collective-permute-start.32) | collective-permute-done | bytes 90144 | tf_op jit(solution)/shard_map/ppermute | solution.py:652
  111.2 0.7 collective-permute-done.31.refs_1_
  112.0 4.0 %collective-permute-start.36 = (bf16[416,256]{1,0:T(8,128)(2,1)S(1)}, bf16[416,256]{1,0:T(8,128)(2,1)S(1)}, u32[]{:S(2)}, u32[]{:S(2)}) collective-permute-start(bf16[416,256]{1,0:T(8,128)(2,1)S(1)} %get-tuple-element.207.high), channel_id=1, source_target_pairs={{0,4},{4,0},{8,12},{12,8},{16,20},{20,16},{24,28},{28,24},{1,5},{5... | collective-permute-start | bytes 638984 | tf_op jit(solution)/shard_map/ppermute | solution.py:652
  116.2 0.5 collective-permute-start.37
  116.7 0.9 collective-permute-done.37.late_other
  117.6 1.3 %finish.1 = (f32[2,3,64,256]{3,2,1,0:T(8,128)}, f32[2,64,256]{2,1,0:T(8,128)}, f32[2,256,256]{2,1,0:T(8,128)}, f32[2,256,256]{2,1,0:T(8,128)}, f32[2,64,256]{2,1...) custom-call(bf16[272,256]{1,0:T(8,128)(2,1)S(1)} %get-tuple-element.206.low, ...), custom_call_target="tpu_custom_call" | custom-call | flops 1000 | bytes 1024 | tf_op jit(solution)/shard_map/finish/pallas_call | solution.py:629
  (62 shorter events, 1.8 us)
Async XLA Ops:
  3.3 12.0 %collective-permute-start.3 = (bf16[304,256]{1,0:T(8,128)(2,1)}, bf16[304,256]{1,0:T(8,128)(2,1)S(1)}, u32[]{:S(2)}, u32[]{:S(2)}) collective-permute-start(bf16[304,256]{1,0:T(8,128)(2,1)} %get-tuple-element.114), channel_id=1, source_target_pairs={{0,3},{1,2},{2,1},{3,0},{4,7},{5,6},{6,5},{7,4},{8,11},{9,10},{10,... | collective-permute-start | bytes 466952 | tf_op jit(solution)/shard_map/ppermute | solution.py:652
  4.7 13.0 %collective-permute-start.2 = (bf16[304,256]{1,0:T(8,128)(2,1)}, bf16[304,256]{1,0:T(8,128)(2,1)S(1)}, u32[]{:S(2)}, u32[]{:S(2)}) collective-permute-start(bf16[304,256]{1,0:T(8,128)(2,1)} %get-tuple-element.114), channel_id=1, source_target_pairs={{0,2},{1,3},{2,0},{3,1},{4,6},{5,7},{6,4},{7,5},{8,10},{9,11},{10,... | collective-permute-start | bytes 466952 | tf_op jit(solution)/shard_map/ppermute | solution.py:652
  5.8 11.9 %collective-permute-start.1 = (bf16[304,256]{1,0:T(8,128)(2,1)}, bf16[304,256]{1,0:T(8,128)(2,1)S(1)}, u32[]{:S(2)}, u32[]{:S(2)}) collective-permute-start(bf16[304,256]{1,0:T(8,128)(2,1)} %get-tuple-element.114), channel_id=1, source_target_pairs={{0,1},{1,0},{2,3},{3,2},{4,5},{5,4},{6,7},{7,6},{8,9},{9,8},{10,11... | collective-permute-start | bytes 466952 | tf_op jit(solution)/shard_map/ppermute | solution.py:652
  17.7 6.4 %collective-permute-start.5 = (bf16[528,256]{1,0:T(8,128)(2,1)S(1)}, bf16[528,256]{1,0:T(8,128)(2,1)S(1)}, u32[]{:S(2)}, u32[]{:S(2)}) collective-permute-start(bf16[528,256]{1,0:T(8,128)(2,1)S(1)} %get-tuple-element.117.refs_1_), channel_id=1, source_target_pairs={{0,4},{4,0},{8,12},{12,8},{16,20},{20,16},{24,28},{28,24},{1,5},{5... | collective-permute-start | bytes 811016 | tf_op jit(solution)/shard_map/ppermute | solution.py:652
  19.3 17.6 %collective-permute-start.9 = (bf16[432,256]{1,0:T(8,128)(2,1)}, bf16[432,256]{1,0:T(8,128)(2,1)S(1)}, u32[]{:S(2)}, u32[]{:S(2)}) collective-permute-start(bf16[432,256]{1,0:T(8,128)(2,1)} %get-tuple-element.113), channel_id=1, source_target_pairs={{0,3},{1,2},{2,1},{3,0},{4,7},{5,6},{6,5},{7,4},{8,11},{9,10},{10,... | collective-permute-start | bytes 663560 | tf_op jit(solution)/shard_map/ppermute | solution.py:652
  19.5 19.3 %collective-permute-start.8 = (bf16[432,256]{1,0:T(8,128)(2,1)}, bf16[432,256]{1,0:T(8,128)(2,1)S(1)}, u32[]{:S(2)}, u32[]{:S(2)}) collective-permute-start(bf16[432,256]{1,0:T(8,128)(2,1)} %get-tuple-element.113), channel_id=1, source_target_pairs={{0,2},{1,3},{2,0},{3,1},{4,6},{5,7},{6,4},{7,5},{8,10},{9,11},{10,... | collective-permute-start | bytes 663560 | tf_op jit(solution)/shard_map/ppermute | solution.py:652
  23.4 15.4 %collective-permute-start = (bf16[432,256]{1,0:T(8,128)(2,1)}, bf16[432,256]{1,0:T(8,128)(2,1)S(1)}, u32[]{:S(2)}, u32[]{:S(2)}) collective-permute-start(bf16[432,256]{1,0:T(8,128)(2,1)} %get-tuple-element.113), channel_id=1, source_target_pairs={{0,1},{1,0},{2,3},{3,2},{4,5},{5,4},{6,7},{7,6},{8,9},{9,8},{10,11... | collective-permute-start | bytes 663560 | tf_op jit(solution)/shard_map/ppermute | solution.py:652
  23.5 9.6 %collective-permute-start.6 = (bf16[384,256]{1,0:T(8,128)(2,1)S(1)}, bf16[384,256]{1,0:T(8,128)(2,1)S(1)}, u32[]{:S(2)}, u32[]{:S(2)}) collective-permute-start(bf16[384,256]{1,0:T(8,128)(2,1)S(1)} %get-tuple-element.115.refs_2_), channel_id=1, source_target_pairs={{0,4},{4,0},{8,12},{12,8},{16,20},{20,16},{24,28},{28,24},{1,5},{5... | collective-permute-start | bytes 589832 | tf_op jit(solution)/shard_map/ppermute | solution.py:652
  24.2 8.7 %collective-permute-start.4 = (bf16[384,256]{1,0:T(8,128)(2,1)S(1)}, bf16[384,256]{1,0:T(8,128)(2,1)S(1)}, u32[]{:S(2)}, u32[]{:S(2)}) collective-permute-start(bf16[384,256]{1,0:T(8,128)(2,1)S(1)} %get-tuple-element.115.refs_2_), channel_id=1, source_target_pairs={{0,8},{4,12},{8,0},{12,4},{16,24},{20,28},{24,16},{28,20},{1,9},{5... | collective-permute-start | bytes 589832 | tf_op jit(solution)/shard_map/ppermute | solution.py:652
  25.4 1.0 copy-start.3
  26.4 0.9 copy-start.5
  27.3 0.8 copy-start.8
  28.1 0.7 copy-start.10
  28.8 5.6 %copy-start = (bf16[2,256,256]{2,1,0:T(8,128)(2,1)S(1)}, bf16[2,256,256]{2,1,0:T(8,128)(2,1)}, u32[]{:S(2)}) copy-start(bf16[2,256,256]{2,1,0:T(8,128)(2,1)} %refs_0_.5) | copy-start | bytes 786436
  28.8 5.6 %copy-start.1 = (bf16[2,256,256]{2,1,0:T(8,128)(2,1)S(1)}, bf16[2,256,256]{2,1,0:T(8,128)(2,1)}, u32[]{:S(2)}) copy-start(bf16[2,256,256]{2,1,0:T(8,128)(2,1)} %refs_1_.5) | copy-start | bytes 786436
  28.8 5.6 %copy-start.12 = (f32[2,256]{1,0:T(2,128)S(1)}, f32[2,256]{1,0:T(2,128)}, u32[]{:S(2)}) copy-start(f32[2,256]{1,0:T(2,128)} %refs_10_.3) | copy-start | bytes 6148
  32.8 1.5 %collective-permute-start.7 = (bf16[384,256]{1,0:T(8,128)(2,1)S(1)}, bf16[384,256]{1,0:T(8,128)(2,1)S(1)}, u32[]{:S(2)}, u32[]{:S(2)}) collective-permute-start(bf16[384,256]{1,0:T(8,128)(2,1)S(1)} %collective-permute-done.4.refs_3_), channel_id=1, source_target_pairs={{0,4},{4,0},{8,12},{12,8},{16,20},{20,16},{24,28},{28,24},{1,5},{5... | collective-permute-start | bytes 589832 | tf_op jit(solution)/shard_map/ppermute | solution.py:652
  34.3 7.2 %copy-start.7 = (bf16[352,256]{1,0:T(8,128)(2,1)S(1)}, bf16[352,256]{1,0:T(8,128)(2,1)}, u32[]{:S(2)}) copy-start(bf16[352,256]{1,0:T(8,128)(2,1)} %get-tuple-element.126.refs_0_) | copy-start | bytes 540676
  36.9 8.6 %copy-start.2 = (bf16[1024,256]{1,0:T(8,128)(2,1)S(1)}, bf16[1024,256]{1,0:T(8,128)(2,1)}, u32[]{:S(2)}) copy-start(bf16[1024,256]{1,0:T(8,128)(2,1)} %refs_7_.2) | copy-start | bytes 1572868
  38.9 2.0 %collective-permute-start.10 = (bf16[432,256]{1,0:T(8,128)(2,1)S(1)}, bf16[432,256]{1,0:T(8,128)(2,1)S(1)}, u32[]{:S(2)}, u32[]{:S(2)}) collective-permute-start(bf16[432,256]{1,0:T(8,128)(2,1)S(1)} %collective-permute-done.refs_1_.refs_2_), channel_id=1, source_target_pairs={{0,4},{4,0},{8,12},{12,8},{16,20},{20,16},{24,28},{28,24},{1,5},{5... | collective-permute-start | bytes 663560 | tf_op jit(solution)/shard_map/ppermute | solution.py:652
  39.7 1.5 %collective-permute-start.11 = (bf16[432,256]{1,0:T(8,128)(2,1)S(1)}, bf16[432,256]{1,0:T(8,128)(2,1)S(1)}, u32[]{:S(2)}, u32[]{:S(2)}) collective-permute-start(bf16[432,256]{1,0:T(8,128)(2,1)S(1)} %collective-permute-done.8.refs_2_.refs_3_), channel_id=1, source_target_pairs={{0,4},{4,0},{8,12},{12,8},{16,20},{20,16},{24,28},{28,24},{1,5},{5... | collective-permute-start | bytes 663560 | tf_op jit(solution)/shard_map/ppermute | solution.py:652
  39.7 1.8 %collective-permute-start.12 = (bf16[432,256]{1,0:T(8,128)(2,1)S(1)}, bf16[432,256]{1,0:T(8,128)(2,1)S(1)}, u32[]{:S(2)}, u32[]{:S(2)}) collective-permute-start(bf16[432,256]{1,0:T(8,128)(2,1)S(1)} %collective-permute-done.9.refs_3_.refs_4_), channel_id=1, source_target_pairs={{0,4},{4,0},{8,12},{12,8},{16,20},{20,16},{24,28},{28,24},{1,5},{5... | collective-permute-start | bytes 663560 | tf_op jit(solution)/shard_map/ppermute | solution.py:652
  51.1 1.9 %collective-permute-start.13 = (bf16[4,256,256]{2,1,0:T(8,128)(2,1)S(1)}, bf16[4,256,256]{2,1,0:T(8,128)(2,1)S(1)}, u32[]{:S(2)}, u32[]{:S(2)}) collective-permute-start(bf16[4,256,256]{2,1,0:T(8,128)(2,1)S(1)} %get-tuple-element.134), channel_id=1, source_target_pairs={{0,4},{4,0},{8,12},{12,8},{16,20},{20,16},{24,28},{28,24},{1,5},{5... | collective-permute-start | bytes 1572872 | tf_op jit(solution)/shard_map/ppermute | solution.py:652
  51.5 3.0 %copy-start.9 = (bf16[64,256]{1,0:T(8,128)(2,1)S(1)}, bf16[64,256]{1,0:T(8,128)(2,1)}, u32[]{:S(2)}) copy-start(bf16[64,256]{1,0:T(8,128)(2,1)} %get-tuple-element.141.refs_4_.refs_8_.refs_7_.refs_3_) | copy-start | bytes 98308
  51.5 3.0 %copy-start.11 = (f32[2,256]{1,0:T(2,128)S(1)}, f32[2,256]{1,0:T(2,128)}, u32[]{:S(2)}) copy-start(f32[2,256]{1,0:T(2,128)} %refs_4_.1) | copy-start | bytes 6148
  53.2 7.6 %collective-permute-start.14 = (bf16[4,128,256]{2,1,0:T(8,128)(2,1)S(1)}, bf16[4,128,256]{2,1,0:T(8,128)(2,1)S(1)}, u32[]{:S(2)}, u32[]{:S(2)}) collective-permute-start(bf16[4,128,256]{2,1,0:T(8,128)(2,1)S(1)} %get-tuple-element.140), channel_id=1, source_target_pairs={{0,8},{4,12},{8,0},{12,4},{16,24},{20,28},{24,16},{28,20},{1,9},{5... | collective-permute-start | bytes 786440 | tf_op jit(solution)/shard_map/ppermute | solution.py:652
  59.7 1.9 %collective-permute-start.15 = (bf16[4,176,256]{2,1,0:T(8,128)(2,1)S(1)}, bf16[4,176,256]{2,1,0:T(8,128)(2,1)S(1)}, u32[]{:S(2)}, u32[]{:S(2)}) collective-permute-start(bf16[4,176,256]{2,1,0:T(8,128)(2,1)S(1)} %get-tuple-element.155), channel_id=1, source_target_pairs={{0,4},{4,0},{8,12},{12,8},{16,20},{20,16},{24,28},{28,24},{1,5},{5... | collective-permute-start | bytes 1081352 | tf_op jit(solution)/shard_map/ppermute | solution.py:652
  61.7 14.9 %collective-permute-start.19 = (bf16[304,256]{1,0:T(8,128)(2,1)S(1)}, bf16[304,256]{1,0:T(8,128)(2,1)S(1)}, u32[]{:S(2)}, u32[]{:S(2)}) collective-permute-start(bf16[304,256]{1,0:T(8,128)(2,1)S(1)} %get-tuple-element.160), channel_id=1, source_target_pairs={{0,3},{1,2},{2,1},{3,0},{4,7},{5,6},{6,5},{7,4},{8,11},{9,10},{10,... | collective-permute-start | bytes 466952 | tf_op jit(solution)/shard_map/ppermute | solution.py:652
  63.1 14.0 %collective-permute-start.18 = (bf16[304,256]{1,0:T(8,128)(2,1)S(1)}, bf16[304,256]{1,0:T(8,128)(2,1)S(1)}, u32[]{:S(2)}, u32[]{:S(2)}) collective-permute-start(bf16[304,256]{1,0:T(8,128)(2,1)S(1)} %get-tuple-element.159), channel_id=1, source_target_pairs={{0,2},{1,3},{2,0},{3,1},{4,6},{5,7},{6,4},{7,5},{8,10},{9,11},{10,... | collective-permute-start | bytes 466952 | tf_op jit(solution)/shard_map/ppermute | solution.py:652
  67.0 10.1 %collective-permute-start.17 = (bf16[304,256]{1,0:T(8,128)(2,1)S(1)}, bf16[304,256]{1,0:T(8,128)(2,1)S(1)}, u32[]{:S(2)}, u32[]{:S(2)}) collective-permute-start(bf16[304,256]{1,0:T(8,128)(2,1)S(1)} %get-tuple-element.158), channel_id=1, source_target_pairs={{0,1},{1,0},{2,3},{3,2},{4,5},{5,4},{6,7},{7,6},{8,9},{9,8},{10,11... | collective-permute-start | bytes 466952 | tf_op jit(solution)/shard_map/ppermute | solution.py:652
  67.0 3.2 %copy-start.4 = (bf16[1024,256]{1,0:T(8,128)(2,1)S(1)}, bf16[1024,256]{1,0:T(8,128)(2,1)}, u32[]{:S(2)}) copy-start(bf16[1024,256]{1,0:T(8,128)(2,1)} %refs_5_.5) | copy-start | bytes 1572868
  67.0 3.2 %copy-start.6 = (bf16[352,256]{1,0:T(8,128)(2,1)S(1)}, bf16[352,256]{1,0:T(8,128)(2,1)}, u32[]{:S(2)}) copy-start(bf16[352,256]{1,0:T(8,128)(2,1)} %get-tuple-element.116.refs_0_) | copy-start | bytes 540676
  75.5 6.4 %collective-permute-start.24 = (bf16[2,176,256]{2,1,0:T(8,128)(2,1)S(1)}, bf16[2,176,256]{2,1,0:T(8,128)(2,1)S(1)}, u32[]{:S(2)}, u32[]{:S(2)}) collective-permute-start(bf16[2,176,256]{2,1,0:T(8,128)(2,1)S(1)} %get-tuple-element.193), channel_id=1, source_target_pairs={{0,4},{4,0},{8,12},{12,8},{16,20},{20,16},{24,28},{28,24},{1,5},{5... | collective-permute-start | bytes 540680 | tf_op jit(solution)/shard_map/ppermute | solution.py:652
  76.6 5.4 %collective-permute-start.25 = (bf16[2,176,256]{2,1,0:T(8,128)(2,1)S(1)}, bf16[2,176,256]{2,1,0:T(8,128)(2,1)S(1)}, u32[]{:S(2)}, u32[]{:S(2)}) collective-permute-start(bf16[2,176,256]{2,1,0:T(8,128)(2,1)S(1)} %get-tuple-element.194), channel_id=1, source_target_pairs={{0,4},{4,0},{8,12},{12,8},{16,20},{20,16},{24,28},{28,24},{1,5},{5... | collective-permute-start | bytes 540680 | tf_op jit(solution)/shard_map/ppermute | solution.py:652
  76.7 2.1 %collective-permute-start.16 = (bf16[4,256,256]{2,1,0:T(8,128)(2,1)S(1)}, bf16[4,256,256]{2,1,0:T(8,128)(2,1)S(1)}, u32[]{:S(2)}, u32[]{:S(2)}) collective-permute-start(bf16[4,256,256]{2,1,0:T(8,128)(2,1)S(1)} %get-tuple-element.174), channel_id=1, source_target_pairs={{0,4},{4,0},{8,12},{12,8},{16,20},{20,16},{24,28},{28,24},{1,5},{5... | collective-permute-start | bytes 1572872 | tf_op jit(solution)/shard_map/ppermute | solution.py:652
  78.9 5.9 %collective-permute-start.20 = (bf16[256,256]{1,0:T(8,128)(2,1)S(1)}, bf16[256,256]{1,0:T(8,128)(2,1)S(1)}, u32[]{:S(2)}, u32[]{:S(2)}) collective-permute-start(bf16[256,256]{1,0:T(8,128)(2,1)S(1)} %get-tuple-element.181), channel_id=1, source_target_pairs={{0,1},{1,0},{2,3},{3,2},{4,5},{5,4},{6,7},{7,6},{8,9},{9,8},{10,11... | collective-permute-start | bytes 393224 | tf_op jit(solution)/shard_map/ppermute | solution.py:652
  80.7 7.4 %collective-permute-start.21 = (bf16[256,256]{1,0:T(8,128)(2,1)S(1)}, bf16[256,256]{1,0:T(8,128)(2,1)S(1)}, u32[]{:S(2)}, u32[]{:S(2)}) collective-permute-start(bf16[256,256]{1,0:T(8,128)(2,1)S(1)} %get-tuple-element.182), channel_id=1, source_target_pairs={{0,2},{1,3},{2,0},{3,1},{4,6},{5,7},{6,4},{7,5},{8,10},{9,11},{10,... | collective-permute-start | bytes 393224 | tf_op jit(solution)/shard_map/ppermute | solution.py:652
  80.7 17.0 %collective-permute-start.22 = (bf16[256,256]{1,0:T(8,128)(2,1)S(1)}, bf16[256,256]{1,0:T(8,128)(2,1)S(1)}, u32[]{:S(2)}, u32[]{:S(2)}) collective-permute-start(bf16[256,256]{1,0:T(8,128)(2,1)S(1)} %get-tuple-element.183), channel_id=1, source_target_pairs={{0,3},{1,2},{2,1},{3,0},{4,7},{5,6},{6,5},{7,4},{8,11},{9,10},{10,... | collective-permute-start | bytes 393224 | tf_op jit(solution)/shard_map/ppermute | solution.py:652
  82.0 18.3 %collective-permute-start.26 = (bf16[176,256]{1,0:T(8,128)(2,1)S(1)}, bf16[176,256]{1,0:T(8,128)(2,1)S(1)}, u32[]{:S(2)}, u32[]{:S(2)}) collective-permute-start(bf16[176,256]{1,0:T(8,128)(2,1)S(1)} %get-tuple-element.196), channel_id=1, source_target_pairs={{0,1},{1,0},{2,3},{3,2},{4,5},{5,4},{6,7},{7,6},{8,9},{9,8},{10,11... | collective-permute-start | bytes 270344 | tf_op jit(solution)/shard_map/ppermute | solution.py:652
  84.4 15.9 %collective-permute-start.27 = (bf16[176,256]{1,0:T(8,128)(2,1)S(1)}, bf16[176,256]{1,0:T(8,128)(2,1)S(1)}, u32[]{:S(2)}, u32[]{:S(2)}) collective-permute-start(bf16[176,256]{1,0:T(8,128)(2,1)S(1)} %get-tuple-element.197), channel_id=1, source_target_pairs={{0,2},{1,3},{2,0},{3,1},{4,6},{5,7},{6,4},{7,5},{8,10},{9,11},{10,... | collective-permute-start | bytes 270344 | tf_op jit(solution)/shard_map/ppermute | solution.py:652
  84.8 16.7 %collective-permute-start.28 = (bf16[176,256]{1,0:T(8,128)(2,1)S(1)}, bf16[176,256]{1,0:T(8,128)(2,1)S(1)}, u32[]{:S(2)}, u32[]{:S(2)}) collective-permute-start(bf16[176,256]{1,0:T(8,128)(2,1)S(1)} %get-tuple-element.198), channel_id=1, source_target_pairs={{0,3},{1,2},{2,1},{3,0},{4,7},{5,6},{6,5},{7,4},{8,11},{9,10},{10,... | collective-permute-start | bytes 270344 | tf_op jit(solution)/shard_map/ppermute | solution.py:652
  97.8 4.3 %collective-permute-start.23 = (bf16[272,256]{1,0:T(8,128)(2,1)S(1)}, bf16[272,256]{1,0:T(8,128)(2,1)S(1)}, u32[]{:S(2)}, u32[]{:S(2)}) collective-permute-start(bf16[272,256]{1,0:T(8,128)(2,1)S(1)} %get-tuple-element.191.low), channel_id=1, source_target_pairs={{0,8},{4,12},{8,0},{12,4},{16,24},{20,28},{24,16},{28,20},{1,9},{5... | collective-permute-start | bytes 417800 | tf_op jit(solution)/shard_map/ppermute | solution.py:652
  99.1 4.3 %collective-permute-start.29 = (bf16[288,256]{1,0:T(8,128)(2,1)S(1)}, bf16[288,256]{1,0:T(8,128)(2,1)S(1)}, u32[]{:S(2)}, u32[]{:S(2)}) collective-permute-start(bf16[288,256]{1,0:T(8,128)(2,1)S(1)} %get-tuple-element.200.high), channel_id=1, source_target_pairs={{0,16},{4,20},{8,24},{12,28},{16,0},{20,4},{24,8},{28,12},{1,17},{... | collective-permute-start | bytes 442376 | tf_op jit(solution)/shard_map/ppermute | solution.py:652
  103.4 8.5 %collective-permute-start.34 = (bf16[288,256]{1,0:T(8,128)(2,1)S(1)}, bf16[288,256]{1,0:T(8,128)(2,1)S(1)}, u32[]{:S(2)}, u32[]{:S(2)}) collective-permute-start(bf16[288,256]{1,0:T(8,128)(2,1)S(1)} %get-tuple-element.204.high), channel_id=1, source_target_pairs={{0,8},{4,12},{8,0},{12,4},{16,24},{20,28},{24,16},{28,20},{1,9},{5... | collective-permute-start | bytes 442376 | tf_op jit(solution)/shard_map/ppermute | solution.py:652
  103.6 8.4 %collective-permute-start.30 = (bf16[272,256]{1,0:T(8,128)(2,1)S(1)}, bf16[272,256]{1,0:T(8,128)(2,1)S(1)}, u32[]{:S(2)}, u32[]{:S(2)}) collective-permute-start(bf16[272,256]{1,0:T(8,128)(2,1)S(1)} %get-tuple-element.202.low), channel_id=1, source_target_pairs={{0,16},{4,20},{8,24},{12,28},{16,0},{20,4},{24,8},{28,12},{1,17},{... | collective-permute-start | bytes 417800 | tf_op jit(solution)/shard_map/ppermute | solution.py:652
  104.8 4.7 %collective-permute-start.33 = (bf16[176,256]{1,0:T(8,128)(2,1)S(1)}, bf16[176,256]{1,0:T(8,128)(2,1)S(1)}, u32[]{:S(2)}, u32[]{:S(2)}) collective-permute-start(bf16[176,256]{1,0:T(8,128)(2,1)S(1)} %four_sum.4.refs_0_), channel_id=1, source_target_pairs={{0,24},{4,28},{8,16},{12,20},{16,8},{20,12},{24,0},{28,4},{1,25},{... | collective-permute-start | bytes 270344 | tf_op jit(solution)/shard_map/ppermute | solution.py:652
  106.1 5.1 %collective-permute-start.32 = (bf16[176,256]{1,0:T(8,128)(2,1)S(1)}, bf16[176,256]{1,0:T(8,128)(2,1)S(1)}, u32[]{:S(2)}, u32[]{:S(2)}) collective-permute-start(bf16[176,256]{1,0:T(8,128)(2,1)S(1)} %four_sum.4.refs_0_), channel_id=1, source_target_pairs={{0,16},{4,20},{8,24},{12,28},{16,0},{20,4},{24,8},{28,12},{1,17},{... | collective-permute-start | bytes 270344 | tf_op jit(solution)/shard_map/ppermute | solution.py:652
  107.4 4.6 %collective-permute-start.31 = (bf16[176,256]{1,0:T(8,128)(2,1)S(1)}, bf16[176,256]{1,0:T(8,128)(2,1)S(1)}, u32[]{:S(2)}, u32[]{:S(2)}) collective-permute-start(bf16[176,256]{1,0:T(8,128)(2,1)S(1)} %four_sum.4.refs_0_), channel_id=1, source_target_pairs={{0,8},{4,12},{8,0},{12,4},{16,24},{20,28},{24,16},{28,20},{1,9},{5... | collective-permute-start | bytes 270344 | tf_op jit(solution)/shard_map/ppermute | solution.py:652
  112.0 5.6 %collective-permute-start.36 = (bf16[416,256]{1,0:T(8,128)(2,1)S(1)}, bf16[416,256]{1,0:T(8,128)(2,1)S(1)}, u32[]{:S(2)}, u32[]{:S(2)}) collective-permute-start(bf16[416,256]{1,0:T(8,128)(2,1)S(1)} %get-tuple-element.207.high), channel_id=1, source_target_pairs={{0,4},{4,0},{8,12},{12,8},{16,20},{20,16},{24,28},{28,24},{1,5},{5... | collective-permute-start | bytes 638984 | tf_op jit(solution)/shard_map/ppermute | solution.py:652
  116.0 1.6 %collective-permute-start.35 = (bf16[272,256]{1,0:T(8,128)(2,1)S(1)}, bf16[272,256]{1,0:T(8,128)(2,1)S(1)}, u32[]{:S(2)}, u32[]{:S(2)}) collective-permute-start(bf16[272,256]{1,0:T(8,128)(2,1)S(1)} %get-tuple-element.206.low), channel_id=1, source_target_pairs={{0,4},{4,0},{8,12},{12,8},{16,20},{20,16},{24,28},{28,24},{1,5},{5... | collective-permute-start | bytes 417800 | tf_op jit(solution)/shard_map/ppermute | solution.py:652
  116.2 1.4 %collective-permute-start.37 = (bf16[176,256]{1,0:T(8,128)(2,1)S(1)}, bf16[176,256]{1,0:T(8,128)(2,1)S(1)}, u32[]{:S(2)}, u32[]{:S(2)}) collective-permute-start(bf16[176,256]{1,0:T(8,128)(2,1)S(1)} %four_sum.5.late), channel_id=1, source_target_pairs={{0,4},{4,0},{8,12},{12,8},{16,20},{20,16},{24,28},{28,24},{1,5},{5... | collective-permute-start | bytes 270344 | tf_op jit(solution)/shard_map/ppermute | solution.py:652

commit v3 on v2

--- a/solution.py
+++ b/solution.py
@@ -16,7 +16,6 @@
 
 VMEM_LIMIT = 32 * 2**20
 SMALL_LIMIT = 12 * 2**20
-CUT = 96
 UNROLL = {"attn_fwd": 4, "mlp_fwd": 4, "mlp_both": 4, "mlp_bwd": 4, "attn_bwd": 2, "attn_pre": 2, "attn_post": 2}
 KERNEL_FLOPS = 1000
 LONG = 50 * 10**9
@@ -479,12 +478,18 @@
             lambda i, j: (s[i:j].astype(F32) + a[i:j].astype(F32)) + (b[i:j].astype(F32) + c[i:j].astype(F32)))
 
 
-def early_sum_kernel(one, s, a, b, c, low, high):
-    total = (s[...].astype(F32) + a[...].astype(F32)) + (b[...].astype(F32) + c[...].astype(F32))
-    low[0:176, :] = one[128:304, :]
-    low[176:176 + CUT, :] = total[0:CUT].astype(BF)
-    high[0:256 - CUT, :] = total[CUT:256].astype(BF)
-    high[256 - CUT:384 - CUT, :] = one[0:128, :]
+def four_split_kernel(*refs):
+    done, (s, a, b, c, mlp, attn) = refs[:-6], refs[-6:]
+
+    def total(i, j):
+        return (s[i:j].astype(F32) + a[i:j].astype(F32)) + (b[i:j].astype(F32) + c[i:j].astype(F32))
+
+    at = 0
+    for ref in done:
+        mlp[at:at + 128, :] = ref[...]
+        at += 128
+    mlp[at:at + 128, :] = total(0, 128).astype(BF)
+    put_sum(attn, 0, 160, 176, lambda i, j: total(i + 128, j + 128))
 
 
 def pair_sum_kernel(low, low_got, high, high_got, low_out, high_out):
@@ -494,15 +499,12 @@
 
 def last_pair_kernel(low, low_got, high, high_got, low_out, high_out):
     put_sum(low_out, 0, 160, low.shape[0], lambda i, j: low[i:j].astype(F32) + low_got[i:j].astype(F32))
-    rows = 256 - CUT
-    high_out[0:rows, :] = (high[0:rows].astype(F32) + high_got[0:rows].astype(F32)).astype(BF)
-    high_out[rows:rows + 128, :] = high[rows:rows + 128]
-    high_out[rows + 128:rows + 256, :] = high_got[rows:rows + 128]
+    high_out[0:256, :] = high[...]
+    high_out[256:512, :] = high_got[...]
 
 
 def finish_kernel(low, low_other, high, high_other, late, late_other,
                   d_qkv, d_out, d_up, d_down, d_cross, gain_attn, gain_mlp, bias):
-    rows = 256 - CUT
     mine = pl.multiple_of(quarter_index() * 128, 16)
     other = pl.multiple_of((1 - quarter_index()) * 128, 16)
 
@@ -514,11 +516,10 @@
             d_qkv[l, 2, 32:64] = b[0:32].astype(F32)
             d_cross[l] = b[32:96].astype(F32)
             d_out[l] = b[96:160].astype(F32)
-        for dst, (lo, hi, _) in ((d_up, first), (d_down, second)):
-            dst[0, 0:CUT] = lo[176:176 + CUT].astype(F32)
-            dst[0, CUT:256] = hi[0:rows].astype(F32)
-            dst[1, pl.ds(mine, 128)] = hi[rows:rows + 128].astype(F32)
-            dst[1, pl.ds(other, 128)] = hi[rows + 128:rows + 256].astype(F32)
+        for dst, ref in ((d_up, first[1]), (d_down, second[1])):
+            for l, at in ((1, 0), (0, 128)):
+                dst[l, pl.ds(mine, 128)] = ref[at:at + 128].astype(F32)
+                dst[l, pl.ds(other, 128)] = ref[at + 256:at + 384].astype(F32)
 
     @pl.when(half_index() == 0)
     def _():
@@ -668,28 +669,28 @@
     def scatter(sums):
         return [sums[0]] + [swap(sums[m], "head", head_size, m) for m in range(1, head_size)]
 
+    def split(keep, got):
+        return small_call(core_split_kernel, [((4, 128, 256), BF)] * 2, "core_split")(keep, got)
+
+    def four_split(terms, done=(), flops=1000):
+        return small_call(four_split_kernel, [((128 * (len(done) + 1), 256), BF), ((176, 256), BF)], "four_split", flops)(*done, *terms)
+
     bits = [1 << i for i in range(1, dp_size.bit_length() - 1)]
 
-    def late_steps():
-        return [(bits[i], bits[i + 1], bits[i] + bits[i + 1]) if i + 1 < len(bits) else (bits[i],) for i in range(0, len(bits), 2)]
-
-    def sum_early_late(low, high, late):
+    def sum_direct(x):
+        for i in range(0, len(bits), 2):
+            masks = (bits[i], bits[i + 1], bits[i] + bits[i + 1]) if i + 1 < len(bits) else (bits[i],)
+            terms = [x] + [swap(x, "dp", dp_size, mask) for mask in masks]
+            x = four_sum(160, terms + [jnp.zeros_like(x)] * (4 - len(terms)))
+        return x
+
+    def sum_pairs(low, high):
         pairs = list(zip(bits, bits[1:] + bits[:1]))
-
-        def pair(low, high, masks, before, last):
-            got = [tie(swap(x, "dp", dp_size, mask), *before) for x, mask in zip((low, high), masks)]
-            kernel, more = (last_pair_kernel, 128) if last else (pair_sum_kernel, 0)
-            return small_call(kernel, [(low.shape, BF), ((high.shape[0] + more, 256), BF)], "pair_sum")(low, got[0], high, got[1])
-
-        late = four_sum(160, late, LONG)
-        low, high = pair(low, high, pairs[0], [late], len(pairs) == 1)
-        for masks in late_steps():
-            terms = [late] + [swap(late, "dp", dp_size, mask) for mask in masks]
-            before = terms[1:]
-            late = four_sum(160, terms + [jnp.zeros_like(late)] * (4 - len(terms)))
-        for i, masks in enumerate(pairs[1:]):
-            low, high = pair(low, high, masks, before, i == len(pairs) - 2)
-        return low, high, late
+        for i, (one, two) in enumerate(pairs):
+            kernel, more = (last_pair_kernel, 256) if i == len(pairs) - 1 else (pair_sum_kernel, 0)
+            low, high = small_call(kernel, [(low.shape, BF), ((high.shape[0] + more, 256), BF)], "pair_sum")(
+                low, swap(low, "dp", dp_size, one), high, swap(high, "dp", dp_size, two))
+        return low, high
 
     def body(tokens, lengths, cotangent, gain_attn, gain_mlp, w_qkv, w_out, w_up, w_down, w_cross, b_cross):
         rows = tokens.shape[0]
@@ -716,32 +717,30 @@
         mid1, base1, *saved1 = attn_fwd(1, cur1, mask, gain_attn, a1)
         output, gm1, keep_m1, send_m1, small_m1 = mlp_both(1, mid1, base1, cotangent, gain_mlp, m1)
         pre = attn_pre(1, cotangent, gm1, cur1, saved1, a1)
-        pre_done = pre[0]
-        keep_m1, send_m1 = small_call(core_split_kernel, [((4, 128, 256), BF)] * 2, "core_split")(
-            keep_m1, tie(core_swap(send_m1), pre_done))
+        keep_m1, send_m1 = split(keep_m1, tie(core_swap(send_m1), pre[0]))
         got_m1 = swap(send_m1, "dp", dp_size, 2)
         grad1, keep_a1, send_a1 = attn_bwd(1, cur1, tie(mask, send_m1), saved1, gain_attn, pre, small_m1, a1)
-        m1_sum = small_call(add_kernel, [((4, 128, 256), BF)], "add", LONG)(keep_m1, tie(got_m1, grad1))[0]
+        gm0, keep_m0, send_m0, small_m0 = mlp_bwd(0, grad1, mid0, hid0, slope0, gain_mlp, m0)
+        m1_sum = small_call(add_kernel, [((4, 128, 256), BF)], "add", LONG)(keep_m1, tie(got_m1, gm0))[0]
         sums = core_sum((None, 160), (m1_sum,), (keep_a1, tie(core_swap(send_a1), m1_sum)))
         got = scatter(sums)
-        gm0, keep_m0, send_m0, small_m0 = mlp_bwd(0, tie(grad1, *sums), mid0, hid0, slope0, gain_mlp, m0)
         pre = attn_pre(0, grad1, gm0, tokens, saved0, a0)
-        gqkv, keep_a0, *send_a0 = attn_grads(0, mask, saved0, gain_attn, pre, small_m0, a0)
-        one = four_sum(288, [tie(x, gqkv) for x in got], LONG)
-        sums = core_sum((256,), (keep_m0, tie(core_swap(send_m0), one)))
+        keep_m0, send_m0 = split(keep_m0, tie(core_swap(send_m0), pre[0]))
+        got_m0 = swap(send_m0, "dp", dp_size, 2)
+        gqkv, keep_a0, *send_a0 = attn_grads(0, tie(mask, send_m0), saved0, gain_attn, pre, small_m0, a0)
+        mlp1, attn1 = four_split([tie(x, gqkv) for x in got], (), LONG)
+        sums = core_sum((128, 160), (keep_m0, tie(got_m0, mlp1)), (keep_a0, *[core_swap(x) for x in send_a0]))
         got = scatter(sums)
         grad0 = attn_post(0, tie(gqkv, *sums), gain_attn, tokens, pre, a0)
-        low, high = small_call(early_sum_kernel, [((176 + CUT, 256), BF), ((384 - CUT, 256), BF)], "early_sum")(
-            one, *[tie(x, grad0) for x in got])
-        sums_a0 = core_sum((160,), (keep_a0, *[core_swap(x) for x in send_a0]))
-        late = scatter(sums_a0)
-        low, high, late = sum_early_late(low, high, late)
+        attn1 = sum_direct(attn1)
+        mlp, attn0 = four_split([tie(x, grad0, attn1) for x in got], (mlp1,))
+        attn0, mlp = sum_pairs(attn0, mlp)
         d_qkv, d_out, d_up, d_down, d_cross, d_ga, d_gm, d_bias = small_call(
             finish_kernel,
             [((LAYERS, 3, HD, 256), F32), ((LAYERS, HD, 256), F32), ((LAYERS, 256, 256), F32), ((LAYERS, 256, 256), F32),
              ((LAYERS, HD, 256), F32), ((LAYERS, 256), F32), ((LAYERS, 256), F32), ((LAYERS, HD), F32)],
             "finish",
-        )(low, core_swap(low), high, core_swap(high), late, core_swap(late))
+        )(attn1, core_swap(attn1), mlp, core_swap(mlp), attn0, core_swap(attn0))
         return (output, grad0, d_ga, d_gm, d_qkv.transpose(0, 3, 1, 2), d_out, d_up, d_down,
                 d_cross.transpose(0, 2, 1), d_bias)
 

time: 119 us -> 115 us (0.966)
  starting transfers between devices: 39.5 us -> 35.2 us
    ppermute x38 -> x36, starting transfers between devices: 39.5 us -> 35.2 us  [swap(): return lax.ppermute(x, axis, [(i, i ^ mask) for i in range(size)])]
    ppermute x38 -> x36, waiting for transfers between devices: 36.7 us -> 36.1 us  [swap(): return lax.ppermute(x, axis, [(i, i ^ mask) for i in range(size)])]
  transfers between devices with their start and end apart: 38 -> 36, of which waited for: 20 -> 17; matrix products, arithmetic and copies ran while one was open for 0% -> 0% of each run, Pallas kernels for 21% -> 22%
where the time goes in v3:
time: 115 us; the launch traced here: 114 us
  Pallas kernels  38.5 us (33%)
  waiting for transfers between devices  36.1 us (31%)
  starting transfers between devices  35.2 us (31%)
  local copies, waits for them, and re-layouts  3.45 us (3%)
    ppermute x36, waiting for transfers between devices, swap(): return lax.ppermute(x, axis, [(i, i ^ mask) for i in range(size)])  36.1 us
    ppermute x36, starting transfers between devices, swap(): return lax.ppermute(x, axis, [(i, i ^ mask) for i in range(size)])  35.2 us
    pallas_call x10, Pallas kernels, call(): pl.pallas_call(kernel, in_specs=[VMEM] * len(args), out_specs=[VMEM] * le...  33.6 us
    unnamed x26, local copies, waits for them, and re-layouts  3.45 us
    pallas_call x1, Pallas kernels, body(): pl.pallas_call(pack_kernel, in_specs=[SMEM] + [ANY] * 5 + [VMEM], out_spe...  2.66 us
  transfers between devices with their start and end apart: 36, of which 17 were waited for; matrix products, arithmetic and copies ran while one was open for 0% of the time, Pallas kernels for 22%

profile of v3, /device:TPU:9, one launch (start us, length us, event | category | flops | bytes accessed | tf_op | source)
XLA Modules:
  0.0 114.1 jit_solution(11352073292838180760)
XLA Ops:
  0.6 2.7 %pack.1 = (bf16[352,256]{1,0:T(8,128)(2,1)}, bf16[352,256]{1,0:T(8,128)(2,1)}, bf16[304,256]{1,0:T(8,128)(2,1)}, bf16[432,256]{1,0:T(8,128)(2,1)}, bf16[64,256]{1,0:T(8,128)(2,1)}) custom-call(s32[16]{0:T(128)} %lens.1, bf16[2,3,64,256]{3,2,1,0:T(8,128)(2,1)} %bitcast.4, bf16[2,64,256]{2,1,0:T(8,128)(2,1)} %bitcast.5, bf16[2,64,256]{2,1,0:T(8,128)(2,1)} %out.1, ...), custom_call_target="tpu_custom_call" | custom-call | tf_op jit(solution)/shard_map/pack/pallas_call | solution.py:697
  3.3 1.4 %collective-permute-start.3 = (bf16[304,256]{1,0:T(8,128)(2,1)}, bf16[304,256]{1,0:T(8,128)(2,1)S(1)}, u32[]{:S(2)}, u32[]{:S(2)}) collective-permute-start(bf16[304,256]{1,0:T(8,128)(2,1)} %get-tuple-element.111), channel_id=1, source_target_pairs={{0,3},{1,2},{2,1},{3,0},{4,7},{5,6},{6,5},{7,4},{8,11},{9,10},{10,... | collective-permute-start | bytes 466952 | tf_op jit(solution)/shard_map/ppermute | solution.py:653
  4.7 1.1 collective-permute-start.2
  5.8 1.1 collective-permute-start.1
  6.9 8.5 %collective-permute-done.3.c = bf16[304,256]{1,0:T(8,128)(2,1)S(1)} collective-permute-done((bf16[304,256]{1,0:T(8,128)(2,1)}, bf16[304,256]{1,0:T(8,128)(2,1)S(1)}, u32[]{:S(2)}, u32[]{:S(2)}) %collective-permute-start.3) | collective-permute-done | bytes 155680 | tf_op jit(solution)/shard_map/ppermute | solution.py:653
  15.3 2.4 %collective-permute-done.2.b = bf16[304,256]{1,0:T(8,128)(2,1)S(1)} collective-permute-done((bf16[304,256]{1,0:T(8,128)(2,1)}, bf16[304,256]{1,0:T(8,128)(2,1)S(1)}, u32[]{:S(2)}, u32[]{:S(2)}) %collective-permute-start.2) | collective-permute-done | bytes 155680 | tf_op jit(solution)/shard_map/ppermute | solution.py:653
  17.7 1.6 %collective-permute-start.5 = (bf16[528,256]{1,0:T(8,128)(2,1)S(1)}, bf16[528,256]{1,0:T(8,128)(2,1)S(1)}, u32[]{:S(2)}, u32[]{:S(2)}) collective-permute-start(bf16[528,256]{1,0:T(8,128)(2,1)S(1)} %get-tuple-element.114.refs_1_), channel_id=1, source_target_pairs={{0,4},{4,0},{8,12},{12,8},{16,20},{20,16},{24,28},{28,24},{1,5},{5... | collective-permute-start | bytes 811016 | tf_op jit(solution)/shard_map/ppermute | solution.py:653
  19.3 0.2 collective-permute-start.9
  19.5 3.9 %collective-permute-start.8 = (bf16[432,256]{1,0:T(8,128)(2,1)}, bf16[432,256]{1,0:T(8,128)(2,1)S(1)}, u32[]{:S(2)}, u32[]{:S(2)}) collective-permute-start(bf16[432,256]{1,0:T(8,128)(2,1)} %get-tuple-element.110), channel_id=1, source_target_pairs={{0,2},{1,3},{2,0},{3,1},{4,6},{5,7},{6,4},{7,5},{8,10},{9,11},{10,... | collective-permute-start | bytes 663560 | tf_op jit(solution)/shard_map/ppermute | solution.py:653
  23.5 0.6 collective-permute-start.6
  24.2 1.2 %collective-permute-start.4 = (bf16[384,256]{1,0:T(8,128)(2,1)S(1)}, bf16[384,256]{1,0:T(8,128)(2,1)S(1)}, u32[]{:S(2)}, u32[]{:S(2)}) collective-permute-start(bf16[384,256]{1,0:T(8,128)(2,1)S(1)} %get-tuple-element.112.refs_2_), channel_id=1, source_target_pairs={{0,8},{4,12},{8,0},{12,4},{16,24},{20,28},{24,16},{28,20},{1,9},{5... | collective-permute-start | bytes 589832 | tf_op jit(solution)/shard_map/ppermute | solution.py:653
  25.4 1.0 copy-done.3
  26.4 0.9 copy-done.5
  27.3 0.8 copy-done.8
  28.1 0.7 copy-done.10
  28.8 4.0 %attn_fwd.2 = (f32[1024,256]{1,0:T(8,128)S(1)}, f32[1024,256]{1,0:T(8,128)S(1)}, bf16[1024,256]{1,0:T(8,128)(2,1)S(1)}, bf16[768,1024]{1,0:T(8,128)(2,1)S(1)}, b...) custom-call(bf16[352,256]{1,0:T(8,128)(2,1)S(1)} %copy-done.5, bf16[528,256]{1,0:T(8,128)(2,1)S(1)} %get-tuple-element.114.refs_1_, ...), custom_call_target="tpu_custom_call" | custom-call | flops 49999998976 | bytes 1024 | tf_op jit(solution)/shard_map/attn_fwd/pallas_call | solution.py:547
  32.8 0.3 collective-permute-start.7
  33.2 1.2 %collective-permute-done.7.refs_5_ = bf16[384,256]{1,0:T(8,128)(2,1)S(1)} collective-permute-done((bf16[384,256]{1,0:T(8,128)(2,1)S(1)}, bf16[384,256]{1,0:T(8,128)(2,1)S(1)}, u32[]{:S(2)}, u32[]{:S(2)}) %collective-permute-start.7) | collective-permute-done | bytes 196640 | tf_op jit(solution)/shard_map/ppermute | solution.py:653
  34.4 2.5 %mlp_fwd.1 = (f32[1024,256]{1,0:T(8,128)S(1)}, bf16[1024,1024]{1,0:T(8,128)(2,1)S(1)}, bf16[1024,1024]{1,0:T(8,128)(2,1)S(1)}) custom-call(bf16[2,256,256]{2,1,0:T(8,128)(2,1)S(1)} %copy-done, bf16[2,256,256]{2,1,0:T(8,128)(2,1)S(1)} %copy-done.1, bf16[384,256]{1,0:T(8,128)(2,1)S(1)} %get-tuple-element.112.refs_2_, ...), custom_call_target="tpu_custom_call" | custom-call | flops 1000 | bytes 1024 | tf_op jit(solution)/shard_map/mlp_fwd/pallas_call | solution.py:547
  37.0 1.9 %collective-permute-done.8.refs_2_.refs_3_ = bf16[432,256]{1,0:T(8,128)(2,1)S(1)} collective-permute-done((bf16[432,256]{1,0:T(8,128)(2,1)}, bf16[432,256]{1,0:T(8,128)(2,1)S(1)}, u32[]{:S(2)}, u32[]{:S(2)}) %collective-permute-start.8) | collective-permute-done | bytes 221216 | tf_op jit(solution)/shard_map/ppermute | solution.py:653
  38.9 0.8 collective-permute-start.10
  39.7 0.5 collective-permute-start.12
  40.2 0.6 collective-permute-done.10.refs_4_.refs_5_
  40.8 0.4 collective-permute-done.11.refs_5_.refs_6_
  41.2 0.3 collective-permute-done.12.refs_6_.refs_7_
  41.5 4.0 %attn_fwd.3 = (f32[1024,256]{1,0:T(8,128)S(1)}, f32[1024,256]{1,0:T(8,128)S(1)}, bf16[1024,256]{1,0:T(8,128)(2,1)S(1)}, bf16[768,1024]{1,0:T(8,128)(2,1)S(1)}, b...) custom-call(bf16[352,256]{1,0:T(8,128)(2,1)S(1)} %copy-done.7, ...), custom_call_target="tpu_custom_call" | custom-call | flops 1000 | bytes 1024 | tf_op jit(solution)/shard_map/attn_fwd/pallas_call | solution.py:547
  45.6 5.6 %mlp_both.1 = (f32[1024,256]{1,0:T(8,128)}, f32[1024,256]{1,0:T(8,128)S(1)}, bf16[4,256,256]{2,1,0:T(8,128)(2,1)S(1)}, bf16[4,256,256]{2,1,0:T(8,128)(2,1)S(1)}, f32[8,256]{1,0:T(8,128)S(1)}) custom-call(bf16[2,256,256]{2,1,0:T(8,128)(2,1)S(1)} %copy-done, bf16[2,256,256]{2,1,0:T(8,128)(2,1)S(1)} %copy-done.1, ...), custom_call_target="tpu_custom_call" | custom-call | flops 1000 | bytes 1024 | tf_op jit(solution)/shard_map/mlp_both/pallas_call | solution.py:547
  51.1 0.3 collective-permute-start.13
  51.5 1.4 %attn_pre.2 = (bf16[256,1024]{1,0:T(8,128)(2,1)S(1)}, bf16[256,256]{1,0:T(8,128)(2,1)S(1)}, bf16[256,256]{1,0:T(8,128)(2,1)S(1)}, f32[1024,256]{1,0:T(8,128)S(1)...) custom-call(bf16[352,256]{1,0:T(8,128)(2,1)S(1)} %copy-done.7, ...), custom_call_target="tpu_custom_call" | custom-call | flops 1000 | bytes 1024 | tf_op jit(solution)/shard_map/attn_pre/pallas_call | solution.py:547
  52.8 0.2 collective-permute-done.13.got
  53.0 0.1 core_split.2
  53.2 1.3 %collective-permute-start.16 = (bf16[4,128,256]{2,1,0:T(8,128)(2,1)S(1)}, bf16[4,128,256]{2,1,0:T(8,128)(2,1)S(1)}, u32[]{:S(2)}, u32[]{:S(2)}) collective-permute-start(bf16[4,128,256]{2,1,0:T(8,128)(2,1)S(1)} %get-tuple-element.134), channel_id=1, source_target_pairs={{0,8},{4,12},{8,0},{12,4},{16,24},{20,28},{24,16},{28,20},{1,9},{5... | collective-permute-start | bytes 786440 | tf_op jit(solution)/shard_map/ppermute | solution.py:653
  54.5 5.2 %attn_bwd.1 = (f32[1024,256]{1,0:T(8,128)S(1)}, bf16[4,176,256]{2,1,0:T(8,128)(2,1)S(1)}, bf16[4,176,256]{2,1,0:T(8,128)(2,1)S(1)}) custom-call(bf16[352,256]{1,0:T(8,128)(2,1)S(1)} %copy-done.7, bf16[432,256]{1,0:T(8,128)(2,1)S(1)} %collective-permute-done.refs_1_.refs_2_, bf16[432,256]{1,0:T(8,128)(2,1)S(1)} %collective-permute-done.8.refs_2_.refs_3_, ...), custom_call_target="tpu_custom_call" | custom-call | flops 1000 | bytes 1024 | tf_op jit(solution)/shard_map/attn_bwd/pallas_call | solution.py:547
  59.7 0.7 collective-permute-start.17
  60.3 3.2 %mlp_bwd.1 = (f32[1024,256]{1,0:T(8,128)S(1)}, bf16[4,256,256]{2,1,0:T(8,128)(2,1)S(1)}, bf16[4,256,256]{2,1,0:T(8,128)(2,1)S(1)}, f32[8,256]{1,0:T(8,128)S(1)}) custom-call(bf16[2,256,256]{2,1,0:T(8,128)(2,1)S(1)} %copy-done, bf16[2,256,256]{2,1,0:T(8,128)(2,1)S(1)} %copy-done.1, bf16[384,256]{1,0:T(8,128)(2,1)S(1)} %get-tuple-element.112.refs_2_, ...), custom_call_target="tpu_custom_call" | custom-call | flops 1000 | bytes 1024 | tf_op jit(solution)/shard_map/mlp_bwd/pallas_call | solution.py:547
  63.8 1.4 %collective-permute-start.20 = (bf16[304,256]{1,0:T(8,128)(2,1)S(1)}, bf16[304,256]{1,0:T(8,128)(2,1)S(1)}, u32[]{:S(2)}, u32[]{:S(2)}) collective-permute-start(bf16[304,256]{1,0:T(8,128)(2,1)S(1)} %get-tuple-element.177), channel_id=1, source_target_pairs={{0,3},{1,2},{2,1},{3,0},{4,7},{5,6},{6,5},{7,4},{8,11},{9,10},{10,... | collective-permute-start | bytes 466952 | tf_op jit(solution)/shard_map/ppermute | solution.py:653
  65.2 3.9 %collective-permute-start.19 = (bf16[304,256]{1,0:T(8,128)(2,1)S(1)}, bf16[304,256]{1,0:T(8,128)(2,1)S(1)}, u32[]{:S(2)}, u32[]{:S(2)}) collective-permute-start(bf16[304,256]{1,0:T(8,128)(2,1)S(1)} %get-tuple-element.175), channel_id=1, source_target_pairs={{0,2},{1,3},{2,0},{3,1},{4,6},{5,7},{6,4},{7,5},{8,10},{9,11},{10,... | collective-permute-start | bytes 466952 | tf_op jit(solution)/shard_map/ppermute | solution.py:653
  69.1 1.4 %attn_pre.3 = (bf16[256,1024]{1,0:T(8,128)(2,1)S(1)}, bf16[256,256]{1,0:T(8,128)(2,1)S(1)}, bf16[256,256]{1,0:T(8,128)(2,1)S(1)}, f32[1024,256]{1,0:T(8,128)S(1)...) custom-call(bf16[352,256]{1,0:T(8,128)(2,1)S(1)} %copy-done.6, ...), custom_call_target="tpu_custom_call" | custom-call | flops 1000 | bytes 1024 | tf_op jit(solution)/shard_map/attn_pre/pallas_call | solution.py:547
  70.5 0.1 core_split.3
  70.6 0.3 collective-permute-start.15
  70.9 3.9 %attn_grads.1 = (bf16[768,1024]{1,0:T(8,128)(2,1)S(1)}, bf16[4,176,256]{2,1,0:T(8,128)(2,1)S(1)}, bf16[2,176,256]{2,1,0:T(8,128)(2,1)S(1)}, bf16[2,176,256]{2,1,0:T(8,128)(2,1)S(1)}) custom-call(bf16[352,256]{1,0:T(8,128)(2,1)S(1)} %copy-done.6, bf16[528,256]{1,0:T(8,128)(2,1)S(1)} %get-tuple-element.114.refs_1_, ...), custom_call_target="tpu_custom_call" | custom-call | flops 1000 | bytes 1024 | tf_op jit(solution)/shard_map/attn_grads/pallas_call | solution.py:547
  74.9 3.5 %collective-permute-done.19.refs_2_ = bf16[304,256]{1,0:T(8,128)(2,1)S(1)} collective-permute-done((bf16[304,256]{1,0:T(8,128)(2,1)S(1)}, bf16[304,256]{1,0:T(8,128)(2,1)S(1)}, u32[]{:S(2)}, u32[]{:S(2)}) %collective-permute-start.19) | collective-permute-done | bytes 155680 | tf_op jit(solution)/shard_map/ppermute | solution.py:653
  78.5 1.3 %collective-permute-start.21 = (bf16[2,176,256]{2,1,0:T(8,128)(2,1)S(1)}, bf16[2,176,256]{2,1,0:T(8,128)(2,1)S(1)}, u32[]{:S(2)}, u32[]{:S(2)}) collective-permute-start(bf16[2,176,256]{2,1,0:T(8,128)(2,1)S(1)} %get-tuple-element.182), channel_id=1, source_target_pairs={{0,4},{4,0},{8,12},{12,8},{16,20},{20,16},{24,28},{28,24},{1,5},{5... | collective-permute-start | bytes 540680 | tf_op jit(solution)/shard_map/ppermute | solution.py:653
  79.9 1.3 %collective-permute-start.25 = (bf16[176,256]{1,0:T(8,128)(2,1)S(1)}, bf16[176,256]{1,0:T(8,128)(2,1)S(1)}, u32[]{:S(2)}, u32[]{:S(2)}) collective-permute-start(bf16[176,256]{1,0:T(8,128)(2,1)S(1)} %get-tuple-element.191.refs_0_), channel_id=1, source_target_pairs={{0,24},{4,28},{8,16},{12,20},{16,8},{20,12},{24,0},{28,4},{1,25},{... | collective-permute-start | bytes 270344 | tf_op jit(solution)/shard_map/ppermute | solution.py:653
  81.2 0.2 core_sum.3
  81.3 2.2 %collective-permute-start.27 = (bf16[304,256]{1,0:T(8,128)(2,1)S(1)}, bf16[304,256]{1,0:T(8,128)(2,1)S(1)}, u32[]{:S(2)}, u32[]{:S(2)}) collective-permute-start(bf16[304,256]{1,0:T(8,128)(2,1)S(1)} %get-tuple-element.185), channel_id=1, source_target_pairs={{0,1},{1,0},{2,3},{3,2},{4,5},{5,4},{6,7},{7,6},{8,9},{9,8},{10,11... | collective-permute-start | bytes 466952 | tf_op jit(solution)/shard_map/ppermute | solution.py:653
  83.6 0.7 collective-permute-start.28
  84.2 0.6 collective-permute-start.29
  84.8 1.2 %collective-permute-start.24 = (bf16[176,256]{1,0:T(8,128)(2,1)S(1)}, bf16[176,256]{1,0:T(8,128)(2,1)S(1)}, u32[]{:S(2)}, u32[]{:S(2)}) collective-permute-start(bf16[176,256]{1,0:T(8,128)(2,1)S(1)} %get-tuple-element.191.refs_0_), channel_id=1, source_target_pairs={{0,16},{4,20},{8,24},{12,28},{16,0},{20,4},{24,8},{28,12},{1,17},{... | collective-permute-start | bytes 270344 | tf_op jit(solution)/shard_map/ppermute | solution.py:653
  86.1 0.3 collective-permute-start.23
  86.3 2.2 %collective-permute-done.24.refs_2_ = bf16[176,256]{1,0:T(8,128)(2,1)S(1)} collective-permute-done((bf16[176,256]{1,0:T(8,128)(2,1)S(1)}, bf16[176,256]{1,0:T(8,128)(2,1)S(1)}, u32[]{:S(2)}, u32[]{:S(2)}) %collective-permute-start.24) | collective-permute-done | bytes 90144 | tf_op jit(solution)/shard_map/ppermute | solution.py:653
  88.5 1.2 %collective-permute-done.23.refs_1_ = bf16[176,256]{1,0:T(8,128)(2,1)S(1)} collective-permute-done((bf16[176,256]{1,0:T(8,128)(2,1)S(1)}, bf16[176,256]{1,0:T(8,128)(2,1)S(1)}, u32[]{:S(2)}, u32[]{:S(2)}) %collective-permute-start.23) | collective-permute-done | bytes 90144 | tf_op jit(solution)/shard_map/ppermute | solution.py:653
  89.8 2.4 %attn_post.1 = f32[1024,256]{1,0:T(8,128)} custom-call(bf16[352,256]{1,0:T(8,128)(2,1)S(1)} %copy-done.6, bf16[528,256]{1,0:T(8,128)(2,1)S(1)} %get-tuple-element.114.refs_1_, bf16[528,256]{1,0:T(8,128)(2,1)S(1)} %collective-permute-done.5.refs_2_, bf16[768,1024]{1,0:T(8,128)(2,1)S(1)} %get-tuple-element.188.refs_3_, f32[2,256]{1,0:T(2,128)S(1)} %copy-done.11, ...), custom_call_target="tpu_custom_call" | custom-call | flops 1000 | bytes 1024 | tf_op jit(solution)/shard_map/attn_post/pallas_call | solution.py:547
  92.2 6.1 %collective-permute-done.29.refs_4_ = bf16[304,256]{1,0:T(8,128)(2,1)S(1)} collective-permute-done((bf16[304,256]{1,0:T(8,128)(2,1)S(1)}, bf16[304,256]{1,0:T(8,128)(2,1)S(1)}, u32[]{:S(2)}, u32[]{:S(2)}) %collective-permute-start.29) | collective-permute-done | bytes 155680 | tf_op jit(solution)/shard_map/ppermute | solution.py:653
  98.4 1.8 %collective-permute-start.31 = (bf16[256,256]{1,0:T(8,128)(2,1)S(1)}, bf16[256,256]{1,0:T(8,128)(2,1)S(1)}, u32[]{:S(2)}, u32[]{:S(2)}) collective-permute-start(bf16[256,256]{1,0:T(8,128)(2,1)S(1)} %get-tuple-element.197.high), channel_id=1, source_target_pairs={{0,16},{4,20},{8,24},{12,28},{16,0},{20,4},{24,8},{28,12},{1,17},{... | collective-permute-start | bytes 393224 | tf_op jit(solution)/shard_map/ppermute | solution.py:653
  100.2 3.7 %collective-permute-done.30.low_got = bf16[176,256]{1,0:T(8,128)(2,1)S(1)} collective-permute-done((bf16[176,256]{1,0:T(8,128)(2,1)S(1)}, bf16[176,256]{1,0:T(8,128)(2,1)S(1)}, u32[]{:S(2)}, u32[]{:S(2)}) %collective-permute-start.30) | collective-permute-done | bytes 90144 | tf_op jit(solution)/shard_map/ppermute | solution.py:653
  104.0 0.9 collective-permute-start.32
  104.8 2.6 %collective-permute-done.32.low_got = bf16[176,256]{1,0:T(8,128)(2,1)S(1)} collective-permute-done((bf16[176,256]{1,0:T(8,128)(2,1)S(1)}, bf16[176,256]{1,0:T(8,128)(2,1)S(1)}, u32[]{:S(2)}, u32[]{:S(2)}) %collective-permute-start.32) | collective-permute-done | bytes 90144 | tf_op jit(solution)/shard_map/ppermute | solution.py:653
  107.4 0.4 collective-permute-done.33.high_got
  107.8 3.5 %collective-permute-start.34 = (bf16[512,256]{1,0:T(8,128)(2,1)S(1)}, bf16[512,256]{1,0:T(8,128)(2,1)S(1)}, u32[]{:S(2)}, u32[]{:S(2)}) collective-permute-start(bf16[512,256]{1,0:T(8,128)(2,1)S(1)} %get-tuple-element.200.high), channel_id=1, source_target_pairs={{0,4},{4,0},{8,12},{12,8},{16,20},{20,16},{24,28},{28,24},{1,5},{5... | collective-permute-start | bytes 786440 | tf_op jit(solution)/shard_map/ppermute | solution.py:653
  111.4 0.4 collective-permute-start.35
  111.9 0.8 collective-permute-done.26.low_other
  112.7 0.2 collective-permute-done.35.late_other
  112.8 1.3 %finish.1 = (f32[2,3,64,256]{3,2,1,0:T(8,128)}, f32[2,64,256]{2,1,0:T(8,128)}, f32[2,256,256]{2,1,0:T(8,128)}, f32[2,256,256]{2,1,0:T(8,128)}, f32[2,64,256]{2,1...) custom-call(bf16[176,256]{1,0:T(8,128)(2,1)S(1)} %four_sum.1.low, ...), custom_call_target="tpu_custom_call" | custom-call | flops 1000 | bytes 1024 | tf_op jit(solution)/shard_map/finish/pallas_call | solution.py:630
  (57 shorter events, 1.1 us)
Async XLA Ops:
  3.3 12.0 %collective-permute-start.3 = (bf16[304,256]{1,0:T(8,128)(2,1)}, bf16[304,256]{1,0:T(8,128)(2,1)S(1)}, u32[]{:S(2)}, u32[]{:S(2)}) collective-permute-start(bf16[304,256]{1,0:T(8,128)(2,1)} %get-tuple-element.111), channel_id=1, source_target_pairs={{0,3},{1,2},{2,1},{3,0},{4,7},{5,6},{6,5},{7,4},{8,11},{9,10},{10,... | collective-permute-start | bytes 466952 | tf_op jit(solution)/shard_map/ppermute | solution.py:653
  4.7 13.0 %collective-permute-start.2 = (bf16[304,256]{1,0:T(8,128)(2,1)}, bf16[304,256]{1,0:T(8,128)(2,1)S(1)}, u32[]{:S(2)}, u32[]{:S(2)}) collective-permute-start(bf16[304,256]{1,0:T(8,128)(2,1)} %get-tuple-element.111), channel_id=1, source_target_pairs={{0,2},{1,3},{2,0},{3,1},{4,6},{5,7},{6,4},{7,5},{8,10},{9,11},{10,... | collective-permute-start | bytes 466952 | tf_op jit(solution)/shard_map/ppermute | solution.py:653
  5.8 11.9 %collective-permute-start.1 = (bf16[304,256]{1,0:T(8,128)(2,1)}, bf16[304,256]{1,0:T(8,128)(2,1)S(1)}, u32[]{:S(2)}, u32[]{:S(2)}) collective-permute-start(bf16[304,256]{1,0:T(8,128)(2,1)} %get-tuple-element.111), channel_id=1, source_target_pairs={{0,1},{1,0},{2,3},{3,2},{4,5},{5,4},{6,7},{7,6},{8,9},{9,8},{10,11... | collective-permute-start | bytes 466952 | tf_op jit(solution)/shard_map/ppermute | solution.py:653
  17.7 6.4 %collective-permute-start.5 = (bf16[528,256]{1,0:T(8,128)(2,1)S(1)}, bf16[528,256]{1,0:T(8,128)(2,1)S(1)}, u32[]{:S(2)}, u32[]{:S(2)}) collective-permute-start(bf16[528,256]{1,0:T(8,128)(2,1)S(1)} %get-tuple-element.114.refs_1_), channel_id=1, source_target_pairs={{0,4},{4,0},{8,12},{12,8},{16,20},{20,16},{24,28},{28,24},{1,5},{5... | collective-permute-start | bytes 811016 | tf_op jit(solution)/shard_map/ppermute | solution.py:653
  19.3 17.6 %collective-permute-start.9 = (bf16[432,256]{1,0:T(8,128)(2,1)}, bf16[432,256]{1,0:T(8,128)(2,1)S(1)}, u32[]{:S(2)}, u32[]{:S(2)}) collective-permute-start(bf16[432,256]{1,0:T(8,128)(2,1)} %get-tuple-element.110), channel_id=1, source_target_pairs={{0,3},{1,2},{2,1},{3,0},{4,7},{5,6},{6,5},{7,4},{8,11},{9,10},{10,... | collective-permute-start | bytes 663560 | tf_op jit(solution)/shard_map/ppermute | solution.py:653
  19.5 19.3 %collective-permute-start.8 = (bf16[432,256]{1,0:T(8,128)(2,1)}, bf16[432,256]{1,0:T(8,128)(2,1)S(1)}, u32[]{:S(2)}, u32[]{:S(2)}) collective-permute-start(bf16[432,256]{1,0:T(8,128)(2,1)} %get-tuple-element.110), channel_id=1, source_target_pairs={{0,2},{1,3},{2,0},{3,1},{4,6},{5,7},{6,4},{7,5},{8,10},{9,11},{10,... | collective-permute-start | bytes 663560 | tf_op jit(solution)/shard_map/ppermute | solution.py:653
  23.4 15.4 %collective-permute-start = (bf16[432,256]{1,0:T(8,128)(2,1)}, bf16[432,256]{1,0:T(8,128)(2,1)S(1)}, u32[]{:S(2)}, u32[]{:S(2)}) collective-permute-start(bf16[432,256]{1,0:T(8,128)(2,1)} %get-tuple-element.110), channel_id=1, source_target_pairs={{0,1},{1,0},{2,3},{3,2},{4,5},{5,4},{6,7},{7,6},{8,9},{9,8},{10,11... | collective-permute-start | bytes 663560 | tf_op jit(solution)/shard_map/ppermute | solution.py:653
  23.5 9.6 %collective-permute-start.6 = (bf16[384,256]{1,0:T(8,128)(2,1)S(1)}, bf16[384,256]{1,0:T(8,128)(2,1)S(1)}, u32[]{:S(2)}, u32[]{:S(2)}) collective-permute-start(bf16[384,256]{1,0:T(8,128)(2,1)S(1)} %get-tuple-element.112.refs_2_), channel_id=1, source_target_pairs={{0,4},{4,0},{8,12},{12,8},{16,20},{20,16},{24,28},{28,24},{1,5},{5... | collective-permute-start | bytes 589832 | tf_op jit(solution)/shard_map/ppermute | solution.py:653
  24.2 8.7 %collective-permute-start.4 = (bf16[384,256]{1,0:T(8,128)(2,1)S(1)}, bf16[384,256]{1,0:T(8,128)(2,1)S(1)}, u32[]{:S(2)}, u32[]{:S(2)}) collective-permute-start(bf16[384,256]{1,0:T(8,128)(2,1)S(1)} %get-tuple-element.112.refs_2_), channel_id=1, source_target_pairs={{0,8},{4,12},{8,0},{12,4},{16,24},{20,28},{24,16},{28,20},{1,9},{5... | collective-permute-start | bytes 589832 | tf_op jit(solution)/shard_map/ppermute | solution.py:653
  25.4 1.0 copy-start.3
  26.4 0.9 copy-start.5
  27.3 0.8 copy-start.8
  28.1 0.7 copy-start.10
  28.8 5.6 %copy-start = (bf16[2,256,256]{2,1,0:T(8,128)(2,1)S(1)}, bf16[2,256,256]{2,1,0:T(8,128)(2,1)}, u32[]{:S(2)}) copy-start(bf16[2,256,256]{2,1,0:T(8,128)(2,1)} %refs_0_.5) | copy-start | bytes 786436
  28.8 5.6 %copy-start.1 = (bf16[2,256,256]{2,1,0:T(8,128)(2,1)S(1)}, bf16[2,256,256]{2,1,0:T(8,128)(2,1)}, u32[]{:S(2)}) copy-start(bf16[2,256,256]{2,1,0:T(8,128)(2,1)} %refs_1_.5) | copy-start | bytes 786436
  28.8 5.6 %copy-start.12 = (f32[2,256]{1,0:T(2,128)S(1)}, f32[2,256]{1,0:T(2,128)}, u32[]{:S(2)}) copy-start(f32[2,256]{1,0:T(2,128)} %refs_10_.3) | copy-start | bytes 6148
  32.8 1.5 %collective-permute-start.7 = (bf16[384,256]{1,0:T(8,128)(2,1)S(1)}, bf16[384,256]{1,0:T(8,128)(2,1)S(1)}, u32[]{:S(2)}, u32[]{:S(2)}) collective-permute-start(bf16[384,256]{1,0:T(8,128)(2,1)S(1)} %collective-permute-done.4.refs_3_), channel_id=1, source_target_pairs={{0,4},{4,0},{8,12},{12,8},{16,20},{20,16},{24,28},{28,24},{1,5},{5... | collective-permute-start | bytes 589832 | tf_op jit(solution)/shard_map/ppermute | solution.py:653
  34.3 7.2 %copy-start.7 = (bf16[352,256]{1,0:T(8,128)(2,1)S(1)}, bf16[352,256]{1,0:T(8,128)(2,1)}, u32[]{:S(2)}) copy-start(bf16[352,256]{1,0:T(8,128)(2,1)} %get-tuple-element.123.refs_0_) | copy-start | bytes 540676
  34.4 7.1 %copy-start.9 = (bf16[64,256]{1,0:T(8,128)(2,1)S(1)}, bf16[64,256]{1,0:T(8,128)(2,1)}, u32[]{:S(2)}) copy-start(bf16[64,256]{1,0:T(8,128)(2,1)} %get-tuple-element.156.refs_4_.refs_8_.refs_7_.refs_3_) | copy-start | bytes 98308
  34.4 7.1 %copy-start.11 = (f32[2,256]{1,0:T(2,128)S(1)}, f32[2,256]{1,0:T(2,128)}, u32[]{:S(2)}) copy-start(f32[2,256]{1,0:T(2,128)} %refs_4_.1) | copy-start | bytes 6148
  36.9 8.6 %copy-start.2 = (bf16[1024,256]{1,0:T(8,128)(2,1)S(1)}, bf16[1024,256]{1,0:T(8,128)(2,1)}, u32[]{:S(2)}) copy-start(bf16[1024,256]{1,0:T(8,128)(2,1)} %refs_7_.2) | copy-start | bytes 1572868
  38.9 2.0 %collective-permute-start.10 = (bf16[432,256]{1,0:T(8,128)(2,1)S(1)}, bf16[432,256]{1,0:T(8,128)(2,1)S(1)}, u32[]{:S(2)}, u32[]{:S(2)}) collective-permute-start(bf16[432,256]{1,0:T(8,128)(2,1)S(1)} %collective-permute-done.refs_1_.refs_2_), channel_id=1, source_target_pairs={{0,4},{4,0},{8,12},{12,8},{16,20},{20,16},{24,28},{28,24},{1,5},{5... | collective-permute-start | bytes 663560 | tf_op jit(solution)/shard_map/ppermute | solution.py:653
  39.7 1.5 %collective-permute-start.11 = (bf16[432,256]{1,0:T(8,128)(2,1)S(1)}, bf16[432,256]{1,0:T(8,128)(2,1)S(1)}, u32[]{:S(2)}, u32[]{:S(2)}) collective-permute-start(bf16[432,256]{1,0:T(8,128)(2,1)S(1)} %collective-permute-done.8.refs_2_.refs_3_), channel_id=1, source_target_pairs={{0,4},{4,0},{8,12},{12,8},{16,20},{20,16},{24,28},{28,24},{1,5},{5... | collective-permute-start | bytes 663560 | tf_op jit(solution)/shard_map/ppermute | solution.py:653
  39.7 1.8 %collective-permute-start.12 = (bf16[432,256]{1,0:T(8,128)(2,1)S(1)}, bf16[432,256]{1,0:T(8,128)(2,1)S(1)}, u32[]{:S(2)}, u32[]{:S(2)}) collective-permute-start(bf16[432,256]{1,0:T(8,128)(2,1)S(1)} %collective-permute-done.9.refs_3_.refs_4_), channel_id=1, source_target_pairs={{0,4},{4,0},{8,12},{12,8},{16,20},{20,16},{24,28},{28,24},{1,5},{5... | collective-permute-start | bytes 663560 | tf_op jit(solution)/shard_map/ppermute | solution.py:653
  51.1 1.9 %collective-permute-start.13 = (bf16[4,256,256]{2,1,0:T(8,128)(2,1)S(1)}, bf16[4,256,256]{2,1,0:T(8,128)(2,1)S(1)}, u32[]{:S(2)}, u32[]{:S(2)}) collective-permute-start(bf16[4,256,256]{2,1,0:T(8,128)(2,1)S(1)} %get-tuple-element.128), channel_id=1, source_target_pairs={{0,4},{4,0},{8,12},{12,8},{16,20},{20,16},{24,28},{28,24},{1,5},{5... | collective-permute-start | bytes 1572872 | tf_op jit(solution)/shard_map/ppermute | solution.py:653
  53.2 10.4 %collective-permute-start.16 = (bf16[4,128,256]{2,1,0:T(8,128)(2,1)S(1)}, bf16[4,128,256]{2,1,0:T(8,128)(2,1)S(1)}, u32[]{:S(2)}, u32[]{:S(2)}) collective-permute-start(bf16[4,128,256]{2,1,0:T(8,128)(2,1)S(1)} %get-tuple-element.134), channel_id=1, source_target_pairs={{0,8},{4,12},{8,0},{12,4},{16,24},{20,28},{24,16},{28,20},{1,9},{5... | collective-permute-start | bytes 786440 | tf_op jit(solution)/shard_map/ppermute | solution.py:653
  59.7 4.0 %collective-permute-start.17 = (bf16[4,176,256]{2,1,0:T(8,128)(2,1)S(1)}, bf16[4,176,256]{2,1,0:T(8,128)(2,1)S(1)}, u32[]{:S(2)}, u32[]{:S(2)}) collective-permute-start(bf16[4,176,256]{2,1,0:T(8,128)(2,1)S(1)} %get-tuple-element.169), channel_id=1, source_target_pairs={{0,4},{4,0},{8,12},{12,8},{16,20},{20,16},{24,28},{28,24},{1,5},{5... | collective-permute-start | bytes 1081352 | tf_op jit(solution)/shard_map/ppermute | solution.py:653
  63.5 7.0 %collective-permute-start.14 = (bf16[4,256,256]{2,1,0:T(8,128)(2,1)S(1)}, bf16[4,256,256]{2,1,0:T(8,128)(2,1)S(1)}, u32[]{:S(2)}, u32[]{:S(2)}) collective-permute-start(bf16[4,256,256]{2,1,0:T(8,128)(2,1)S(1)} %get-tuple-element.149), channel_id=1, source_target_pairs={{0,4},{4,0},{8,12},{12,8},{16,20},{20,16},{24,28},{28,24},{1,5},{5... | collective-permute-start | bytes 1572872 | tf_op jit(solution)/shard_map/ppermute | solution.py:653
  63.6 5.5 %copy-start.4 = (bf16[1024,256]{1,0:T(8,128)(2,1)S(1)}, bf16[1024,256]{1,0:T(8,128)(2,1)}, u32[]{:S(2)}) copy-start(bf16[1024,256]{1,0:T(8,128)(2,1)} %refs_5_.5) | copy-start | bytes 1572868
  63.6 5.5 %copy-start.6 = (bf16[352,256]{1,0:T(8,128)(2,1)S(1)}, bf16[352,256]{1,0:T(8,128)(2,1)}, u32[]{:S(2)}) copy-start(bf16[352,256]{1,0:T(8,128)(2,1)} %get-tuple-element.113.refs_0_) | copy-start | bytes 540676
  63.8 11.1 %collective-permute-start.20 = (bf16[304,256]{1,0:T(8,128)(2,1)S(1)}, bf16[304,256]{1,0:T(8,128)(2,1)S(1)}, u32[]{:S(2)}, u32[]{:S(2)}) collective-permute-start(bf16[304,256]{1,0:T(8,128)(2,1)S(1)} %get-tuple-element.177), channel_id=1, source_target_pairs={{0,3},{1,2},{2,1},{3,0},{4,7},{5,6},{6,5},{7,4},{8,11},{9,10},{10,... | collective-permute-start | bytes 466952 | tf_op jit(solution)/shard_map/ppermute | solution.py:653
  65.2 13.3 %collective-permute-start.19 = (bf16[304,256]{1,0:T(8,128)(2,1)S(1)}, bf16[304,256]{1,0:T(8,128)(2,1)S(1)}, u32[]{:S(2)}, u32[]{:S(2)}) collective-permute-start(bf16[304,256]{1,0:T(8,128)(2,1)S(1)} %get-tuple-element.175), channel_id=1, source_target_pairs={{0,2},{1,3},{2,0},{3,1},{4,6},{5,7},{6,4},{7,5},{8,10},{9,11},{10,... | collective-permute-start | bytes 466952 | tf_op jit(solution)/shard_map/ppermute | solution.py:653
  69.0 9.4 %collective-permute-start.18 = (bf16[304,256]{1,0:T(8,128)(2,1)S(1)}, bf16[304,256]{1,0:T(8,128)(2,1)S(1)}, u32[]{:S(2)}, u32[]{:S(2)}) collective-permute-start(bf16[304,256]{1,0:T(8,128)(2,1)S(1)} %get-tuple-element.173), channel_id=1, source_target_pairs={{0,1},{1,0},{2,3},{3,2},{4,5},{5,4},{6,7},{7,6},{8,9},{9,8},{10,11... | collective-permute-start | bytes 466952 | tf_op jit(solution)/shard_map/ppermute | solution.py:653
  70.6 10.5 %collective-permute-start.15 = (bf16[4,128,256]{2,1,0:T(8,128)(2,1)S(1)}, bf16[4,128,256]{2,1,0:T(8,128)(2,1)S(1)}, u32[]{:S(2)}, u32[]{:S(2)}) collective-permute-start(bf16[4,128,256]{2,1,0:T(8,128)(2,1)S(1)} %get-tuple-element.155), channel_id=1, source_target_pairs={{0,8},{4,12},{8,0},{12,4},{16,24},{20,28},{24,16},{28,20},{1,9},{5... | collective-permute-start | bytes 786440 | tf_op jit(solution)/shard_map/ppermute | solution.py:653
  78.5 2.7 %collective-permute-start.21 = (bf16[2,176,256]{2,1,0:T(8,128)(2,1)S(1)}, bf16[2,176,256]{2,1,0:T(8,128)(2,1)S(1)}, u32[]{:S(2)}, u32[]{:S(2)}) collective-permute-start(bf16[2,176,256]{2,1,0:T(8,128)(2,1)S(1)} %get-tuple-element.182), channel_id=1, source_target_pairs={{0,4},{4,0},{8,12},{12,8},{16,20},{20,16},{24,28},{28,24},{1,5},{5... | collective-permute-start | bytes 540680 | tf_op jit(solution)/shard_map/ppermute | solution.py:653
  79.8 1.4 %collective-permute-start.22 = (bf16[2,176,256]{2,1,0:T(8,128)(2,1)S(1)}, bf16[2,176,256]{2,1,0:T(8,128)(2,1)S(1)}, u32[]{:S(2)}, u32[]{:S(2)}) collective-permute-start(bf16[2,176,256]{2,1,0:T(8,128)(2,1)S(1)} %get-tuple-element.183), channel_id=1, source_target_pairs={{0,4},{4,0},{8,12},{12,8},{16,20},{20,16},{24,28},{28,24},{1,5},{5... | collective-permute-start | bytes 540680 | tf_op jit(solution)/shard_map/ppermute | solution.py:653
  79.9 6.2 %collective-permute-start.25 = (bf16[176,256]{1,0:T(8,128)(2,1)S(1)}, bf16[176,256]{1,0:T(8,128)(2,1)S(1)}, u32[]{:S(2)}, u32[]{:S(2)}) collective-permute-start(bf16[176,256]{1,0:T(8,128)(2,1)S(1)} %get-tuple-element.191.refs_0_), channel_id=1, source_target_pairs={{0,24},{4,28},{8,16},{12,20},{16,8},{20,12},{24,0},{28,4},{1,25},{... | collective-permute-start | bytes 270344 | tf_op jit(solution)/shard_map/ppermute | solution.py:653
  81.3 10.8 %collective-permute-start.27 = (bf16[304,256]{1,0:T(8,128)(2,1)S(1)}, bf16[304,256]{1,0:T(8,128)(2,1)S(1)}, u32[]{:S(2)}, u32[]{:S(2)}) collective-permute-start(bf16[304,256]{1,0:T(8,128)(2,1)S(1)} %get-tuple-element.185), channel_id=1, source_target_pairs={{0,1},{1,0},{2,3},{3,2},{4,5},{5,4},{6,7},{7,6},{8,9},{9,8},{10,11... | collective-permute-start | bytes 466952 | tf_op jit(solution)/shard_map/ppermute | solution.py:653
  83.6 8.6 %collective-permute-start.28 = (bf16[304,256]{1,0:T(8,128)(2,1)S(1)}, bf16[304,256]{1,0:T(8,128)(2,1)S(1)}, u32[]{:S(2)}, u32[]{:S(2)}) collective-permute-start(bf16[304,256]{1,0:T(8,128)(2,1)S(1)} %get-tuple-element.186), channel_id=1, source_target_pairs={{0,2},{1,3},{2,0},{3,1},{4,6},{5,7},{6,4},{7,5},{8,10},{9,11},{10,... | collective-permute-start | bytes 466952 | tf_op jit(solution)/shard_map/ppermute | solution.py:653
  84.2 14.0 %collective-permute-start.29 = (bf16[304,256]{1,0:T(8,128)(2,1)S(1)}, bf16[304,256]{1,0:T(8,128)(2,1)S(1)}, u32[]{:S(2)}, u32[]{:S(2)}) collective-permute-start(bf16[304,256]{1,0:T(8,128)(2,1)S(1)} %get-tuple-element.187), channel_id=1, source_target_pairs={{0,3},{1,2},{2,1},{3,0},{4,7},{5,6},{6,5},{7,4},{8,11},{9,10},{10,... | collective-permute-start | bytes 466952 | tf_op jit(solution)/shard_map/ppermute | solution.py:653
  84.8 3.7 %collective-permute-start.24 = (bf16[176,256]{1,0:T(8,128)(2,1)S(1)}, bf16[176,256]{1,0:T(8,128)(2,1)S(1)}, u32[]{:S(2)}, u32[]{:S(2)}) collective-permute-start(bf16[176,256]{1,0:T(8,128)(2,1)S(1)} %get-tuple-element.191.refs_0_), channel_id=1, source_target_pairs={{0,16},{4,20},{8,24},{12,28},{16,0},{20,4},{24,8},{28,12},{1,17},{... | collective-permute-start | bytes 270344 | tf_op jit(solution)/shard_map/ppermute | solution.py:653
  86.1 3.7 %collective-permute-start.23 = (bf16[176,256]{1,0:T(8,128)(2,1)S(1)}, bf16[176,256]{1,0:T(8,128)(2,1)S(1)}, u32[]{:S(2)}, u32[]{:S(2)}) collective-permute-start(bf16[176,256]{1,0:T(8,128)(2,1)S(1)} %get-tuple-element.191.refs_0_), channel_id=1, source_target_pairs={{0,8},{4,12},{8,0},{12,4},{16,24},{20,28},{24,16},{28,20},{1,9},{5... | collective-permute-start | bytes 270344 | tf_op jit(solution)/shard_map/ppermute | solution.py:653
  98.4 5.5 %collective-permute-start.31 = (bf16[256,256]{1,0:T(8,128)(2,1)S(1)}, bf16[256,256]{1,0:T(8,128)(2,1)S(1)}, u32[]{:S(2)}, u32[]{:S(2)}) collective-permute-start(bf16[256,256]{1,0:T(8,128)(2,1)S(1)} %get-tuple-element.197.high), channel_id=1, source_target_pairs={{0,16},{4,20},{8,24},{12,28},{16,0},{20,4},{24,8},{28,12},{1,17},{... | collective-permute-start | bytes 393224 | tf_op jit(solution)/shard_map/ppermute | solution.py:653
  100.2 3.7 %collective-permute-start.30 = (bf16[176,256]{1,0:T(8,128)(2,1)S(1)}, bf16[176,256]{1,0:T(8,128)(2,1)S(1)}, u32[]{:S(2)}, u32[]{:S(2)}) collective-permute-start(bf16[176,256]{1,0:T(8,128)(2,1)S(1)} %get-tuple-element.196.low), channel_id=1, source_target_pairs={{0,8},{4,12},{8,0},{12,4},{16,24},{20,28},{24,16},{28,20},{1,9},{5... | collective-permute-start | bytes 270344 | tf_op jit(solution)/shard_map/ppermute | solution.py:653
  103.9 3.9 %collective-permute-start.33 = (bf16[256,256]{1,0:T(8,128)(2,1)S(1)}, bf16[256,256]{1,0:T(8,128)(2,1)S(1)}, u32[]{:S(2)}, u32[]{:S(2)}) collective-permute-start(bf16[256,256]{1,0:T(8,128)(2,1)S(1)} %get-tuple-element.199.high), channel_id=1, source_target_pairs={{0,8},{4,12},{8,0},{12,4},{16,24},{20,28},{24,16},{28,20},{1,9},{5... | collective-permute-start | bytes 393224 | tf_op jit(solution)/shard_map/ppermute | solution.py:653
  104.0 3.4 %collective-permute-start.32 = (bf16[176,256]{1,0:T(8,128)(2,1)S(1)}, bf16[176,256]{1,0:T(8,128)(2,1)S(1)}, u32[]{:S(2)}, u32[]{:S(2)}) collective-permute-start(bf16[176,256]{1,0:T(8,128)(2,1)S(1)} %get-tuple-element.198.low), channel_id=1, source_target_pairs={{0,16},{4,20},{8,24},{12,28},{16,0},{20,4},{24,8},{28,12},{1,17},{... | collective-permute-start | bytes 270344 | tf_op jit(solution)/shard_map/ppermute | solution.py:653
  107.8 5.0 %collective-permute-start.34 = (bf16[512,256]{1,0:T(8,128)(2,1)S(1)}, bf16[512,256]{1,0:T(8,128)(2,1)S(1)}, u32[]{:S(2)}, u32[]{:S(2)}) collective-permute-start(bf16[512,256]{1,0:T(8,128)(2,1)S(1)} %get-tuple-element.200.high), channel_id=1, source_target_pairs={{0,4},{4,0},{8,12},{12,8},{16,20},{20,16},{24,28},{28,24},{1,5},{5... | collective-permute-start | bytes 786440 | tf_op jit(solution)/shard_map/ppermute | solution.py:653
  111.4 1.3 %collective-permute-start.26 = (bf16[176,256]{1,0:T(8,128)(2,1)S(1)}, bf16[176,256]{1,0:T(8,128)(2,1)S(1)}, u32[]{:S(2)}, u32[]{:S(2)}) collective-permute-start(bf16[176,256]{1,0:T(8,128)(2,1)S(1)} %four_sum.1.low), channel_id=1, source_target_pairs={{0,4},{4,0},{8,12},{12,8},{16,20},{20,16},{24,28},{28,24},{1,5},{5... | collective-permute-start | bytes 270344 | tf_op jit(solution)/shard_map/ppermute | solution.py:653
  111.4 1.4 %collective-permute-start.35 = (bf16[176,256]{1,0:T(8,128)(2,1)S(1)}, bf16[176,256]{1,0:T(8,128)(2,1)S(1)}, u32[]{:S(2)}, u32[]{:S(2)}) collective-permute-start(bf16[176,256]{1,0:T(8,128)(2,1)S(1)} %get-tuple-element.201.late), channel_id=1, source_target_pairs={{0,4},{4,0},{8,12},{12,8},{16,20},{20,16},{24,28},{28,24},{1,5},{5... | collective-permute-start | bytes 270344 | tf_op jit(solution)/shard_map/ppermute | solution.py:653

commit v4 on v3

--- a/solution.py
+++ b/solution.py
@@ -16,7 +16,7 @@
 
 VMEM_LIMIT = 32 * 2**20
 SMALL_LIMIT = 12 * 2**20
-UNROLL = {"attn_fwd": 4, "mlp_fwd": 4, "mlp_both": 4, "mlp_bwd": 4, "attn_bwd": 2, "attn_pre": 2, "attn_post": 2}
+UNROLL = {"attn_fwd": 4, "mlp_fwd": 1, "mlp_both": 1, "mlp_bwd": 1, "attn_bwd": 4, "attn_pre": 4, "attn_post": 2}
 KERNEL_FLOPS = 1000
 LONG = 50 * 10**9
 
@@ -90,12 +90,22 @@
     return [(place * rows, [ref.at[pl.ds(m * rows, rows)] for m in range(3)]) for place, ref in zip(places, pieces)]
 
 
-def place_qkv(layer, pieces, wa):
+def place_attn_pieces(layer, pieces, wa):
     place_pieces((pieces[0][...],), parts_of(pieces[1:], 176), wa, 256 * layer, 176)
 
 
+def place_qkv(layer, pieces, wa, wq):
+    place_attn_pieces(layer, pieces, wa)
+    side_by_side(wa, wq)
+
+
+def side_by_side(wa, wq):
+    for m in range(4):
+        wq[m * 192:(m + 1) * 192, :] = wa[m, 0:192, :]
+
+
 def place_attn(layer, pieces, wa, w_cross, w_out):
-    place_qkv(layer, pieces, wa)
+    place_attn_pieces(layer, pieces, wa)
     total = jnp.zeros((1, 256), F32)
     for m in range(4):
         place = pl.multiple_of((head_index() ^ m) * HD, HD)
@@ -105,9 +115,12 @@
     return total
 
 
-def place_mlp(layer, pieces, wm):
+def place_mlp(layer, pieces, wm, up_all, down_all):
     rows = 256 if len(pieces) == 8 else 128
     place_pieces((pieces[0][layer], pieces[1][layer]), parts_of(pieces[2:], rows), wm, 0, rows)
+    for m in range(4):
+        up_all[:, m * 256:(m + 1) * 256] = wm[m, 0:256, :]
+        down_all[m * 256:(m + 1) * 256, :] = wm[m, 256:512, :]
 
 
 def each_sample(rows, unroll, step, *init, size=256):
@@ -119,20 +132,23 @@
 
 def attn_fwd_kernel(layer, count, *refs):
     pieces = refs[:count]
-    (cur_ref, mask_ref, gain_ref, middle_ref, base_ref, nrm_ref, qkv_ref, mix_ref, lse_ref, wa, w_cross, w_out) = refs[count:]
+    (cur_ref, mask_ref, gain_ref, middle_ref, base_ref, nrm_ref, qkv_ref, mix_ref, lse_ref, wa, w_cross, w_out,
+     wq) = refs[count:]
     bias = place_attn(layer, pieces, wa, w_cross, w_out)
+    side_by_side(wa, wq)
     gain = gain_ref[layer:layer + 1, :]
     def step(rows):
         cur = cur_ref[rows, :].astype(F32)
         nrm = (cur * rescale_of(cur) * gain).astype(BF)
         nrm_ref[rows, :] = nrm
         mask = mask_rows(mask_ref, rows)
-        qkv = [nt(wa[m, 0:192, :], nrm).astype(BF) for m in range(4)]
+        qkv_all = nt(wq[...], nrm).astype(BF)
+        qkv_ref[:, rows] = qkv_all
+        qkv = [qkv_all[m * 192:(m + 1) * 192] for m in range(4)]
         scores = [slot_scores(qkv[m][0:64], qkv[m][64:128], mask) for m in range(4)]
         cross = nt(nrm, w_cross[...]) + bias
         probs = []
         for m in range(4):
-            qkv_ref[m * 192:(m + 1) * 192, rows] = qkv[m]
             top = jnp.max(scores[m], axis=0, keepdims=True)
             e = jnp.exp(scores[m] - top)
             total = jnp.sum(e, axis=0, keepdims=True)
@@ -148,83 +164,77 @@
     each_sample(cur_ref.shape[0], UNROLL["attn_fwd"], step)
 
 
-def mlp_fwd_block(middle, gain, wm):
+def mlp_fwd_block(middle, gain, up_all, down_all):
     r = rescale_of(middle)
     n2 = (middle * r * gain).astype(BF)
-    us = [nn(n2, wm[m, 0:256, :]) for m in range(4)]
-    kept = []
-    for u in us:
-        hid, slope = gelu_and_slope(u)
-        kept.append((hid.astype(BF), slope.astype(BF)))
-    feed = [nn(kept[m][0], wm[m, 256:512, :]) for m in range(4)]
-    return r, n2, kept, (feed[0] + feed[1]) + (feed[2] + feed[3])
+    hid, slope = gelu_and_slope(nn(n2, up_all[...]))
+    hid = hid.astype(BF)
+    return r, n2, hid, slope.astype(BF), nn(hid, down_all[...])
 
 
 def mlp_fwd_kernel(layer, count, *refs):
     pieces = refs[:count]
-    (middle_ref, base_ref, gain_ref, out_ref, hid_ref, slope_ref, wm) = refs[count:]
-    place_mlp(layer, pieces, wm)
+    (middle_ref, base_ref, gain_ref, out_ref, hid_ref, slope_ref, wm, up_all, down_all) = refs[count:]
+    place_mlp(layer, pieces, wm, up_all, down_all)
     gain = gain_ref[layer:layer + 1, :]
+
     def step(rows):
-        _, _, kept, feed = mlp_fwd_block(middle_ref[rows, :], gain, wm)
-        for m, (hid, slope) in enumerate(kept):
-            hid_ref[rows, m * 256:(m + 1) * 256] = hid
-            slope_ref[rows, m * 256:(m + 1) * 256] = slope
+        _, _, hid, slope, feed = mlp_fwd_block(middle_ref[rows, :], gain, up_all, down_all)
+        hid_ref[rows, :] = hid
+        slope_ref[rows, :] = slope
         out_ref[rows, :] = base_ref[rows, :] + feed
         return ()
 
-    each_sample(middle_ref.shape[0], UNROLL["mlp_fwd"], step)
-
-
-def mlp_bwd_block(gf, kept, wm):
-    ghs = [nt(gf, wm[m, 256:512, :]) for m in range(4)]
-    gps = [(gh * slope.astype(F32)).astype(BF) for gh, (_, slope) in zip(ghs, kept)]
-    gn = [nt(gps[m], wm[m, 0:256, :]) for m in range(4)]
-    return gps, (gn[0] + gn[1]) + (gn[2] + gn[3])
+    each_sample(middle_ref.shape[0], UNROLL["mlp_fwd"], step, size=middle_ref.shape[0])
+
+
+def mlp_bwd_block(gf, slope, up_all, down_all):
+    gp = (nt(gf, down_all[...]) * slope.astype(F32)).astype(BF)
+    return gp, nt(gp, up_all[...])
 
 
 def put_mlp_grads(hid, gp, n2, gf, keep_ref, send_ref):
+    up = tn(n2[...], gp[...]).astype(BF)
+    down = tn(hid[...], gf[...]).astype(BF)
+    own_up = half_index() == 0
     for m in range(4):
-        columns = slice(m * 256, (m + 1) * 256)
-        up = tn(n2[...], gp[:, columns]).astype(BF)
-        down = tn(hid[:, columns], gf[...]).astype(BF)
-        own_up = half_index() == 0
-        keep_ref[m] = jnp.where(own_up, up, down)
-        send_ref[m] = jnp.where(own_up, down, up)
+        part = slice(m * 256, (m + 1) * 256)
+        keep_ref[m] = jnp.where(own_up, up[:, part], down[part])
+        send_ref[m] = jnp.where(own_up, down[part], up[:, part])
 
 
 def mlp_both_kernel(layer, count, *refs):
     pieces = refs[:count]
-    (middle_ref, base_ref, cot_ref, gain_ref, out_ref, gm_ref, keep_ref, send_ref, small_ref, wm, hid_all, gp_all,
-     n2_all) = refs[count:]
-    place_mlp(layer, pieces, wm)
+    (middle_ref, base_ref, cot_ref, gain_ref, out_ref, gm_ref, keep_ref, send_ref, small_ref,
+     wm, up_all, down_all, hid_all, gp_all, n2_all) = refs[count:]
+    place_mlp(layer, pieces, wm, up_all, down_all)
     gain = gain_ref[layer:layer + 1, :]
+
     def step(rows, gain_grad):
         middle = middle_ref[rows, :]
-        r, n2, kept, feed = mlp_fwd_block(middle, gain, wm)
+        r, n2, hid, slope, feed = mlp_fwd_block(middle, gain, up_all, down_all)
         out_ref[rows, :] = base_ref[rows, :] + feed
         gf = cot_ref[rows, :]
-        gps, gn = mlp_bwd_block(gf, kept, wm)
+        gp, gn = mlp_bwd_block(gf, slope, up_all, down_all)
         n2_all[rows, :] = n2
-        for m in range(4):
-            hid_all[rows, m * 256:(m + 1) * 256] = kept[m][0]
-            gp_all[rows, m * 256:(m + 1) * 256] = gps[m]
+        hid_all[rows, :] = hid
+        gp_all[rows, :] = gp
         back, part = norm_back(middle, r, gain, gn)
-        gain_grad = gain_grad + part
         gm_ref[rows, :] = gf.astype(F32) + back
-        return (gain_grad, )
-
-    gain_grad, = each_sample(middle_ref.shape[0], UNROLL["mlp_both"], step, jnp.zeros((1, 256), F32))
+        return (gain_grad + part, )
+
+    gain_grad, = each_sample(middle_ref.shape[0], UNROLL["mlp_both"], step, jnp.zeros((1, 256), F32), size=middle_ref.shape[0])
     small_ref[...] = jnp.broadcast_to(gain_grad, small_ref.shape)
     put_mlp_grads(hid_all, gp_all, n2_all, cot_ref, keep_ref, send_ref)
 
 
 def mlp_bwd_kernel(layer, count, *refs):
     pieces = refs[:count]
-    (grad_ref, middle_ref, hid_ref, slope_ref, gain_ref, gm_ref, keep_ref, send_ref, small_ref, wm, gp_all, n2_all,
-     gf_all) = refs[count:]
-    place_mlp(layer, pieces, wm)
+    (grad_ref, middle_ref, hid_ref, slope_ref, gain_ref, gm_ref, keep_ref, send_ref, small_ref,
+     wm, up_all, down_all, gp_all, n2_all, gf_all) = refs[count:]
+    place_mlp(layer, pieces, wm, up_all, down_all)
     gain = gain_ref[layer:layer + 1, :]
+
     def step(rows, gain_grad):
         middle = middle_ref[rows, :]
         r = rescale_of(middle)
@@ -232,16 +242,13 @@
         grad = grad_ref[rows, :]
         gf = grad.astype(BF)
         gf_all[rows, :] = gf
-        kept = [(None, slope_ref[rows, m * 256:(m + 1) * 256]) for m in range(4)]
-        gps, gn = mlp_bwd_block(gf, kept, wm)
-        for m in range(4):
-            gp_all[rows, m * 256:(m + 1) * 256] = gps[m]
+        gp, gn = mlp_bwd_block(gf, slope_ref[rows, :], up_all, down_all)
+        gp_all[rows, :] = gp
         back, part = norm_back(middle, r, gain, gn)
-        gain_grad = gain_grad + part
         gm_ref[rows, :] = grad + back
-        return (gain_grad, )
-
-    gain_grad, = each_sample(middle_ref.shape[0], UNROLL["mlp_bwd"], step, jnp.zeros((1, 256), F32))
+        return (gain_grad + part, )
+
+    gain_grad, = each_sample(middle_ref.shape[0], UNROLL["mlp_bwd"], step, jnp.zeros((1, 256), F32), size=middle_ref.shape[0])
     small_ref[...] = jnp.broadcast_to(gain_grad, small_ref.shape)
     put_mlp_grads(hid_ref, gp_all, n2_all, gf_all, keep_ref, send_ref)
 
@@ -302,13 +309,12 @@
     return r * (scaled - cur * (r * r * jnp.mean(cur * scaled, axis=-1, keepdims=True)))
 
 
-def put_attn_grads(layer, nrm, gqkv_all, wa, gain_ref, d_cross_ref, d_out_ref, small, mlp_small, payload, keep_ref, sends):
-    gain_grad = small[1:2, :]
+def put_attn_grads(layer, nrm, gqkv_all, wq, gain_ref, d_cross_ref, d_out_ref, small, mlp_small, payload, keep_ref, sends):
+    d_qkv = nn(gqkv_all[...], nrm)
+    gain_grad = small[1:2, :] + jnp.sum(d_qkv * wq[...].astype(F32), axis=0, keepdims=True)
     for m in range(4):
         place = pl.multiple_of((head_index() ^ m) * HD, HD)
-        d_qkv = nn(gqkv_all[m * 192:(m + 1) * 192, :], nrm)
-        gain_grad = gain_grad + jnp.sum(d_qkv * wa[m, 0:192, :].astype(F32), axis=0, keepdims=True)
-        payload[m, 0:192, :] = d_qkv.astype(BF)
+        payload[m, 0:192, :] = d_qkv[m * 192:(m + 1) * 192].astype(BF)
         payload[m, 192:256, :] = d_cross_ref[pl.ds(place, HD), :]
         payload[m, 256:320, :] = d_out_ref[m * HD:(m + 1) * HD, :]
     gain_grad = gain_grad / gain_ref[layer:layer + 1, :]
@@ -326,27 +332,27 @@
 def attn_bwd_kernel(layer, count, *refs):
     pieces = refs[:count]
     (mask_ref, nrm_ref, qkv_ref, lse_ref, gain_ref, gmix_ref, d_cross_ref, d_out_ref, small, dot_ref, mlp_small,
-     cur_ref, base_ref, gn_ref, out_ref, keep_ref, send_ref, wa, gqkv_all, payload) = refs[count:]
-    place_qkv(layer, pieces, wa)
+     cur_ref, base_ref, gn_ref, out_ref, keep_ref, send_ref, wa, wq, gqkv_all, payload) = refs[count:]
+    place_qkv(layer, pieces, wa, wq)
 
     def step(rows):
         gn = gn_ref[rows, :]
-        for m, gqkv in enumerate(qkv_back(rows, mask_ref, qkv_ref, lse_ref, gmix_ref, dot_ref)):
-            gqkv_all[m * 192:(m + 1) * 192, rows] = gqkv
-            gn = gn + tn(gqkv, wa[m, 0:192, :])
+        gqkv = jnp.concatenate(qkv_back(rows, mask_ref, qkv_ref, lse_ref, gmix_ref, dot_ref), axis=0)
+        gqkv_all[:, rows] = gqkv
+        gn = gn + tn(gqkv, wq[...])
         out_ref[rows, :] = base_ref[rows, :] + norm_grad(cur_ref[rows, :].astype(F32), gain_ref[layer:layer + 1, :], gn)
         return ()
 
     each_sample(nrm_ref.shape[0], UNROLL["attn_bwd"], step)
-    put_attn_grads(layer, nrm_ref[...], gqkv_all, wa, gain_ref, d_cross_ref, d_out_ref, small, mlp_small,
+    put_attn_grads(layer, nrm_ref[...], gqkv_all, wq, gain_ref, d_cross_ref, d_out_ref, small, mlp_small,
                    payload, keep_ref, (send_ref,))
 
 
 def attn_grads_kernel(layer, count, *refs):
     pieces = refs[:count]
     (mask_ref, nrm_ref, qkv_ref, lse_ref, gain_ref, gmix_ref, d_cross_ref, d_out_ref, small, dot_ref, mlp_small,
-     gqkv_all, keep_ref, send_low, send_high, wa, payload) = refs[count:]
-    place_qkv(layer, pieces, wa)
+     gqkv_all, keep_ref, send_low, send_high, wa, wq, payload) = refs[count:]
+    place_qkv(layer, pieces, wa, wq)
 
     def step(rows):
         for m, gqkv in enumerate(qkv_back(rows, mask_ref, qkv_ref, lse_ref, gmix_ref, dot_ref)):
@@ -354,19 +360,18 @@
         return ()
 
     each_sample(nrm_ref.shape[0], UNROLL["attn_bwd"], step)
-    put_attn_grads(layer, nrm_ref[...], gqkv_all, wa, gain_ref, d_cross_ref, d_out_ref, small, mlp_small,
+    put_attn_grads(layer, nrm_ref[...], gqkv_all, wq, gain_ref, d_cross_ref, d_out_ref, small, mlp_small,
                    payload, keep_ref, (send_low, send_high))
 
 
 def attn_post_kernel(layer, count, *refs):
     pieces = refs[:count]
-    (gqkv_all, gain_ref, cur_ref, base_ref, gn_ref, out_ref, wa) = refs[count:]
-    place_qkv(layer, pieces, wa)
+    (gqkv_all, gain_ref, cur_ref, base_ref, gn_ref, out_ref, wa, wq) = refs[count:]
+    place_qkv(layer, pieces, wa, wq)
 
     def step(rows):
         gn = gn_ref[rows, :]
-        for m in range(4):
-            gn = gn + tn(gqkv_all[m * 192:(m + 1) * 192, rows], wa[m, 0:192, :])
+        gn = gn + tn(gqkv_all[:, rows], wq[...])
         out_ref[rows, :] = base_ref[rows, :] + norm_grad(cur_ref[rows, :].astype(F32), gain_ref[layer:layer + 1, :], gn)
         return ()
 
@@ -556,35 +561,37 @@
     )(*args)
 
 
+QKV_SCRATCH = [((4, 352, 256), BF), ((768, 256), BF)]
 ATTN_SCRATCH = [((4, 352, 256), BF), ((256, 256), BF), ((256, 256), BF)]
+MLP_SCRATCH = [((4, 512, 256), BF), ((256, 1024), BF), ((1024, 256), BF)]
 MLP_GRADS = [((4, 256, 256), BF), ((4, 256, 256), BF), ((8, 256), F32)]
 
 
 def attn_fwd(layer, cur, mask, gain, pieces):
     rows = cur.shape[0]
     outs = [((rows, 256), F32), ((rows, 256), F32), ((rows, 256), BF), ((768, rows), BF), ((256, rows), BF), ((8, rows), F32)]
-    return call(functools.partial(attn_fwd_kernel, layer, len(pieces)), outs, ATTN_SCRATCH, "attn_fwd", *pieces, cur, mask, gain,
+    return call(functools.partial(attn_fwd_kernel, layer, len(pieces)), outs, ATTN_SCRATCH + [((768, 256), BF)], "attn_fwd", *pieces, cur, mask, gain,
                 flops=(LONG, KERNEL_FLOPS)[layer])
 
 
 def mlp_fwd(layer, middle, base, gain, pieces):
     rows = middle.shape[0]
     outs = [((rows, 256), F32), ((rows, 1024), BF), ((rows, 1024), BF)]
-    return call(functools.partial(mlp_fwd_kernel, layer, len(pieces)), outs, [((4, 512, 256), BF)], "mlp_fwd", *pieces,
+    return call(functools.partial(mlp_fwd_kernel, layer, len(pieces)), outs, MLP_SCRATCH, "mlp_fwd", *pieces,
                 middle, base, gain)
 
 
 def mlp_both(layer, middle, base, cot, gain, pieces):
     rows = middle.shape[0]
     outs = [((rows, 256), F32), ((rows, 256), F32)] + MLP_GRADS
-    scratch = [((4, 512, 256), BF), ((rows, 1024), BF), ((rows, 1024), BF), ((rows, 256), BF)]
+    scratch = MLP_SCRATCH + [((rows, 1024), BF), ((rows, 1024), BF), ((rows, 256), BF)]
     return call(functools.partial(mlp_both_kernel, layer, len(pieces)), outs, scratch, "mlp_both", *pieces, middle, base, cot, gain)
 
 
 def mlp_bwd(layer, grad, middle, hid, slope, gain, pieces):
     rows = middle.shape[0]
     outs = [((rows, 256), F32)] + MLP_GRADS
-    scratch = [((4, 512, 256), BF), ((rows, 1024), BF), ((rows, 256), BF), ((rows, 256), BF)]
+    scratch = MLP_SCRATCH + [((rows, 1024), BF), ((rows, 256), BF), ((rows, 256), BF)]
     return call(functools.partial(mlp_bwd_kernel, layer, len(pieces)), outs, scratch, "mlp_bwd", *pieces,
                 grad, middle, hid, slope, gain)
 
@@ -604,7 +611,7 @@
     rows = cur.shape[0]
     nrm, qkv, _, lse = saved
     gmix, d_cross, d_out, base, gn, small, dot = pre
-    scratch = [((4, 352, 256), BF), ((768, rows), BF), ((4, 320, 256), BF)]
+    scratch = QKV_SCRATCH + [((768, rows), BF), ((4, 320, 256), BF)]
     return call(functools.partial(attn_bwd_kernel, layer, len(pieces)), [((rows, 256), F32)] + PAYLOAD, scratch, "attn_bwd", *pieces,
                 mask, nrm, qkv, lse, gain, gmix, d_cross, d_out, small, dot, mlp_small, cur, base, gn)
 
@@ -612,13 +619,13 @@
 def attn_grads(layer, mask, saved, gain, pre, mlp_small, pieces):
     nrm, qkv, _, lse = saved
     gmix, d_cross, d_out, _, _, small, dot = pre
-    scratch = [((4, 352, 256), BF), ((4, 320, 256), BF)]
+    scratch = QKV_SCRATCH + [((4, 320, 256), BF)]
     return call(functools.partial(attn_grads_kernel, layer, len(pieces)), [((768, nrm.shape[0]), BF), ((4, 176, 256), BF), ((2, 176, 256), BF), ((2, 176, 256), BF)], scratch, "attn_grads", *pieces,
                 mask, nrm, qkv, lse, gain, gmix, d_cross, d_out, small, dot, mlp_small)
 
 
 def attn_post(layer, gqkv, gain, cur, pre, pieces):
-    return call(functools.partial(attn_post_kernel, layer, len(pieces)), [((cur.shape[0], 256), F32)], [((4, 352, 256), BF)], "attn_post", *pieces,
+    return call(functools.partial(attn_post_kernel, layer, len(pieces)), [((cur.shape[0], 256), F32)], QKV_SCRATCH, "attn_post", *pieces,
                 gqkv, gain, cur, pre[3], pre[4])[0]
 
 

time: 115 us -> 113 us (0.983)
  Pallas kernels: 38.5 us -> 34.6 us
  waiting for transfers between devices: 36.1 us -> 37.5 us
    pallas_call x10, Pallas kernels: 33.6 us -> 29.7 us  [call(): pl.pallas_call(kernel, in_specs=[VMEM] * len(args), out_specs=[VMEM] * le...]
    ppermute x36, waiting for transfers between devices: 36.1 us -> 37.5 us  [swap(): return lax.ppermute(x, axis, [(i, i ^ mask) for i in range(size)])]
  transfers between devices with their start and end apart: 36 -> 36, of which waited for: 17 -> 17; matrix products, arithmetic and copies ran while one was open for 0% -> 0% of each run, Pallas kernels for 22% -> 20%
where the time goes in v4:
time: 113 us; the launch traced here: 112 us
  waiting for transfers between devices  37.5 us (33%)
  starting transfers between devices  35.1 us (31%)
  Pallas kernels  34.6 us (31%)
  local copies, waits for them, and re-layouts  3.45 us (3%)
    ppermute x36, waiting for transfers between devices, swap(): return lax.ppermute(x, axis, [(i, i ^ mask) for i in range(size)])  37.5 us
    ppermute x36, starting transfers between devices, swap(): return lax.ppermute(x, axis, [(i, i ^ mask) for i in range(size)])  35.1 us
    pallas_call x10, Pallas kernels, call(): pl.pallas_call(kernel, in_specs=[VMEM] * len(args), out_specs=[VMEM] * le...  29.7 us
    unnamed x26, local copies, waits for them, and re-layouts  3.45 us
    pallas_call x1, Pallas kernels, body(): pl.pallas_call(pack_kernel, in_specs=[SMEM] + [ANY] * 5 + [VMEM], out_spe...  2.66 us
  transfers between devices with their start and end apart: 36, of which 17 were waited for; matrix products, arithmetic and copies ran while one was open for 0% of the time, Pallas kernels for 20%

profile of v4, /device:TPU:9, one launch (start us, length us, event | category | flops | bytes accessed | tf_op | source)
XLA Modules:
  0.0 111.6 jit_solution(507457183925506155)
XLA Ops:
  0.6 2.7 %pack.1 = (bf16[352,256]{1,0:T(8,128)(2,1)}, bf16[352,256]{1,0:T(8,128)(2,1)}, bf16[304,256]{1,0:T(8,128)(2,1)}, bf16[432,256]{1,0:T(8,128)(2,1)}, bf16[64,256]{1,0:T(8,128)(2,1)}) custom-call(s32[16]{0:T(128)} %lens.1, bf16[2,3,64,256]{3,2,1,0:T(8,128)(2,1)} %bitcast.4, bf16[2,64,256]{2,1,0:T(8,128)(2,1)} %bitcast.5, bf16[2,64,256]{2,1,0:T(8,128)(2,1)} %out.1, ...), custom_call_target="tpu_custom_call" | custom-call | tf_op jit(solution)/shard_map/pack/pallas_call | solution.py:704
  3.3 1.4 %collective-permute-start.3 = (bf16[304,256]{1,0:T(8,128)(2,1)}, bf16[304,256]{1,0:T(8,128)(2,1)S(1)}, u32[]{:S(2)}, u32[]{:S(2)}) collective-permute-start(bf16[304,256]{1,0:T(8,128)(2,1)} %get-tuple-element.111), channel_id=1, source_target_pairs={{0,3},{1,2},{2,1},{3,0},{4,7},{5,6},{6,5},{7,4},{8,11},{9,10},{10,... | collective-permute-start | bytes 466952 | tf_op jit(solution)/shard_map/ppermute | solution.py:660
  4.7 1.1 collective-permute-start.2
  5.8 1.1 collective-permute-start.1
  6.9 8.5 %collective-permute-done.3.c = bf16[304,256]{1,0:T(8,128)(2,1)S(1)} collective-permute-done((bf16[304,256]{1,0:T(8,128)(2,1)}, bf16[304,256]{1,0:T(8,128)(2,1)S(1)}, u32[]{:S(2)}, u32[]{:S(2)}) %collective-permute-start.3) | collective-permute-done | bytes 155680 | tf_op jit(solution)/shard_map/ppermute | solution.py:660
  15.3 2.4 %collective-permute-done.2.b = bf16[304,256]{1,0:T(8,128)(2,1)S(1)} collective-permute-done((bf16[304,256]{1,0:T(8,128)(2,1)}, bf16[304,256]{1,0:T(8,128)(2,1)S(1)}, u32[]{:S(2)}, u32[]{:S(2)}) %collective-permute-start.2) | collective-permute-done | bytes 155680 | tf_op jit(solution)/shard_map/ppermute | solution.py:660
  17.7 1.6 %collective-permute-start.5 = (bf16[528,256]{1,0:T(8,128)(2,1)S(1)}, bf16[528,256]{1,0:T(8,128)(2,1)S(1)}, u32[]{:S(2)}, u32[]{:S(2)}) collective-permute-start(bf16[528,256]{1,0:T(8,128)(2,1)S(1)} %get-tuple-element.114.refs_1_), channel_id=1, source_target_pairs={{0,4},{4,0},{8,12},{12,8},{16,20},{20,16},{24,28},{28,24},{1,5},{5... | collective-permute-start | bytes 811016 | tf_op jit(solution)/shard_map/ppermute | solution.py:660
  19.3 0.2 collective-permute-start.9
  19.5 3.9 %collective-permute-start.8 = (bf16[432,256]{1,0:T(8,128)(2,1)}, bf16[432,256]{1,0:T(8,128)(2,1)S(1)}, u32[]{:S(2)}, u32[]{:S(2)}) collective-permute-start(bf16[432,256]{1,0:T(8,128)(2,1)} %get-tuple-element.110), channel_id=1, source_target_pairs={{0,2},{1,3},{2,0},{3,1},{4,6},{5,7},{6,4},{7,5},{8,10},{9,11},{10,... | collective-permute-start | bytes 663560 | tf_op jit(solution)/shard_map/ppermute | solution.py:660
  23.5 0.6 collective-permute-start.6
  24.2 1.2 %collective-permute-start.4 = (bf16[384,256]{1,0:T(8,128)(2,1)S(1)}, bf16[384,256]{1,0:T(8,128)(2,1)S(1)}, u32[]{:S(2)}, u32[]{:S(2)}) collective-permute-start(bf16[384,256]{1,0:T(8,128)(2,1)S(1)} %get-tuple-element.112.refs_2_), channel_id=1, source_target_pairs={{0,8},{4,12},{8,0},{12,4},{16,24},{20,28},{24,16},{28,20},{1,9},{5... | collective-permute-start | bytes 589832 | tf_op jit(solution)/shard_map/ppermute | solution.py:660
  25.4 1.0 copy-done.3
  26.4 0.9 copy-done.5
  27.3 0.8 copy-done.8
  28.1 0.7 copy-done.10
  28.8 3.8 %attn_fwd.2 = (f32[1024,256]{1,0:T(8,128)S(1)}, f32[1024,256]{1,0:T(8,128)S(1)}, bf16[1024,256]{1,0:T(8,128)(2,1)S(1)}, bf16[768,1024]{1,0:T(8,128)(2,1)S(1)}, b...) custom-call(bf16[352,256]{1,0:T(8,128)(2,1)S(1)} %copy-done.5, bf16[528,256]{1,0:T(8,128)(2,1)S(1)} %get-tuple-element.114.refs_1_, ...), custom_call_target="tpu_custom_call" | custom-call | flops 49999998976 | bytes 1024 | tf_op jit(solution)/shard_map/attn_fwd/pallas_call | solution.py:552
  32.6 0.4 collective-permute-start.7
  33.0 1.1 %collective-permute-done.7.refs_5_ = bf16[384,256]{1,0:T(8,128)(2,1)S(1)} collective-permute-done((bf16[384,256]{1,0:T(8,128)(2,1)S(1)}, bf16[384,256]{1,0:T(8,128)(2,1)S(1)}, u32[]{:S(2)}, u32[]{:S(2)}) %collective-permute-start.7) | collective-permute-done | bytes 196640 | tf_op jit(solution)/shard_map/ppermute | solution.py:660
  34.2 2.2 %mlp_fwd.1 = (f32[1024,256]{1,0:T(8,128)S(1)}, bf16[1024,1024]{1,0:T(8,128)(2,1)S(1)}, bf16[1024,1024]{1,0:T(8,128)(2,1)S(1)}) custom-call(bf16[2,256,256]{2,1,0:T(8,128)(2,1)S(1)} %copy-done, bf16[2,256,256]{2,1,0:T(8,128)(2,1)S(1)} %copy-done.1, bf16[384,256]{1,0:T(8,128)(2,1)S(1)} %get-tuple-element.112.refs_2_, ...), custom_call_target="tpu_custom_call" | custom-call | flops 1000 | bytes 1024 | tf_op jit(solution)/shard_map/mlp_fwd/pallas_call | solution.py:552
  36.4 2.5 %collective-permute-done.8.refs_2_.refs_3_ = bf16[432,256]{1,0:T(8,128)(2,1)S(1)} collective-permute-done((bf16[432,256]{1,0:T(8,128)(2,1)}, bf16[432,256]{1,0:T(8,128)(2,1)S(1)}, u32[]{:S(2)}, u32[]{:S(2)}) %collective-permute-start.8) | collective-permute-done | bytes 221216 | tf_op jit(solution)/shard_map/ppermute | solution.py:660
  38.9 0.8 collective-permute-start.10
  39.7 0.5 collective-permute-start.12
  40.2 0.6 collective-permute-done.10.refs_4_.refs_5_
  40.8 0.4 collective-permute-done.11.refs_5_.refs_6_
  41.2 0.3 collective-permute-done.12.refs_6_.refs_7_
  41.5 3.8 %attn_fwd.3 = (f32[1024,256]{1,0:T(8,128)S(1)}, f32[1024,256]{1,0:T(8,128)S(1)}, bf16[1024,256]{1,0:T(8,128)(2,1)S(1)}, bf16[768,1024]{1,0:T(8,128)(2,1)S(1)}, b...) custom-call(bf16[352,256]{1,0:T(8,128)(2,1)S(1)} %copy-done.7, ...), custom_call_target="tpu_custom_call" | custom-call | flops 1000 | bytes 1024 | tf_op jit(solution)/shard_map/attn_fwd/pallas_call | solution.py:552
  45.3 4.5 %mlp_both.1 = (f32[1024,256]{1,0:T(8,128)}, f32[1024,256]{1,0:T(8,128)S(1)}, bf16[4,256,256]{2,1,0:T(8,128)(2,1)S(1)}, bf16[4,256,256]{2,1,0:T(8,128)(2,1)S(1)}, f32[8,256]{1,0:T(8,128)S(1)}) custom-call(bf16[2,256,256]{2,1,0:T(8,128)(2,1)S(1)} %copy-done, bf16[2,256,256]{2,1,0:T(8,128)(2,1)S(1)} %copy-done.1, ...), custom_call_target="tpu_custom_call" | custom-call | flops 1000 | bytes 1024 | tf_op jit(solution)/shard_map/mlp_both/pallas_call | solution.py:552
  49.8 0.3 collective-permute-start.13
  50.1 1.1 attn_pre.2
  51.2 0.5 collective-permute-done.13.got
  51.8 0.1 core_split.2
  51.9 1.3 %collective-permute-start.16 = (bf16[4,128,256]{2,1,0:T(8,128)(2,1)S(1)}, bf16[4,128,256]{2,1,0:T(8,128)(2,1)S(1)}, u32[]{:S(2)}, u32[]{:S(2)}) collective-permute-start(bf16[4,128,256]{2,1,0:T(8,128)(2,1)S(1)} %get-tuple-element.134), channel_id=1, source_target_pairs={{0,8},{4,12},{8,0},{12,4},{16,24},{20,28},{24,16},{28,20},{1,9},{5... | collective-permute-start | bytes 786440 | tf_op jit(solution)/shard_map/ppermute | solution.py:660
  53.2 4.3 %attn_bwd.1 = (f32[1024,256]{1,0:T(8,128)S(1)}, bf16[4,176,256]{2,1,0:T(8,128)(2,1)S(1)}, bf16[4,176,256]{2,1,0:T(8,128)(2,1)S(1)}) custom-call(bf16[352,256]{1,0:T(8,128)(2,1)S(1)} %copy-done.7, bf16[432,256]{1,0:T(8,128)(2,1)S(1)} %collective-permute-done.refs_1_.refs_2_, bf16[432,256]{1,0:T(8,128)(2,1)S(1)} %collective-permute-done.8.refs_2_.refs_3_, ...), custom_call_target="tpu_custom_call" | custom-call | flops 1000 | bytes 1024 | tf_op jit(solution)/shard_map/attn_bwd/pallas_call | solution.py:552
  57.5 0.6 collective-permute-start.17
  58.1 2.8 %mlp_bwd.1 = (f32[1024,256]{1,0:T(8,128)S(1)}, bf16[4,256,256]{2,1,0:T(8,128)(2,1)S(1)}, bf16[4,256,256]{2,1,0:T(8,128)(2,1)S(1)}, f32[8,256]{1,0:T(8,128)S(1)}) custom-call(bf16[2,256,256]{2,1,0:T(8,128)(2,1)S(1)} %copy-done, bf16[2,256,256]{2,1,0:T(8,128)(2,1)S(1)} %copy-done.1, bf16[384,256]{1,0:T(8,128)(2,1)S(1)} %get-tuple-element.112.refs_2_, ...), custom_call_target="tpu_custom_call" | custom-call | flops 1000 | bytes 1024 | tf_op jit(solution)/shard_map/mlp_bwd/pallas_call | solution.py:552
  61.2 1.4 %collective-permute-start.20 = (bf16[304,256]{1,0:T(8,128)(2,1)S(1)}, bf16[304,256]{1,0:T(8,128)(2,1)S(1)}, u32[]{:S(2)}, u32[]{:S(2)}) collective-permute-start(bf16[304,256]{1,0:T(8,128)(2,1)S(1)} %get-tuple-element.177), channel_id=1, source_target_pairs={{0,3},{1,2},{2,1},{3,0},{4,7},{5,6},{6,5},{7,4},{8,11},{9,10},{10,... | collective-permute-start | bytes 466952 | tf_op jit(solution)/shard_map/ppermute | solution.py:660
  62.6 3.9 %collective-permute-start.19 = (bf16[304,256]{1,0:T(8,128)(2,1)S(1)}, bf16[304,256]{1,0:T(8,128)(2,1)S(1)}, u32[]{:S(2)}, u32[]{:S(2)}) collective-permute-start(bf16[304,256]{1,0:T(8,128)(2,1)S(1)} %get-tuple-element.175), channel_id=1, source_target_pairs={{0,2},{1,3},{2,0},{3,1},{4,6},{5,7},{6,4},{7,5},{8,10},{9,11},{10,... | collective-permute-start | bytes 466952 | tf_op jit(solution)/shard_map/ppermute | solution.py:660
  66.5 1.2 %attn_pre.3 = (bf16[256,1024]{1,0:T(8,128)(2,1)S(1)}, bf16[256,256]{1,0:T(8,128)(2,1)S(1)}, bf16[256,256]{1,0:T(8,128)(2,1)S(1)}, f32[1024,256]{1,0:T(8,128)S(1)...) custom-call(bf16[352,256]{1,0:T(8,128)(2,1)S(1)} %copy-done.6, ...), custom_call_target="tpu_custom_call" | custom-call | flops 1000 | bytes 1024 | tf_op jit(solution)/shard_map/attn_pre/pallas_call | solution.py:552
  67.7 0.1 core_split.3
  67.8 0.3 collective-permute-start.15
  68.1 3.8 %attn_grads.1 = (bf16[768,1024]{1,0:T(8,128)(2,1)S(1)}, bf16[4,176,256]{2,1,0:T(8,128)(2,1)S(1)}, bf16[2,176,256]{2,1,0:T(8,128)(2,1)S(1)}, bf16[2,176,256]{2,1,0:T(8,128)(2,1)S(1)}) custom-call(bf16[352,256]{1,0:T(8,128)(2,1)S(1)} %copy-done.6, bf16[528,256]{1,0:T(8,128)(2,1)S(1)} %get-tuple-element.114.refs_1_, ...), custom_call_target="tpu_custom_call" | custom-call | flops 1000 | bytes 1024 | tf_op jit(solution)/shard_map/attn_grads/pallas_call | solution.py:552
  72.0 3.9 %collective-permute-done.19.refs_2_ = bf16[304,256]{1,0:T(8,128)(2,1)S(1)} collective-permute-done((bf16[304,256]{1,0:T(8,128)(2,1)S(1)}, bf16[304,256]{1,0:T(8,128)(2,1)S(1)}, u32[]{:S(2)}, u32[]{:S(2)}) %collective-permute-start.19) | collective-permute-done | bytes 155680 | tf_op jit(solution)/shard_map/ppermute | solution.py:660
  75.9 1.3 %collective-permute-start.21 = (bf16[2,176,256]{2,1,0:T(8,128)(2,1)S(1)}, bf16[2,176,256]{2,1,0:T(8,128)(2,1)S(1)}, u32[]{:S(2)}, u32[]{:S(2)}) collective-permute-start(bf16[2,176,256]{2,1,0:T(8,128)(2,1)S(1)} %get-tuple-element.182), channel_id=1, source_target_pairs={{0,4},{4,0},{8,12},{12,8},{16,20},{20,16},{24,28},{28,24},{1,5},{5... | collective-permute-start | bytes 540680 | tf_op jit(solution)/shard_map/ppermute | solution.py:660
  77.3 1.3 %collective-permute-start.25 = (bf16[176,256]{1,0:T(8,128)(2,1)S(1)}, bf16[176,256]{1,0:T(8,128)(2,1)S(1)}, u32[]{:S(2)}, u32[]{:S(2)}) collective-permute-start(bf16[176,256]{1,0:T(8,128)(2,1)S(1)} %get-tuple-element.191.refs_0_), channel_id=1, source_target_pairs={{0,24},{4,28},{8,16},{12,20},{16,8},{20,12},{24,0},{28,4},{1,25},{... | collective-permute-start | bytes 270344 | tf_op jit(solution)/shard_map/ppermute | solution.py:660
  78.6 0.2 core_sum.3
  78.8 2.2 %collective-permute-start.27 = (bf16[304,256]{1,0:T(8,128)(2,1)S(1)}, bf16[304,256]{1,0:T(8,128)(2,1)S(1)}, u32[]{:S(2)}, u32[]{:S(2)}) collective-permute-start(bf16[304,256]{1,0:T(8,128)(2,1)S(1)} %get-tuple-element.185), channel_id=1, source_target_pairs={{0,1},{1,0},{2,3},{3,2},{4,5},{5,4},{6,7},{7,6},{8,9},{9,8},{10,11... | collective-permute-start | bytes 466952 | tf_op jit(solution)/shard_map/ppermute | solution.py:660
  81.0 0.7 collective-permute-start.28
  81.7 0.6 collective-permute-start.29
  82.3 1.2 %collective-permute-start.24 = (bf16[176,256]{1,0:T(8,128)(2,1)S(1)}, bf16[176,256]{1,0:T(8,128)(2,1)S(1)}, u32[]{:S(2)}, u32[]{:S(2)}) collective-permute-start(bf16[176,256]{1,0:T(8,128)(2,1)S(1)} %get-tuple-element.191.refs_0_), channel_id=1, source_target_pairs={{0,16},{4,20},{8,24},{12,28},{16,0},{20,4},{24,8},{28,12},{1,17},{... | collective-permute-start | bytes 270344 | tf_op jit(solution)/shard_map/ppermute | solution.py:660
  83.5 0.2 collective-permute-start.23
  83.8 2.2 %collective-permute-done.24.refs_2_ = bf16[176,256]{1,0:T(8,128)(2,1)S(1)} collective-permute-done((bf16[176,256]{1,0:T(8,128)(2,1)S(1)}, bf16[176,256]{1,0:T(8,128)(2,1)S(1)}, u32[]{:S(2)}, u32[]{:S(2)}) %collective-permute-start.24) | collective-permute-done | bytes 90144 | tf_op jit(solution)/shard_map/ppermute | solution.py:660
  86.0 1.2 %collective-permute-done.23.refs_1_ = bf16[176,256]{1,0:T(8,128)(2,1)S(1)} collective-permute-done((bf16[176,256]{1,0:T(8,128)(2,1)S(1)}, bf16[176,256]{1,0:T(8,128)(2,1)S(1)}, u32[]{:S(2)}, u32[]{:S(2)}) %collective-permute-start.23) | collective-permute-done | bytes 90144 | tf_op jit(solution)/shard_map/ppermute | solution.py:660
  87.3 2.2 %attn_post.1 = f32[1024,256]{1,0:T(8,128)} custom-call(bf16[352,256]{1,0:T(8,128)(2,1)S(1)} %copy-done.6, bf16[528,256]{1,0:T(8,128)(2,1)S(1)} %get-tuple-element.114.refs_1_, bf16[528,256]{1,0:T(8,128)(2,1)S(1)} %collective-permute-done.5.refs_2_, bf16[768,1024]{1,0:T(8,128)(2,1)S(1)} %get-tuple-element.188.refs_3_, f32[2,256]{1,0:T(2,128)S(1)} %copy-done.11, ...), custom_call_target="tpu_custom_call" | custom-call | flops 1000 | bytes 1024 | tf_op jit(solution)/shard_map/attn_post/pallas_call | solution.py:552
  89.5 6.2 %collective-permute-done.29.refs_4_ = bf16[304,256]{1,0:T(8,128)(2,1)S(1)} collective-permute-done((bf16[304,256]{1,0:T(8,128)(2,1)S(1)}, bf16[304,256]{1,0:T(8,128)(2,1)S(1)}, u32[]{:S(2)}, u32[]{:S(2)}) %collective-permute-start.29) | collective-permute-done | bytes 155680 | tf_op jit(solution)/shard_map/ppermute | solution.py:660
  95.8 1.8 %collective-permute-start.31 = (bf16[256,256]{1,0:T(8,128)(2,1)S(1)}, bf16[256,256]{1,0:T(8,128)(2,1)S(1)}, u32[]{:S(2)}, u32[]{:S(2)}) collective-permute-start(bf16[256,256]{1,0:T(8,128)(2,1)S(1)} %get-tuple-element.197.high), channel_id=1, source_target_pairs={{0,16},{4,20},{8,24},{12,28},{16,0},{20,4},{24,8},{28,12},{1,17},{... | collective-permute-start | bytes 393224 | tf_op jit(solution)/shard_map/ppermute | solution.py:660
  97.6 3.7 %collective-permute-done.30.low_got = bf16[176,256]{1,0:T(8,128)(2,1)S(1)} collective-permute-done((bf16[176,256]{1,0:T(8,128)(2,1)S(1)}, bf16[176,256]{1,0:T(8,128)(2,1)S(1)}, u32[]{:S(2)}, u32[]{:S(2)}) %collective-permute-start.30) | collective-permute-done | bytes 90144 | tf_op jit(solution)/shard_map/ppermute | solution.py:660
  101.5 0.9 collective-permute-start.32
  102.3 2.6 %collective-permute-done.32.low_got = bf16[176,256]{1,0:T(8,128)(2,1)S(1)} collective-permute-done((bf16[176,256]{1,0:T(8,128)(2,1)S(1)}, bf16[176,256]{1,0:T(8,128)(2,1)S(1)}, u32[]{:S(2)}, u32[]{:S(2)}) %collective-permute-start.32) | collective-permute-done | bytes 90144 | tf_op jit(solution)/shard_map/ppermute | solution.py:660
  104.9 0.4 collective-permute-done.33.high_got
  105.3 3.5 %collective-permute-start.34 = (bf16[512,256]{1,0:T(8,128)(2,1)S(1)}, bf16[512,256]{1,0:T(8,128)(2,1)S(1)}, u32[]{:S(2)}, u32[]{:S(2)}) collective-permute-start(bf16[512,256]{1,0:T(8,128)(2,1)S(1)} %get-tuple-element.200.high), channel_id=1, source_target_pairs={{0,4},{4,0},{8,12},{12,8},{16,20},{20,16},{24,28},{28,24},{1,5},{5... | collective-permute-start | bytes 786440 | tf_op jit(solution)/shard_map/ppermute | solution.py:660
  108.9 0.4 collective-permute-start.35
  109.3 0.8 collective-permute-done.26.low_other
  110.1 0.2 collective-permute-done.35.late_other
  110.3 1.3 %finish.1 = (f32[2,3,64,256]{3,2,1,0:T(8,128)}, f32[2,64,256]{2,1,0:T(8,128)}, f32[2,256,256]{2,1,0:T(8,128)}, f32[2,256,256]{2,1,0:T(8,128)}, f32[2,64,256]{2,1...) custom-call(bf16[176,256]{1,0:T(8,128)(2,1)S(1)} %four_sum.1.low, ...), custom_call_target="tpu_custom_call" | custom-call | flops 1000 | bytes 1024 | tf_op jit(solution)/shard_map/finish/pallas_call | solution.py:637
  (57 shorter events, 1.1 us)
Async XLA Ops:
  3.3 12.0 %collective-permute-start.3 = (bf16[304,256]{1,0:T(8,128)(2,1)}, bf16[304,256]{1,0:T(8,128)(2,1)S(1)}, u32[]{:S(2)}, u32[]{:S(2)}) collective-permute-start(bf16[304,256]{1,0:T(8,128)(2,1)} %get-tuple-element.111), channel_id=1, source_target_pairs={{0,3},{1,2},{2,1},{3,0},{4,7},{5,6},{6,5},{7,4},{8,11},{9,10},{10,... | collective-permute-start | bytes 466952 | tf_op jit(solution)/shard_map/ppermute | solution.py:660
  4.7 13.0 %collective-permute-start.2 = (bf16[304,256]{1,0:T(8,128)(2,1)}, bf16[304,256]{1,0:T(8,128)(2,1)S(1)}, u32[]{:S(2)}, u32[]{:S(2)}) collective-permute-start(bf16[304,256]{1,0:T(8,128)(2,1)} %get-tuple-element.111), channel_id=1, source_target_pairs={{0,2},{1,3},{2,0},{3,1},{4,6},{5,7},{6,4},{7,5},{8,10},{9,11},{10,... | collective-permute-start | bytes 466952 | tf_op jit(solution)/shard_map/ppermute | solution.py:660
  5.8 11.9 %collective-permute-start.1 = (bf16[304,256]{1,0:T(8,128)(2,1)}, bf16[304,256]{1,0:T(8,128)(2,1)S(1)}, u32[]{:S(2)}, u32[]{:S(2)}) collective-permute-start(bf16[304,256]{1,0:T(8,128)(2,1)} %get-tuple-element.111), channel_id=1, source_target_pairs={{0,1},{1,0},{2,3},{3,2},{4,5},{5,4},{6,7},{7,6},{8,9},{9,8},{10,11... | collective-permute-start | bytes 466952 | tf_op jit(solution)/shard_map/ppermute | solution.py:660
  17.7 6.4 %collective-permute-start.5 = (bf16[528,256]{1,0:T(8,128)(2,1)S(1)}, bf16[528,256]{1,0:T(8,128)(2,1)S(1)}, u32[]{:S(2)}, u32[]{:S(2)}) collective-permute-start(bf16[528,256]{1,0:T(8,128)(2,1)S(1)} %get-tuple-element.114.refs_1_), channel_id=1, source_target_pairs={{0,4},{4,0},{8,12},{12,8},{16,20},{20,16},{24,28},{28,24},{1,5},{5... | collective-permute-start | bytes 811016 | tf_op jit(solution)/shard_map/ppermute | solution.py:660
  19.3 17.0 %collective-permute-start.9 = (bf16[432,256]{1,0:T(8,128)(2,1)}, bf16[432,256]{1,0:T(8,128)(2,1)S(1)}, u32[]{:S(2)}, u32[]{:S(2)}) collective-permute-start(bf16[432,256]{1,0:T(8,128)(2,1)} %get-tuple-element.110), channel_id=1, source_target_pairs={{0,3},{1,2},{2,1},{3,0},{4,7},{5,6},{6,5},{7,4},{8,11},{9,10},{10,... | collective-permute-start | bytes 663560 | tf_op jit(solution)/shard_map/ppermute | solution.py:660
  19.5 19.3 %collective-permute-start.8 = (bf16[432,256]{1,0:T(8,128)(2,1)}, bf16[432,256]{1,0:T(8,128)(2,1)S(1)}, u32[]{:S(2)}, u32[]{:S(2)}) collective-permute-start(bf16[432,256]{1,0:T(8,128)(2,1)} %get-tuple-element.110), channel_id=1, source_target_pairs={{0,2},{1,3},{2,0},{3,1},{4,6},{5,7},{6,4},{7,5},{8,10},{9,11},{10,... | collective-permute-start | bytes 663560 | tf_op jit(solution)/shard_map/ppermute | solution.py:660
  23.4 15.4 %collective-permute-start = (bf16[432,256]{1,0:T(8,128)(2,1)}, bf16[432,256]{1,0:T(8,128)(2,1)S(1)}, u32[]{:S(2)}, u32[]{:S(2)}) collective-permute-start(bf16[432,256]{1,0:T(8,128)(2,1)} %get-tuple-element.110), channel_id=1, source_target_pairs={{0,1},{1,0},{2,3},{3,2},{4,5},{5,4},{6,7},{7,6},{8,9},{9,8},{10,11... | collective-permute-start | bytes 663560 | tf_op jit(solution)/shard_map/ppermute | solution.py:660
  23.5 9.4 %collective-permute-start.6 = (bf16[384,256]{1,0:T(8,128)(2,1)S(1)}, bf16[384,256]{1,0:T(8,128)(2,1)S(1)}, u32[]{:S(2)}, u32[]{:S(2)}) collective-permute-start(bf16[384,256]{1,0:T(8,128)(2,1)S(1)} %get-tuple-element.112.refs_2_), channel_id=1, source_target_pairs={{0,4},{4,0},{8,12},{12,8},{16,20},{20,16},{24,28},{28,24},{1,5},{5... | collective-permute-start | bytes 589832 | tf_op jit(solution)/shard_map/ppermute | solution.py:660
  24.2 8.4 %collective-permute-start.4 = (bf16[384,256]{1,0:T(8,128)(2,1)S(1)}, bf16[384,256]{1,0:T(8,128)(2,1)S(1)}, u32[]{:S(2)}, u32[]{:S(2)}) collective-permute-start(bf16[384,256]{1,0:T(8,128)(2,1)S(1)} %get-tuple-element.112.refs_2_), channel_id=1, source_target_pairs={{0,8},{4,12},{8,0},{12,4},{16,24},{20,28},{24,16},{28,20},{1,9},{5... | collective-permute-start | bytes 589832 | tf_op jit(solution)/shard_map/ppermute | solution.py:660
  25.4 1.0 copy-start.3
  26.4 0.9 copy-start.5
  27.3 0.8 copy-start.8
  28.1 0.7 copy-start.10
  28.8 5.3 %copy-start = (bf16[2,256,256]{2,1,0:T(8,128)(2,1)S(1)}, bf16[2,256,256]{2,1,0:T(8,128)(2,1)}, u32[]{:S(2)}) copy-start(bf16[2,256,256]{2,1,0:T(8,128)(2,1)} %refs_0_.5) | copy-start | bytes 786436
  28.8 5.3 %copy-start.1 = (bf16[2,256,256]{2,1,0:T(8,128)(2,1)S(1)}, bf16[2,256,256]{2,1,0:T(8,128)(2,1)}, u32[]{:S(2)}) copy-start(bf16[2,256,256]{2,1,0:T(8,128)(2,1)} %refs_1_.5) | copy-start | bytes 786436
  28.8 5.3 %copy-start.12 = (f32[2,256]{1,0:T(2,128)S(1)}, f32[2,256]{1,0:T(2,128)}, u32[]{:S(2)}) copy-start(f32[2,256]{1,0:T(2,128)} %refs_10_.3) | copy-start | bytes 6148
  32.6 1.5 %collective-permute-start.7 = (bf16[384,256]{1,0:T(8,128)(2,1)S(1)}, bf16[384,256]{1,0:T(8,128)(2,1)S(1)}, u32[]{:S(2)}, u32[]{:S(2)}) collective-permute-start(bf16[384,256]{1,0:T(8,128)(2,1)S(1)} %collective-permute-done.4.refs_3_), channel_id=1, source_target_pairs={{0,4},{4,0},{8,12},{12,8},{16,20},{20,16},{24,28},{28,24},{1,5},{5... | collective-permute-start | bytes 589832 | tf_op jit(solution)/shard_map/ppermute | solution.py:660
  34.1 7.4 %copy-start.7 = (bf16[352,256]{1,0:T(8,128)(2,1)S(1)}, bf16[352,256]{1,0:T(8,128)(2,1)}, u32[]{:S(2)}) copy-start(bf16[352,256]{1,0:T(8,128)(2,1)} %get-tuple-element.123.refs_0_) | copy-start | bytes 540676
  34.1 7.4 %copy-start.9 = (bf16[64,256]{1,0:T(8,128)(2,1)S(1)}, bf16[64,256]{1,0:T(8,128)(2,1)}, u32[]{:S(2)}) copy-start(bf16[64,256]{1,0:T(8,128)(2,1)} %get-tuple-element.156.refs_4_.refs_8_.refs_7_.refs_3_) | copy-start | bytes 98308
  34.1 7.4 %copy-start.11 = (f32[2,256]{1,0:T(2,128)S(1)}, f32[2,256]{1,0:T(2,128)}, u32[]{:S(2)}) copy-start(f32[2,256]{1,0:T(2,128)} %refs_4_.1) | copy-start | bytes 6148
  36.3 9.0 %copy-start.2 = (bf16[1024,256]{1,0:T(8,128)(2,1)S(1)}, bf16[1024,256]{1,0:T(8,128)(2,1)}, u32[]{:S(2)}) copy-start(bf16[1024,256]{1,0:T(8,128)(2,1)} %refs_7_.2) | copy-start | bytes 1572868
  38.9 2.0 %collective-permute-start.10 = (bf16[432,256]{1,0:T(8,128)(2,1)S(1)}, bf16[432,256]{1,0:T(8,128)(2,1)S(1)}, u32[]{:S(2)}, u32[]{:S(2)}) collective-permute-start(bf16[432,256]{1,0:T(8,128)(2,1)S(1)} %collective-permute-done.refs_1_.refs_2_), channel_id=1, source_target_pairs={{0,4},{4,0},{8,12},{12,8},{16,20},{20,16},{24,28},{28,24},{1,5},{5... | collective-permute-start | bytes 663560 | tf_op jit(solution)/shard_map/ppermute | solution.py:660
  39.7 1.5 %collective-permute-start.11 = (bf16[432,256]{1,0:T(8,128)(2,1)S(1)}, bf16[432,256]{1,0:T(8,128)(2,1)S(1)}, u32[]{:S(2)}, u32[]{:S(2)}) collective-permute-start(bf16[432,256]{1,0:T(8,128)(2,1)S(1)} %collective-permute-done.8.refs_2_.refs_3_), channel_id=1, source_target_pairs={{0,4},{4,0},{8,12},{12,8},{16,20},{20,16},{24,28},{28,24},{1,5},{5... | collective-permute-start | bytes 663560 | tf_op jit(solution)/shard_map/ppermute | solution.py:660
  39.7 1.8 %collective-permute-start.12 = (bf16[432,256]{1,0:T(8,128)(2,1)S(1)}, bf16[432,256]{1,0:T(8,128)(2,1)S(1)}, u32[]{:S(2)}, u32[]{:S(2)}) collective-permute-start(bf16[432,256]{1,0:T(8,128)(2,1)S(1)} %collective-permute-done.9.refs_3_.refs_4_), channel_id=1, source_target_pairs={{0,4},{4,0},{8,12},{12,8},{16,20},{20,16},{24,28},{28,24},{1,5},{5... | collective-permute-start | bytes 663560 | tf_op jit(solution)/shard_map/ppermute | solution.py:660
  49.8 2.0 %collective-permute-start.13 = (bf16[4,256,256]{2,1,0:T(8,128)(2,1)S(1)}, bf16[4,256,256]{2,1,0:T(8,128)(2,1)S(1)}, u32[]{:S(2)}, u32[]{:S(2)}) collective-permute-start(bf16[4,256,256]{2,1,0:T(8,128)(2,1)S(1)} %get-tuple-element.128), channel_id=1, source_target_pairs={{0,4},{4,0},{8,12},{12,8},{16,20},{20,16},{24,28},{28,24},{1,5},{5... | collective-permute-start | bytes 1572872 | tf_op jit(solution)/shard_map/ppermute | solution.py:660
  51.9 9.1 %collective-permute-start.16 = (bf16[4,128,256]{2,1,0:T(8,128)(2,1)S(1)}, bf16[4,128,256]{2,1,0:T(8,128)(2,1)S(1)}, u32[]{:S(2)}, u32[]{:S(2)}) collective-permute-start(bf16[4,128,256]{2,1,0:T(8,128)(2,1)S(1)} %get-tuple-element.134), channel_id=1, source_target_pairs={{0,8},{4,12},{8,0},{12,4},{16,24},{20,28},{24,16},{28,20},{1,9},{5... | collective-permute-start | bytes 786440 | tf_op jit(solution)/shard_map/ppermute | solution.py:660
  57.5 3.6 %collective-permute-start.17 = (bf16[4,176,256]{2,1,0:T(8,128)(2,1)S(1)}, bf16[4,176,256]{2,1,0:T(8,128)(2,1)S(1)}, u32[]{:S(2)}, u32[]{:S(2)}) collective-permute-start(bf16[4,176,256]{2,1,0:T(8,128)(2,1)S(1)} %get-tuple-element.169), channel_id=1, source_target_pairs={{0,4},{4,0},{8,12},{12,8},{16,20},{20,16},{24,28},{28,24},{1,5},{5... | collective-permute-start | bytes 1081352 | tf_op jit(solution)/shard_map/ppermute | solution.py:660
  60.9 6.8 %collective-permute-start.14 = (bf16[4,256,256]{2,1,0:T(8,128)(2,1)S(1)}, bf16[4,256,256]{2,1,0:T(8,128)(2,1)S(1)}, u32[]{:S(2)}, u32[]{:S(2)}) collective-permute-start(bf16[4,256,256]{2,1,0:T(8,128)(2,1)S(1)} %get-tuple-element.149), channel_id=1, source_target_pairs={{0,4},{4,0},{8,12},{12,8},{16,20},{20,16},{24,28},{28,24},{1,5},{5... | collective-permute-start | bytes 1572872 | tf_op jit(solution)/shard_map/ppermute | solution.py:660
  61.0 5.5 %copy-start.4 = (bf16[1024,256]{1,0:T(8,128)(2,1)S(1)}, bf16[1024,256]{1,0:T(8,128)(2,1)}, u32[]{:S(2)}) copy-start(bf16[1024,256]{1,0:T(8,128)(2,1)} %refs_5_.5) | copy-start | bytes 1572868
  61.0 5.5 %copy-start.6 = (bf16[352,256]{1,0:T(8,128)(2,1)S(1)}, bf16[352,256]{1,0:T(8,128)(2,1)}, u32[]{:S(2)}) copy-start(bf16[352,256]{1,0:T(8,128)(2,1)} %get-tuple-element.113.refs_0_) | copy-start | bytes 540676
  61.2 10.7 %collective-permute-start.20 = (bf16[304,256]{1,0:T(8,128)(2,1)S(1)}, bf16[304,256]{1,0:T(8,128)(2,1)S(1)}, u32[]{:S(2)}, u32[]{:S(2)}) collective-permute-start(bf16[304,256]{1,0:T(8,128)(2,1)S(1)} %get-tuple-element.177), channel_id=1, source_target_pairs={{0,3},{1,2},{2,1},{3,0},{4,7},{5,6},{6,5},{7,4},{8,11},{9,10},{10,... | collective-permute-start | bytes 466952 | tf_op jit(solution)/shard_map/ppermute | solution.py:660
  62.6 13.3 %collective-permute-start.19 = (bf16[304,256]{1,0:T(8,128)(2,1)S(1)}, bf16[304,256]{1,0:T(8,128)(2,1)S(1)}, u32[]{:S(2)}, u32[]{:S(2)}) collective-permute-start(bf16[304,256]{1,0:T(8,128)(2,1)S(1)} %get-tuple-element.175), channel_id=1, source_target_pairs={{0,2},{1,3},{2,0},{3,1},{4,6},{5,7},{6,4},{7,5},{8,10},{9,11},{10,... | collective-permute-start | bytes 466952 | tf_op jit(solution)/shard_map/ppermute | solution.py:660
  66.5 9.4 %collective-permute-start.18 = (bf16[304,256]{1,0:T(8,128)(2,1)S(1)}, bf16[304,256]{1,0:T(8,128)(2,1)S(1)}, u32[]{:S(2)}, u32[]{:S(2)}) collective-permute-start(bf16[304,256]{1,0:T(8,128)(2,1)S(1)} %get-tuple-element.173), channel_id=1, source_target_pairs={{0,1},{1,0},{2,3},{3,2},{4,5},{5,4},{6,7},{7,6},{8,9},{9,8},{10,11... | collective-permute-start | bytes 466952 | tf_op jit(solution)/shard_map/ppermute | solution.py:660
  67.8 10.8 %collective-permute-start.15 = (bf16[4,128,256]{2,1,0:T(8,128)(2,1)S(1)}, bf16[4,128,256]{2,1,0:T(8,128)(2,1)S(1)}, u32[]{:S(2)}, u32[]{:S(2)}) collective-permute-start(bf16[4,128,256]{2,1,0:T(8,128)(2,1)S(1)} %get-tuple-element.155), channel_id=1, source_target_pairs={{0,8},{4,12},{8,0},{12,4},{16,24},{20,28},{24,16},{28,20},{1,9},{5... | collective-permute-start | bytes 786440 | tf_op jit(solution)/shard_map/ppermute | solution.py:660
  75.9 2.7 %collective-permute-start.21 = (bf16[2,176,256]{2,1,0:T(8,128)(2,1)S(1)}, bf16[2,176,256]{2,1,0:T(8,128)(2,1)S(1)}, u32[]{:S(2)}, u32[]{:S(2)}) collective-permute-start(bf16[2,176,256]{2,1,0:T(8,128)(2,1)S(1)} %get-tuple-element.182), channel_id=1, source_target_pairs={{0,4},{4,0},{8,12},{12,8},{16,20},{20,16},{24,28},{28,24},{1,5},{5... | collective-permute-start | bytes 540680 | tf_op jit(solution)/shard_map/ppermute | solution.py:660
  77.2 1.4 %collective-permute-start.22 = (bf16[2,176,256]{2,1,0:T(8,128)(2,1)S(1)}, bf16[2,176,256]{2,1,0:T(8,128)(2,1)S(1)}, u32[]{:S(2)}, u32[]{:S(2)}) collective-permute-start(bf16[2,176,256]{2,1,0:T(8,128)(2,1)S(1)} %get-tuple-element.183), channel_id=1, source_target_pairs={{0,4},{4,0},{8,12},{12,8},{16,20},{20,16},{24,28},{28,24},{1,5},{5... | collective-permute-start | bytes 540680 | tf_op jit(solution)/shard_map/ppermute | solution.py:660
  77.3 6.2 %collective-permute-start.25 = (bf16[176,256]{1,0:T(8,128)(2,1)S(1)}, bf16[176,256]{1,0:T(8,128)(2,1)S(1)}, u32[]{:S(2)}, u32[]{:S(2)}) collective-permute-start(bf16[176,256]{1,0:T(8,128)(2,1)S(1)} %get-tuple-element.191.refs_0_), channel_id=1, source_target_pairs={{0,24},{4,28},{8,16},{12,20},{16,8},{20,12},{24,0},{28,4},{1,25},{... | collective-permute-start | bytes 270344 | tf_op jit(solution)/shard_map/ppermute | solution.py:660
  78.8 10.7 %collective-permute-start.27 = (bf16[304,256]{1,0:T(8,128)(2,1)S(1)}, bf16[304,256]{1,0:T(8,128)(2,1)S(1)}, u32[]{:S(2)}, u32[]{:S(2)}) collective-permute-start(bf16[304,256]{1,0:T(8,128)(2,1)S(1)} %get-tuple-element.185), channel_id=1, source_target_pairs={{0,1},{1,0},{2,3},{3,2},{4,5},{5,4},{6,7},{7,6},{8,9},{9,8},{10,11... | collective-permute-start | bytes 466952 | tf_op jit(solution)/shard_map/ppermute | solution.py:660
  81.0 8.5 %collective-permute-start.28 = (bf16[304,256]{1,0:T(8,128)(2,1)S(1)}, bf16[304,256]{1,0:T(8,128)(2,1)S(1)}, u32[]{:S(2)}, u32[]{:S(2)}) collective-permute-start(bf16[304,256]{1,0:T(8,128)(2,1)S(1)} %get-tuple-element.186), channel_id=1, source_target_pairs={{0,2},{1,3},{2,0},{3,1},{4,6},{5,7},{6,4},{7,5},{8,10},{9,11},{10,... | collective-permute-start | bytes 466952 | tf_op jit(solution)/shard_map/ppermute | solution.py:660
  81.7 14.1 %collective-permute-start.29 = (bf16[304,256]{1,0:T(8,128)(2,1)S(1)}, bf16[304,256]{1,0:T(8,128)(2,1)S(1)}, u32[]{:S(2)}, u32[]{:S(2)}) collective-permute-start(bf16[304,256]{1,0:T(8,128)(2,1)S(1)} %get-tuple-element.187), channel_id=1, source_target_pairs={{0,3},{1,2},{2,1},{3,0},{4,7},{5,6},{6,5},{7,4},{8,11},{9,10},{10,... | collective-permute-start | bytes 466952 | tf_op jit(solution)/shard_map/ppermute | solution.py:660
  82.3 3.7 %collective-permute-start.24 = (bf16[176,256]{1,0:T(8,128)(2,1)S(1)}, bf16[176,256]{1,0:T(8,128)(2,1)S(1)}, u32[]{:S(2)}, u32[]{:S(2)}) collective-permute-start(bf16[176,256]{1,0:T(8,128)(2,1)S(1)} %get-tuple-element.191.refs_0_), channel_id=1, source_target_pairs={{0,16},{4,20},{8,24},{12,28},{16,0},{20,4},{24,8},{28,12},{1,17},{... | collective-permute-start | bytes 270344 | tf_op jit(solution)/shard_map/ppermute | solution.py:660
  83.5 3.7 %collective-permute-start.23 = (bf16[176,256]{1,0:T(8,128)(2,1)S(1)}, bf16[176,256]{1,0:T(8,128)(2,1)S(1)}, u32[]{:S(2)}, u32[]{:S(2)}) collective-permute-start(bf16[176,256]{1,0:T(8,128)(2,1)S(1)} %get-tuple-element.191.refs_0_), channel_id=1, source_target_pairs={{0,8},{4,12},{8,0},{12,4},{16,24},{20,28},{24,16},{28,20},{1,9},{5... | collective-permute-start | bytes 270344 | tf_op jit(solution)/shard_map/ppermute | solution.py:660
  95.8 5.5 %collective-permute-start.31 = (bf16[256,256]{1,0:T(8,128)(2,1)S(1)}, bf16[256,256]{1,0:T(8,128)(2,1)S(1)}, u32[]{:S(2)}, u32[]{:S(2)}) collective-permute-start(bf16[256,256]{1,0:T(8,128)(2,1)S(1)} %get-tuple-element.197.high), channel_id=1, source_target_pairs={{0,16},{4,20},{8,24},{12,28},{16,0},{20,4},{24,8},{28,12},{1,17},{... | collective-permute-start | bytes 393224 | tf_op jit(solution)/shard_map/ppermute | solution.py:660
  97.6 3.7 %collective-permute-start.30 = (bf16[176,256]{1,0:T(8,128)(2,1)S(1)}, bf16[176,256]{1,0:T(8,128)(2,1)S(1)}, u32[]{:S(2)}, u32[]{:S(2)}) collective-permute-start(bf16[176,256]{1,0:T(8,128)(2,1)S(1)} %get-tuple-element.196.low), channel_id=1, source_target_pairs={{0,8},{4,12},{8,0},{12,4},{16,24},{20,28},{24,16},{28,20},{1,9},{5... | collective-permute-start | bytes 270344 | tf_op jit(solution)/shard_map/ppermute | solution.py:660
  101.4 3.9 %collective-permute-start.33 = (bf16[256,256]{1,0:T(8,128)(2,1)S(1)}, bf16[256,256]{1,0:T(8,128)(2,1)S(1)}, u32[]{:S(2)}, u32[]{:S(2)}) collective-permute-start(bf16[256,256]{1,0:T(8,128)(2,1)S(1)} %get-tuple-element.199.high), channel_id=1, source_target_pairs={{0,8},{4,12},{8,0},{12,4},{16,24},{20,28},{24,16},{28,20},{1,9},{5... | collective-permute-start | bytes 393224 | tf_op jit(solution)/shard_map/ppermute | solution.py:660
  101.5 3.4 %collective-permute-start.32 = (bf16[176,256]{1,0:T(8,128)(2,1)S(1)}, bf16[176,256]{1,0:T(8,128)(2,1)S(1)}, u32[]{:S(2)}, u32[]{:S(2)}) collective-permute-start(bf16[176,256]{1,0:T(8,128)(2,1)S(1)} %get-tuple-element.198.low), channel_id=1, source_target_pairs={{0,16},{4,20},{8,24},{12,28},{16,0},{20,4},{24,8},{28,12},{1,17},{... | collective-permute-start | bytes 270344 | tf_op jit(solution)/shard_map/ppermute | solution.py:660
  105.3 5.0 %collective-permute-start.34 = (bf16[512,256]{1,0:T(8,128)(2,1)S(1)}, bf16[512,256]{1,0:T(8,128)(2,1)S(1)}, u32[]{:S(2)}, u32[]{:S(2)}) collective-permute-start(bf16[512,256]{1,0:T(8,128)(2,1)S(1)} %get-tuple-element.200.high), channel_id=1, source_target_pairs={{0,4},{4,0},{8,12},{12,8},{16,20},{20,16},{24,28},{28,24},{1,5},{5... | collective-permute-start | bytes 786440 | tf_op jit(solution)/shard_map/ppermute | solution.py:660
  108.8 1.3 %collective-permute-start.26 = (bf16[176,256]{1,0:T(8,128)(2,1)S(1)}, bf16[176,256]{1,0:T(8,128)(2,1)S(1)}, u32[]{:S(2)}, u32[]{:S(2)}) collective-permute-start(bf16[176,256]{1,0:T(8,128)(2,1)S(1)} %four_sum.1.low), channel_id=1, source_target_pairs={{0,4},{4,0},{8,12},{12,8},{16,20},{20,16},{24,28},{28,24},{1,5},{5... | collective-permute-start | bytes 270344 | tf_op jit(solution)/shard_map/ppermute | solution.py:660
  108.9 1.4 %collective-permute-start.35 = (bf16[176,256]{1,0:T(8,128)(2,1)S(1)}, bf16[176,256]{1,0:T(8,128)(2,1)S(1)}, u32[]{:S(2)}, u32[]{:S(2)}) collective-permute-start(bf16[176,256]{1,0:T(8,128)(2,1)S(1)} %get-tuple-element.201.late), channel_id=1, source_target_pairs={{0,4},{4,0},{8,12},{12,8},{16,20},{20,16},{24,28},{28,24},{1,5},{5... | collective-permute-start | bytes 270344 | tf_op jit(solution)/shard_map/ppermute | solution.py:660

commit v5 on v4

--- a/solution.py
+++ b/solution.py
@@ -72,30 +72,32 @@
     return (lax.axis_index("dp") >> 1) & 1
 
 
-def place_pieces(own, parts, dst, first, rows):
+def place_pieces(own, parts, dst):
     at = 0
     for ref in own:
         dst[0, at:at + ref.shape[0], :] = ref
         at += ref.shape[0]
-    for start, refs in parts:
-        for m, ref in enumerate(refs):
-            dst[m + 1, pl.ds(pl.multiple_of(start, 16), rows), :] = ref[first:first + rows, :]
+    for place, rows, ref in parts:
+        for m in range(3):
+            dst[m + 1, pl.ds(pl.multiple_of(place * rows, 16), rows), :] = ref[m * rows:(m + 1) * rows, :]
 
 
 def parts_of(pieces, rows):
     c, x = half_index(), quarter_index()
-    if len(pieces) == 6:
-        return [(c * rows, pieces[0:3]), ((1 - c) * rows, pieces[3:6])]
-    places = [c, 1 - c] if len(pieces) == 2 else [2 * i + j for i, j in ((c, x), (c, 1 - x), (1 - c, x), (1 - c, 1 - x))]
-    return [(place * rows, [ref.at[pl.ds(m * rows, rows)] for m in range(3)]) for place, ref in zip(places, pieces)]
-
-
-def place_attn_pieces(layer, pieces, wa):
-    place_pieces((pieces[0][...],), parts_of(pieces[1:], 176), wa, 256 * layer, 176)
+    if len(pieces) == 2:
+        places = [c, 1 - c]
+    else:
+        each = len(pieces) // 4
+        places = [each * (2 * i + j) + part for i, j in ((c, x), (c, 1 - x), (1 - c, x), (1 - c, 1 - x)) for part in range(each)]
+    return [(place, rows, ref) for place, ref in zip(places, pieces)]
+
+
+def place_attn_pieces(pieces, wa):
+    place_pieces((pieces[0][...],), parts_of(pieces[1:], 176), wa)
 
 
 def place_qkv(layer, pieces, wa, wq):
-    place_attn_pieces(layer, pieces, wa)
+    place_attn_pieces(pieces, wa)
     side_by_side(wa, wq)
 
 
@@ -105,7 +107,7 @@
 
 
 def place_attn(layer, pieces, wa, w_cross, w_out):
-    place_attn_pieces(layer, pieces, wa)
+    place_attn_pieces(pieces, wa)
     total = jnp.zeros((1, 256), F32)
     for m in range(4):
         place = pl.multiple_of((head_index() ^ m) * HD, HD)
@@ -116,8 +118,7 @@
 
 
 def place_mlp(layer, pieces, wm, up_all, down_all):
-    rows = 256 if len(pieces) == 8 else 128
-    place_pieces((pieces[0][layer], pieces[1][layer]), parts_of(pieces[2:], rows), wm, 0, rows)
+    place_pieces((pieces[0][layer], pieces[1][layer]), parts_of(pieces[2:], 512 // (len(pieces) - 2)), wm)
     for m in range(4):
         up_all[:, m * 256:(m + 1) * 256] = wm[m, 0:256, :]
         down_all[m * 256:(m + 1) * 256, :] = wm[m, 256:512, :]
@@ -383,7 +384,7 @@
     return high, (x - high.astype(F32)).astype(BF)
 
 
-def pack_kernel(lens, qkv, cross, out, up, down, b, own0, own1, first_l0, half_l1, mask, sems):
+def pack_kernel(lens, qkv, cross, out, up, down, b, own0, own1, group0, group1, mask, sems):
     copies = []
     for l, own in ((0, own0), (1, own1)):
         for t in range(3):
@@ -396,8 +397,8 @@
     x = pl.multiple_of(quarter_index() * 128, 16)
 
     def mlp_parts(weight):
-        return (pltpu.make_async_copy(weight.at[0, pl.ds(x, 128)], first_l0.at[pl.ds(176, 128)], sems.at[1]),
-                pltpu.make_async_copy(weight.at[1], half_l1.at[pl.ds(0, 256)], sems.at[1]))
+        return [pltpu.make_async_copy(weight.at[l, pl.ds(x, 128)], group.at[pl.ds(176, 128)], sems.at[1])
+                for l, group in ((0, group0), (1, group1))]
 
     @pl.when(half_index() == 0)
     def _():
@@ -423,16 +424,24 @@
     for copy in copies:
         copy.wait()
     at = pl.multiple_of(half_index() * 176, 16)
-    first_l0[0:176, :] = own0[pl.ds(at, 176), :]
-    half_l1[256:432, :] = own1[pl.ds(at, 176), :]
+    group0[0:176, :] = own0[pl.ds(at, 176), :]
+    group1[0:176, :] = own1[pl.ds(at, 176), :]
     for copy in mlp_parts(up):
         copy.wait()
 
 
-def stack_kernel(a, b, c, attn, mlp):
+def bring_kernel(*refs):
+    half = len(refs) // 2
+    for src, dst in zip(refs[:half], refs[half:]):
+        dst[...] = src[...]
+
+
+def stack_kernel(a, b, c, attn, *mlp):
+    rows = 128 // len(mlp)
     for m, ref in enumerate((a, b, c)):
         attn[m * 176:(m + 1) * 176, :] = ref[0:176, :]
-        mlp[m * 128:(m + 1) * 128, :] = ref[176:304, :]
+        for i, out in enumerate(mlp):
+            out[m * rows:(m + 1) * rows, :] = ref[176 + i * rows:176 + (i + 1) * rows, :]
 
 
 def put_sum(out, at, small_at, rows, total):
@@ -701,27 +710,35 @@
 
     def body(tokens, lengths, cotangent, gain_attn, gain_mlp, w_qkv, w_out, w_up, w_down, w_cross, b_cross):
         rows = tokens.shape[0]
-        own0, own1, first_l0, half_l1, mask = pl.pallas_call(
+        own0, own1, group0, group1, mask = pl.pallas_call(
             pack_kernel,
             in_specs=[SMEM] + [ANY] * 5 + [VMEM],
             out_specs=[VMEM] * 5,
-            out_shape=[jax.ShapeDtypeStruct((n, 256), BF) for n in (352, 352, 304, 432)]
+            out_shape=[jax.ShapeDtypeStruct((n, 256), BF) for n in (352, 352, 304, 304)]
             + [jax.ShapeDtypeStruct((rows // 16, 256), BF)],
             scratch_shapes=[pltpu.SemaphoreType.DMA((2,))],
             name="pack",
         )(lengths, w_qkv.transpose(0, 2, 3, 1), w_cross.transpose(0, 2, 1), w_out, w_up, w_down, b_cross)
 
-        l1 = fetch(half_l1)
-        a0, m0 = small_call(stack_kernel, [((528, 256), BF), ((384, 256), BF)], "stack")(*fetch(first_l0))
+        def stack(pieces, arrays):
+            return small_call(stack_kernel, [((528, 256), BF)] + [((384 // arrays, 256), BF)] * arrays, "stack")(*pieces)
+
+        def quarters(own, before):
+            parts = own + [tie(swap(x, "dp", dp_size, 2), before) for x in own]
+            return [w_up, w_down] + parts + [core_swap(x) for x in parts]
+
+        pieces0, pieces1 = fetch(group0), fetch(group1)
+        near = (tokens, mask, gain_attn, own0)
+        tokens, mask, gain_attn, own0 = small_call(bring_kernel, [(x.shape, x.dtype) for x in near], "bring")(*near)
+        a0, *m0 = stack([tie(x, own0) for x in pieces0], 2)
         a0 = [own0, a0, core_swap(a0)]
         mid0, base0, *saved0 = attn_fwd(0, tokens, mask, gain_attn, a0)
-        m0 = [m0, tie(swap(m0, "dp", dp_size, 2), mid0)]
-        m0 = [w_up, w_down] + m0 + [core_swap(x) for x in m0]
+        m0 = quarters(m0, mid0)
         cur1, hid0, slope0 = mlp_fwd(0, mid0, base0, gain_mlp, m0)
-        l1 = [tie(x, cur1) for x in l1]
-        l1 = l1 + [core_swap(x) for x in l1]
-        a1, m1 = [own1] + l1, [w_up, w_down] + l1
+        a1, *m1 = stack([tie(x, cur1) for x in pieces1], 1)
+        a1 = [own1, a1, core_swap(a1)]
         mid1, base1, *saved1 = attn_fwd(1, cur1, mask, gain_attn, a1)
+        m1 = quarters(m1, mid1)
         output, gm1, keep_m1, send_m1, small_m1 = mlp_both(1, mid1, base1, cotangent, gain_mlp, m1)
         pre = attn_pre(1, cotangent, gm1, cur1, saved1, a1)
         keep_m1, send_m1 = split(keep_m1, tie(core_swap(send_m1), pre[0]))

time: 113 us -> 112 us (level)
  waiting for transfers between devices: 37.5 us -> 33.2 us
  starting transfers between devices: 35.1 us -> 39.2 us
    ppermute x36 -> x40, waiting for transfers between devices: 37.5 us -> 33.2 us  [swap(): return lax.ppermute(x, axis, [(i, i ^ mask) for i in range(size)])]
    ppermute x36 -> x40, starting transfers between devices: 35.1 us -> 39.2 us  [swap(): return lax.ppermute(x, axis, [(i, i ^ mask) for i in range(size)])]
    pallas_call x12 -> x14, Pallas kernels: 2.26 us -> 2.3 us  [run(): pl.pallas_call(kernel, in_specs=[VMEM] * len(args), out_specs=[VMEM] * le...]
    unnamed x26 -> x18, local copies, waits for them, and re-layouts: 3.45 us -> 3.42 us
  transfers between devices with their start and end apart: 36 -> 40, of which waited for: 17 -> 18; matrix products, arithmetic and copies ran while one was open for 0% -> 0% of each run, Pallas kernels for 20% -> 23%
where the time goes in v5:
time: 112 us; the launch traced here: 111 us
  starting transfers between devices  39.2 us (35%)
  Pallas kernels  34.4 us (31%)
  waiting for transfers between devices  33.2 us (30%)
  local copies, waits for them, and re-layouts  3.42 us (3%)
    ppermute x40, starting transfers between devices, swap(): return lax.ppermute(x, axis, [(i, i ^ mask) for i in range(size)])  39.2 us
    ppermute x40, waiting for transfers between devices, swap(): return lax.ppermute(x, axis, [(i, i ^ mask) for i in range(size)])  33.2 us
    pallas_call x10, Pallas kernels, call(): pl.pallas_call(kernel, in_specs=[VMEM] * len(args), out_specs=[VMEM] * le...  29.5 us
    unnamed x18, local copies, waits for them, and re-layouts  3.42 us
    pallas_call x1, Pallas kernels, body(): pl.pallas_call(pack_kernel, in_specs=[SMEM] + [ANY] * 5 + [VMEM], out_spe...  2.57 us
    pallas_call x14, Pallas kernels, run(): pl.pallas_call(kernel, in_specs=[VMEM] * len(args), out_specs=[VMEM] * le...  2.3 us
  transfers between devices with their start and end apart: 40, of which 18 were waited for; matrix products, arithmetic and copies ran while one was open for 0% of the time, Pallas kernels for 23%

profile of v5, /device:TPU:9, one launch (start us, length us, event | category | flops | bytes accessed | tf_op | source)
XLA Modules:
  0.0 111.1 jit_solution(6612647314140645782)
XLA Ops:
  0.6 2.6 %pack.1 = (bf16[352,256]{1,0:T(8,128)(2,1)}, bf16[352,256]{1,0:T(8,128)(2,1)}, bf16[304,256]{1,0:T(8,128)(2,1)}, bf16[304,256]{1,0:T(8,128)(2,1)}, bf16[64,256]{1,0:T(8,128)(2,1)}) custom-call(s32[16]{0:T(128)} %lens.1, bf16[2,3,64,256]{3,2,1,0:T(8,128)(2,1)} %bitcast.4, bf16[2,64,256]{2,1,0:T(8,128)(2,1)} %bitcast.5, bf16[2,64,256]{2,1,0:T(8,128)(2,1)} %out.1, ...), custom_call_target="tpu_custom_call" | custom-call | tf_op jit(solution)/shard_map/pack/pallas_call | solution.py:713
  3.2 1.4 %collective-permute-start.3 = (bf16[304,256]{1,0:T(8,128)(2,1)}, bf16[304,256]{1,0:T(8,128)(2,1)S(1)}, u32[]{:S(2)}, u32[]{:S(2)}) collective-permute-start(bf16[304,256]{1,0:T(8,128)(2,1)} %get-tuple-element.123), channel_id=1, source_target_pairs={{0,3},{1,2},{2,1},{3,0},{4,7},{5,6},{6,5},{7,4},{8,11},{9,10},{10,... | collective-permute-start | bytes 466952 | tf_op jit(solution)/shard_map/ppermute | solution.py:669
  4.6 1.1 collective-permute-start.2
  5.7 1.1 collective-permute-start.1
  6.8 1.0 copy-done.4
  7.8 0.9 copy-done.5
  8.7 0.8 copy-done.6
  9.5 0.7 copy-done.8
  10.2 5.0 %collective-permute-done.3.c = bf16[304,256]{1,0:T(8,128)(2,1)S(1)} collective-permute-done((bf16[304,256]{1,0:T(8,128)(2,1)}, bf16[304,256]{1,0:T(8,128)(2,1)S(1)}, u32[]{:S(2)}, u32[]{:S(2)}) %collective-permute-start.3) | collective-permute-done | bytes 155680 | tf_op jit(solution)/shard_map/ppermute | solution.py:669
  15.2 2.4 %collective-permute-done.2.b = bf16[304,256]{1,0:T(8,128)(2,1)S(1)} collective-permute-done((bf16[304,256]{1,0:T(8,128)(2,1)}, bf16[304,256]{1,0:T(8,128)(2,1)S(1)}, u32[]{:S(2)}, u32[]{:S(2)}) %collective-permute-start.2) | collective-permute-done | bytes 155680 | tf_op jit(solution)/shard_map/ppermute | solution.py:669
  17.6 1.6 %collective-permute-start.5 = (bf16[528,256]{1,0:T(8,128)(2,1)S(1)}, bf16[528,256]{1,0:T(8,128)(2,1)S(1)}, u32[]{:S(2)}, u32[]{:S(2)}) collective-permute-start(bf16[528,256]{1,0:T(8,128)(2,1)S(1)} %get-tuple-element.132.refs_1_), channel_id=1, source_target_pairs={{0,4},{4,0},{8,12},{12,8},{16,20},{20,16},{24,28},{28,24},{1,5},{5... | collective-permute-start | bytes 811016 | tf_op jit(solution)/shard_map/ppermute | solution.py:669
  19.2 1.2 %collective-permute-start.4 = (bf16[192,256]{1,0:T(8,128)(2,1)S(1)}, bf16[192,256]{1,0:T(8,128)(2,1)S(1)}, u32[]{:S(2)}, u32[]{:S(2)}) collective-permute-start(bf16[192,256]{1,0:T(8,128)(2,1)S(1)} %get-tuple-element.130.refs_2_), channel_id=1, source_target_pairs={{0,8},{4,12},{8,0},{12,4},{16,24},{20,28},{24,16},{28,20},{1,9},{5... | collective-permute-start | bytes 294920 | tf_op jit(solution)/shard_map/ppermute | solution.py:669
  20.5 0.3 collective-permute-start.6
  20.7 0.2 collective-permute-start.12
  20.9 3.9 %collective-permute-start.11 = (bf16[304,256]{1,0:T(8,128)(2,1)}, bf16[304,256]{1,0:T(8,128)(2,1)S(1)}, u32[]{:S(2)}, u32[]{:S(2)}) collective-permute-start(bf16[304,256]{1,0:T(8,128)(2,1)} %get-tuple-element.122), channel_id=1, source_target_pairs={{0,2},{1,3},{2,0},{3,1},{4,6},{5,7},{6,4},{7,5},{8,10},{9,11},{10,... | collective-permute-start | bytes 466952 | tf_op jit(solution)/shard_map/ppermute | solution.py:669
  24.8 0.8 collective-permute-start
  25.7 1.5 %collective-permute-start.7 = (bf16[192,256]{1,0:T(8,128)(2,1)S(1)}, bf16[192,256]{1,0:T(8,128)(2,1)S(1)}, u32[]{:S(2)}, u32[]{:S(2)}) collective-permute-start(bf16[192,256]{1,0:T(8,128)(2,1)S(1)} %get-tuple-element.130.refs_2_), channel_id=1, source_target_pairs={{0,4},{4,0},{8,12},{12,8},{16,20},{20,16},{24,28},{28,24},{1,5},{5... | collective-permute-start | bytes 294920 | tf_op jit(solution)/shard_map/ppermute | solution.py:669
  27.3 3.8 %attn_fwd.2 = (f32[1024,256]{1,0:T(8,128)S(1)}, f32[1024,256]{1,0:T(8,128)S(1)}, bf16[1024,256]{1,0:T(8,128)(2,1)S(1)}, bf16[768,1024]{1,0:T(8,128)(2,1)S(1)}, b...) custom-call(bf16[352,256]{1,0:T(8,128)(2,1)S(1)} %get-tuple-element.126.refs_0_, ...), custom_call_target="tpu_custom_call" | custom-call | flops 49999998976 | bytes 1024 | tf_op jit(solution)/shard_map/attn_fwd/pallas_call | solution.py:561
  31.1 0.5 collective-permute-start.9
  31.7 0.9 collective-permute-done.9.refs_8_
  32.5 0.4 collective-permute-done.10.refs_9_
  32.9 2.2 %mlp_fwd.1 = (f32[1024,256]{1,0:T(8,128)S(1)}, bf16[1024,1024]{1,0:T(8,128)(2,1)S(1)}, bf16[1024,1024]{1,0:T(8,128)(2,1)S(1)}) custom-call(bf16[2,256,256]{2,1,0:T(8,128)(2,1)S(1)} %copy-done, bf16[2,256,256]{2,1,0:T(8,128)(2,1)S(1)} %copy-done.1, bf16[192,256]{1,0:T(8,128)(2,1)S(1)} %get-tuple-element.130.refs_2_, ...), custom_call_target="tpu_custom_call" | custom-call | flops 1000 | bytes 1024 | tf_op jit(solution)/shard_map/mlp_fwd/pallas_call | solution.py:561
  35.1 0.2 collective-permute-done.11.b
  35.4 1.5 %collective-permute-start.14 = (bf16[528,256]{1,0:T(8,128)(2,1)S(1)}, bf16[528,256]{1,0:T(8,128)(2,1)S(1)}, u32[]{:S(2)}, u32[]{:S(2)}) collective-permute-start(bf16[528,256]{1,0:T(8,128)(2,1)S(1)} %get-tuple-element.146.refs_1_), channel_id=1, source_target_pairs={{0,4},{4,0},{8,12},{12,8},{16,20},{20,16},{24,28},{28,24},{1,5},{5... | collective-permute-start | bytes 811016 | tf_op jit(solution)/shard_map/ppermute | solution.py:669
  36.9 1.2 %collective-permute-start.13 = (bf16[384,256]{1,0:T(8,128)(2,1)S(1)}, bf16[384,256]{1,0:T(8,128)(2,1)S(1)}, u32[]{:S(2)}, u32[]{:S(2)}) collective-permute-start(bf16[384,256]{1,0:T(8,128)(2,1)S(1)} %get-tuple-element.144.refs_2_), channel_id=1, source_target_pairs={{0,8},{4,12},{8,0},{12,4},{16,24},{20,28},{24,16},{28,20},{1,9},{5... | collective-permute-start | bytes 589832 | tf_op jit(solution)/shard_map/ppermute | solution.py:669
  38.1 0.3 collective-permute-start.15
  38.5 3.8 %attn_fwd.3 = (f32[1024,256]{1,0:T(8,128)S(1)}, f32[1024,256]{1,0:T(8,128)S(1)}, bf16[1024,256]{1,0:T(8,128)(2,1)S(1)}, bf16[768,1024]{1,0:T(8,128)(2,1)S(1)}, b...) custom-call(bf16[352,256]{1,0:T(8,128)(2,1)S(1)} %copy-done.3, bf16[528,256]{1,0:T(8,128)(2,1)S(1)} %get-tuple-element.146.refs_1_, ...), custom_call_target="tpu_custom_call" | custom-call | flops 1000 | bytes 1024 | tf_op jit(solution)/shard_map/attn_fwd/pallas_call | solution.py:561
  42.3 1.1 collective-permute-done.13.refs_3_
  43.4 0.8 collective-permute-start.16
  44.2 1.1 collective-permute-done.16.refs_5_
  45.3 4.4 %mlp_both.1 = (f32[1024,256]{1,0:T(8,128)}, f32[1024,256]{1,0:T(8,128)S(1)}, bf16[4,256,256]{2,1,0:T(8,128)(2,1)S(1)}, bf16[4,256,256]{2,1,0:T(8,128)(2,1)S(1)}, f32[8,256]{1,0:T(8,128)S(1)}) custom-call(bf16[2,256,256]{2,1,0:T(8,128)(2,1)S(1)} %copy-done, bf16[2,256,256]{2,1,0:T(8,128)(2,1)S(1)} %copy-done.1, ...), custom_call_target="tpu_custom_call" | custom-call | flops 1000 | bytes 1024 | tf_op jit(solution)/shard_map/mlp_both/pallas_call | solution.py:561
  49.7 0.4 collective-permute-start.17
  50.1 1.1 attn_pre.2
  51.2 0.5 collective-permute-done.17.got
  51.8 1.3 %collective-permute-start.20 = (bf16[4,128,256]{2,1,0:T(8,128)(2,1)S(1)}, bf16[4,128,256]{2,1,0:T(8,128)(2,1)S(1)}, u32[]{:S(2)}, u32[]{:S(2)}) collective-permute-start(bf16[4,128,256]{2,1,0:T(8,128)(2,1)S(1)} %get-tuple-element.158), channel_id=1, source_target_pairs={{0,8},{4,12},{8,0},{12,4},{16,24},{20,28},{24,16},{28,20},{1,9},{5... | collective-permute-start | bytes 786440 | tf_op jit(solution)/shard_map/ppermute | solution.py:669
  53.1 4.4 %attn_bwd.1 = (f32[1024,256]{1,0:T(8,128)S(1)}, bf16[4,176,256]{2,1,0:T(8,128)(2,1)S(1)}, bf16[4,176,256]{2,1,0:T(8,128)(2,1)S(1)}) custom-call(bf16[352,256]{1,0:T(8,128)(2,1)S(1)} %copy-done.3, bf16[528,256]{1,0:T(8,128)(2,1)S(1)} %get-tuple-element.146.refs_1_, bf16[528,256]{1,0:T(8,128)(2,1)S(1)} %collective-permute-done.14.refs_2_, ...), custom_call_target="tpu_custom_call" | custom-call | flops 1000 | bytes 1024 | tf_op jit(solution)/shard_map/attn_bwd/pallas_call | solution.py:561
  57.5 0.7 collective-permute-start.21
  58.1 2.8 %mlp_bwd.1 = (f32[1024,256]{1,0:T(8,128)S(1)}, bf16[4,256,256]{2,1,0:T(8,128)(2,1)S(1)}, bf16[4,256,256]{2,1,0:T(8,128)(2,1)S(1)}, f32[8,256]{1,0:T(8,128)S(1)}) custom-call(bf16[2,256,256]{2,1,0:T(8,128)(2,1)S(1)} %copy-done, bf16[2,256,256]{2,1,0:T(8,128)(2,1)S(1)} %copy-done.1, bf16[192,256]{1,0:T(8,128)(2,1)S(1)} %get-tuple-element.130.refs_2_, ...), custom_call_target="tpu_custom_call" | custom-call | flops 1000 | bytes 1024 | tf_op jit(solution)/shard_map/mlp_bwd/pallas_call | solution.py:561
  61.2 0.2 collective-permute-start.24
  61.5 3.7 %collective-permute-start.23 = (bf16[304,256]{1,0:T(8,128)(2,1)S(1)}, bf16[304,256]{1,0:T(8,128)(2,1)S(1)}, u32[]{:S(2)}, u32[]{:S(2)}) collective-permute-start(bf16[304,256]{1,0:T(8,128)(2,1)S(1)} %get-tuple-element.199), channel_id=1, source_target_pairs={{0,2},{1,3},{2,0},{3,1},{4,6},{5,7},{6,4},{7,5},{8,10},{9,11},{10,... | collective-permute-start | bytes 466952 | tf_op jit(solution)/shard_map/ppermute | solution.py:669
  65.1 1.1 attn_pre.3
  66.4 0.3 collective-permute-start.19
  66.7 3.8 %attn_grads.1 = (bf16[768,1024]{1,0:T(8,128)(2,1)S(1)}, bf16[4,176,256]{2,1,0:T(8,128)(2,1)S(1)}, bf16[2,176,256]{2,1,0:T(8,128)(2,1)S(1)}, bf16[2,176,256]{2,1,0:T(8,128)(2,1)S(1)}) custom-call(bf16[352,256]{1,0:T(8,128)(2,1)S(1)} %get-tuple-element.126.refs_0_, bf16[528,256]{1,0:T(8,128)(2,1)S(1)} %get-tuple-element.132.refs_1_, ...), custom_call_target="tpu_custom_call" | custom-call | flops 1000 | bytes 1024 | tf_op jit(solution)/shard_map/attn_grads/pallas_call | solution.py:561
  70.5 4.4 %collective-permute-done.23.refs_2_ = bf16[304,256]{1,0:T(8,128)(2,1)S(1)} collective-permute-done((bf16[304,256]{1,0:T(8,128)(2,1)S(1)}, bf16[304,256]{1,0:T(8,128)(2,1)S(1)}, u32[]{:S(2)}, u32[]{:S(2)}) %collective-permute-start.23) | collective-permute-done | bytes 155680 | tf_op jit(solution)/shard_map/ppermute | solution.py:669
  74.9 1.3 %collective-permute-start.25 = (bf16[2,176,256]{2,1,0:T(8,128)(2,1)S(1)}, bf16[2,176,256]{2,1,0:T(8,128)(2,1)S(1)}, u32[]{:S(2)}, u32[]{:S(2)}) collective-permute-start(bf16[2,176,256]{2,1,0:T(8,128)(2,1)S(1)} %get-tuple-element.206), channel_id=1, source_target_pairs={{0,4},{4,0},{8,12},{12,8},{16,20},{20,16},{24,28},{28,24},{1,5},{5... | collective-permute-start | bytes 540680 | tf_op jit(solution)/shard_map/ppermute | solution.py:669
  76.3 1.3 %collective-permute-start.29 = (bf16[176,256]{1,0:T(8,128)(2,1)S(1)}, bf16[176,256]{1,0:T(8,128)(2,1)S(1)}, u32[]{:S(2)}, u32[]{:S(2)}) collective-permute-start(bf16[176,256]{1,0:T(8,128)(2,1)S(1)} %get-tuple-element.215.refs_0_), channel_id=1, source_target_pairs={{0,24},{4,28},{8,16},{12,20},{16,8},{20,12},{24,0},{28,4},{1,25},{... | collective-permute-start | bytes 270344 | tf_op jit(solution)/shard_map/ppermute | solution.py:669
  77.8 2.7 %collective-permute-start.31 = (bf16[304,256]{1,0:T(8,128)(2,1)S(1)}, bf16[304,256]{1,0:T(8,128)(2,1)S(1)}, u32[]{:S(2)}, u32[]{:S(2)}) collective-permute-start(bf16[304,256]{1,0:T(8,128)(2,1)S(1)} %get-tuple-element.209), channel_id=1, source_target_pairs={{0,1},{1,0},{2,3},{3,2},{4,5},{5,4},{6,7},{7,6},{8,9},{9,8},{10,11... | collective-permute-start | bytes 466952 | tf_op jit(solution)/shard_map/ppermute | solution.py:669
  80.5 1.3 %collective-permute-start.33 = (bf16[304,256]{1,0:T(8,128)(2,1)S(1)}, bf16[304,256]{1,0:T(8,128)(2,1)S(1)}, u32[]{:S(2)}, u32[]{:S(2)}) collective-permute-start(bf16[304,256]{1,0:T(8,128)(2,1)S(1)} %get-tuple-element.211), channel_id=1, source_target_pairs={{0,3},{1,2},{2,1},{3,0},{4,7},{5,6},{6,5},{7,4},{8,11},{9,10},{10,... | collective-permute-start | bytes 466952 | tf_op jit(solution)/shard_map/ppermute | solution.py:669
  81.8 1.2 %collective-permute-start.28 = (bf16[176,256]{1,0:T(8,128)(2,1)S(1)}, bf16[176,256]{1,0:T(8,128)(2,1)S(1)}, u32[]{:S(2)}, u32[]{:S(2)}) collective-permute-start(bf16[176,256]{1,0:T(8,128)(2,1)S(1)} %get-tuple-element.215.refs_0_), channel_id=1, source_target_pairs={{0,16},{4,20},{8,24},{12,28},{16,0},{20,4},{24,8},{28,12},{1,17},{... | collective-permute-start | bytes 270344 | tf_op jit(solution)/shard_map/ppermute | solution.py:669
  83.0 0.3 collective-permute-start.27
  83.3 2.2 %collective-permute-done.28.refs_2_ = bf16[176,256]{1,0:T(8,128)(2,1)S(1)} collective-permute-done((bf16[176,256]{1,0:T(8,128)(2,1)S(1)}, bf16[176,256]{1,0:T(8,128)(2,1)S(1)}, u32[]{:S(2)}, u32[]{:S(2)}) %collective-permute-start.28) | collective-permute-done | bytes 90144 | tf_op jit(solution)/shard_map/ppermute | solution.py:669
  85.5 1.2 %collective-permute-done.27.refs_1_ = bf16[176,256]{1,0:T(8,128)(2,1)S(1)} collective-permute-done((bf16[176,256]{1,0:T(8,128)(2,1)S(1)}, bf16[176,256]{1,0:T(8,128)(2,1)S(1)}, u32[]{:S(2)}, u32[]{:S(2)}) %collective-permute-start.27) | collective-permute-done | bytes 90144 | tf_op jit(solution)/shard_map/ppermute | solution.py:669
  86.8 2.2 %attn_post.1 = f32[1024,256]{1,0:T(8,128)} custom-call(bf16[352,256]{1,0:T(8,128)(2,1)S(1)} %get-tuple-element.126.refs_0_, bf16[528,256]{1,0:T(8,128)(2,1)S(1)} %get-tuple-element.132.refs_1_, bf16[528,256]{1,0:T(8,128)(2,1)S(1)} %collective-permute-done.5.refs_2_, bf16[768,1024]{1,0:T(8,128)(2,1)S(1)} %get-tuple-element.212.refs_3_, ...), custom_call_target="tpu_custom_call" | custom-call | flops 1000 | bytes 1024 | tf_op jit(solution)/shard_map/attn_post/pallas_call | solution.py:561
  89.0 6.2 %collective-permute-done.33.refs_4_ = bf16[304,256]{1,0:T(8,128)(2,1)S(1)} collective-permute-done((bf16[304,256]{1,0:T(8,128)(2,1)S(1)}, bf16[304,256]{1,0:T(8,128)(2,1)S(1)}, u32[]{:S(2)}, u32[]{:S(2)}) %collective-permute-start.33) | collective-permute-done | bytes 155680 | tf_op jit(solution)/shard_map/ppermute | solution.py:669
  95.3 1.8 %collective-permute-start.35 = (bf16[256,256]{1,0:T(8,128)(2,1)S(1)}, bf16[256,256]{1,0:T(8,128)(2,1)S(1)}, u32[]{:S(2)}, u32[]{:S(2)}) collective-permute-start(bf16[256,256]{1,0:T(8,128)(2,1)S(1)} %get-tuple-element.221.high), channel_id=1, source_target_pairs={{0,16},{4,20},{8,24},{12,28},{16,0},{20,4},{24,8},{28,12},{1,17},{... | collective-permute-start | bytes 393224 | tf_op jit(solution)/shard_map/ppermute | solution.py:669
  97.2 3.7 %collective-permute-done.34.low_got = bf16[176,256]{1,0:T(8,128)(2,1)S(1)} collective-permute-done((bf16[176,256]{1,0:T(8,128)(2,1)S(1)}, bf16[176,256]{1,0:T(8,128)(2,1)S(1)}, u32[]{:S(2)}, u32[]{:S(2)}) %collective-permute-start.34) | collective-permute-done | bytes 90144 | tf_op jit(solution)/shard_map/ppermute | solution.py:669
  101.0 0.9 collective-permute-start.36
  101.8 2.6 %collective-permute-done.36.low_got = bf16[176,256]{1,0:T(8,128)(2,1)S(1)} collective-permute-done((bf16[176,256]{1,0:T(8,128)(2,1)S(1)}, bf16[176,256]{1,0:T(8,128)(2,1)S(1)}, u32[]{:S(2)}, u32[]{:S(2)}) %collective-permute-start.36) | collective-permute-done | bytes 90144 | tf_op jit(solution)/shard_map/ppermute | solution.py:669
  104.4 0.4 collective-permute-done.37.high_got
  104.8 3.5 %collective-permute-start.38 = (bf16[512,256]{1,0:T(8,128)(2,1)S(1)}, bf16[512,256]{1,0:T(8,128)(2,1)S(1)}, u32[]{:S(2)}, u32[]{:S(2)}) collective-permute-start(bf16[512,256]{1,0:T(8,128)(2,1)S(1)} %get-tuple-element.224.high), channel_id=1, source_target_pairs={{0,4},{4,0},{8,12},{12,8},{16,20},{20,16},{24,28},{28,24},{1,5},{5... | collective-permute-start | bytes 786440 | tf_op jit(solution)/shard_map/ppermute | solution.py:669
  108.4 0.4 collective-permute-start.39
  108.9 0.8 collective-permute-done.30.low_other
  109.6 0.2 collective-permute-done.39.late_other
  109.8 1.3 %finish.1 = (f32[2,3,64,256]{3,2,1,0:T(8,128)}, f32[2,64,256]{2,1,0:T(8,128)}, f32[2,256,256]{2,1,0:T(8,128)}, f32[2,256,256]{2,1,0:T(8,128)}, f32[2,64,256]{2,1...) custom-call(bf16[176,256]{1,0:T(8,128)(2,1)S(1)} %four_sum.1.low, ...), custom_call_target="tpu_custom_call" | custom-call | flops 1000 | bytes 1024 | tf_op jit(solution)/shard_map/finish/pallas_call | solution.py:646
  (59 shorter events, 1.7 us)
Async XLA Ops:
  3.2 12.0 %collective-permute-start.3 = (bf16[304,256]{1,0:T(8,128)(2,1)}, bf16[304,256]{1,0:T(8,128)(2,1)S(1)}, u32[]{:S(2)}, u32[]{:S(2)}) collective-permute-start(bf16[304,256]{1,0:T(8,128)(2,1)} %get-tuple-element.123), channel_id=1, source_target_pairs={{0,3},{1,2},{2,1},{3,0},{4,7},{5,6},{6,5},{7,4},{8,11},{9,10},{10,... | collective-permute-start | bytes 466952 | tf_op jit(solution)/shard_map/ppermute | solution.py:669
  4.6 13.0 %collective-permute-start.2 = (bf16[304,256]{1,0:T(8,128)(2,1)}, bf16[304,256]{1,0:T(8,128)(2,1)S(1)}, u32[]{:S(2)}, u32[]{:S(2)}) collective-permute-start(bf16[304,256]{1,0:T(8,128)(2,1)} %get-tuple-element.123), channel_id=1, source_target_pairs={{0,2},{1,3},{2,0},{3,1},{4,6},{5,7},{6,4},{7,5},{8,10},{9,11},{10,... | collective-permute-start | bytes 466952 | tf_op jit(solution)/shard_map/ppermute | solution.py:669
  5.7 11.9 %collective-permute-start.1 = (bf16[304,256]{1,0:T(8,128)(2,1)}, bf16[304,256]{1,0:T(8,128)(2,1)S(1)}, u32[]{:S(2)}, u32[]{:S(2)}) collective-permute-start(bf16[304,256]{1,0:T(8,128)(2,1)} %get-tuple-element.123), channel_id=1, source_target_pairs={{0,1},{1,0},{2,3},{3,2},{4,5},{5,4},{6,7},{7,6},{8,9},{9,8},{10,11... | collective-permute-start | bytes 466952 | tf_op jit(solution)/shard_map/ppermute | solution.py:669
  6.8 1.0 copy-start.4
  7.8 0.9 copy-start.5
  8.7 0.8 copy-start.6
  9.5 0.7 copy-start.8
  17.6 9.6 %collective-permute-start.5 = (bf16[528,256]{1,0:T(8,128)(2,1)S(1)}, bf16[528,256]{1,0:T(8,128)(2,1)S(1)}, u32[]{:S(2)}, u32[]{:S(2)}) collective-permute-start(bf16[528,256]{1,0:T(8,128)(2,1)S(1)} %get-tuple-element.132.refs_1_), channel_id=1, source_target_pairs={{0,4},{4,0},{8,12},{12,8},{16,20},{20,16},{24,28},{28,24},{1,5},{5... | collective-permute-start | bytes 811016 | tf_op jit(solution)/shard_map/ppermute | solution.py:669
  19.2 5.5 %collective-permute-start.4 = (bf16[192,256]{1,0:T(8,128)(2,1)S(1)}, bf16[192,256]{1,0:T(8,128)(2,1)S(1)}, u32[]{:S(2)}, u32[]{:S(2)}) collective-permute-start(bf16[192,256]{1,0:T(8,128)(2,1)S(1)} %get-tuple-element.130.refs_2_), channel_id=1, source_target_pairs={{0,8},{4,12},{8,0},{12,4},{16,24},{20,28},{24,16},{28,20},{1,9},{5... | collective-permute-start | bytes 294920 | tf_op jit(solution)/shard_map/ppermute | solution.py:669
  20.5 5.3 %collective-permute-start.6 = (bf16[192,256]{1,0:T(8,128)(2,1)S(1)}, bf16[192,256]{1,0:T(8,128)(2,1)S(1)}, u32[]{:S(2)}, u32[]{:S(2)}) collective-permute-start(bf16[192,256]{1,0:T(8,128)(2,1)S(1)} %get-tuple-element.131.refs_3_), channel_id=1, source_target_pairs={{0,8},{4,12},{8,0},{12,4},{16,24},{20,28},{24,16},{28,20},{1,9},{5... | collective-permute-start | bytes 294920 | tf_op jit(solution)/shard_map/ppermute | solution.py:669
  20.7 14.4 %collective-permute-start.12 = (bf16[304,256]{1,0:T(8,128)(2,1)}, bf16[304,256]{1,0:T(8,128)(2,1)S(1)}, u32[]{:S(2)}, u32[]{:S(2)}) collective-permute-start(bf16[304,256]{1,0:T(8,128)(2,1)} %get-tuple-element.122), channel_id=1, source_target_pairs={{0,3},{1,2},{2,1},{3,0},{4,7},{5,6},{6,5},{7,4},{8,11},{9,10},{10,... | collective-permute-start | bytes 466952 | tf_op jit(solution)/shard_map/ppermute | solution.py:669
  20.9 14.5 %collective-permute-start.11 = (bf16[304,256]{1,0:T(8,128)(2,1)}, bf16[304,256]{1,0:T(8,128)(2,1)S(1)}, u32[]{:S(2)}, u32[]{:S(2)}) collective-permute-start(bf16[304,256]{1,0:T(8,128)(2,1)} %get-tuple-element.122), channel_id=1, source_target_pairs={{0,2},{1,3},{2,0},{3,1},{4,6},{5,7},{6,4},{7,5},{8,10},{9,11},{10,... | collective-permute-start | bytes 466952 | tf_op jit(solution)/shard_map/ppermute | solution.py:669
  24.8 10.6 %collective-permute-start = (bf16[304,256]{1,0:T(8,128)(2,1)}, bf16[304,256]{1,0:T(8,128)(2,1)S(1)}, u32[]{:S(2)}, u32[]{:S(2)}) collective-permute-start(bf16[304,256]{1,0:T(8,128)(2,1)} %get-tuple-element.122), channel_id=1, source_target_pairs={{0,1},{1,0},{2,3},{3,2},{4,5},{5,4},{6,7},{7,6},{8,9},{9,8},{10,11... | collective-permute-start | bytes 466952 | tf_op jit(solution)/shard_map/ppermute | solution.py:669
  25.7 5.4 %collective-permute-start.7 = (bf16[192,256]{1,0:T(8,128)(2,1)S(1)}, bf16[192,256]{1,0:T(8,128)(2,1)S(1)}, u32[]{:S(2)}, u32[]{:S(2)}) collective-permute-start(bf16[192,256]{1,0:T(8,128)(2,1)S(1)} %get-tuple-element.130.refs_2_), channel_id=1, source_target_pairs={{0,4},{4,0},{8,12},{12,8},{16,20},{20,16},{24,28},{28,24},{1,5},{5... | collective-permute-start | bytes 294920 | tf_op jit(solution)/shard_map/ppermute | solution.py:669
  27.2 4.4 %collective-permute-start.8 = (bf16[192,256]{1,0:T(8,128)(2,1)S(1)}, bf16[192,256]{1,0:T(8,128)(2,1)S(1)}, u32[]{:S(2)}, u32[]{:S(2)}) collective-permute-start(bf16[192,256]{1,0:T(8,128)(2,1)S(1)} %get-tuple-element.131.refs_3_), channel_id=1, source_target_pairs={{0,4},{4,0},{8,12},{12,8},{16,20},{20,16},{24,28},{28,24},{1,5},{5... | collective-permute-start | bytes 294920 | tf_op jit(solution)/shard_map/ppermute | solution.py:669
  27.3 5.6 %copy-start = (bf16[2,256,256]{2,1,0:T(8,128)(2,1)S(1)}, bf16[2,256,256]{2,1,0:T(8,128)(2,1)}, u32[]{:S(2)}) copy-start(bf16[2,256,256]{2,1,0:T(8,128)(2,1)} %refs_0_.7) | copy-start | bytes 786436
  27.3 5.6 %copy-start.1 = (bf16[2,256,256]{2,1,0:T(8,128)(2,1)S(1)}, bf16[2,256,256]{2,1,0:T(8,128)(2,1)}, u32[]{:S(2)}) copy-start(bf16[2,256,256]{2,1,0:T(8,128)(2,1)} %refs_1_.5) | copy-start | bytes 786436
  27.3 5.6 %copy-start.7 = (f32[2,256]{1,0:T(2,128)S(1)}, f32[2,256]{1,0:T(2,128)}, u32[]{:S(2)}) copy-start(f32[2,256]{1,0:T(2,128)} %refs_14_.1) | copy-start | bytes 6148
  31.1 1.4 %collective-permute-start.9 = (bf16[192,256]{1,0:T(8,128)(2,1)S(1)}, bf16[192,256]{1,0:T(8,128)(2,1)S(1)}, u32[]{:S(2)}, u32[]{:S(2)}) collective-permute-start(bf16[192,256]{1,0:T(8,128)(2,1)S(1)} %collective-permute-done.4.refs_4_), channel_id=1, source_target_pairs={{0,4},{4,0},{8,12},{12,8},{16,20},{20,16},{24,28},{28,24},{1,5},{5... | collective-permute-start | bytes 294920 | tf_op jit(solution)/shard_map/ppermute | solution.py:669
  31.6 1.3 %collective-permute-start.10 = (bf16[192,256]{1,0:T(8,128)(2,1)S(1)}, bf16[192,256]{1,0:T(8,128)(2,1)S(1)}, u32[]{:S(2)}, u32[]{:S(2)}) collective-permute-start(bf16[192,256]{1,0:T(8,128)(2,1)S(1)} %collective-permute-done.6.refs_5_), channel_id=1, source_target_pairs={{0,4},{4,0},{8,12},{12,8},{16,20},{20,16},{24,28},{28,24},{1,5},{5... | collective-permute-start | bytes 294920 | tf_op jit(solution)/shard_map/ppermute | solution.py:669
  32.9 5.6 %copy-start.3 = (bf16[352,256]{1,0:T(8,128)(2,1)S(1)}, bf16[352,256]{1,0:T(8,128)(2,1)}, u32[]{:S(2)}) copy-start(bf16[352,256]{1,0:T(8,128)(2,1)} %get-tuple-element.145.refs_0_) | copy-start | bytes 540676
  35.1 10.2 %copy-start.2 = (bf16[1024,256]{1,0:T(8,128)(2,1)S(1)}, bf16[1024,256]{1,0:T(8,128)(2,1)}, u32[]{:S(2)}) copy-start(bf16[1024,256]{1,0:T(8,128)(2,1)} %refs_3_.1) | copy-start | bytes 1572868
  35.4 3.1 %collective-permute-start.14 = (bf16[528,256]{1,0:T(8,128)(2,1)S(1)}, bf16[528,256]{1,0:T(8,128)(2,1)S(1)}, u32[]{:S(2)}, u32[]{:S(2)}) collective-permute-start(bf16[528,256]{1,0:T(8,128)(2,1)S(1)} %get-tuple-element.146.refs_1_), channel_id=1, source_target_pairs={{0,4},{4,0},{8,12},{12,8},{16,20},{20,16},{24,28},{28,24},{1,5},{5... | collective-permute-start | bytes 811016 | tf_op jit(solution)/shard_map/ppermute | solution.py:669
  36.9 6.5 %collective-permute-start.13 = (bf16[384,256]{1,0:T(8,128)(2,1)S(1)}, bf16[384,256]{1,0:T(8,128)(2,1)S(1)}, u32[]{:S(2)}, u32[]{:S(2)}) collective-permute-start(bf16[384,256]{1,0:T(8,128)(2,1)S(1)} %get-tuple-element.144.refs_2_), channel_id=1, source_target_pairs={{0,8},{4,12},{8,0},{12,4},{16,24},{20,28},{24,16},{28,20},{1,9},{5... | collective-permute-start | bytes 589832 | tf_op jit(solution)/shard_map/ppermute | solution.py:669
  38.1 6.1 %collective-permute-start.15 = (bf16[384,256]{1,0:T(8,128)(2,1)S(1)}, bf16[384,256]{1,0:T(8,128)(2,1)S(1)}, u32[]{:S(2)}, u32[]{:S(2)}) collective-permute-start(bf16[384,256]{1,0:T(8,128)(2,1)S(1)} %get-tuple-element.144.refs_2_), channel_id=1, source_target_pairs={{0,4},{4,0},{8,12},{12,8},{16,20},{20,16},{24,28},{28,24},{1,5},{5... | collective-permute-start | bytes 589832 | tf_op jit(solution)/shard_map/ppermute | solution.py:669
  43.4 1.9 %collective-permute-start.16 = (bf16[384,256]{1,0:T(8,128)(2,1)S(1)}, bf16[384,256]{1,0:T(8,128)(2,1)S(1)}, u32[]{:S(2)}, u32[]{:S(2)}) collective-permute-start(bf16[384,256]{1,0:T(8,128)(2,1)S(1)} %collective-permute-done.13.refs_3_), channel_id=1, source_target_pairs={{0,4},{4,0},{8,12},{12,8},{16,20},{20,16},{24,28},{28,24},{1,5},{5... | collective-permute-start | bytes 589832 | tf_op jit(solution)/shard_map/ppermute | solution.py:669
  49.7 2.0 %collective-permute-start.17 = (bf16[4,256,256]{2,1,0:T(8,128)(2,1)S(1)}, bf16[4,256,256]{2,1,0:T(8,128)(2,1)S(1)}, u32[]{:S(2)}, u32[]{:S(2)}) collective-permute-start(bf16[4,256,256]{2,1,0:T(8,128)(2,1)S(1)} %get-tuple-element.152), channel_id=1, source_target_pairs={{0,4},{4,0},{8,12},{12,8},{16,20},{20,16},{24,28},{28,24},{1,5},{5... | collective-permute-start | bytes 1572872 | tf_op jit(solution)/shard_map/ppermute | solution.py:669
  51.8 9.2 %collective-permute-start.20 = (bf16[4,128,256]{2,1,0:T(8,128)(2,1)S(1)}, bf16[4,128,256]{2,1,0:T(8,128)(2,1)S(1)}, u32[]{:S(2)}, u32[]{:S(2)}) collective-permute-start(bf16[4,128,256]{2,1,0:T(8,128)(2,1)S(1)} %get-tuple-element.158), channel_id=1, source_target_pairs={{0,8},{4,12},{8,0},{12,4},{16,24},{20,28},{24,16},{28,20},{1,9},{5... | collective-permute-start | bytes 786440 | tf_op jit(solution)/shard_map/ppermute | solution.py:669
  57.5 3.6 %collective-permute-start.21 = (bf16[4,176,256]{2,1,0:T(8,128)(2,1)S(1)}, bf16[4,176,256]{2,1,0:T(8,128)(2,1)S(1)}, u32[]{:S(2)}, u32[]{:S(2)}) collective-permute-start(bf16[4,176,256]{2,1,0:T(8,128)(2,1)S(1)} %get-tuple-element.193), channel_id=1, source_target_pairs={{0,4},{4,0},{8,12},{12,8},{16,20},{20,16},{24,28},{28,24},{1,5},{5... | collective-permute-start | bytes 1081352 | tf_op jit(solution)/shard_map/ppermute | solution.py:669
  60.9 5.3 %collective-permute-start.18 = (bf16[4,256,256]{2,1,0:T(8,128)(2,1)S(1)}, bf16[4,256,256]{2,1,0:T(8,128)(2,1)S(1)}, u32[]{:S(2)}, u32[]{:S(2)}) collective-permute-start(bf16[4,256,256]{2,1,0:T(8,128)(2,1)S(1)} %get-tuple-element.173), channel_id=1, source_target_pairs={{0,4},{4,0},{8,12},{12,8},{16,20},{20,16},{24,28},{28,24},{1,5},{5... | collective-permute-start | bytes 1572872 | tf_op jit(solution)/shard_map/ppermute | solution.py:669
  61.2 9.3 %collective-permute-start.24 = (bf16[304,256]{1,0:T(8,128)(2,1)S(1)}, bf16[304,256]{1,0:T(8,128)(2,1)S(1)}, u32[]{:S(2)}, u32[]{:S(2)}) collective-permute-start(bf16[304,256]{1,0:T(8,128)(2,1)S(1)} %get-tuple-element.201), channel_id=1, source_target_pairs={{0,3},{1,2},{2,1},{3,0},{4,7},{5,6},{6,5},{7,4},{8,11},{9,10},{10,... | collective-permute-start | bytes 466952 | tf_op jit(solution)/shard_map/ppermute | solution.py:669
  61.5 13.4 %collective-permute-start.23 = (bf16[304,256]{1,0:T(8,128)(2,1)S(1)}, bf16[304,256]{1,0:T(8,128)(2,1)S(1)}, u32[]{:S(2)}, u32[]{:S(2)}) collective-permute-start(bf16[304,256]{1,0:T(8,128)(2,1)S(1)} %get-tuple-element.199), channel_id=1, source_target_pairs={{0,2},{1,3},{2,0},{3,1},{4,6},{5,7},{6,4},{7,5},{8,10},{9,11},{10,... | collective-permute-start | bytes 466952 | tf_op jit(solution)/shard_map/ppermute | solution.py:669
  65.1 9.8 %collective-permute-start.22 = (bf16[304,256]{1,0:T(8,128)(2,1)S(1)}, bf16[304,256]{1,0:T(8,128)(2,1)S(1)}, u32[]{:S(2)}, u32[]{:S(2)}) collective-permute-start(bf16[304,256]{1,0:T(8,128)(2,1)S(1)} %get-tuple-element.197), channel_id=1, source_target_pairs={{0,1},{1,0},{2,3},{3,2},{4,5},{5,4},{6,7},{7,6},{8,9},{9,8},{10,11... | collective-permute-start | bytes 466952 | tf_op jit(solution)/shard_map/ppermute | solution.py:669
  66.4 11.2 %collective-permute-start.19 = (bf16[4,128,256]{2,1,0:T(8,128)(2,1)S(1)}, bf16[4,128,256]{2,1,0:T(8,128)(2,1)S(1)}, u32[]{:S(2)}, u32[]{:S(2)}) collective-permute-start(bf16[4,128,256]{2,1,0:T(8,128)(2,1)S(1)} %get-tuple-element.179), channel_id=1, source_target_pairs={{0,8},{4,12},{8,0},{12,4},{16,24},{20,28},{24,16},{28,20},{1,9},{5... | collective-permute-start | bytes 786440 | tf_op jit(solution)/shard_map/ppermute | solution.py:669
  74.9 2.7 %collective-permute-start.25 = (bf16[2,176,256]{2,1,0:T(8,128)(2,1)S(1)}, bf16[2,176,256]{2,1,0:T(8,128)(2,1)S(1)}, u32[]{:S(2)}, u32[]{:S(2)}) collective-permute-start(bf16[2,176,256]{2,1,0:T(8,128)(2,1)S(1)} %get-tuple-element.206), channel_id=1, source_target_pairs={{0,4},{4,0},{8,12},{12,8},{16,20},{20,16},{24,28},{28,24},{1,5},{5... | collective-permute-start | bytes 540680 | tf_op jit(solution)/shard_map/ppermute | solution.py:669
  76.2 1.4 %collective-permute-start.26 = (bf16[2,176,256]{2,1,0:T(8,128)(2,1)S(1)}, bf16[2,176,256]{2,1,0:T(8,128)(2,1)S(1)}, u32[]{:S(2)}, u32[]{:S(2)}) collective-permute-start(bf16[2,176,256]{2,1,0:T(8,128)(2,1)S(1)} %get-tuple-element.207), channel_id=1, source_target_pairs={{0,4},{4,0},{8,12},{12,8},{16,20},{20,16},{24,28},{28,24},{1,5},{5... | collective-permute-start | bytes 540680 | tf_op jit(solution)/shard_map/ppermute | solution.py:669
  76.3 6.7 %collective-permute-start.29 = (bf16[176,256]{1,0:T(8,128)(2,1)S(1)}, bf16[176,256]{1,0:T(8,128)(2,1)S(1)}, u32[]{:S(2)}, u32[]{:S(2)}) collective-permute-start(bf16[176,256]{1,0:T(8,128)(2,1)S(1)} %get-tuple-element.215.refs_0_), channel_id=1, source_target_pairs={{0,24},{4,28},{8,16},{12,20},{16,8},{20,12},{24,0},{28,4},{1,25},{... | collective-permute-start | bytes 270344 | tf_op jit(solution)/shard_map/ppermute | solution.py:669
  77.8 11.2 %collective-permute-start.31 = (bf16[304,256]{1,0:T(8,128)(2,1)S(1)}, bf16[304,256]{1,0:T(8,128)(2,1)S(1)}, u32[]{:S(2)}, u32[]{:S(2)}) collective-permute-start(bf16[304,256]{1,0:T(8,128)(2,1)S(1)} %get-tuple-element.209), channel_id=1, source_target_pairs={{0,1},{1,0},{2,3},{3,2},{4,5},{5,4},{6,7},{7,6},{8,9},{9,8},{10,11... | collective-permute-start | bytes 466952 | tf_op jit(solution)/shard_map/ppermute | solution.py:669
  80.5 8.5 %collective-permute-start.32 = (bf16[304,256]{1,0:T(8,128)(2,1)S(1)}, bf16[304,256]{1,0:T(8,128)(2,1)S(1)}, u32[]{:S(2)}, u32[]{:S(2)}) collective-permute-start(bf16[304,256]{1,0:T(8,128)(2,1)S(1)} %get-tuple-element.210), channel_id=1, source_target_pairs={{0,2},{1,3},{2,0},{3,1},{4,6},{5,7},{6,4},{7,5},{8,10},{9,11},{10,... | collective-permute-start | bytes 466952 | tf_op jit(solution)/shard_map/ppermute | solution.py:669
  80.5 14.7 %collective-permute-start.33 = (bf16[304,256]{1,0:T(8,128)(2,1)S(1)}, bf16[304,256]{1,0:T(8,128)(2,1)S(1)}, u32[]{:S(2)}, u32[]{:S(2)}) collective-permute-start(bf16[304,256]{1,0:T(8,128)(2,1)S(1)} %get-tuple-element.211), channel_id=1, source_target_pairs={{0,3},{1,2},{2,1},{3,0},{4,7},{5,6},{6,5},{7,4},{8,11},{9,10},{10,... | collective-permute-start | bytes 466952 | tf_op jit(solution)/shard_map/ppermute | solution.py:669
  81.8 3.7 %collective-permute-start.28 = (bf16[176,256]{1,0:T(8,128)(2,1)S(1)}, bf16[176,256]{1,0:T(8,128)(2,1)S(1)}, u32[]{:S(2)}, u32[]{:S(2)}) collective-permute-start(bf16[176,256]{1,0:T(8,128)(2,1)S(1)} %get-tuple-element.215.refs_0_), channel_id=1, source_target_pairs={{0,16},{4,20},{8,24},{12,28},{16,0},{20,4},{24,8},{28,12},{1,17},{... | collective-permute-start | bytes 270344 | tf_op jit(solution)/shard_map/ppermute | solution.py:669
  83.0 3.7 %collective-permute-start.27 = (bf16[176,256]{1,0:T(8,128)(2,1)S(1)}, bf16[176,256]{1,0:T(8,128)(2,1)S(1)}, u32[]{:S(2)}, u32[]{:S(2)}) collective-permute-start(bf16[176,256]{1,0:T(8,128)(2,1)S(1)} %get-tuple-element.215.refs_0_), channel_id=1, source_target_pairs={{0,8},{4,12},{8,0},{12,4},{16,24},{20,28},{24,16},{28,20},{1,9},{5... | collective-permute-start | bytes 270344 | tf_op jit(solution)/shard_map/ppermute | solution.py:669
  95.3 5.5 %collective-permute-start.35 = (bf16[256,256]{1,0:T(8,128)(2,1)S(1)}, bf16[256,256]{1,0:T(8,128)(2,1)S(1)}, u32[]{:S(2)}, u32[]{:S(2)}) collective-permute-start(bf16[256,256]{1,0:T(8,128)(2,1)S(1)} %get-tuple-element.221.high), channel_id=1, source_target_pairs={{0,16},{4,20},{8,24},{12,28},{16,0},{20,4},{24,8},{28,12},{1,17},{... | collective-permute-start | bytes 393224 | tf_op jit(solution)/shard_map/ppermute | solution.py:669
  97.2 3.7 %collective-permute-start.34 = (bf16[176,256]{1,0:T(8,128)(2,1)S(1)}, bf16[176,256]{1,0:T(8,128)(2,1)S(1)}, u32[]{:S(2)}, u32[]{:S(2)}) collective-permute-start(bf16[176,256]{1,0:T(8,128)(2,1)S(1)} %get-tuple-element.220.low), channel_id=1, source_target_pairs={{0,8},{4,12},{8,0},{12,4},{16,24},{20,28},{24,16},{28,20},{1,9},{5... | collective-permute-start | bytes 270344 | tf_op jit(solution)/shard_map/ppermute | solution.py:669
  100.9 3.9 %collective-permute-start.37 = (bf16[256,256]{1,0:T(8,128)(2,1)S(1)}, bf16[256,256]{1,0:T(8,128)(2,1)S(1)}, u32[]{:S(2)}, u32[]{:S(2)}) collective-permute-start(bf16[256,256]{1,0:T(8,128)(2,1)S(1)} %get-tuple-element.223.high), channel_id=1, source_target_pairs={{0,8},{4,12},{8,0},{12,4},{16,24},{20,28},{24,16},{28,20},{1,9},{5... | collective-permute-start | bytes 393224 | tf_op jit(solution)/shard_map/ppermute | solution.py:669
  101.0 3.4 %collective-permute-start.36 = (bf16[176,256]{1,0:T(8,128)(2,1)S(1)}, bf16[176,256]{1,0:T(8,128)(2,1)S(1)}, u32[]{:S(2)}, u32[]{:S(2)}) collective-permute-start(bf16[176,256]{1,0:T(8,128)(2,1)S(1)} %get-tuple-element.222.low), channel_id=1, source_target_pairs={{0,16},{4,20},{8,24},{12,28},{16,0},{20,4},{24,8},{28,12},{1,17},{... | collective-permute-start | bytes 270344 | tf_op jit(solution)/shard_map/ppermute | solution.py:669
  104.8 5.0 %collective-permute-start.38 = (bf16[512,256]{1,0:T(8,128)(2,1)S(1)}, bf16[512,256]{1,0:T(8,128)(2,1)S(1)}, u32[]{:S(2)}, u32[]{:S(2)}) collective-permute-start(bf16[512,256]{1,0:T(8,128)(2,1)S(1)} %get-tuple-element.224.high), channel_id=1, source_target_pairs={{0,4},{4,0},{8,12},{12,8},{16,20},{20,16},{24,28},{28,24},{1,5},{5... | collective-permute-start | bytes 786440 | tf_op jit(solution)/shard_map/ppermute | solution.py:669
  108.3 1.3 %collective-permute-start.30 = (bf16[176,256]{1,0:T(8,128)(2,1)S(1)}, bf16[176,256]{1,0:T(8,128)(2,1)S(1)}, u32[]{:S(2)}, u32[]{:S(2)}) collective-permute-start(bf16[176,256]{1,0:T(8,128)(2,1)S(1)} %four_sum.1.low), channel_id=1, source_target_pairs={{0,4},{4,0},{8,12},{12,8},{16,20},{20,16},{24,28},{28,24},{1,5},{5... | collective-permute-start | bytes 270344 | tf_op jit(solution)/shard_map/ppermute | solution.py:669
  108.4 1.4 %collective-permute-start.39 = (bf16[176,256]{1,0:T(8,128)(2,1)S(1)}, bf16[176,256]{1,0:T(8,128)(2,1)S(1)}, u32[]{:S(2)}, u32[]{:S(2)}) collective-permute-start(bf16[176,256]{1,0:T(8,128)(2,1)S(1)} %get-tuple-element.225.late), channel_id=1, source_target_pairs={{0,4},{4,0},{8,12},{12,8},{16,20},{20,16},{24,28},{28,24},{1,5},{5... | collective-permute-start | bytes 270344 | tf_op jit(solution)/shard_map/ppermute | solution.py:669

commit v6 on v5

--- a/solution.py
+++ b/solution.py
@@ -693,10 +693,10 @@
 
     bits = [1 << i for i in range(1, dp_size.bit_length() - 1)]
 
-    def sum_direct(x):
+    def sum_direct(x, after):
         for i in range(0, len(bits), 2):
             masks = (bits[i], bits[i + 1], bits[i] + bits[i + 1]) if i + 1 < len(bits) else (bits[i],)
-            terms = [x] + [swap(x, "dp", dp_size, mask) for mask in masks]
+            terms = [x] + [swap(tie(x, after) if k == 2 else x, "dp", dp_size, mask) for k, mask in enumerate(masks)]
             x = four_sum(160, terms + [jnp.zeros_like(x)] * (4 - len(terms)))
         return x
 
@@ -756,7 +756,7 @@
         sums = core_sum((128, 160), (keep_m0, tie(got_m0, mlp1)), (keep_a0, *[core_swap(x) for x in send_a0]))
         got = scatter(sums)
         grad0 = attn_post(0, tie(gqkv, *sums), gain_attn, tokens, pre, a0)
-        attn1 = sum_direct(attn1)
+        attn1 = sum_direct(attn1, got[1])
         mlp, attn0 = four_split([tie(x, grad0, attn1) for x in got], (mlp1,))
         attn0, mlp = sum_pairs(attn0, mlp)
         d_qkv, d_out, d_up, d_down, d_cross, d_ga, d_gm, d_bias = small_call(

time: 112 us -> 111 us (level)
  transfers between devices with their start and end apart: 40 -> 40, of which waited for: 18 -> 20; matrix products, arithmetic and copies ran while one was open for 0% -> 0% of each run, Pallas kernels for 23% -> 23%
where the time goes in v6:
time: 111 us
  starting transfers between devices  38.4 us (35%)
  Pallas kernels  34.4 us (31%)
  waiting for transfers between devices  34 us (31%)
  local copies, waits for them, and re-layouts  3.42 us (3%)
    ppermute x40, starting transfers between devices, swap(): return lax.ppermute(x, axis, [(i, i ^ mask) for i in range(size)])  38.4 us
    ppermute x40, waiting for transfers between devices, swap(): return lax.ppermute(x, axis, [(i, i ^ mask) for i in range(size)])  34 us
    pallas_call x10, Pallas kernels, call(): pl.pallas_call(kernel, in_specs=[VMEM] * len(args), out_specs=[VMEM] * le...  29.5 us
    unnamed x18, local copies, waits for them, and re-layouts  3.42 us
    pallas_call x1, Pallas kernels, body(): pl.pallas_call(pack_kernel, in_specs=[SMEM] + [ANY] * 5 + [VMEM], out_spe...  2.57 us
    pallas_call x14, Pallas kernels, run(): pl.pallas_call(kernel, in_specs=[VMEM] * len(args), out_specs=[VMEM] * le...  2.3 us
  transfers between devices with their start and end apart: 40, of which 20 were waited for; matrix products, arithmetic and copies ran while one was open for 0% of the time, Pallas kernels for 23%

profile of v6, /device:TPU:9, one launch (start us, length us, event | category | flops | bytes accessed | tf_op | source)
XLA Modules:
  0.0 111.1 jit_solution(9617587788943366825)
XLA Ops:
  0.6 2.6 %pack.1 = (bf16[352,256]{1,0:T(8,128)(2,1)}, bf16[352,256]{1,0:T(8,128)(2,1)}, bf16[304,256]{1,0:T(8,128)(2,1)}, bf16[304,256]{1,0:T(8,128)(2,1)}, bf16[64,256]{1,0:T(8,128)(2,1)}) custom-call(s32[16]{0:T(128)} %lens.1, bf16[2,3,64,256]{3,2,1,0:T(8,128)(2,1)} %bitcast.4, bf16[2,64,256]{2,1,0:T(8,128)(2,1)} %bitcast.5, bf16[2,64,256]{2,1,0:T(8,128)(2,1)} %out.1, ...), custom_call_target="tpu_custom_call" | custom-call | tf_op jit(solution)/shard_map/pack/pallas_call | solution.py:713
  3.2 1.4 %collective-permute-start.3 = (bf16[304,256]{1,0:T(8,128)(2,1)}, bf16[304,256]{1,0:T(8,128)(2,1)S(1)}, u32[]{:S(2)}, u32[]{:S(2)}) collective-permute-start(bf16[304,256]{1,0:T(8,128)(2,1)} %get-tuple-element.124), channel_id=1, source_target_pairs={{0,3},{1,2},{2,1},{3,0},{4,7},{5,6},{6,5},{7,4},{8,11},{9,10},{10,... | collective-permute-start | bytes 466952 | tf_op jit(solution)/shard_map/ppermute | solution.py:669
  4.6 1.1 collective-permute-start.2
  5.7 1.1 collective-permute-start.1
  6.8 1.0 copy-done.4
  7.8 0.9 copy-done.5
  8.7 0.8 copy-done.6
  9.5 0.7 copy-done.8
  10.2 5.0 %collective-permute-done.3.c = bf16[304,256]{1,0:T(8,128)(2,1)S(1)} collective-permute-done((bf16[304,256]{1,0:T(8,128)(2,1)}, bf16[304,256]{1,0:T(8,128)(2,1)S(1)}, u32[]{:S(2)}, u32[]{:S(2)}) %collective-permute-start.3) | collective-permute-done | bytes 155680 | tf_op jit(solution)/shard_map/ppermute | solution.py:669
  15.2 2.4 %collective-permute-done.2.b = bf16[304,256]{1,0:T(8,128)(2,1)S(1)} collective-permute-done((bf16[304,256]{1,0:T(8,128)(2,1)}, bf16[304,256]{1,0:T(8,128)(2,1)S(1)}, u32[]{:S(2)}, u32[]{:S(2)}) %collective-permute-start.2) | collective-permute-done | bytes 155680 | tf_op jit(solution)/shard_map/ppermute | solution.py:669
  17.6 1.6 %collective-permute-start.5 = (bf16[528,256]{1,0:T(8,128)(2,1)S(1)}, bf16[528,256]{1,0:T(8,128)(2,1)S(1)}, u32[]{:S(2)}, u32[]{:S(2)}) collective-permute-start(bf16[528,256]{1,0:T(8,128)(2,1)S(1)} %get-tuple-element.133.refs_1_), channel_id=1, source_target_pairs={{0,4},{4,0},{8,12},{12,8},{16,20},{20,16},{24,28},{28,24},{1,5},{5... | collective-permute-start | bytes 811016 | tf_op jit(solution)/shard_map/ppermute | solution.py:669
  19.2 1.2 %collective-permute-start.4 = (bf16[192,256]{1,0:T(8,128)(2,1)S(1)}, bf16[192,256]{1,0:T(8,128)(2,1)S(1)}, u32[]{:S(2)}, u32[]{:S(2)}) collective-permute-start(bf16[192,256]{1,0:T(8,128)(2,1)S(1)} %get-tuple-element.131.refs_2_), channel_id=1, source_target_pairs={{0,8},{4,12},{8,0},{12,4},{16,24},{20,28},{24,16},{28,20},{1,9},{5... | collective-permute-start | bytes 294920 | tf_op jit(solution)/shard_map/ppermute | solution.py:669
  20.5 0.3 collective-permute-start.6
  20.9 3.9 %collective-permute-start.11 = (bf16[304,256]{1,0:T(8,128)(2,1)}, bf16[304,256]{1,0:T(8,128)(2,1)S(1)}, u32[]{:S(2)}, u32[]{:S(2)}) collective-permute-start(bf16[304,256]{1,0:T(8,128)(2,1)} %get-tuple-element.123), channel_id=1, source_target_pairs={{0,2},{1,3},{2,0},{3,1},{4,6},{5,7},{6,4},{7,5},{8,10},{9,11},{10,... | collective-permute-start | bytes 466952 | tf_op jit(solution)/shard_map/ppermute | solution.py:669
  24.8 0.8 collective-permute-start
  25.7 1.5 %collective-permute-start.7 = (bf16[192,256]{1,0:T(8,128)(2,1)S(1)}, bf16[192,256]{1,0:T(8,128)(2,1)S(1)}, u32[]{:S(2)}, u32[]{:S(2)}) collective-permute-start(bf16[192,256]{1,0:T(8,128)(2,1)S(1)} %get-tuple-element.131.refs_2_), channel_id=1, source_target_pairs={{0,4},{4,0},{8,12},{12,8},{16,20},{20,16},{24,28},{28,24},{1,5},{5... | collective-permute-start | bytes 294920 | tf_op jit(solution)/shard_map/ppermute | solution.py:669
  27.3 3.8 %attn_fwd.2 = (f32[1024,256]{1,0:T(8,128)S(1)}, f32[1024,256]{1,0:T(8,128)S(1)}, bf16[1024,256]{1,0:T(8,128)(2,1)S(1)}, bf16[768,1024]{1,0:T(8,128)(2,1)S(1)}, b...) custom-call(bf16[352,256]{1,0:T(8,128)(2,1)S(1)} %get-tuple-element.127.refs_0_, ...), custom_call_target="tpu_custom_call" | custom-call | flops 49999998976 | bytes 1024 | tf_op jit(solution)/shard_map/attn_fwd/pallas_call | solution.py:561
  31.1 0.5 collective-permute-start.9
  31.7 0.9 collective-permute-done.9.refs_8_
  32.5 0.4 collective-permute-done.10.refs_9_
  32.9 2.2 %mlp_fwd.1 = (f32[1024,256]{1,0:T(8,128)S(1)}, bf16[1024,1024]{1,0:T(8,128)(2,1)S(1)}, bf16[1024,1024]{1,0:T(8,128)(2,1)S(1)}) custom-call(bf16[2,256,256]{2,1,0:T(8,128)(2,1)S(1)} %copy-done, bf16[2,256,256]{2,1,0:T(8,128)(2,1)S(1)} %copy-done.1, bf16[192,256]{1,0:T(8,128)(2,1)S(1)} %get-tuple-element.131.refs_2_, ...), custom_call_target="tpu_custom_call" | custom-call | flops 1000 | bytes 1024 | tf_op jit(solution)/shard_map/mlp_fwd/pallas_call | solution.py:561
  35.1 0.2 collective-permute-done.11.b
  35.4 1.5 %collective-permute-start.14 = (bf16[528,256]{1,0:T(8,128)(2,1)S(1)}, bf16[528,256]{1,0:T(8,128)(2,1)S(1)}, u32[]{:S(2)}, u32[]{:S(2)}) collective-permute-start(bf16[528,256]{1,0:T(8,128)(2,1)S(1)} %get-tuple-element.147.refs_1_), channel_id=1, source_target_pairs={{0,4},{4,0},{8,12},{12,8},{16,20},{20,16},{24,28},{28,24},{1,5},{5... | collective-permute-start | bytes 811016 | tf_op jit(solution)/shard_map/ppermute | solution.py:669
  36.9 1.2 %collective-permute-start.13 = (bf16[384,256]{1,0:T(8,128)(2,1)S(1)}, bf16[384,256]{1,0:T(8,128)(2,1)S(1)}, u32[]{:S(2)}, u32[]{:S(2)}) collective-permute-start(bf16[384,256]{1,0:T(8,128)(2,1)S(1)} %get-tuple-element.145.refs_2_), channel_id=1, source_target_pairs={{0,8},{4,12},{8,0},{12,4},{16,24},{20,28},{24,16},{28,20},{1,9},{5... | collective-permute-start | bytes 589832 | tf_op jit(solution)/shard_map/ppermute | solution.py:669
  38.1 0.3 collective-permute-start.15
  38.5 3.8 %attn_fwd.3 = (f32[1024,256]{1,0:T(8,128)S(1)}, f32[1024,256]{1,0:T(8,128)S(1)}, bf16[1024,256]{1,0:T(8,128)(2,1)S(1)}, bf16[768,1024]{1,0:T(8,128)(2,1)S(1)}, b...) custom-call(bf16[352,256]{1,0:T(8,128)(2,1)S(1)} %copy-done.3, bf16[528,256]{1,0:T(8,128)(2,1)S(1)} %get-tuple-element.147.refs_1_, ...), custom_call_target="tpu_custom_call" | custom-call | flops 1000 | bytes 1024 | tf_op jit(solution)/shard_map/attn_fwd/pallas_call | solution.py:561
  42.3 1.1 collective-permute-done.13.refs_3_
  43.4 0.8 collective-permute-start.16
  44.2 1.1 collective-permute-done.16.refs_5_
  45.3 4.4 %mlp_both.1 = (f32[1024,256]{1,0:T(8,128)}, f32[1024,256]{1,0:T(8,128)S(1)}, bf16[4,256,256]{2,1,0:T(8,128)(2,1)S(1)}, bf16[4,256,256]{2,1,0:T(8,128)(2,1)S(1)}, f32[8,256]{1,0:T(8,128)S(1)}) custom-call(bf16[2,256,256]{2,1,0:T(8,128)(2,1)S(1)} %copy-done, bf16[2,256,256]{2,1,0:T(8,128)(2,1)S(1)} %copy-done.1, ...), custom_call_target="tpu_custom_call" | custom-call | flops 1000 | bytes 1024 | tf_op jit(solution)/shard_map/mlp_both/pallas_call | solution.py:561
  49.7 0.4 collective-permute-start.17
  50.1 1.1 attn_pre.2
  51.2 0.5 collective-permute-done.17.got
  51.8 1.3 %collective-permute-start.20 = (bf16[4,128,256]{2,1,0:T(8,128)(2,1)S(1)}, bf16[4,128,256]{2,1,0:T(8,128)(2,1)S(1)}, u32[]{:S(2)}, u32[]{:S(2)}) collective-permute-start(bf16[4,128,256]{2,1,0:T(8,128)(2,1)S(1)} %get-tuple-element.159), channel_id=1, source_target_pairs={{0,8},{4,12},{8,0},{12,4},{16,24},{20,28},{24,16},{28,20},{1,9},{5... | collective-permute-start | bytes 786440 | tf_op jit(solution)/shard_map/ppermute | solution.py:669
  53.1 4.4 %attn_bwd.1 = (f32[1024,256]{1,0:T(8,128)S(1)}, bf16[4,176,256]{2,1,0:T(8,128)(2,1)S(1)}, bf16[4,176,256]{2,1,0:T(8,128)(2,1)S(1)}) custom-call(bf16[352,256]{1,0:T(8,128)(2,1)S(1)} %copy-done.3, bf16[528,256]{1,0:T(8,128)(2,1)S(1)} %get-tuple-element.147.refs_1_, bf16[528,256]{1,0:T(8,128)(2,1)S(1)} %collective-permute-done.14.refs_2_, ...), custom_call_target="tpu_custom_call" | custom-call | flops 1000 | bytes 1024 | tf_op jit(solution)/shard_map/attn_bwd/pallas_call | solution.py:561
  57.5 0.7 collective-permute-start.21
  58.1 2.8 %mlp_bwd.1 = (f32[1024,256]{1,0:T(8,128)S(1)}, bf16[4,256,256]{2,1,0:T(8,128)(2,1)S(1)}, bf16[4,256,256]{2,1,0:T(8,128)(2,1)S(1)}, f32[8,256]{1,0:T(8,128)S(1)}) custom-call(bf16[2,256,256]{2,1,0:T(8,128)(2,1)S(1)} %copy-done, bf16[2,256,256]{2,1,0:T(8,128)(2,1)S(1)} %copy-done.1, bf16[192,256]{1,0:T(8,128)(2,1)S(1)} %get-tuple-element.131.refs_2_, ...), custom_call_target="tpu_custom_call" | custom-call | flops 1000 | bytes 1024 | tf_op jit(solution)/shard_map/mlp_bwd/pallas_call | solution.py:561
  61.2 0.2 collective-permute-start.24
  61.5 3.7 %collective-permute-start.23 = (bf16[304,256]{1,0:T(8,128)(2,1)S(1)}, bf16[304,256]{1,0:T(8,128)(2,1)S(1)}, u32[]{:S(2)}, u32[]{:S(2)}) collective-permute-start(bf16[304,256]{1,0:T(8,128)(2,1)S(1)} %get-tuple-element.200), channel_id=1, source_target_pairs={{0,2},{1,3},{2,0},{3,1},{4,6},{5,7},{6,4},{7,5},{8,10},{9,11},{10,... | collective-permute-start | bytes 466952 | tf_op jit(solution)/shard_map/ppermute | solution.py:669
  65.1 1.1 attn_pre.3
  66.4 0.3 collective-permute-start.19
  66.7 3.8 %attn_grads.1 = (bf16[768,1024]{1,0:T(8,128)(2,1)S(1)}, bf16[4,176,256]{2,1,0:T(8,128)(2,1)S(1)}, bf16[2,176,256]{2,1,0:T(8,128)(2,1)S(1)}, bf16[2,176,256]{2,1,0:T(8,128)(2,1)S(1)}) custom-call(bf16[352,256]{1,0:T(8,128)(2,1)S(1)} %get-tuple-element.127.refs_0_, bf16[528,256]{1,0:T(8,128)(2,1)S(1)} %get-tuple-element.133.refs_1_, ...), custom_call_target="tpu_custom_call" | custom-call | flops 1000 | bytes 1024 | tf_op jit(solution)/shard_map/attn_grads/pallas_call | solution.py:561
  70.5 4.4 %collective-permute-done.23.refs_2_ = bf16[304,256]{1,0:T(8,128)(2,1)S(1)} collective-permute-done((bf16[304,256]{1,0:T(8,128)(2,1)S(1)}, bf16[304,256]{1,0:T(8,128)(2,1)S(1)}, u32[]{:S(2)}, u32[]{:S(2)}) %collective-permute-start.23) | collective-permute-done | bytes 155680 | tf_op jit(solution)/shard_map/ppermute | solution.py:669
  74.9 1.3 %collective-permute-start.25 = (bf16[2,176,256]{2,1,0:T(8,128)(2,1)S(1)}, bf16[2,176,256]{2,1,0:T(8,128)(2,1)S(1)}, u32[]{:S(2)}, u32[]{:S(2)}) collective-permute-start(bf16[2,176,256]{2,1,0:T(8,128)(2,1)S(1)} %get-tuple-element.207), channel_id=1, source_target_pairs={{0,4},{4,0},{8,12},{12,8},{16,20},{20,16},{24,28},{28,24},{1,5},{5... | collective-permute-start | bytes 540680 | tf_op jit(solution)/shard_map/ppermute | solution.py:669
  76.3 1.0 collective-permute-done.25.refs_3_
  77.3 0.4 collective-permute-done.26.refs_4_
  77.8 2.7 %collective-permute-start.29 = (bf16[304,256]{1,0:T(8,128)(2,1)S(1)}, bf16[304,256]{1,0:T(8,128)(2,1)S(1)}, u32[]{:S(2)}, u32[]{:S(2)}) collective-permute-start(bf16[304,256]{1,0:T(8,128)(2,1)S(1)} %get-tuple-element.210), channel_id=1, source_target_pairs={{0,1},{1,0},{2,3},{3,2},{4,5},{5,4},{6,7},{7,6},{8,9},{9,8},{10,11... | collective-permute-start | bytes 466952 | tf_op jit(solution)/shard_map/ppermute | solution.py:669
  80.5 1.3 %collective-permute-start.33 = (bf16[304,256]{1,0:T(8,128)(2,1)S(1)}, bf16[304,256]{1,0:T(8,128)(2,1)S(1)}, u32[]{:S(2)}, u32[]{:S(2)}) collective-permute-start(bf16[304,256]{1,0:T(8,128)(2,1)S(1)} %get-tuple-element.212), channel_id=1, source_target_pairs={{0,3},{1,2},{2,1},{3,0},{4,7},{5,6},{6,5},{7,4},{8,11},{9,10},{10,... | collective-permute-start | bytes 466952 | tf_op jit(solution)/shard_map/ppermute | solution.py:669
  81.8 1.2 %collective-permute-start.28 = (bf16[176,256]{1,0:T(8,128)(2,1)S(1)}, bf16[176,256]{1,0:T(8,128)(2,1)S(1)}, u32[]{:S(2)}, u32[]{:S(2)}) collective-permute-start(bf16[176,256]{1,0:T(8,128)(2,1)S(1)} %get-tuple-element.217.refs_0_), channel_id=1, source_target_pairs={{0,16},{4,20},{8,24},{12,28},{16,0},{20,4},{24,8},{28,12},{1,17},{... | collective-permute-start | bytes 270344 | tf_op jit(solution)/shard_map/ppermute | solution.py:669
  83.0 0.3 collective-permute-start.27
  83.3 2.4 %collective-permute-done.29.refs_2_ = bf16[304,256]{1,0:T(8,128)(2,1)S(1)} collective-permute-done((bf16[304,256]{1,0:T(8,128)(2,1)S(1)}, bf16[304,256]{1,0:T(8,128)(2,1)S(1)}, u32[]{:S(2)}, u32[]{:S(2)}) %collective-permute-start.29) | collective-permute-done | bytes 155680 | tf_op jit(solution)/shard_map/ppermute | solution.py:669
  85.7 1.2 %collective-permute-start.30 = (bf16[176,256]{1,0:T(8,128)(2,1)S(1)}, bf16[176,256]{1,0:T(8,128)(2,1)S(1)}, u32[]{:S(2)}, u32[]{:S(2)}) collective-permute-start(bf16[176,256]{1,0:T(8,128)(2,1)S(1)} %get-tuple-element.217.refs_0_), channel_id=1, source_target_pairs={{0,24},{4,28},{8,16},{12,20},{16,8},{20,12},{24,0},{28,4},{1,25},{... | collective-permute-start | bytes 270344 | tf_op jit(solution)/shard_map/ppermute | solution.py:669
  87.0 2.2 %attn_post.1 = f32[1024,256]{1,0:T(8,128)} custom-call(bf16[352,256]{1,0:T(8,128)(2,1)S(1)} %get-tuple-element.127.refs_0_, bf16[528,256]{1,0:T(8,128)(2,1)S(1)} %get-tuple-element.133.refs_1_, bf16[528,256]{1,0:T(8,128)(2,1)S(1)} %collective-permute-done.5.refs_2_, bf16[768,1024]{1,0:T(8,128)(2,1)S(1)} %get-tuple-element.213.refs_3_, ...), custom_call_target="tpu_custom_call" | custom-call | flops 1000 | bytes 1024 | tf_op jit(solution)/shard_map/attn_post/pallas_call | solution.py:561
  89.2 0.8 collective-permute-done.30.refs_3_
  90.1 5.7 %collective-permute-done.33.refs_4_ = bf16[304,256]{1,0:T(8,128)(2,1)S(1)} collective-permute-done((bf16[304,256]{1,0:T(8,128)(2,1)S(1)}, bf16[304,256]{1,0:T(8,128)(2,1)S(1)}, u32[]{:S(2)}, u32[]{:S(2)}) %collective-permute-start.33) | collective-permute-done | bytes 155680 | tf_op jit(solution)/shard_map/ppermute | solution.py:669
  95.9 1.3 %collective-permute-start.35 = (bf16[256,256]{1,0:T(8,128)(2,1)S(1)}, bf16[256,256]{1,0:T(8,128)(2,1)S(1)}, u32[]{:S(2)}, u32[]{:S(2)}) collective-permute-start(bf16[256,256]{1,0:T(8,128)(2,1)S(1)} %get-tuple-element.223.high), channel_id=1, source_target_pairs={{0,16},{4,20},{8,24},{12,28},{16,0},{20,4},{24,8},{28,12},{1,17},{... | collective-permute-start | bytes 393224 | tf_op jit(solution)/shard_map/ppermute | solution.py:669
  97.2 0.3 collective-permute-start.34
  97.4 3.4 %collective-permute-done.34.low_got = bf16[176,256]{1,0:T(8,128)(2,1)S(1)} collective-permute-done((bf16[176,256]{1,0:T(8,128)(2,1)S(1)}, bf16[176,256]{1,0:T(8,128)(2,1)S(1)}, u32[]{:S(2)}, u32[]{:S(2)}) %collective-permute-start.34) | collective-permute-done | bytes 90144 | tf_op jit(solution)/shard_map/ppermute | solution.py:669
  100.9 0.3 collective-permute-start.37
  101.4 3.2 %collective-permute-done.36.low_got = bf16[176,256]{1,0:T(8,128)(2,1)S(1)} collective-permute-done((bf16[176,256]{1,0:T(8,128)(2,1)S(1)}, bf16[176,256]{1,0:T(8,128)(2,1)S(1)}, u32[]{:S(2)}, u32[]{:S(2)}) %collective-permute-start.36) | collective-permute-done | bytes 90144 | tf_op jit(solution)/shard_map/ppermute | solution.py:669
  104.8 3.5 %collective-permute-start.38 = (bf16[512,256]{1,0:T(8,128)(2,1)S(1)}, bf16[512,256]{1,0:T(8,128)(2,1)S(1)}, u32[]{:S(2)}, u32[]{:S(2)}) collective-permute-start(bf16[512,256]{1,0:T(8,128)(2,1)S(1)} %get-tuple-element.226.high), channel_id=1, source_target_pairs={{0,4},{4,0},{8,12},{12,8},{16,20},{20,16},{24,28},{28,24},{1,5},{5... | collective-permute-start | bytes 786440 | tf_op jit(solution)/shard_map/ppermute | solution.py:669
  108.4 0.4 collective-permute-start.39
  108.9 0.8 collective-permute-done.31.low_other
  109.8 1.3 %finish.1 = (f32[2,3,64,256]{3,2,1,0:T(8,128)}, f32[2,64,256]{2,1,0:T(8,128)}, f32[2,256,256]{2,1,0:T(8,128)}, f32[2,256,256]{2,1,0:T(8,128)}, f32[2,64,256]{2,1...) custom-call(bf16[176,256]{1,0:T(8,128)(2,1)S(1)} %four_sum.1.low, ...), custom_call_target="tpu_custom_call" | custom-call | flops 1000 | bytes 1024 | tf_op jit(solution)/shard_map/finish/pallas_call | solution.py:646
  (59 shorter events, 2.2 us)
Async XLA Ops:
  3.2 12.0 %collective-permute-start.3 = (bf16[304,256]{1,0:T(8,128)(2,1)}, bf16[304,256]{1,0:T(8,128)(2,1)S(1)}, u32[]{:S(2)}, u32[]{:S(2)}) collective-permute-start(bf16[304,256]{1,0:T(8,128)(2,1)} %get-tuple-element.124), channel_id=1, source_target_pairs={{0,3},{1,2},{2,1},{3,0},{4,7},{5,6},{6,5},{7,4},{8,11},{9,10},{10,... | collective-permute-start | bytes 466952 | tf_op jit(solution)/shard_map/ppermute | solution.py:669
  4.6 13.0 %collective-permute-start.2 = (bf16[304,256]{1,0:T(8,128)(2,1)}, bf16[304,256]{1,0:T(8,128)(2,1)S(1)}, u32[]{:S(2)}, u32[]{:S(2)}) collective-permute-start(bf16[304,256]{1,0:T(8,128)(2,1)} %get-tuple-element.124), channel_id=1, source_target_pairs={{0,2},{1,3},{2,0},{3,1},{4,6},{5,7},{6,4},{7,5},{8,10},{9,11},{10,... | collective-permute-start | bytes 466952 | tf_op jit(solution)/shard_map/ppermute | solution.py:669
  5.7 11.9 %collective-permute-start.1 = (bf16[304,256]{1,0:T(8,128)(2,1)}, bf16[304,256]{1,0:T(8,128)(2,1)S(1)}, u32[]{:S(2)}, u32[]{:S(2)}) collective-permute-start(bf16[304,256]{1,0:T(8,128)(2,1)} %get-tuple-element.124), channel_id=1, source_target_pairs={{0,1},{1,0},{2,3},{3,2},{4,5},{5,4},{6,7},{7,6},{8,9},{9,8},{10,11... | collective-permute-start | bytes 466952 | tf_op jit(solution)/shard_map/ppermute | solution.py:669
  6.8 1.0 copy-start.4
  7.8 0.9 copy-start.5
  8.7 0.8 copy-start.6
  9.5 0.7 copy-start.8
  17.6 9.6 %collective-permute-start.5 = (bf16[528,256]{1,0:T(8,128)(2,1)S(1)}, bf16[528,256]{1,0:T(8,128)(2,1)S(1)}, u32[]{:S(2)}, u32[]{:S(2)}) collective-permute-start(bf16[528,256]{1,0:T(8,128)(2,1)S(1)} %get-tuple-element.133.refs_1_), channel_id=1, source_target_pairs={{0,4},{4,0},{8,12},{12,8},{16,20},{20,16},{24,28},{28,24},{1,5},{5... | collective-permute-start | bytes 811016 | tf_op jit(solution)/shard_map/ppermute | solution.py:669
  19.2 5.5 %collective-permute-start.4 = (bf16[192,256]{1,0:T(8,128)(2,1)S(1)}, bf16[192,256]{1,0:T(8,128)(2,1)S(1)}, u32[]{:S(2)}, u32[]{:S(2)}) collective-permute-start(bf16[192,256]{1,0:T(8,128)(2,1)S(1)} %get-tuple-element.131.refs_2_), channel_id=1, source_target_pairs={{0,8},{4,12},{8,0},{12,4},{16,24},{20,28},{24,16},{28,20},{1,9},{5... | collective-permute-start | bytes 294920 | tf_op jit(solution)/shard_map/ppermute | solution.py:669
  20.5 5.3 %collective-permute-start.6 = (bf16[192,256]{1,0:T(8,128)(2,1)S(1)}, bf16[192,256]{1,0:T(8,128)(2,1)S(1)}, u32[]{:S(2)}, u32[]{:S(2)}) collective-permute-start(bf16[192,256]{1,0:T(8,128)(2,1)S(1)} %get-tuple-element.132.refs_3_), channel_id=1, source_target_pairs={{0,8},{4,12},{8,0},{12,4},{16,24},{20,28},{24,16},{28,20},{1,9},{5... | collective-permute-start | bytes 294920 | tf_op jit(solution)/shard_map/ppermute | solution.py:669
  20.7 14.4 %collective-permute-start.12 = (bf16[304,256]{1,0:T(8,128)(2,1)}, bf16[304,256]{1,0:T(8,128)(2,1)S(1)}, u32[]{:S(2)}, u32[]{:S(2)}) collective-permute-start(bf16[304,256]{1,0:T(8,128)(2,1)} %get-tuple-element.123), channel_id=1, source_target_pairs={{0,3},{1,2},{2,1},{3,0},{4,7},{5,6},{6,5},{7,4},{8,11},{9,10},{10,... | collective-permute-start | bytes 466952 | tf_op jit(solution)/shard_map/ppermute | solution.py:669
  20.9 14.5 %collective-permute-start.11 = (bf16[304,256]{1,0:T(8,128)(2,1)}, bf16[304,256]{1,0:T(8,128)(2,1)S(1)}, u32[]{:S(2)}, u32[]{:S(2)}) collective-permute-start(bf16[304,256]{1,0:T(8,128)(2,1)} %get-tuple-element.123), channel_id=1, source_target_pairs={{0,2},{1,3},{2,0},{3,1},{4,6},{5,7},{6,4},{7,5},{8,10},{9,11},{10,... | collective-permute-start | bytes 466952 | tf_op jit(solution)/shard_map/ppermute | solution.py:669
  24.8 10.6 %collective-permute-start = (bf16[304,256]{1,0:T(8,128)(2,1)}, bf16[304,256]{1,0:T(8,128)(2,1)S(1)}, u32[]{:S(2)}, u32[]{:S(2)}) collective-permute-start(bf16[304,256]{1,0:T(8,128)(2,1)} %get-tuple-element.123), channel_id=1, source_target_pairs={{0,1},{1,0},{2,3},{3,2},{4,5},{5,4},{6,7},{7,6},{8,9},{9,8},{10,11... | collective-permute-start | bytes 466952 | tf_op jit(solution)/shard_map/ppermute | solution.py:669
  25.7 5.4 %collective-permute-start.7 = (bf16[192,256]{1,0:T(8,128)(2,1)S(1)}, bf16[192,256]{1,0:T(8,128)(2,1)S(1)}, u32[]{:S(2)}, u32[]{:S(2)}) collective-permute-start(bf16[192,256]{1,0:T(8,128)(2,1)S(1)} %get-tuple-element.131.refs_2_), channel_id=1, source_target_pairs={{0,4},{4,0},{8,12},{12,8},{16,20},{20,16},{24,28},{28,24},{1,5},{5... | collective-permute-start | bytes 294920 | tf_op jit(solution)/shard_map/ppermute | solution.py:669
  27.2 4.4 %collective-permute-start.8 = (bf16[192,256]{1,0:T(8,128)(2,1)S(1)}, bf16[192,256]{1,0:T(8,128)(2,1)S(1)}, u32[]{:S(2)}, u32[]{:S(2)}) collective-permute-start(bf16[192,256]{1,0:T(8,128)(2,1)S(1)} %get-tuple-element.132.refs_3_), channel_id=1, source_target_pairs={{0,4},{4,0},{8,12},{12,8},{16,20},{20,16},{24,28},{28,24},{1,5},{5... | collective-permute-start | bytes 294920 | tf_op jit(solution)/shard_map/ppermute | solution.py:669
  27.3 5.6 %copy-start = (bf16[2,256,256]{2,1,0:T(8,128)(2,1)S(1)}, bf16[2,256,256]{2,1,0:T(8,128)(2,1)}, u32[]{:S(2)}) copy-start(bf16[2,256,256]{2,1,0:T(8,128)(2,1)} %refs_0_.7) | copy-start | bytes 786436
  27.3 5.6 %copy-start.1 = (bf16[2,256,256]{2,1,0:T(8,128)(2,1)S(1)}, bf16[2,256,256]{2,1,0:T(8,128)(2,1)}, u32[]{:S(2)}) copy-start(bf16[2,256,256]{2,1,0:T(8,128)(2,1)} %refs_1_.5) | copy-start | bytes 786436
  27.3 5.6 %copy-start.7 = (f32[2,256]{1,0:T(2,128)S(1)}, f32[2,256]{1,0:T(2,128)}, u32[]{:S(2)}) copy-start(f32[2,256]{1,0:T(2,128)} %refs_14_.1) | copy-start | bytes 6148
  31.1 1.4 %collective-permute-start.9 = (bf16[192,256]{1,0:T(8,128)(2,1)S(1)}, bf16[192,256]{1,0:T(8,128)(2,1)S(1)}, u32[]{:S(2)}, u32[]{:S(2)}) collective-permute-start(bf16[192,256]{1,0:T(8,128)(2,1)S(1)} %collective-permute-done.4.refs_4_), channel_id=1, source_target_pairs={{0,4},{4,0},{8,12},{12,8},{16,20},{20,16},{24,28},{28,24},{1,5},{5... | collective-permute-start | bytes 294920 | tf_op jit(solution)/shard_map/ppermute | solution.py:669
  31.6 1.3 %collective-permute-start.10 = (bf16[192,256]{1,0:T(8,128)(2,1)S(1)}, bf16[192,256]{1,0:T(8,128)(2,1)S(1)}, u32[]{:S(2)}, u32[]{:S(2)}) collective-permute-start(bf16[192,256]{1,0:T(8,128)(2,1)S(1)} %collective-permute-done.6.refs_5_), channel_id=1, source_target_pairs={{0,4},{4,0},{8,12},{12,8},{16,20},{20,16},{24,28},{28,24},{1,5},{5... | collective-permute-start | bytes 294920 | tf_op jit(solution)/shard_map/ppermute | solution.py:669
  32.9 5.6 %copy-start.3 = (bf16[352,256]{1,0:T(8,128)(2,1)S(1)}, bf16[352,256]{1,0:T(8,128)(2,1)}, u32[]{:S(2)}) copy-start(bf16[352,256]{1,0:T(8,128)(2,1)} %get-tuple-element.146.refs_0_) | copy-start | bytes 540676
  35.1 10.2 %copy-start.2 = (bf16[1024,256]{1,0:T(8,128)(2,1)S(1)}, bf16[1024,256]{1,0:T(8,128)(2,1)}, u32[]{:S(2)}) copy-start(bf16[1024,256]{1,0:T(8,128)(2,1)} %refs_3_.1) | copy-start | bytes 1572868
  35.4 3.1 %collective-permute-start.14 = (bf16[528,256]{1,0:T(8,128)(2,1)S(1)}, bf16[528,256]{1,0:T(8,128)(2,1)S(1)}, u32[]{:S(2)}, u32[]{:S(2)}) collective-permute-start(bf16[528,256]{1,0:T(8,128)(2,1)S(1)} %get-tuple-element.147.refs_1_), channel_id=1, source_target_pairs={{0,4},{4,0},{8,12},{12,8},{16,20},{20,16},{24,28},{28,24},{1,5},{5... | collective-permute-start | bytes 811016 | tf_op jit(solution)/shard_map/ppermute | solution.py:669
  36.9 6.5 %collective-permute-start.13 = (bf16[384,256]{1,0:T(8,128)(2,1)S(1)}, bf16[384,256]{1,0:T(8,128)(2,1)S(1)}, u32[]{:S(2)}, u32[]{:S(2)}) collective-permute-start(bf16[384,256]{1,0:T(8,128)(2,1)S(1)} %get-tuple-element.145.refs_2_), channel_id=1, source_target_pairs={{0,8},{4,12},{8,0},{12,4},{16,24},{20,28},{24,16},{28,20},{1,9},{5... | collective-permute-start | bytes 589832 | tf_op jit(solution)/shard_map/ppermute | solution.py:669
  38.1 6.1 %collective-permute-start.15 = (bf16[384,256]{1,0:T(8,128)(2,1)S(1)}, bf16[384,256]{1,0:T(8,128)(2,1)S(1)}, u32[]{:S(2)}, u32[]{:S(2)}) collective-permute-start(bf16[384,256]{1,0:T(8,128)(2,1)S(1)} %get-tuple-element.145.refs_2_), channel_id=1, source_target_pairs={{0,4},{4,0},{8,12},{12,8},{16,20},{20,16},{24,28},{28,24},{1,5},{5... | collective-permute-start | bytes 589832 | tf_op jit(solution)/shard_map/ppermute | solution.py:669
  43.4 1.9 %collective-permute-start.16 = (bf16[384,256]{1,0:T(8,128)(2,1)S(1)}, bf16[384,256]{1,0:T(8,128)(2,1)S(1)}, u32[]{:S(2)}, u32[]{:S(2)}) collective-permute-start(bf16[384,256]{1,0:T(8,128)(2,1)S(1)} %collective-permute-done.13.refs_3_), channel_id=1, source_target_pairs={{0,4},{4,0},{8,12},{12,8},{16,20},{20,16},{24,28},{28,24},{1,5},{5... | collective-permute-start | bytes 589832 | tf_op jit(solution)/shard_map/ppermute | solution.py:669
  49.7 2.0 %collective-permute-start.17 = (bf16[4,256,256]{2,1,0:T(8,128)(2,1)S(1)}, bf16[4,256,256]{2,1,0:T(8,128)(2,1)S(1)}, u32[]{:S(2)}, u32[]{:S(2)}) collective-permute-start(bf16[4,256,256]{2,1,0:T(8,128)(2,1)S(1)} %get-tuple-element.153), channel_id=1, source_target_pairs={{0,4},{4,0},{8,12},{12,8},{16,20},{20,16},{24,28},{28,24},{1,5},{5... | collective-permute-start | bytes 1572872 | tf_op jit(solution)/shard_map/ppermute | solution.py:669
  51.8 9.2 %collective-permute-start.20 = (bf16[4,128,256]{2,1,0:T(8,128)(2,1)S(1)}, bf16[4,128,256]{2,1,0:T(8,128)(2,1)S(1)}, u32[]{:S(2)}, u32[]{:S(2)}) collective-permute-start(bf16[4,128,256]{2,1,0:T(8,128)(2,1)S(1)} %get-tuple-element.159), channel_id=1, source_target_pairs={{0,8},{4,12},{8,0},{12,4},{16,24},{20,28},{24,16},{28,20},{1,9},{5... | collective-permute-start | bytes 786440 | tf_op jit(solution)/shard_map/ppermute | solution.py:669
  57.5 3.6 %collective-permute-start.21 = (bf16[4,176,256]{2,1,0:T(8,128)(2,1)S(1)}, bf16[4,176,256]{2,1,0:T(8,128)(2,1)S(1)}, u32[]{:S(2)}, u32[]{:S(2)}) collective-permute-start(bf16[4,176,256]{2,1,0:T(8,128)(2,1)S(1)} %get-tuple-element.194), channel_id=1, source_target_pairs={{0,4},{4,0},{8,12},{12,8},{16,20},{20,16},{24,28},{28,24},{1,5},{5... | collective-permute-start | bytes 1081352 | tf_op jit(solution)/shard_map/ppermute | solution.py:669
  60.9 5.3 %collective-permute-start.18 = (bf16[4,256,256]{2,1,0:T(8,128)(2,1)S(1)}, bf16[4,256,256]{2,1,0:T(8,128)(2,1)S(1)}, u32[]{:S(2)}, u32[]{:S(2)}) collective-permute-start(bf16[4,256,256]{2,1,0:T(8,128)(2,1)S(1)} %get-tuple-element.174), channel_id=1, source_target_pairs={{0,4},{4,0},{8,12},{12,8},{16,20},{20,16},{24,28},{28,24},{1,5},{5... | collective-permute-start | bytes 1572872 | tf_op jit(solution)/shard_map/ppermute | solution.py:669
  61.2 9.3 %collective-permute-start.24 = (bf16[304,256]{1,0:T(8,128)(2,1)S(1)}, bf16[304,256]{1,0:T(8,128)(2,1)S(1)}, u32[]{:S(2)}, u32[]{:S(2)}) collective-permute-start(bf16[304,256]{1,0:T(8,128)(2,1)S(1)} %get-tuple-element.202), channel_id=1, source_target_pairs={{0,3},{1,2},{2,1},{3,0},{4,7},{5,6},{6,5},{7,4},{8,11},{9,10},{10,... | collective-permute-start | bytes 466952 | tf_op jit(solution)/shard_map/ppermute | solution.py:669
  61.5 13.4 %collective-permute-start.23 = (bf16[304,256]{1,0:T(8,128)(2,1)S(1)}, bf16[304,256]{1,0:T(8,128)(2,1)S(1)}, u32[]{:S(2)}, u32[]{:S(2)}) collective-permute-start(bf16[304,256]{1,0:T(8,128)(2,1)S(1)} %get-tuple-element.200), channel_id=1, source_target_pairs={{0,2},{1,3},{2,0},{3,1},{4,6},{5,7},{6,4},{7,5},{8,10},{9,11},{10,... | collective-permute-start | bytes 466952 | tf_op jit(solution)/shard_map/ppermute | solution.py:669
  65.1 9.8 %collective-permute-start.22 = (bf16[304,256]{1,0:T(8,128)(2,1)S(1)}, bf16[304,256]{1,0:T(8,128)(2,1)S(1)}, u32[]{:S(2)}, u32[]{:S(2)}) collective-permute-start(bf16[304,256]{1,0:T(8,128)(2,1)S(1)} %get-tuple-element.198), channel_id=1, source_target_pairs={{0,1},{1,0},{2,3},{3,2},{4,5},{5,4},{6,7},{7,6},{8,9},{9,8},{10,11... | collective-permute-start | bytes 466952 | tf_op jit(solution)/shard_map/ppermute | solution.py:669
  66.4 10.0 %collective-permute-start.19 = (bf16[4,128,256]{2,1,0:T(8,128)(2,1)S(1)}, bf16[4,128,256]{2,1,0:T(8,128)(2,1)S(1)}, u32[]{:S(2)}, u32[]{:S(2)}) collective-permute-start(bf16[4,128,256]{2,1,0:T(8,128)(2,1)S(1)} %get-tuple-element.180), channel_id=1, source_target_pairs={{0,8},{4,12},{8,0},{12,4},{16,24},{20,28},{24,16},{28,20},{1,9},{5... | collective-permute-start | bytes 786440 | tf_op jit(solution)/shard_map/ppermute | solution.py:669
  74.9 2.4 %collective-permute-start.25 = (bf16[2,176,256]{2,1,0:T(8,128)(2,1)S(1)}, bf16[2,176,256]{2,1,0:T(8,128)(2,1)S(1)}, u32[]{:S(2)}, u32[]{:S(2)}) collective-permute-start(bf16[2,176,256]{2,1,0:T(8,128)(2,1)S(1)} %get-tuple-element.207), channel_id=1, source_target_pairs={{0,4},{4,0},{8,12},{12,8},{16,20},{20,16},{24,28},{28,24},{1,5},{5... | collective-permute-start | bytes 540680 | tf_op jit(solution)/shard_map/ppermute | solution.py:669
  76.2 1.4 %collective-permute-start.26 = (bf16[2,176,256]{2,1,0:T(8,128)(2,1)S(1)}, bf16[2,176,256]{2,1,0:T(8,128)(2,1)S(1)}, u32[]{:S(2)}, u32[]{:S(2)}) collective-permute-start(bf16[2,176,256]{2,1,0:T(8,128)(2,1)S(1)} %get-tuple-element.208), channel_id=1, source_target_pairs={{0,4},{4,0},{8,12},{12,8},{16,20},{20,16},{24,28},{28,24},{1,5},{5... | collective-permute-start | bytes 540680 | tf_op jit(solution)/shard_map/ppermute | solution.py:669
  77.8 7.9 %collective-permute-start.29 = (bf16[304,256]{1,0:T(8,128)(2,1)S(1)}, bf16[304,256]{1,0:T(8,128)(2,1)S(1)}, u32[]{:S(2)}, u32[]{:S(2)}) collective-permute-start(bf16[304,256]{1,0:T(8,128)(2,1)S(1)} %get-tuple-element.210), channel_id=1, source_target_pairs={{0,1},{1,0},{2,3},{3,2},{4,5},{5,4},{6,7},{7,6},{8,9},{9,8},{10,11... | collective-permute-start | bytes 466952 | tf_op jit(solution)/shard_map/ppermute | solution.py:669
  80.5 9.5 %collective-permute-start.32 = (bf16[304,256]{1,0:T(8,128)(2,1)S(1)}, bf16[304,256]{1,0:T(8,128)(2,1)S(1)}, u32[]{:S(2)}, u32[]{:S(2)}) collective-permute-start(bf16[304,256]{1,0:T(8,128)(2,1)S(1)} %get-tuple-element.211), channel_id=1, source_target_pairs={{0,2},{1,3},{2,0},{3,1},{4,6},{5,7},{6,4},{7,5},{8,10},{9,11},{10,... | collective-permute-start | bytes 466952 | tf_op jit(solution)/shard_map/ppermute | solution.py:669
  80.5 15.2 %collective-permute-start.33 = (bf16[304,256]{1,0:T(8,128)(2,1)S(1)}, bf16[304,256]{1,0:T(8,128)(2,1)S(1)}, u32[]{:S(2)}, u32[]{:S(2)}) collective-permute-start(bf16[304,256]{1,0:T(8,128)(2,1)S(1)} %get-tuple-element.212), channel_id=1, source_target_pairs={{0,3},{1,2},{2,1},{3,0},{4,7},{5,6},{6,5},{7,4},{8,11},{9,10},{10,... | collective-permute-start | bytes 466952 | tf_op jit(solution)/shard_map/ppermute | solution.py:669
  81.8 7.4 %collective-permute-start.28 = (bf16[176,256]{1,0:T(8,128)(2,1)S(1)}, bf16[176,256]{1,0:T(8,128)(2,1)S(1)}, u32[]{:S(2)}, u32[]{:S(2)}) collective-permute-start(bf16[176,256]{1,0:T(8,128)(2,1)S(1)} %get-tuple-element.217.refs_0_), channel_id=1, source_target_pairs={{0,16},{4,20},{8,24},{12,28},{16,0},{20,4},{24,8},{28,12},{1,17},{... | collective-permute-start | bytes 270344 | tf_op jit(solution)/shard_map/ppermute | solution.py:669
  83.0 6.1 %collective-permute-start.27 = (bf16[176,256]{1,0:T(8,128)(2,1)S(1)}, bf16[176,256]{1,0:T(8,128)(2,1)S(1)}, u32[]{:S(2)}, u32[]{:S(2)}) collective-permute-start(bf16[176,256]{1,0:T(8,128)(2,1)S(1)} %get-tuple-element.217.refs_0_), channel_id=1, source_target_pairs={{0,8},{4,12},{8,0},{12,4},{16,24},{20,28},{24,16},{28,20},{1,9},{5... | collective-permute-start | bytes 270344 | tf_op jit(solution)/shard_map/ppermute | solution.py:669
  85.7 4.3 %collective-permute-start.30 = (bf16[176,256]{1,0:T(8,128)(2,1)S(1)}, bf16[176,256]{1,0:T(8,128)(2,1)S(1)}, u32[]{:S(2)}, u32[]{:S(2)}) collective-permute-start(bf16[176,256]{1,0:T(8,128)(2,1)S(1)} %get-tuple-element.217.refs_0_), channel_id=1, source_target_pairs={{0,24},{4,28},{8,16},{12,20},{16,8},{20,12},{24,0},{28,4},{1,25},{... | collective-permute-start | bytes 270344 | tf_op jit(solution)/shard_map/ppermute | solution.py:669
  95.9 5.0 %collective-permute-start.35 = (bf16[256,256]{1,0:T(8,128)(2,1)S(1)}, bf16[256,256]{1,0:T(8,128)(2,1)S(1)}, u32[]{:S(2)}, u32[]{:S(2)}) collective-permute-start(bf16[256,256]{1,0:T(8,128)(2,1)S(1)} %get-tuple-element.223.high), channel_id=1, source_target_pairs={{0,16},{4,20},{8,24},{12,28},{16,0},{20,4},{24,8},{28,12},{1,17},{... | collective-permute-start | bytes 393224 | tf_op jit(solution)/shard_map/ppermute | solution.py:669
  97.2 3.7 %collective-permute-start.34 = (bf16[176,256]{1,0:T(8,128)(2,1)S(1)}, bf16[176,256]{1,0:T(8,128)(2,1)S(1)}, u32[]{:S(2)}, u32[]{:S(2)}) collective-permute-start(bf16[176,256]{1,0:T(8,128)(2,1)S(1)} %get-tuple-element.222.low), channel_id=1, source_target_pairs={{0,8},{4,12},{8,0},{12,4},{16,24},{20,28},{24,16},{28,20},{1,9},{5... | collective-permute-start | bytes 270344 | tf_op jit(solution)/shard_map/ppermute | solution.py:669
  100.9 3.9 %collective-permute-start.37 = (bf16[256,256]{1,0:T(8,128)(2,1)S(1)}, bf16[256,256]{1,0:T(8,128)(2,1)S(1)}, u32[]{:S(2)}, u32[]{:S(2)}) collective-permute-start(bf16[256,256]{1,0:T(8,128)(2,1)S(1)} %get-tuple-element.225.high), channel_id=1, source_target_pairs={{0,8},{4,12},{8,0},{12,4},{16,24},{20,28},{24,16},{28,20},{1,9},{5... | collective-permute-start | bytes 393224 | tf_op jit(solution)/shard_map/ppermute | solution.py:669
  101.2 3.4 %collective-permute-start.36 = (bf16[176,256]{1,0:T(8,128)(2,1)S(1)}, bf16[176,256]{1,0:T(8,128)(2,1)S(1)}, u32[]{:S(2)}, u32[]{:S(2)}) collective-permute-start(bf16[176,256]{1,0:T(8,128)(2,1)S(1)} %get-tuple-element.224.low), channel_id=1, source_target_pairs={{0,16},{4,20},{8,24},{12,28},{16,0},{20,4},{24,8},{28,12},{1,17},{... | collective-permute-start | bytes 270344 | tf_op jit(solution)/shard_map/ppermute | solution.py:669
  104.8 5.0 %collective-permute-start.38 = (bf16[512,256]{1,0:T(8,128)(2,1)S(1)}, bf16[512,256]{1,0:T(8,128)(2,1)S(1)}, u32[]{:S(2)}, u32[]{:S(2)}) collective-permute-start(bf16[512,256]{1,0:T(8,128)(2,1)S(1)} %get-tuple-element.226.high), channel_id=1, source_target_pairs={{0,4},{4,0},{8,12},{12,8},{16,20},{20,16},{24,28},{28,24},{1,5},{5... | collective-permute-start | bytes 786440 | tf_op jit(solution)/shard_map/ppermute | solution.py:669
  108.3 1.3 %collective-permute-start.31 = (bf16[176,256]{1,0:T(8,128)(2,1)S(1)}, bf16[176,256]{1,0:T(8,128)(2,1)S(1)}, u32[]{:S(2)}, u32[]{:S(2)}) collective-permute-start(bf16[176,256]{1,0:T(8,128)(2,1)S(1)} %four_sum.1.low), channel_id=1, source_target_pairs={{0,4},{4,0},{8,12},{12,8},{16,20},{20,16},{24,28},{28,24},{1,5},{5... | collective-permute-start | bytes 270344 | tf_op jit(solution)/shard_map/ppermute | solution.py:669
  108.4 1.4 %collective-permute-start.39 = (bf16[176,256]{1,0:T(8,128)(2,1)S(1)}, bf16[176,256]{1,0:T(8,128)(2,1)S(1)}, u32[]{:S(2)}, u32[]{:S(2)}) collective-permute-start(bf16[176,256]{1,0:T(8,128)(2,1)S(1)} %get-tuple-element.227.late), channel_id=1, source_target_pairs={{0,4},{4,0},{8,12},{12,8},{16,20},{20,16},{24,28},{28,24},{1,5},{5... | collective-permute-start | bytes 270344 | tf_op jit(solution)/shard_map/ppermute | solution.py:669

commit v7 on v6

--- a/solution.py
+++ b/solution.py
@@ -752,10 +752,10 @@
         keep_m0, send_m0 = split(keep_m0, tie(core_swap(send_m0), pre[0]))
         got_m0 = swap(send_m0, "dp", dp_size, 2)
         gqkv, keep_a0, *send_a0 = attn_grads(0, tie(mask, send_m0), saved0, gain_attn, pre, small_m0, a0)
-        mlp1, attn1 = four_split([tie(x, gqkv) for x in got], (), LONG)
+        grad0 = attn_post(0, gqkv, gain_attn, tokens, pre, a0)
+        mlp1, attn1 = four_split([tie(x, grad0) for x in got], (), LONG)
         sums = core_sum((128, 160), (keep_m0, tie(got_m0, mlp1)), (keep_a0, *[core_swap(x) for x in send_a0]))
         got = scatter(sums)
-        grad0 = attn_post(0, tie(gqkv, *sums), gain_attn, tokens, pre, a0)
         attn1 = sum_direct(attn1, got[1])
         mlp, attn0 = four_split([tie(x, grad0, attn1) for x in got], (mlp1,))
         attn0, mlp = sum_pairs(attn0, mlp)

time: 111 us -> 111 us (level)
  no operation moved by 1% of the time
where the time goes in v7:
time: 111 us
  starting transfers between devices  38.4 us (35%)
  Pallas kernels  34.4 us (31%)
  waiting for transfers between devices  34 us (31%)
  local copies, waits for them, and re-layouts  3.42 us (3%)
    ppermute x40, starting transfers between devices, swap(): return lax.ppermute(x, axis, [(i, i ^ mask) for i in range(size)])  38.4 us
    ppermute x40, waiting for transfers between devices, swap(): return lax.ppermute(x, axis, [(i, i ^ mask) for i in range(size)])  34 us
    pallas_call x10, Pallas kernels, call(): pl.pallas_call(kernel, in_specs=[VMEM] * len(args), out_specs=[VMEM] * le...  29.5 us
    unnamed x18, local copies, waits for them, and re-layouts  3.42 us
    pallas_call x1, Pallas kernels, body(): pl.pallas_call(pack_kernel, in_specs=[SMEM] + [ANY] * 5 + [VMEM], out_spe...  2.57 us
    pallas_call x14, Pallas kernels, run(): pl.pallas_call(kernel, in_specs=[VMEM] * len(args), out_specs=[VMEM] * le...  2.31 us
  transfers between devices with their start and end apart: 40, of which 20 were waited for; matrix products, arithmetic and copies ran while one was open for 0% of the time, Pallas kernels for 23%

profile of v7, /device:TPU:9, one launch (start us, length us, event | category | flops | bytes accessed | tf_op | source)
XLA Modules:
  0.0 111.1 jit_solution(10865368443064228204)
XLA Ops:
  0.6 2.6 %pack.1 = (bf16[352,256]{1,0:T(8,128)(2,1)}, bf16[352,256]{1,0:T(8,128)(2,1)}, bf16[304,256]{1,0:T(8,128)(2,1)}, bf16[304,256]{1,0:T(8,128)(2,1)}, bf16[64,256]{1,0:T(8,128)(2,1)}) custom-call(s32[16]{0:T(128)} %lens.1, bf16[2,3,64,256]{3,2,1,0:T(8,128)(2,1)} %bitcast.4, bf16[2,64,256]{2,1,0:T(8,128)(2,1)} %bitcast.5, bf16[2,64,256]{2,1,0:T(8,128)(2,1)} %out.1, ...), custom_call_target="tpu_custom_call" | custom-call | tf_op jit(solution)/shard_map/pack/pallas_call | solution.py:713
  3.2 1.4 %collective-permute-start.3 = (bf16[304,256]{1,0:T(8,128)(2,1)}, bf16[304,256]{1,0:T(8,128)(2,1)S(1)}, u32[]{:S(2)}, u32[]{:S(2)}) collective-permute-start(bf16[304,256]{1,0:T(8,128)(2,1)} %get-tuple-element.123), channel_id=1, source_target_pairs={{0,3},{1,2},{2,1},{3,0},{4,7},{5,6},{6,5},{7,4},{8,11},{9,10},{10,... | collective-permute-start | bytes 466952 | tf_op jit(solution)/shard_map/ppermute | solution.py:669
  4.6 1.1 collective-permute-start.2
  5.7 1.1 collective-permute-start.1
  6.8 1.0 copy-done.4
  7.8 0.9 copy-done.5
  8.7 0.8 copy-done.6
  9.5 0.7 copy-done.8
  10.2 5.0 %collective-permute-done.3.c = bf16[304,256]{1,0:T(8,128)(2,1)S(1)} collective-permute-done((bf16[304,256]{1,0:T(8,128)(2,1)}, bf16[304,256]{1,0:T(8,128)(2,1)S(1)}, u32[]{:S(2)}, u32[]{:S(2)}) %collective-permute-start.3) | collective-permute-done | bytes 155680 | tf_op jit(solution)/shard_map/ppermute | solution.py:669
  15.2 2.4 %collective-permute-done.2.b = bf16[304,256]{1,0:T(8,128)(2,1)S(1)} collective-permute-done((bf16[304,256]{1,0:T(8,128)(2,1)}, bf16[304,256]{1,0:T(8,128)(2,1)S(1)}, u32[]{:S(2)}, u32[]{:S(2)}) %collective-permute-start.2) | collective-permute-done | bytes 155680 | tf_op jit(solution)/shard_map/ppermute | solution.py:669
  17.6 1.6 %collective-permute-start.5 = (bf16[528,256]{1,0:T(8,128)(2,1)S(1)}, bf16[528,256]{1,0:T(8,128)(2,1)S(1)}, u32[]{:S(2)}, u32[]{:S(2)}) collective-permute-start(bf16[528,256]{1,0:T(8,128)(2,1)S(1)} %get-tuple-element.132.refs_1_), channel_id=1, source_target_pairs={{0,4},{4,0},{8,12},{12,8},{16,20},{20,16},{24,28},{28,24},{1,5},{5... | collective-permute-start | bytes 811016 | tf_op jit(solution)/shard_map/ppermute | solution.py:669
  19.2 1.2 %collective-permute-start.4 = (bf16[192,256]{1,0:T(8,128)(2,1)S(1)}, bf16[192,256]{1,0:T(8,128)(2,1)S(1)}, u32[]{:S(2)}, u32[]{:S(2)}) collective-permute-start(bf16[192,256]{1,0:T(8,128)(2,1)S(1)} %get-tuple-element.130.refs_2_), channel_id=1, source_target_pairs={{0,8},{4,12},{8,0},{12,4},{16,24},{20,28},{24,16},{28,20},{1,9},{5... | collective-permute-start | bytes 294920 | tf_op jit(solution)/shard_map/ppermute | solution.py:669
  20.5 0.3 collective-permute-start.6
  20.9 3.9 %collective-permute-start.11 = (bf16[304,256]{1,0:T(8,128)(2,1)}, bf16[304,256]{1,0:T(8,128)(2,1)S(1)}, u32[]{:S(2)}, u32[]{:S(2)}) collective-permute-start(bf16[304,256]{1,0:T(8,128)(2,1)} %get-tuple-element.122), channel_id=1, source_target_pairs={{0,2},{1,3},{2,0},{3,1},{4,6},{5,7},{6,4},{7,5},{8,10},{9,11},{10,... | collective-permute-start | bytes 466952 | tf_op jit(solution)/shard_map/ppermute | solution.py:669
  24.8 0.8 collective-permute-start
  25.7 1.5 %collective-permute-start.7 = (bf16[192,256]{1,0:T(8,128)(2,1)S(1)}, bf16[192,256]{1,0:T(8,128)(2,1)S(1)}, u32[]{:S(2)}, u32[]{:S(2)}) collective-permute-start(bf16[192,256]{1,0:T(8,128)(2,1)S(1)} %get-tuple-element.130.refs_2_), channel_id=1, source_target_pairs={{0,4},{4,0},{8,12},{12,8},{16,20},{20,16},{24,28},{28,24},{1,5},{5... | collective-permute-start | bytes 294920 | tf_op jit(solution)/shard_map/ppermute | solution.py:669
  27.3 3.8 %attn_fwd.2 = (f32[1024,256]{1,0:T(8,128)S(1)}, f32[1024,256]{1,0:T(8,128)S(1)}, bf16[1024,256]{1,0:T(8,128)(2,1)S(1)}, bf16[768,1024]{1,0:T(8,128)(2,1)S(1)}, b...) custom-call(bf16[352,256]{1,0:T(8,128)(2,1)S(1)} %get-tuple-element.126.refs_0_, ...), custom_call_target="tpu_custom_call" | custom-call | flops 49999998976 | bytes 1024 | tf_op jit(solution)/shard_map/attn_fwd/pallas_call | solution.py:561
  31.1 0.5 collective-permute-start.9
  31.7 0.9 collective-permute-done.9.refs_8_
  32.5 0.4 collective-permute-done.10.refs_9_
  32.9 2.2 %mlp_fwd.1 = (f32[1024,256]{1,0:T(8,128)S(1)}, bf16[1024,1024]{1,0:T(8,128)(2,1)S(1)}, bf16[1024,1024]{1,0:T(8,128)(2,1)S(1)}) custom-call(bf16[2,256,256]{2,1,0:T(8,128)(2,1)S(1)} %copy-done, bf16[2,256,256]{2,1,0:T(8,128)(2,1)S(1)} %copy-done.1, bf16[192,256]{1,0:T(8,128)(2,1)S(1)} %get-tuple-element.130.refs_2_, ...), custom_call_target="tpu_custom_call" | custom-call | flops 1000 | bytes 1024 | tf_op jit(solution)/shard_map/mlp_fwd/pallas_call | solution.py:561
  35.1 0.2 collective-permute-done.11.b
  35.4 1.5 %collective-permute-start.14 = (bf16[528,256]{1,0:T(8,128)(2,1)S(1)}, bf16[528,256]{1,0:T(8,128)(2,1)S(1)}, u32[]{:S(2)}, u32[]{:S(2)}) collective-permute-start(bf16[528,256]{1,0:T(8,128)(2,1)S(1)} %get-tuple-element.146.refs_1_), channel_id=1, source_target_pairs={{0,4},{4,0},{8,12},{12,8},{16,20},{20,16},{24,28},{28,24},{1,5},{5... | collective-permute-start | bytes 811016 | tf_op jit(solution)/shard_map/ppermute | solution.py:669
  36.9 1.2 %collective-permute-start.13 = (bf16[384,256]{1,0:T(8,128)(2,1)S(1)}, bf16[384,256]{1,0:T(8,128)(2,1)S(1)}, u32[]{:S(2)}, u32[]{:S(2)}) collective-permute-start(bf16[384,256]{1,0:T(8,128)(2,1)S(1)} %get-tuple-element.144.refs_2_), channel_id=1, source_target_pairs={{0,8},{4,12},{8,0},{12,4},{16,24},{20,28},{24,16},{28,20},{1,9},{5... | collective-permute-start | bytes 589832 | tf_op jit(solution)/shard_map/ppermute | solution.py:669
  38.1 0.3 collective-permute-start.15
  38.5 3.8 %attn_fwd.3 = (f32[1024,256]{1,0:T(8,128)S(1)}, f32[1024,256]{1,0:T(8,128)S(1)}, bf16[1024,256]{1,0:T(8,128)(2,1)S(1)}, bf16[768,1024]{1,0:T(8,128)(2,1)S(1)}, b...) custom-call(bf16[352,256]{1,0:T(8,128)(2,1)S(1)} %copy-done.3, bf16[528,256]{1,0:T(8,128)(2,1)S(1)} %get-tuple-element.146.refs_1_, ...), custom_call_target="tpu_custom_call" | custom-call | flops 1000 | bytes 1024 | tf_op jit(solution)/shard_map/attn_fwd/pallas_call | solution.py:561
  42.3 1.1 collective-permute-done.13.refs_3_
  43.4 0.8 collective-permute-start.16
  44.2 1.1 collective-permute-done.16.refs_5_
  45.3 4.4 %mlp_both.1 = (f32[1024,256]{1,0:T(8,128)}, f32[1024,256]{1,0:T(8,128)S(1)}, bf16[4,256,256]{2,1,0:T(8,128)(2,1)S(1)}, bf16[4,256,256]{2,1,0:T(8,128)(2,1)S(1)}, f32[8,256]{1,0:T(8,128)S(1)}) custom-call(bf16[2,256,256]{2,1,0:T(8,128)(2,1)S(1)} %copy-done, bf16[2,256,256]{2,1,0:T(8,128)(2,1)S(1)} %copy-done.1, ...), custom_call_target="tpu_custom_call" | custom-call | flops 1000 | bytes 1024 | tf_op jit(solution)/shard_map/mlp_both/pallas_call | solution.py:561
  49.7 0.4 collective-permute-start.17
  50.1 1.1 attn_pre.2
  51.2 0.5 collective-permute-done.17.got
  51.8 1.3 %collective-permute-start.19 = (bf16[4,128,256]{2,1,0:T(8,128)(2,1)S(1)}, bf16[4,128,256]{2,1,0:T(8,128)(2,1)S(1)}, u32[]{:S(2)}, u32[]{:S(2)}) collective-permute-start(bf16[4,128,256]{2,1,0:T(8,128)(2,1)S(1)} %get-tuple-element.158), channel_id=1, source_target_pairs={{0,8},{4,12},{8,0},{12,4},{16,24},{20,28},{24,16},{28,20},{1,9},{5... | collective-permute-start | bytes 786440 | tf_op jit(solution)/shard_map/ppermute | solution.py:669
  53.1 4.4 %attn_bwd.1 = (f32[1024,256]{1,0:T(8,128)S(1)}, bf16[4,176,256]{2,1,0:T(8,128)(2,1)S(1)}, bf16[4,176,256]{2,1,0:T(8,128)(2,1)S(1)}) custom-call(bf16[352,256]{1,0:T(8,128)(2,1)S(1)} %copy-done.3, bf16[528,256]{1,0:T(8,128)(2,1)S(1)} %get-tuple-element.146.refs_1_, bf16[528,256]{1,0:T(8,128)(2,1)S(1)} %collective-permute-done.14.refs_2_, ...), custom_call_target="tpu_custom_call" | custom-call | flops 1000 | bytes 1024 | tf_op jit(solution)/shard_map/attn_bwd/pallas_call | solution.py:561
  57.5 0.7 collective-permute-start.20
  58.1 2.8 %mlp_bwd.1 = (f32[1024,256]{1,0:T(8,128)S(1)}, bf16[4,256,256]{2,1,0:T(8,128)(2,1)S(1)}, bf16[4,256,256]{2,1,0:T(8,128)(2,1)S(1)}, f32[8,256]{1,0:T(8,128)S(1)}) custom-call(bf16[2,256,256]{2,1,0:T(8,128)(2,1)S(1)} %copy-done, bf16[2,256,256]{2,1,0:T(8,128)(2,1)S(1)} %copy-done.1, bf16[192,256]{1,0:T(8,128)(2,1)S(1)} %get-tuple-element.130.refs_2_, ...), custom_call_target="tpu_custom_call" | custom-call | flops 1000 | bytes 1024 | tf_op jit(solution)/shard_map/mlp_bwd/pallas_call | solution.py:561
  61.2 0.2 collective-permute-start.23
  61.5 3.7 %collective-permute-start.22 = (bf16[304,256]{1,0:T(8,128)(2,1)S(1)}, bf16[304,256]{1,0:T(8,128)(2,1)S(1)}, u32[]{:S(2)}, u32[]{:S(2)}) collective-permute-start(bf16[304,256]{1,0:T(8,128)(2,1)S(1)} %get-tuple-element.200), channel_id=1, source_target_pairs={{0,2},{1,3},{2,0},{3,1},{4,6},{5,7},{6,4},{7,5},{8,10},{9,11},{10,... | collective-permute-start | bytes 466952 | tf_op jit(solution)/shard_map/ppermute | solution.py:669
  65.1 1.1 attn_pre.3
  66.4 0.3 collective-permute-start.26
  66.7 3.8 %attn_grads.1 = (bf16[768,1024]{1,0:T(8,128)(2,1)S(1)}, bf16[4,176,256]{2,1,0:T(8,128)(2,1)S(1)}, bf16[2,176,256]{2,1,0:T(8,128)(2,1)S(1)}, bf16[2,176,256]{2,1,0:T(8,128)(2,1)S(1)}) custom-call(bf16[352,256]{1,0:T(8,128)(2,1)S(1)} %get-tuple-element.126.refs_0_, bf16[528,256]{1,0:T(8,128)(2,1)S(1)} %get-tuple-element.132.refs_1_, ...), custom_call_target="tpu_custom_call" | custom-call | flops 1000 | bytes 1024 | tf_op jit(solution)/shard_map/attn_grads/pallas_call | solution.py:561
  70.5 2.2 %attn_post.1 = f32[1024,256]{1,0:T(8,128)} custom-call(bf16[352,256]{1,0:T(8,128)(2,1)S(1)} %get-tuple-element.126.refs_0_, bf16[528,256]{1,0:T(8,128)(2,1)S(1)} %get-tuple-element.132.refs_1_, bf16[528,256]{1,0:T(8,128)(2,1)S(1)} %collective-permute-done.5.refs_2_, bf16[768,1024]{1,0:T(8,128)(2,1)S(1)} %get-tuple-element.188.refs_3_, ...), custom_call_target="tpu_custom_call" | custom-call | flops 1000 | bytes 1024 | tf_op jit(solution)/shard_map/attn_post/pallas_call | solution.py:561
  72.8 2.1 %collective-permute-done.22.refs_2_ = bf16[304,256]{1,0:T(8,128)(2,1)S(1)} collective-permute-done((bf16[304,256]{1,0:T(8,128)(2,1)S(1)}, bf16[304,256]{1,0:T(8,128)(2,1)S(1)}, u32[]{:S(2)}, u32[]{:S(2)}) %collective-permute-start.22) | collective-permute-done | bytes 155680 | tf_op jit(solution)/shard_map/ppermute | solution.py:669
  74.9 1.3 %collective-permute-start.27 = (bf16[2,176,256]{2,1,0:T(8,128)(2,1)S(1)}, bf16[2,176,256]{2,1,0:T(8,128)(2,1)S(1)}, u32[]{:S(2)}, u32[]{:S(2)}) collective-permute-start(bf16[2,176,256]{2,1,0:T(8,128)(2,1)S(1)} %get-tuple-element.209), channel_id=1, source_target_pairs={{0,4},{4,0},{8,12},{12,8},{16,20},{20,16},{24,28},{28,24},{1,5},{5... | collective-permute-start | bytes 540680 | tf_op jit(solution)/shard_map/ppermute | solution.py:669
  76.3 1.0 collective-permute-done.27.refs_3_
  77.3 0.4 collective-permute-done.28.refs_4_
  77.8 2.7 %collective-permute-start.29 = (bf16[304,256]{1,0:T(8,128)(2,1)S(1)}, bf16[304,256]{1,0:T(8,128)(2,1)S(1)}, u32[]{:S(2)}, u32[]{:S(2)}) collective-permute-start(bf16[304,256]{1,0:T(8,128)(2,1)S(1)} %get-tuple-element.211), channel_id=1, source_target_pairs={{0,1},{1,0},{2,3},{3,2},{4,5},{5,4},{6,7},{7,6},{8,9},{9,8},{10,11... | collective-permute-start | bytes 466952 | tf_op jit(solution)/shard_map/ppermute | solution.py:669
  80.6 1.3 %collective-permute-start.33 = (bf16[304,256]{1,0:T(8,128)(2,1)S(1)}, bf16[304,256]{1,0:T(8,128)(2,1)S(1)}, u32[]{:S(2)}, u32[]{:S(2)}) collective-permute-start(bf16[304,256]{1,0:T(8,128)(2,1)S(1)} %get-tuple-element.218), channel_id=1, source_target_pairs={{0,3},{1,2},{2,1},{3,0},{4,7},{5,6},{6,5},{7,4},{8,11},{9,10},{10,... | collective-permute-start | bytes 466952 | tf_op jit(solution)/shard_map/ppermute | solution.py:669
  81.8 1.2 %collective-permute-start.25 = (bf16[176,256]{1,0:T(8,128)(2,1)S(1)}, bf16[176,256]{1,0:T(8,128)(2,1)S(1)}, u32[]{:S(2)}, u32[]{:S(2)}) collective-permute-start(bf16[176,256]{1,0:T(8,128)(2,1)S(1)} %get-tuple-element.212.refs_0_), channel_id=1, source_target_pairs={{0,16},{4,20},{8,24},{12,28},{16,0},{20,4},{24,8},{28,12},{1,17},{... | collective-permute-start | bytes 270344 | tf_op jit(solution)/shard_map/ppermute | solution.py:669
  83.1 0.3 collective-permute-start.24
  83.3 2.4 %collective-permute-done.29.refs_2_ = bf16[304,256]{1,0:T(8,128)(2,1)S(1)} collective-permute-done((bf16[304,256]{1,0:T(8,128)(2,1)S(1)}, bf16[304,256]{1,0:T(8,128)(2,1)S(1)}, u32[]{:S(2)}, u32[]{:S(2)}) %collective-permute-start.29) | collective-permute-done | bytes 155680 | tf_op jit(solution)/shard_map/ppermute | solution.py:669
  85.8 1.2 %collective-permute-start.30 = (bf16[176,256]{1,0:T(8,128)(2,1)S(1)}, bf16[176,256]{1,0:T(8,128)(2,1)S(1)}, u32[]{:S(2)}, u32[]{:S(2)}) collective-permute-start(bf16[176,256]{1,0:T(8,128)(2,1)S(1)} %get-tuple-element.212.refs_0_), channel_id=1, source_target_pairs={{0,24},{4,28},{8,16},{12,20},{16,8},{20,12},{24,0},{28,4},{1,25},{... | collective-permute-start | bytes 270344 | tf_op jit(solution)/shard_map/ppermute | solution.py:669
  87.0 3.1 %collective-permute-done.30.refs_3_ = bf16[176,256]{1,0:T(8,128)(2,1)S(1)} collective-permute-done((bf16[176,256]{1,0:T(8,128)(2,1)S(1)}, bf16[176,256]{1,0:T(8,128)(2,1)S(1)}, u32[]{:S(2)}, u32[]{:S(2)}) %collective-permute-start.30) | collective-permute-done | bytes 90144 | tf_op jit(solution)/shard_map/ppermute | solution.py:669
  90.1 5.7 %collective-permute-done.33.refs_4_ = bf16[304,256]{1,0:T(8,128)(2,1)S(1)} collective-permute-done((bf16[304,256]{1,0:T(8,128)(2,1)S(1)}, bf16[304,256]{1,0:T(8,128)(2,1)S(1)}, u32[]{:S(2)}, u32[]{:S(2)}) %collective-permute-start.33) | collective-permute-done | bytes 155680 | tf_op jit(solution)/shard_map/ppermute | solution.py:669
  95.9 1.3 %collective-permute-start.35 = (bf16[256,256]{1,0:T(8,128)(2,1)S(1)}, bf16[256,256]{1,0:T(8,128)(2,1)S(1)}, u32[]{:S(2)}, u32[]{:S(2)}) collective-permute-start(bf16[256,256]{1,0:T(8,128)(2,1)S(1)} %get-tuple-element.221.high), channel_id=1, source_target_pairs={{0,16},{4,20},{8,24},{12,28},{16,0},{20,4},{24,8},{28,12},{1,17},{... | collective-permute-start | bytes 393224 | tf_op jit(solution)/shard_map/ppermute | solution.py:669
  97.2 0.3 collective-permute-start.34
  97.4 3.4 %collective-permute-done.34.low_got = bf16[176,256]{1,0:T(8,128)(2,1)S(1)} collective-permute-done((bf16[176,256]{1,0:T(8,128)(2,1)S(1)}, bf16[176,256]{1,0:T(8,128)(2,1)S(1)}, u32[]{:S(2)}, u32[]{:S(2)}) %collective-permute-start.34) | collective-permute-done | bytes 90144 | tf_op jit(solution)/shard_map/ppermute | solution.py:669
  100.9 0.3 collective-permute-start.37
  101.4 3.2 %collective-permute-done.36.low_got = bf16[176,256]{1,0:T(8,128)(2,1)S(1)} collective-permute-done((bf16[176,256]{1,0:T(8,128)(2,1)S(1)}, bf16[176,256]{1,0:T(8,128)(2,1)S(1)}, u32[]{:S(2)}, u32[]{:S(2)}) %collective-permute-start.36) | collective-permute-done | bytes 90144 | tf_op jit(solution)/shard_map/ppermute | solution.py:669
  104.8 3.5 %collective-permute-start.38 = (bf16[512,256]{1,0:T(8,128)(2,1)S(1)}, bf16[512,256]{1,0:T(8,128)(2,1)S(1)}, u32[]{:S(2)}, u32[]{:S(2)}) collective-permute-start(bf16[512,256]{1,0:T(8,128)(2,1)S(1)} %get-tuple-element.224.high), channel_id=1, source_target_pairs={{0,4},{4,0},{8,12},{12,8},{16,20},{20,16},{24,28},{28,24},{1,5},{5... | collective-permute-start | bytes 786440 | tf_op jit(solution)/shard_map/ppermute | solution.py:669
  108.4 0.4 collective-permute-start.39
  108.9 0.8 collective-permute-done.31.low_other
  109.8 1.3 %finish.1 = (f32[2,3,64,256]{3,2,1,0:T(8,128)}, f32[2,64,256]{2,1,0:T(8,128)}, f32[2,256,256]{2,1,0:T(8,128)}, f32[2,256,256]{2,1,0:T(8,128)}, f32[2,64,256]{2,1...) custom-call(bf16[176,256]{1,0:T(8,128)(2,1)S(1)} %four_sum.1.low, ...), custom_call_target="tpu_custom_call" | custom-call | flops 1000 | bytes 1024 | tf_op jit(solution)/shard_map/finish/pallas_call | solution.py:646
  (59 shorter events, 2.2 us)
Async XLA Ops:
  3.2 12.0 %collective-permute-start.3 = (bf16[304,256]{1,0:T(8,128)(2,1)}, bf16[304,256]{1,0:T(8,128)(2,1)S(1)}, u32[]{:S(2)}, u32[]{:S(2)}) collective-permute-start(bf16[304,256]{1,0:T(8,128)(2,1)} %get-tuple-element.123), channel_id=1, source_target_pairs={{0,3},{1,2},{2,1},{3,0},{4,7},{5,6},{6,5},{7,4},{8,11},{9,10},{10,... | collective-permute-start | bytes 466952 | tf_op jit(solution)/shard_map/ppermute | solution.py:669
  4.6 13.0 %collective-permute-start.2 = (bf16[304,256]{1,0:T(8,128)(2,1)}, bf16[304,256]{1,0:T(8,128)(2,1)S(1)}, u32[]{:S(2)}, u32[]{:S(2)}) collective-permute-start(bf16[304,256]{1,0:T(8,128)(2,1)} %get-tuple-element.123), channel_id=1, source_target_pairs={{0,2},{1,3},{2,0},{3,1},{4,6},{5,7},{6,4},{7,5},{8,10},{9,11},{10,... | collective-permute-start | bytes 466952 | tf_op jit(solution)/shard_map/ppermute | solution.py:669
  5.7 11.9 %collective-permute-start.1 = (bf16[304,256]{1,0:T(8,128)(2,1)}, bf16[304,256]{1,0:T(8,128)(2,1)S(1)}, u32[]{:S(2)}, u32[]{:S(2)}) collective-permute-start(bf16[304,256]{1,0:T(8,128)(2,1)} %get-tuple-element.123), channel_id=1, source_target_pairs={{0,1},{1,0},{2,3},{3,2},{4,5},{5,4},{6,7},{7,6},{8,9},{9,8},{10,11... | collective-permute-start | bytes 466952 | tf_op jit(solution)/shard_map/ppermute | solution.py:669
  6.8 1.0 copy-start.4
  7.8 0.9 copy-start.5
  8.7 0.8 copy-start.6
  9.5 0.7 copy-start.8
  17.6 9.6 %collective-permute-start.5 = (bf16[528,256]{1,0:T(8,128)(2,1)S(1)}, bf16[528,256]{1,0:T(8,128)(2,1)S(1)}, u32[]{:S(2)}, u32[]{:S(2)}) collective-permute-start(bf16[528,256]{1,0:T(8,128)(2,1)S(1)} %get-tuple-element.132.refs_1_), channel_id=1, source_target_pairs={{0,4},{4,0},{8,12},{12,8},{16,20},{20,16},{24,28},{28,24},{1,5},{5... | collective-permute-start | bytes 811016 | tf_op jit(solution)/shard_map/ppermute | solution.py:669
  19.2 5.5 %collective-permute-start.4 = (bf16[192,256]{1,0:T(8,128)(2,1)S(1)}, bf16[192,256]{1,0:T(8,128)(2,1)S(1)}, u32[]{:S(2)}, u32[]{:S(2)}) collective-permute-start(bf16[192,256]{1,0:T(8,128)(2,1)S(1)} %get-tuple-element.130.refs_2_), channel_id=1, source_target_pairs={{0,8},{4,12},{8,0},{12,4},{16,24},{20,28},{24,16},{28,20},{1,9},{5... | collective-permute-start | bytes 294920 | tf_op jit(solution)/shard_map/ppermute | solution.py:669
  20.5 5.3 %collective-permute-start.6 = (bf16[192,256]{1,0:T(8,128)(2,1)S(1)}, bf16[192,256]{1,0:T(8,128)(2,1)S(1)}, u32[]{:S(2)}, u32[]{:S(2)}) collective-permute-start(bf16[192,256]{1,0:T(8,128)(2,1)S(1)} %get-tuple-element.131.refs_3_), channel_id=1, source_target_pairs={{0,8},{4,12},{8,0},{12,4},{16,24},{20,28},{24,16},{28,20},{1,9},{5... | collective-permute-start | bytes 294920 | tf_op jit(solution)/shard_map/ppermute | solution.py:669
  20.7 14.4 %collective-permute-start.12 = (bf16[304,256]{1,0:T(8,128)(2,1)}, bf16[304,256]{1,0:T(8,128)(2,1)S(1)}, u32[]{:S(2)}, u32[]{:S(2)}) collective-permute-start(bf16[304,256]{1,0:T(8,128)(2,1)} %get-tuple-element.122), channel_id=1, source_target_pairs={{0,3},{1,2},{2,1},{3,0},{4,7},{5,6},{6,5},{7,4},{8,11},{9,10},{10,... | collective-permute-start | bytes 466952 | tf_op jit(solution)/shard_map/ppermute | solution.py:669
  20.9 14.5 %collective-permute-start.11 = (bf16[304,256]{1,0:T(8,128)(2,1)}, bf16[304,256]{1,0:T(8,128)(2,1)S(1)}, u32[]{:S(2)}, u32[]{:S(2)}) collective-permute-start(bf16[304,256]{1,0:T(8,128)(2,1)} %get-tuple-element.122), channel_id=1, source_target_pairs={{0,2},{1,3},{2,0},{3,1},{4,6},{5,7},{6,4},{7,5},{8,10},{9,11},{10,... | collective-permute-start | bytes 466952 | tf_op jit(solution)/shard_map/ppermute | solution.py:669
  24.8 10.6 %collective-permute-start = (bf16[304,256]{1,0:T(8,128)(2,1)}, bf16[304,256]{1,0:T(8,128)(2,1)S(1)}, u32[]{:S(2)}, u32[]{:S(2)}) collective-permute-start(bf16[304,256]{1,0:T(8,128)(2,1)} %get-tuple-element.122), channel_id=1, source_target_pairs={{0,1},{1,0},{2,3},{3,2},{4,5},{5,4},{6,7},{7,6},{8,9},{9,8},{10,11... | collective-permute-start | bytes 466952 | tf_op jit(solution)/shard_map/ppermute | solution.py:669
  25.7 5.4 %collective-permute-start.7 = (bf16[192,256]{1,0:T(8,128)(2,1)S(1)}, bf16[192,256]{1,0:T(8,128)(2,1)S(1)}, u32[]{:S(2)}, u32[]{:S(2)}) collective-permute-start(bf16[192,256]{1,0:T(8,128)(2,1)S(1)} %get-tuple-element.130.refs_2_), channel_id=1, source_target_pairs={{0,4},{4,0},{8,12},{12,8},{16,20},{20,16},{24,28},{28,24},{1,5},{5... | collective-permute-start | bytes 294920 | tf_op jit(solution)/shard_map/ppermute | solution.py:669
  27.2 4.4 %collective-permute-start.8 = (bf16[192,256]{1,0:T(8,128)(2,1)S(1)}, bf16[192,256]{1,0:T(8,128)(2,1)S(1)}, u32[]{:S(2)}, u32[]{:S(2)}) collective-permute-start(bf16[192,256]{1,0:T(8,128)(2,1)S(1)} %get-tuple-element.131.refs_3_), channel_id=1, source_target_pairs={{0,4},{4,0},{8,12},{12,8},{16,20},{20,16},{24,28},{28,24},{1,5},{5... | collective-permute-start | bytes 294920 | tf_op jit(solution)/shard_map/ppermute | solution.py:669
  27.3 5.6 %copy-start = (bf16[2,256,256]{2,1,0:T(8,128)(2,1)S(1)}, bf16[2,256,256]{2,1,0:T(8,128)(2,1)}, u32[]{:S(2)}) copy-start(bf16[2,256,256]{2,1,0:T(8,128)(2,1)} %refs_0_.7) | copy-start | bytes 786436
  27.3 5.6 %copy-start.1 = (bf16[2,256,256]{2,1,0:T(8,128)(2,1)S(1)}, bf16[2,256,256]{2,1,0:T(8,128)(2,1)}, u32[]{:S(2)}) copy-start(bf16[2,256,256]{2,1,0:T(8,128)(2,1)} %refs_1_.5) | copy-start | bytes 786436
  27.3 5.6 %copy-start.7 = (f32[2,256]{1,0:T(2,128)S(1)}, f32[2,256]{1,0:T(2,128)}, u32[]{:S(2)}) copy-start(f32[2,256]{1,0:T(2,128)} %refs_14_.1) | copy-start | bytes 6148
  31.1 1.4 %collective-permute-start.9 = (bf16[192,256]{1,0:T(8,128)(2,1)S(1)}, bf16[192,256]{1,0:T(8,128)(2,1)S(1)}, u32[]{:S(2)}, u32[]{:S(2)}) collective-permute-start(bf16[192,256]{1,0:T(8,128)(2,1)S(1)} %collective-permute-done.4.refs_4_), channel_id=1, source_target_pairs={{0,4},{4,0},{8,12},{12,8},{16,20},{20,16},{24,28},{28,24},{1,5},{5... | collective-permute-start | bytes 294920 | tf_op jit(solution)/shard_map/ppermute | solution.py:669
  31.6 1.3 %collective-permute-start.10 = (bf16[192,256]{1,0:T(8,128)(2,1)S(1)}, bf16[192,256]{1,0:T(8,128)(2,1)S(1)}, u32[]{:S(2)}, u32[]{:S(2)}) collective-permute-start(bf16[192,256]{1,0:T(8,128)(2,1)S(1)} %collective-permute-done.6.refs_5_), channel_id=1, source_target_pairs={{0,4},{4,0},{8,12},{12,8},{16,20},{20,16},{24,28},{28,24},{1,5},{5... | collective-permute-start | bytes 294920 | tf_op jit(solution)/shard_map/ppermute | solution.py:669
  32.9 5.6 %copy-start.3 = (bf16[352,256]{1,0:T(8,128)(2,1)S(1)}, bf16[352,256]{1,0:T(8,128)(2,1)}, u32[]{:S(2)}) copy-start(bf16[352,256]{1,0:T(8,128)(2,1)} %get-tuple-element.145.refs_0_) | copy-start | bytes 540676
  35.1 10.2 %copy-start.2 = (bf16[1024,256]{1,0:T(8,128)(2,1)S(1)}, bf16[1024,256]{1,0:T(8,128)(2,1)}, u32[]{:S(2)}) copy-start(bf16[1024,256]{1,0:T(8,128)(2,1)} %refs_3_.1) | copy-start | bytes 1572868
  35.4 3.1 %collective-permute-start.14 = (bf16[528,256]{1,0:T(8,128)(2,1)S(1)}, bf16[528,256]{1,0:T(8,128)(2,1)S(1)}, u32[]{:S(2)}, u32[]{:S(2)}) collective-permute-start(bf16[528,256]{1,0:T(8,128)(2,1)S(1)} %get-tuple-element.146.refs_1_), channel_id=1, source_target_pairs={{0,4},{4,0},{8,12},{12,8},{16,20},{20,16},{24,28},{28,24},{1,5},{5... | collective-permute-start | bytes 811016 | tf_op jit(solution)/shard_map/ppermute | solution.py:669
  36.9 6.5 %collective-permute-start.13 = (bf16[384,256]{1,0:T(8,128)(2,1)S(1)}, bf16[384,256]{1,0:T(8,128)(2,1)S(1)}, u32[]{:S(2)}, u32[]{:S(2)}) collective-permute-start(bf16[384,256]{1,0:T(8,128)(2,1)S(1)} %get-tuple-element.144.refs_2_), channel_id=1, source_target_pairs={{0,8},{4,12},{8,0},{12,4},{16,24},{20,28},{24,16},{28,20},{1,9},{5... | collective-permute-start | bytes 589832 | tf_op jit(solution)/shard_map/ppermute | solution.py:669
  38.1 6.1 %collective-permute-start.15 = (bf16[384,256]{1,0:T(8,128)(2,1)S(1)}, bf16[384,256]{1,0:T(8,128)(2,1)S(1)}, u32[]{:S(2)}, u32[]{:S(2)}) collective-permute-start(bf16[384,256]{1,0:T(8,128)(2,1)S(1)} %get-tuple-element.144.refs_2_), channel_id=1, source_target_pairs={{0,4},{4,0},{8,12},{12,8},{16,20},{20,16},{24,28},{28,24},{1,5},{5... | collective-permute-start | bytes 589832 | tf_op jit(solution)/shard_map/ppermute | solution.py:669
  43.4 1.9 %collective-permute-start.16 = (bf16[384,256]{1,0:T(8,128)(2,1)S(1)}, bf16[384,256]{1,0:T(8,128)(2,1)S(1)}, u32[]{:S(2)}, u32[]{:S(2)}) collective-permute-start(bf16[384,256]{1,0:T(8,128)(2,1)S(1)} %collective-permute-done.13.refs_3_), channel_id=1, source_target_pairs={{0,4},{4,0},{8,12},{12,8},{16,20},{20,16},{24,28},{28,24},{1,5},{5... | collective-permute-start | bytes 589832 | tf_op jit(solution)/shard_map/ppermute | solution.py:669
  49.7 2.0 %collective-permute-start.17 = (bf16[4,256,256]{2,1,0:T(8,128)(2,1)S(1)}, bf16[4,256,256]{2,1,0:T(8,128)(2,1)S(1)}, u32[]{:S(2)}, u32[]{:S(2)}) collective-permute-start(bf16[4,256,256]{2,1,0:T(8,128)(2,1)S(1)} %get-tuple-element.152), channel_id=1, source_target_pairs={{0,4},{4,0},{8,12},{12,8},{16,20},{20,16},{24,28},{28,24},{1,5},{5... | collective-permute-start | bytes 1572872 | tf_op jit(solution)/shard_map/ppermute | solution.py:669
  51.8 9.2 %collective-permute-start.19 = (bf16[4,128,256]{2,1,0:T(8,128)(2,1)S(1)}, bf16[4,128,256]{2,1,0:T(8,128)(2,1)S(1)}, u32[]{:S(2)}, u32[]{:S(2)}) collective-permute-start(bf16[4,128,256]{2,1,0:T(8,128)(2,1)S(1)} %get-tuple-element.158), channel_id=1, source_target_pairs={{0,8},{4,12},{8,0},{12,4},{16,24},{20,28},{24,16},{28,20},{1,9},{5... | collective-permute-start | bytes 786440 | tf_op jit(solution)/shard_map/ppermute | solution.py:669
  57.5 3.6 %collective-permute-start.20 = (bf16[4,176,256]{2,1,0:T(8,128)(2,1)S(1)}, bf16[4,176,256]{2,1,0:T(8,128)(2,1)S(1)}, u32[]{:S(2)}, u32[]{:S(2)}) collective-permute-start(bf16[4,176,256]{2,1,0:T(8,128)(2,1)S(1)} %get-tuple-element.194), channel_id=1, source_target_pairs={{0,4},{4,0},{8,12},{12,8},{16,20},{20,16},{24,28},{28,24},{1,5},{5... | collective-permute-start | bytes 1081352 | tf_op jit(solution)/shard_map/ppermute | solution.py:669
  60.9 5.3 %collective-permute-start.18 = (bf16[4,256,256]{2,1,0:T(8,128)(2,1)S(1)}, bf16[4,256,256]{2,1,0:T(8,128)(2,1)S(1)}, u32[]{:S(2)}, u32[]{:S(2)}) collective-permute-start(bf16[4,256,256]{2,1,0:T(8,128)(2,1)S(1)} %get-tuple-element.173), channel_id=1, source_target_pairs={{0,4},{4,0},{8,12},{12,8},{16,20},{20,16},{24,28},{28,24},{1,5},{5... | collective-permute-start | bytes 1572872 | tf_op jit(solution)/shard_map/ppermute | solution.py:669
  61.2 11.6 %collective-permute-start.23 = (bf16[304,256]{1,0:T(8,128)(2,1)S(1)}, bf16[304,256]{1,0:T(8,128)(2,1)S(1)}, u32[]{:S(2)}, u32[]{:S(2)}) collective-permute-start(bf16[304,256]{1,0:T(8,128)(2,1)S(1)} %get-tuple-element.202), channel_id=1, source_target_pairs={{0,3},{1,2},{2,1},{3,0},{4,7},{5,6},{6,5},{7,4},{8,11},{9,10},{10,... | collective-permute-start | bytes 466952 | tf_op jit(solution)/shard_map/ppermute | solution.py:669
  61.5 13.4 %collective-permute-start.22 = (bf16[304,256]{1,0:T(8,128)(2,1)S(1)}, bf16[304,256]{1,0:T(8,128)(2,1)S(1)}, u32[]{:S(2)}, u32[]{:S(2)}) collective-permute-start(bf16[304,256]{1,0:T(8,128)(2,1)S(1)} %get-tuple-element.200), channel_id=1, source_target_pairs={{0,2},{1,3},{2,0},{3,1},{4,6},{5,7},{6,4},{7,5},{8,10},{9,11},{10,... | collective-permute-start | bytes 466952 | tf_op jit(solution)/shard_map/ppermute | solution.py:669
  65.1 9.8 %collective-permute-start.21 = (bf16[304,256]{1,0:T(8,128)(2,1)S(1)}, bf16[304,256]{1,0:T(8,128)(2,1)S(1)}, u32[]{:S(2)}, u32[]{:S(2)}) collective-permute-start(bf16[304,256]{1,0:T(8,128)(2,1)S(1)} %get-tuple-element.198), channel_id=1, source_target_pairs={{0,1},{1,0},{2,3},{3,2},{4,5},{5,4},{6,7},{7,6},{8,9},{9,8},{10,11... | collective-permute-start | bytes 466952 | tf_op jit(solution)/shard_map/ppermute | solution.py:669
  66.4 10.0 %collective-permute-start.26 = (bf16[4,128,256]{2,1,0:T(8,128)(2,1)S(1)}, bf16[4,128,256]{2,1,0:T(8,128)(2,1)S(1)}, u32[]{:S(2)}, u32[]{:S(2)}) collective-permute-start(bf16[4,128,256]{2,1,0:T(8,128)(2,1)S(1)} %get-tuple-element.179), channel_id=1, source_target_pairs={{0,8},{4,12},{8,0},{12,4},{16,24},{20,28},{24,16},{28,20},{1,9},{5... | collective-permute-start | bytes 786440 | tf_op jit(solution)/shard_map/ppermute | solution.py:669
  74.9 2.4 %collective-permute-start.27 = (bf16[2,176,256]{2,1,0:T(8,128)(2,1)S(1)}, bf16[2,176,256]{2,1,0:T(8,128)(2,1)S(1)}, u32[]{:S(2)}, u32[]{:S(2)}) collective-permute-start(bf16[2,176,256]{2,1,0:T(8,128)(2,1)S(1)} %get-tuple-element.209), channel_id=1, source_target_pairs={{0,4},{4,0},{8,12},{12,8},{16,20},{20,16},{24,28},{28,24},{1,5},{5... | collective-permute-start | bytes 540680 | tf_op jit(solution)/shard_map/ppermute | solution.py:669
  76.2 1.4 %collective-permute-start.28 = (bf16[2,176,256]{2,1,0:T(8,128)(2,1)S(1)}, bf16[2,176,256]{2,1,0:T(8,128)(2,1)S(1)}, u32[]{:S(2)}, u32[]{:S(2)}) collective-permute-start(bf16[2,176,256]{2,1,0:T(8,128)(2,1)S(1)} %get-tuple-element.210), channel_id=1, source_target_pairs={{0,4},{4,0},{8,12},{12,8},{16,20},{20,16},{24,28},{28,24},{1,5},{5... | collective-permute-start | bytes 540680 | tf_op jit(solution)/shard_map/ppermute | solution.py:669
  77.8 7.9 %collective-permute-start.29 = (bf16[304,256]{1,0:T(8,128)(2,1)S(1)}, bf16[304,256]{1,0:T(8,128)(2,1)S(1)}, u32[]{:S(2)}, u32[]{:S(2)}) collective-permute-start(bf16[304,256]{1,0:T(8,128)(2,1)S(1)} %get-tuple-element.211), channel_id=1, source_target_pairs={{0,1},{1,0},{2,3},{3,2},{4,5},{5,4},{6,7},{7,6},{8,9},{9,8},{10,11... | collective-permute-start | bytes 466952 | tf_op jit(solution)/shard_map/ppermute | solution.py:669
  80.6 9.5 %collective-permute-start.32 = (bf16[304,256]{1,0:T(8,128)(2,1)S(1)}, bf16[304,256]{1,0:T(8,128)(2,1)S(1)}, u32[]{:S(2)}, u32[]{:S(2)}) collective-permute-start(bf16[304,256]{1,0:T(8,128)(2,1)S(1)} %get-tuple-element.216), channel_id=1, source_target_pairs={{0,2},{1,3},{2,0},{3,1},{4,6},{5,7},{6,4},{7,5},{8,10},{9,11},{10,... | collective-permute-start | bytes 466952 | tf_op jit(solution)/shard_map/ppermute | solution.py:669
  80.6 15.2 %collective-permute-start.33 = (bf16[304,256]{1,0:T(8,128)(2,1)S(1)}, bf16[304,256]{1,0:T(8,128)(2,1)S(1)}, u32[]{:S(2)}, u32[]{:S(2)}) collective-permute-start(bf16[304,256]{1,0:T(8,128)(2,1)S(1)} %get-tuple-element.218), channel_id=1, source_target_pairs={{0,3},{1,2},{2,1},{3,0},{4,7},{5,6},{6,5},{7,4},{8,11},{9,10},{10,... | collective-permute-start | bytes 466952 | tf_op jit(solution)/shard_map/ppermute | solution.py:669
  81.8 5.1 %collective-permute-start.25 = (bf16[176,256]{1,0:T(8,128)(2,1)S(1)}, bf16[176,256]{1,0:T(8,128)(2,1)S(1)}, u32[]{:S(2)}, u32[]{:S(2)}) collective-permute-start(bf16[176,256]{1,0:T(8,128)(2,1)S(1)} %get-tuple-element.212.refs_0_), channel_id=1, source_target_pairs={{0,16},{4,20},{8,24},{12,28},{16,0},{20,4},{24,8},{28,12},{1,17},{... | collective-permute-start | bytes 270344 | tf_op jit(solution)/shard_map/ppermute | solution.py:669
  83.1 3.9 %collective-permute-start.24 = (bf16[176,256]{1,0:T(8,128)(2,1)S(1)}, bf16[176,256]{1,0:T(8,128)(2,1)S(1)}, u32[]{:S(2)}, u32[]{:S(2)}) collective-permute-start(bf16[176,256]{1,0:T(8,128)(2,1)S(1)} %get-tuple-element.212.refs_0_), channel_id=1, source_target_pairs={{0,8},{4,12},{8,0},{12,4},{16,24},{20,28},{24,16},{28,20},{1,9},{5... | collective-permute-start | bytes 270344 | tf_op jit(solution)/shard_map/ppermute | solution.py:669
  85.8 4.3 %collective-permute-start.30 = (bf16[176,256]{1,0:T(8,128)(2,1)S(1)}, bf16[176,256]{1,0:T(8,128)(2,1)S(1)}, u32[]{:S(2)}, u32[]{:S(2)}) collective-permute-start(bf16[176,256]{1,0:T(8,128)(2,1)S(1)} %get-tuple-element.212.refs_0_), channel_id=1, source_target_pairs={{0,24},{4,28},{8,16},{12,20},{16,8},{20,12},{24,0},{28,4},{1,25},{... | collective-permute-start | bytes 270344 | tf_op jit(solution)/shard_map/ppermute | solution.py:669
  95.9 5.0 %collective-permute-start.35 = (bf16[256,256]{1,0:T(8,128)(2,1)S(1)}, bf16[256,256]{1,0:T(8,128)(2,1)S(1)}, u32[]{:S(2)}, u32[]{:S(2)}) collective-permute-start(bf16[256,256]{1,0:T(8,128)(2,1)S(1)} %get-tuple-element.221.high), channel_id=1, source_target_pairs={{0,16},{4,20},{8,24},{12,28},{16,0},{20,4},{24,8},{28,12},{1,17},{... | collective-permute-start | bytes 393224 | tf_op jit(solution)/shard_map/ppermute | solution.py:669
  97.2 3.7 %collective-permute-start.34 = (bf16[176,256]{1,0:T(8,128)(2,1)S(1)}, bf16[176,256]{1,0:T(8,128)(2,1)S(1)}, u32[]{:S(2)}, u32[]{:S(2)}) collective-permute-start(bf16[176,256]{1,0:T(8,128)(2,1)S(1)} %get-tuple-element.220.low), channel_id=1, source_target_pairs={{0,8},{4,12},{8,0},{12,4},{16,24},{20,28},{24,16},{28,20},{1,9},{5... | collective-permute-start | bytes 270344 | tf_op jit(solution)/shard_map/ppermute | solution.py:669
  100.9 3.9 %collective-permute-start.37 = (bf16[256,256]{1,0:T(8,128)(2,1)S(1)}, bf16[256,256]{1,0:T(8,128)(2,1)S(1)}, u32[]{:S(2)}, u32[]{:S(2)}) collective-permute-start(bf16[256,256]{1,0:T(8,128)(2,1)S(1)} %get-tuple-element.223.high), channel_id=1, source_target_pairs={{0,8},{4,12},{8,0},{12,4},{16,24},{20,28},{24,16},{28,20},{1,9},{5... | collective-permute-start | bytes 393224 | tf_op jit(solution)/shard_map/ppermute | solution.py:669
  101.2 3.4 %collective-permute-start.36 = (bf16[176,256]{1,0:T(8,128)(2,1)S(1)}, bf16[176,256]{1,0:T(8,128)(2,1)S(1)}, u32[]{:S(2)}, u32[]{:S(2)}) collective-permute-start(bf16[176,256]{1,0:T(8,128)(2,1)S(1)} %get-tuple-element.222.low), channel_id=1, source_target_pairs={{0,16},{4,20},{8,24},{12,28},{16,0},{20,4},{24,8},{28,12},{1,17},{... | collective-permute-start | bytes 270344 | tf_op jit(solution)/shard_map/ppermute | solution.py:669
  104.8 5.0 %collective-permute-start.38 = (bf16[512,256]{1,0:T(8,128)(2,1)S(1)}, bf16[512,256]{1,0:T(8,128)(2,1)S(1)}, u32[]{:S(2)}, u32[]{:S(2)}) collective-permute-start(bf16[512,256]{1,0:T(8,128)(2,1)S(1)} %get-tuple-element.224.high), channel_id=1, source_target_pairs={{0,4},{4,0},{8,12},{12,8},{16,20},{20,16},{24,28},{28,24},{1,5},{5... | collective-permute-start | bytes 786440 | tf_op jit(solution)/shard_map/ppermute | solution.py:669
  108.3 1.3 %collective-permute-start.31 = (bf16[176,256]{1,0:T(8,128)(2,1)S(1)}, bf16[176,256]{1,0:T(8,128)(2,1)S(1)}, u32[]{:S(2)}, u32[]{:S(2)}) collective-permute-start(bf16[176,256]{1,0:T(8,128)(2,1)S(1)} %four_sum.1.low), channel_id=1, source_target_pairs={{0,4},{4,0},{8,12},{12,8},{16,20},{20,16},{24,28},{28,24},{1,5},{5... | collective-permute-start | bytes 270344 | tf_op jit(solution)/shard_map/ppermute | solution.py:669
  108.4 1.4 %collective-permute-start.39 = (bf16[176,256]{1,0:T(8,128)(2,1)S(1)}, bf16[176,256]{1,0:T(8,128)(2,1)S(1)}, u32[]{:S(2)}, u32[]{:S(2)}) collective-permute-start(bf16[176,256]{1,0:T(8,128)(2,1)S(1)} %get-tuple-element.225.late), channel_id=1, source_target_pairs={{0,4},{4,0},{8,12},{12,8},{16,20},{20,16},{24,28},{28,24},{1,5},{5... | collective-permute-start | bytes 270344 | tf_op jit(solution)/shard_map/ppermute | solution.py:669
